TPU v7x, 32 devices: a whole 2x2x4 slice. The times are simulated.
32 devices in a mesh: dp: 8 (over z, x), tensor: 4 (over y, core).
Axes of the slice: x: 2, y: 2, z: 4, core: 2. Of those that a mesh axis runs over, the one named last changes fastest.
Arguments:
- tokens: bfloat16 [512, 64, 768], P('tensor', 'dp'), may hold values from -6 to 6
- w_qkv: bfloat16 [768, 3, 768], P('dp', None, 'tensor'), may hold values from -0.21875 to 0.21875
- b_qv: bfloat16 [2, 12, 64], P(None, 'tensor', 'dp'), may hold values from -2 to 2
- w_out: bfloat16 [768, 768], P('tensor', 'dp'), may hold values from -1.75 to 1.75
- w_up: bfloat16 [768, 3072], P('dp', 'tensor'), may hold values from -0.21875 to 0.21875
- b_up: bfloat16 [48, 64], P('tensor', 'dp'), may hold values from -2 to 2
- w_down: bfloat16 [3072, 768], P('tensor', 'dp'), may hold values from -0.109375 to 0.109375
- ln_gains: bfloat16 [2, 768], P(None, 'dp'), may hold values from 0.25 to 1.75
- shifts: bfloat16 [4, 768], P(None, 'dp'), may hold values from -2 to 2
- lengths: int32 [64], P('dp'), may hold values from 170 to 512, as said below
- segments: int32 [64, 512], P('dp'), may hold values from 0 to 3, as said below
- pair_ids: int32 [256], replicated, may hold values from 0 to 255, each once
- targets: float32 [128], replicated, may hold values from 0 to 1
Outputs:
- hidden_out: bfloat16 [512, 64, 768], P('tensor', 'dp')
- grad_tokens: bfloat16 [512, 64, 768], P('tensor', 'dp')
- grad_w_qkv: float32 [768, 3, 768], P('dp', None, 'tensor')
- grad_b_qv: float32 [2, 12, 64], P(None, 'tensor', 'dp')
- grad_w_out: float32 [768, 768], P('tensor', 'dp')
- grad_w_up: float32 [768, 3072], P('dp', 'tensor')
- grad_b_up: float32 [48, 64], P('tensor', 'dp')
- grad_w_down: float32 [3072, 768], P('tensor', 'dp')
- grad_ln_gains: float32 [2, 768], P(None, ('dp', 'tensor'))
- grad_shifts: float32 [4, 768], P(None, ('dp', 'tensor'))
Inputs may be any that keep to these rules, and one draw needn't show every extreme that they name: Rows are grouped by length: the rows of a higher index of dp are drawn from a range of longer lengths; in every index of dp some row has length 448 or more; some row of the batch has length 512. `segments`: ids never fall along a row; every sentence has one or more positions below its row's length; positions at or after the length carry the id 4 - 1.
All inputs are finite; a program needn't handle non-finite values.
Results may differ from a plain program's by a relative error of at most 0.018.
Values may be sent and summed in bfloat16 or wider, within the bound.
No kernel may reach another device: no remote copies, remote signals or barrier semaphores. Data moves between devices by JAX's collectives and lax.ppermute only.
A program may use at most 192 MiB of HBM per device.

v0:
```python
import functools
import math

import jax
import jax.numpy as jnp
import numpy as np
from jax import lax
from jax.experimental import pallas as pl
from jax.experimental.pallas import tpu as pltpu
from jax.sharding import PartitionSpec as P

SEGS = 4
EPS_NORM = 1e-05
EPS_COS = 1e-06
LOSS_SCALE = 4096.0
NEG = -1e30
DEAD = 99

BF = jnp.bfloat16
F32 = jnp.float32
MIB = 1024 * 1024
SHARE = 0.05


def dot(a, b, ca, cb):
    return lax.dot_general(a, b, (((ca,), (cb,)), ((), ())), preferred_element_type=F32)


def nn(a, b):
    return dot(a, b, 1, 0)


def nt(a, b):
    return dot(a, b, 1, 1)


def tn(a, b):
    return dot(a, b, 0, 0)


def call(kernel, grid, ins, outs, scratch=(), limit=60, cost=1.0, scalars=0, after=()):
    def spec(shape, block, index):
        if block is None:
            zeros = (0,) * len(shape)
            return pl.BlockSpec(shape, lambda *_: zeros)
        return pl.BlockSpec(block, index)

    in_specs = [spec(a.shape, b, m) for a, b, m in ins[scalars:]]
    out_specs = [spec(s, b, m) for s, _, b, m in outs]
    flops = int(cost * SHARE * 1.15e9)
    body, known = kernel, len(ins)
    if after:
        in_specs += [pl.BlockSpec(memory_space=pl.ANY)] * len(after)

        def body(*refs):
            return kernel(*refs[:known], *refs[known + len(after) :])

    return pl.pallas_call(
        body,
        grid_spec=pltpu.PrefetchScalarGridSpec(
            num_scalar_prefetch=scalars,
            grid=grid,
            in_specs=in_specs,
            out_specs=out_specs,
            scratch_shapes=list(scratch),
        ),
        out_shape=[jax.ShapeDtypeStruct(s, d) for s, d, _, _ in outs],
        compiler_params=pltpu.CompilerParams(
            dimension_semantics=("arbitrary",) * len(grid), vmem_limit_bytes=limit * MIB
        ),
        cost_estimate=pl.CostEstimate(flops=flops, bytes_accessed=1024, transcendentals=0),
    )(*[a for a, _, _ in ins], *after)


def gate(arrays, after):
    n = len(arrays)
    anywhere = pl.BlockSpec(memory_space=pl.ANY)
    return pl.pallas_call(
        lambda *refs: None,
        in_specs=[anywhere] * (n + len(after)),
        out_specs=[anywhere] * n,
        out_shape=[jax.ShapeDtypeStruct(a.shape, a.dtype) for a in arrays],
        input_output_aliases={i: i for i in range(n)},
        cost_estimate=pl.CostEstimate(flops=1, bytes_accessed=1, transcendentals=0),
    )(*arrays, *after)


def deal_kernel(t_ref, tok_ref, *out_refs):
    size = tok_ref.shape[0]
    parts = len(out_refs)
    rows, block = out_refs[0].shape[0], out_refs[0].shape[1]
    t = t_ref[0]
    m = lax.broadcasted_iota(jnp.int32, (size, size), 0)
    n = lax.broadcasted_iota(jnp.int32, (size, size), 1)
    part, row, place = m // (rows * block), (m // block) % rows, m % block
    source = place * (parts * rows) + jnp.bitwise_xor(part, t) * rows + row
    pick = jnp.where(source == n, 1.0, 0.0).astype(BF)
    moved = nn(pick, tok_ref[...]).astype(BF)
    for j, out in enumerate(out_refs):
        for r in range(rows):
            at = (j * rows + r) * block
            out[r] = moved[at : at + block]


def collect_kernel(t_ref, *refs):
    *in_refs, out_ref = refs
    size = out_ref.shape[0]
    parts = len(in_refs)
    rows, block = in_refs[0].shape[0], in_refs[0].shape[1]
    t = t_ref[0]
    m = lax.broadcasted_iota(jnp.int32, (size, size), 1)
    n = lax.broadcasted_iota(jnp.int32, (size, size), 0)
    part, row, place = m // (rows * block), (m // block) % rows, m % block
    target = place * (parts * rows) + jnp.bitwise_xor(part, t) * rows + row
    pick = jnp.where(target == n, 1.0, 0.0).astype(BF)
    joined = jnp.concatenate([ref[r] for ref in in_refs for r in range(rows)], axis=0)
    out_ref[...] = nn(pick, joined).astype(BF)


def stack_kernel(*refs):
    *ins, out_ref = refs
    for i, ref in enumerate(ins):
        out_ref[i] = ref[...]


def merge_kernel(here_ref, own_ref, other_ref, out_ref):
    depth, rows = own_ref.shape[0], own_ref.shape[1]
    lo = here_ref[0]
    for z in range(depth):
        at = lax.rem(z + depth - here_ref[1], depth)
        mine, theirs = own_ref[at], other_ref[at]
        for b in range(2):
            at = (2 * z + b) * rows
            out_ref[at : at + rows, :] = jnp.where(lo == b, mine, theirs)


def attn_fwd_kernel(parts, *refs):
    x_refs, refs = refs[:parts], refs[parts:]
    w_ref, sqv_ref, kc_ref, qc_ref, qkv_ref, p_ref, o_ref, *refs = refs
    *x_out, bias_ref, mask_ref = refs
    local = o_ref.shape[2]
    heads = p_ref.shape[1]
    hd = local // heads

    @pl.when(pl.program_id(0) == 0)
    def _():
        bias_ref[...] = tn(w_ref[:, 3 * local :][:, :8], sqv_ref[...])

    x = x_refs[0][0]
    if parts > 1:
        x = jnp.concatenate([ref[0] for ref in x_refs], axis=0)
        x_out[0][0] = x
    kc, qc = kc_ref[0], qc_ref[0]
    allowed = (kc == qc) | ((qc == DEAD) & (kc >= 0))
    mask_ref[...] = jnp.where(allowed, 0.0, NEG)

    projected = nn(x, w_ref[:, : 3 * local])
    q_all = ((projected[:, :local] + bias_ref[0:1, :local]) * 0.125).astype(BF)
    k_all = projected[:, local : 2 * local].astype(BF)
    v_all = (projected[:, 2 * local :] + bias_ref[0:1, local:]).astype(BF)
    qkv_ref[0, :, :local] = q_all
    qkv_ref[0, :, local : 2 * local] = k_all
    qkv_ref[0, :, 2 * local :] = v_all
    outs = []
    for h in range(heads):
        at = slice(h * hd, (h + 1) * hd)
        s = nt(q_all[:, at], k_all[:, at]) + mask_ref[...]
        top = jnp.max(s, axis=-1, keepdims=True)
        e = jnp.exp(s - top)
        total = jnp.sum(e, axis=-1, keepdims=True)
        p = (e * (1.0 / total)).astype(BF)
        p_ref[0, h] = p
        outs.append(nn(p, v_all[:, at]).astype(BF))
    o_ref[0] = jnp.concatenate(outs, axis=1)


def norm(z):
    centred = z - jnp.mean(z, axis=-1, keepdims=True)
    rstd = lax.rsqrt(jnp.mean(centred * centred, axis=-1, keepdims=True) + EPS_NORM)
    return centred * rstd, rstd


def norm_back(dy, xh, rstd, gain):
    dxh = dy * gain
    mean = jnp.mean(dxh, axis=-1, keepdims=True)
    proj = jnp.mean(dxh * xh, axis=-1, keepdims=True)
    return rstd * (dxh - mean - xh * proj)


def out_kernel(o0, o1, o2, o3, x_ref, sup_ref, w0, w1, w2, w3, xh_ref, rstd_ref, u_ref, small_ref, bup_ref):
    local = o0.shape[1]
    width = x_ref.shape[1]
    ws = (w0, w1, w2, w3)

    @pl.when(pl.program_id(0) == 0)
    def _():
        eye = (
            lax.broadcasted_iota(jnp.int32, (width, width), 0)
            == lax.broadcasted_iota(jnp.int32, (width, width), 1)
        ).astype(BF)
        small_ref[...] = tn(w0[:, local:][:, :8], eye)
        for j in range(4):
            bup_ref[j] = tn(ws[j][:, local:][:, :8], sup_ref[...])

    a = nt(o0[...], w0[:, :local])
    for w, o in ((w1, o1), (w2, o2), (w3, o3)):
        a += nt(o[...], w[:, :local])
    z = x_ref[...].astype(F32) + (a + small_ref[2:3])
    xh, rstd = norm(z)
    xh_ref[...] = xh
    rstd_ref[...] = rstd
    u_ref[...] = (xh * small_ref[0:1] + small_ref[3:4]).astype(BF)


def turned(a):
    rows = a.shape[1]
    eye = (
        lax.broadcasted_iota(jnp.int32, (rows, rows), 0) == lax.broadcasted_iota(jnp.int32, (rows, rows), 1)
    ).astype(BF)
    return nt(eye, a).astype(BF)


def pack_one_kernel(w_ref, extra_ref, piece_ref):
    piece_ref[...] = jnp.concatenate([w_ref[...], extra_ref[...]], axis=1)


def pack_two_kernel(up_ref, out_ref, extra_ref, piece_ref):
    hidden = up_ref.shape[1]
    piece_ref[0, :, :hidden] = up_ref[...]
    piece_ref[0, :, hidden:] = jnp.concatenate([turned(out_ref[...]), extra_ref[...]], axis=1)


def pack_three_kernel(a_ref, piece_ref):
    piece_ref[0] = turned(a_ref[...])


def gelu_parts(e):
    size = jnp.abs(e)
    density = jnp.exp(-0.5 * e * e)
    t = 1.0 / (1.0 + (0.3275911 / math.sqrt(2.0)) * size)
    poly = t * (
        0.5 * 0.254829592
        + t * (0.5 * -0.284496736 + t * (0.5 * 1.421413741 + t * (0.5 * -1.453152027 + t * (0.5 * 1.061405429))))
    )
    tail = poly * density
    cdf = jnp.where(e < 0, tail, 1.0 - tail)
    return e * cdf, cdf + e * (density * (1.0 / math.sqrt(2.0 * math.pi)))


def up_kernel(u_ref, bup_ref, w0, w1, w2, w3, h_ref, g_ref):
    u = u_ref[...]
    for j, w in enumerate((w0, w1, w2, w3)):
        e = nn(u, w[...]) + bup_ref[j, 6:7]
        h, g = gelu_parts(e)
        h_ref[j] = h.astype(BF)
        g_ref[j] = g.astype(BF)


def split3(v):
    a = v.astype(BF)
    rest = v - a.astype(F32)
    b = rest.astype(BF)
    c = (rest - b.astype(F32)).astype(BF)
    return a, b, c


def down_kernel(
    h_ref, xh1_ref, small_ref, code_ref, inv_ref, w0, w1, w2, w3,
    xh_ref, rstd_ref, y0, y1, y2, y3, pool_ref, acc_ref,
):
    y_refs = (y0, y1, y2, y3)
    step = pl.program_id(0)

    @pl.when(step == 0)
    def _():
        acc_ref[...] = jnp.zeros_like(acc_ref)

    f = nt(h_ref[0], w0[...])
    for j, w in ((1, w1), (2, w2), (3, w3)):
        f += nt(h_ref[j], w[...])
    first = xh1_ref[...] * small_ref[0:1] + small_ref[3:4]
    xh, rstd = norm(first + (f + small_ref[4:5]))
    y2 = xh * small_ref[1:2] + small_ref[5:6]
    xh_ref[...] = xh
    rstd_ref[...] = rstd
    low = y2.astype(BF)
    size = y_refs[0].shape[1]
    here = low.shape[0] // size
    for j, ref in enumerate(y_refs):

        @pl.when(lax.rem(step, 4 // here) == j // here)
        def _():
            ref[0] = low[(j % here) * size : (j % here + 1) * size]

    member = (lax.broadcasted_iota(jnp.int32, (8, y2.shape[0]), 0) == code_ref[...]).astype(BF)
    a, b, c = split3(y2)
    acc_ref[...] += nn(member, a) + nn(member, b) + nn(member, c)

    @pl.when(step == pl.num_programs(0) - 1)
    def _():
        low = (acc_ref[...] * inv_ref[...]).astype(BF)

        def put(i, carry):
            pool_ref[i] = low
            return carry

        lax.fori_loop(0, pool_ref.shape[0], put, 0)


def loss_grad(pooled_ref, ids_ref, mate_ref, target_ref, inv_ref):
    pooled = pooled_ref[...]
    places = lax.broadcasted_iota(jnp.int32, (8, pooled.shape[0]), 1)
    first = nn((places == ids_ref[...]).astype(BF), pooled)
    second = nn((places == mate_ref[...]).astype(BF), pooled)
    inner = jnp.sum(first * second, axis=-1, keepdims=True)
    ra = lax.rsqrt(jnp.sum(first * first, axis=-1, keepdims=True) + EPS_COS)
    rb = lax.rsqrt(jnp.sum(second * second, axis=-1, keepdims=True) + EPS_COS)
    missed = inner * ra * rb - target_ref[...]
    grad = (2.0 * LOSS_SCALE) * missed * (second * (ra * rb) - first * (inner * rb * ra * ra * ra))
    return grad * inv_ref[...]


def rowsum(v):
    return jnp.sum(v, axis=0, keepdims=True)


def feed_back_kernel(
    pooled_ref, ids_ref, mate_ref, target_ref, inv_ref, code_ref, xh_ref, rstd_ref, small_ref, w0, w1, w2, w3, g_ref,
    df_ref, dz_ref, de_ref, sum_ref, bup_ref, gp_ref,
):
    step = pl.program_id(0)

    @pl.when(step == 0)
    def _():
        grad = loss_grad(pooled_ref, ids_ref, mate_ref, target_ref, inv_ref)
        for i, part in enumerate(split3(grad)):
            gp_ref[i] = part
        sum_ref[...] = jnp.zeros_like(sum_ref)
        bup_ref[...] = jnp.zeros_like(bup_ref)

    member = (lax.broadcasted_iota(jnp.int32, (8, xh_ref.shape[0]), 0) == code_ref[...]).astype(BF)
    dy = tn(member, gp_ref[0]) + tn(member, gp_ref[1]) + tn(member, gp_ref[2])
    xh = xh_ref[...]
    dz = norm_back(dy, xh, rstd_ref[...], small_ref[1:2])
    sum_ref[0:1] += rowsum(dy * xh)
    sum_ref[1:2] += rowsum(dy)
    sum_ref[2:3] += rowsum(dz)
    df = dz.astype(BF)
    df_ref[...] = df
    dz_ref[...] = dz
    for j, w in enumerate((w0, w1, w2, w3)):
        de = (nn(df, w[...]) * g_ref[j].astype(F32)).astype(BF)
        de_ref[j] = de
        bup_ref[j, 0:1] += rowsum(de.astype(F32))


def norm_back_kernel(
    de_ref, dz2_ref, xh_ref, rstd_ref, small_ref, w0, w1, w2, w3, o0, o1, o2, o3, dz_ref, da_ref, do_ref, sum_ref
):
    @pl.when(pl.program_id(0) == 0)
    def _():
        sum_ref[...] = jnp.zeros_like(sum_ref)

    dy = nt(de_ref[0], w0[...])
    for j, w in ((1, w1), (2, w2), (3, w3)):
        dy += nt(de_ref[j], w[...])
    dy = dz2_ref[...] + dy
    xh = xh_ref[...]
    dz = norm_back(dy, xh, rstd_ref[...], small_ref[0:1])
    sum_ref[0:1] += rowsum(dy * xh)
    sum_ref[1:2] += rowsum(dy)
    sum_ref[2:3] += rowsum(dz)
    da = dz.astype(BF)
    dz_ref[...] = dz
    da_ref[...] = da
    for j, w in enumerate((o0, o1, o2, o3)):
        do_ref[j] = nn(da, w[:, : do_ref.shape[2]]).astype(BF)


def pieces(grad, here_ref, ref, at):
    depth, rows = ref.shape[1], ref.shape[2]
    lo = here_ref[0]
    low = grad.astype(BF)
    for z in range(depth):
        first, second = (low[(2 * z + b) * rows : (2 * z + b + 1) * rows] for b in range(2))
        ref[0, z, :, at] = jnp.where(lo == 0, first, second)
        ref[1, z, :, at] = jnp.where(lo == 0, second, first)


def grad_send_kernel(here_ref, *refs):
    *ins, send_ref = refs
    at = 0
    for grad in (tn(a[...], b[0]) for a, b in zip(ins[::2], ins[1::2])):
        pieces(grad, here_ref, send_ref.at[0], slice(at, at + grad.shape[1]))
        at += grad.shape[1]


def grad_keep_kernel(by_row, here_ref, *refs):
    *ins, got_ref, stay_ref, fly_ref = refs
    depth, rows = got_ref.shape[2], got_ref.shape[3]
    lo = here_ref[0]
    j = pl.program_id(0)
    at = 0
    for grad in (tn(a[...], b[0]) for a, b in zip(ins[::2], ins[1::2])):
        cols = slice(at, at + grad.shape[1])
        for z in range(depth):
            first, second = (grad[(2 * z + b) * rows : (2 * z + b + 1) * rows] for b in range(2))
            mine, theirs = jnp.where(lo == 0, first, second), jnp.where(lo == 0, second, first)
            mine = (mine + got_ref[0, 0, z, :, cols].astype(F32)).astype(BF)
            theirs = (theirs + got_ref[0, 1, z, :, cols].astype(F32)).astype(BF)
            if by_row:
                stay_ref[0, z, :, cols] = mine
                fly_ref[0, z, :, cols] = theirs
            else:

                @pl.when(j == 0)
                def _():
                    stay_ref[0, z, :, cols] = mine
                    stay_ref[1, z, :, cols] = theirs

                @pl.when(j == 1)
                def _():
                    fly_ref[0, z, :, cols] = mine
                    fly_ref[1, z, :, cols] = theirs

        at += grad.shape[1]


def attn_bwd_kernel(
    here_ref, qkv_ref, p_ref, o_ref, do_ref, x_ref, da_ref, w_ref, dxin_ref, piece_ref, sum_ref, *refs
):
    *dx_refs, acc_ref = refs
    r = pl.program_id(0)
    local = o_ref.shape[2]
    heads = p_ref.shape[1]
    hd = local // heads
    q_all, k_all, v_all = (qkv_ref[0, :, i * local : (i + 1) * local] for i in range(3))
    o_all, do_all = o_ref[0], do_ref[0]
    prod = o_all.astype(F32) * do_all.astype(F32)
    dq, dk, dv = [], [], []
    for h in range(heads):
        at = slice(h * hd, (h + 1) * hd)
        p = p_ref[0, h]
        do = do_all[:, at]
        dv.append(tn(do, p))
        dp = nt(do, v_all[:, at])
        mid = jnp.sum(prod[:, at], axis=-1, keepdims=True)
        ds = (p.astype(F32) * (dp - mid)).astype(BF)
        dq.append(nn(ds, k_all[:, at]))
        dk.append(tn(q_all[:, at], ds))
    dq = (jnp.concatenate(dq, axis=1).astype(BF).astype(F32) * 0.125).astype(BF)
    dkv = jnp.concatenate(dk + dv, axis=0).astype(BF).astype(F32)
    dkv = jnp.transpose(dkv).astype(BF)
    dproj = jnp.concatenate([dq, dkv], axis=1)
    sums = rowsum(dproj.astype(F32))
    grad = jnp.concatenate([tn(x_ref[0], dproj), tn(da_ref[0], o_all)], axis=1)

    @pl.when(r == 0)
    def _():
        acc_ref[...] = grad
        sum_ref[...] = jnp.broadcast_to(sums, sum_ref.shape)

    @pl.when(r > 0)
    def _():
        acc_ref[...] += grad
        sum_ref[...] += jnp.broadcast_to(sums, sum_ref.shape)

    @pl.when(r == pl.num_programs(0) - 1)
    def _():
        pieces(acc_ref[...], here_ref, piece_ref, slice(0, acc_ref.shape[1]))

    dx = dxin_ref[0] + nt(dproj, w_ref[:, : 3 * local])
    if len(dx_refs) == 1:
        dx_refs[0][0] = dx
    else:
        low = dx.astype(BF)
        size = dx_refs[0].shape[1]
        for j, ref in enumerate(dx_refs):
            ref[0] = low[j * size : (j + 1) * size]


def make(mesh):
    nd, ntens = mesh.shape["dp"], mesh.shape["tensor"]
    nh = nd // 2
    groups = [[2 * z + b for z in range(nh)] for b in range(2)]

    def across(array, axis, bit):
        size = nd if axis == "dp" else ntens
        return lax.ppermute(array, axis, [(i, i ^ bit) for i in range(size)])

    def along(array):
        return lax.all_to_all(array, "dp", 0, 0, tiled=True, axis_index_groups=groups)

    def turn(array, k):
        return lax.ppermute(array, "dp", [(2 * ((z + k) % nh) + b, 2 * z + b) for z in range(nh) for b in range(2)])

    def swap(array):
        return across(array, "tensor", 1)

    def total(*arrays):
        out = arrays[0].astype(F32)
        for a in arrays[1:]:
            out = out + a.astype(F32)
        return out

    def settle(array):
        return jnp.sum(array.astype(F32), axis=0)

    def shards(
        tokens, w_qkv, b_qv, w_out, w_up, b_up, w_down, ln_gains, shifts, lengths, segments, pair_ids, targets
    ):
        part_len, row_count, width = tokens.shape
        rb = w_up.shape[0]
        hidden = w_up.shape[1]
        local = w_qkv.shape[2]
        hb = b_up.shape[1]
        hd = hb * nd
        heads = local // hd
        seq = segments.shape[1]
        rows = row_count // ntens
        count = rows * seq
        sents = rows * SEGS
        blk = 256
        steps = count // blk
        t = lax.axis_index("tensor")
        d = lax.axis_index("dp")
        fused = rb % 16 == 0
        depth, rbk = (nh, rb) if fused else (1, width // 2)
        lo_bit = (d % 2 if fused else d * 0).astype(jnp.int32)
        turned_by = (d // 2 if nh <= 4 else d * 0).astype(jnp.int32)
        here, here_first = jnp.stack([lo_bit, lo_bit * 0]), jnp.stack([lo_bit, turned_by])
        t_arr = t.astype(jnp.int32).reshape(1)

        def merged(own, other, after=(), place=here):
            if not fused:
                first = jnp.where(d % 2 == 0, own, other)
                second = jnp.where(d % 2 == 0, other, own)
                return jnp.stack([first, second], axis=1).reshape(width, own.shape[2])
            columns = own.shape[2]
            return call(
                merge_kernel,
                (1,),
                [(place, None, None), (own, None, None), (other, None, None)],
                [((width, columns), BF, None, None)],
                scalars=1,
                after=after,
                cost=1.0,
                limit=16,
            )[0]

        def pack(kernel, arrays, columns, after):
            return call(
                kernel,
                (nh,),
                [(a, None, None) for a in arrays],
                [((nh, rb, columns), BF, (1, rb, columns), lambda i: (i, 0, 0))],
                after=after,
                limit=16,
            )[0]

        def cut(array):
            if fused:
                return array
            lead = array.shape[:-4]
            full = array.reshape(*lead, nh, 2, rb, array.shape[-1])
            first, second = full[..., 0, :, :], full[..., 1, :, :]
            return jnp.stack(
                [jnp.where(d % 2 == 0, first, second), jnp.where(d % 2 == 0, second, first)], axis=len(lead)
            )

        def uncut(array):
            if fused:
                return array
            mine, theirs = array[..., 0, :, :, :], array[..., 1, :, :, :]
            first, second = jnp.where(d % 2 == 0, mine, theirs), jnp.where(d % 2 == 0, theirs, mine)
            return jnp.stack([first, second], axis=-3).reshape(*array.shape[:-4], 2, 1, width // 2, array.shape[-1])

        deal_block = blk // row_count
        dealt = call(
            deal_kernel,
            (part_len // deal_block,),
            [(t_arr, None, None), (tokens.reshape(part_len * row_count, width), (blk, width), lambda i, *_: (i, 0))],
            [((rows, part_len, width), BF, (rows, deal_block, width), lambda i, *_: (0, i, 0))] * ntens,
            scalars=1,
            cost=2.0,
            limit=16,
        )
        x_parts = [dealt[0]] + [across(dealt[j], "tensor", j) for j in range(1, ntens)]

        qv_col = jnp.pad(b_qv.reshape(-1, 1), ((0, rb - b_qv.size), (0, 63)))
        wide = 3 * local + 64
        (first_piece,) = call(
            pack_one_kernel,
            (1,),
            [(w_qkv.reshape(rb, 3 * local), None, None), (qv_col, None, None)],
            [((rb, wide), BF, None, None)],
            limit=16,
        )
        if nh <= 4:
            pieces1 = [first_piece] + [turn(first_piece, k) for k in range(1, nh)]
            own1 = call(
                stack_kernel,
                (1,),
                [(p, None, None) for p in pieces1],
                [((nh, rb, wide), BF, None, None)],
                after=[dealt[1]],
                limit=16,
            )[0]
        else:
            own1 = along(jnp.broadcast_to(first_piece[None], (nh, rb, wide)))
        lo1 = across(own1, "dp", 1)
        w1 = {0: merged(own1, lo1, place=here_first)}
        w1[1] = swap(w1[0])
        w1[2] = across(w1[0], "tensor", 2)
        extra = jnp.concatenate([ln_gains.T, shifts.T, b_up.reshape(-1, 1), jnp.zeros((rb, 57), BF)], axis=1)
        second_piece = pack(pack_two_kernel, [w_up, w_out, extra], hidden + 256, [dealt[1]])
        (second_piece,) = gate([second_piece], [lo1])
        own2 = along(second_piece)
        third_piece = pack(pack_three_kernel, [w_down], hidden, [dealt[1]])

        mine = lax.dynamic_slice_in_dim(segments, t * rows, rows, 0).reshape(rows, ntens, part_len)
        own_len = lax.dynamic_slice_in_dim(lengths, t * rows, rows, 0)
        seg = jnp.stack([lax.dynamic_index_in_dim(mine, t ^ j, 1, False) for j in range(ntens)], axis=1)
        place = jnp.stack([(t ^ j) * part_len + jnp.arange(part_len) for j in range(ntens)])
        live = (place[None] < own_len[:, None, None]).reshape(rows, seq)
        seg = seg.reshape(rows, seq)
        key_code = jnp.where(live, seg, -1)
        query_code = jnp.where(live, seg, DEAD)
        sent_code = jnp.where(live, seg + SEGS * jnp.arange(rows)[:, None], -1).reshape(1, count)
        member = (key_code[:, None, :] == jnp.arange(SEGS)[None, :, None]).astype(F32)
        inv_count = (1.0 / jnp.sum(member, axis=2)).reshape(sents, 1)
        own_ids = (d * row_count + t * rows) * SEGS + jnp.arange(sents, dtype=jnp.int32)
        is_mine = pair_ids[None, :] == own_ids[:, None]
        mates = pair_ids.reshape(-1, 2)[:, ::-1].reshape(-1)
        mate = jnp.sum(jnp.where(is_mine, mates[None, :], 0), axis=1, keepdims=True)
        goal = jnp.sum(jnp.where(is_mine, jnp.repeat(targets, 2)[None, :], 0.0), axis=1, keepdims=True)
        own_ids = own_ids[:, None]

        k = np.arange(width)
        dd, within = k // rb, k % rb
        up_at = (within // hb) * hd + dd * hb + within % hb
        sup = np.zeros((width, width), np.float32)
        sup[k, up_at] = 1.0
        qv = within < 2 * heads * hb
        qv_at = (within // (heads * hb)) * local + ((within // hb) % heads) * hd + dd * hb + within % hb
        sqv = np.zeros((width, 2 * local), np.float32)
        sqv[k[qv], qv_at[qv]] = 1.0
        sup, sqv = jnp.asarray(sup, BF), jnp.asarray(sqv, BF)

        def whole(array):
            return (array, None, None)

        def whole_out(shape, dtype):
            return (shape, dtype, None, None)

        def attend(xs, w, before):
            outs = [
                ((rows, seq, 3 * local), BF, (1, seq, 3 * local), lambda r, *_: (r, 0, 0)),
                ((rows, heads, seq, seq), BF, (1, heads, seq, seq), lambda r, *_: (r, 0, 0, 0)),
                ((rows, seq, local), BF, (1, seq, local), lambda r, *_: (r, 0, 0)),
            ]
            if len(xs) > 1:
                outs.append(((rows, seq, width), BF, (1, seq, width), lambda r, *_: (r, 0, 0)))
            return call(
                functools.partial(attn_fwd_kernel, len(xs)),
                (rows,),
                [(a, (1,) + a.shape[1:], lambda r, *_: (r, 0, 0)) for a in xs]
                + [
                    whole(w),
                    whole(sqv),
                    (key_code.reshape(rows, 1, seq), (1, 1, seq), lambda r, *_: (r, 0, 0)),
                    (query_code.reshape(rows, seq, 1), (1, seq, 1), lambda r, *_: (r, 0, 0)),
                ],
                outs,
                scratch=[pltpu.VMEM((8, 2 * local), F32), pltpu.VMEM((seq, seq), F32)],
                after=before,
                cost=9.0,
            )

        kept = {}
        *kept[0], x = attend(x_parts, w1[0], [second_piece])
        (own2,) = gate([own2], [kept[0][2]])
        lo2 = across(own2, "dp", 1)
        (third_piece,) = gate([third_piece], [own2])
        own3 = along(third_piece)
        kept[1] = attend([x], w1[1], [own2])
        (w1[2],) = gate([w1[2]], [kept[1][2]])
        far2 = across(own2, "tensor", 2)
        w1[3] = swap(w1[2])
        kept[2] = attend([x], w1[2], [])
        own3, lo2 = gate([own3, lo2], [kept[2][2]])
        lo3 = across(own3, "dp", 1)
        w2 = {0: merged(own2, lo2)}
        w2[1] = swap(w2[0])
        kept[3] = attend([x], w1[3], [own3, w2[0]])
        (far2,) = gate([far2], [kept[3][2]])
        far_lo2 = across(far2, "dp", 1)
        (lo3,) = gate([lo3], [kept[3][2]])
        w3 = {0: merged(own3, lo3, [far2])}
        w3[2] = across(w3[0], "tensor", 2)
        w3[1], w3[3] = swap(w3[0]), swap(w3[2])
        w2[2] = merged(far2, far_lo2, [w3[0]])
        w2[3] = swap(w2[2])
        ws2, ws3 = [w2[j] for j in range(4)], [w3[j] for j in range(4)]
        o_parts = [kept[j][2].reshape(count, local) for j in range(4)]
        x_flat = x.reshape(count, width)

        def rows_of(array, *lead):
            if array.ndim == 3:
                return (array, (array.shape[0], blk, array.shape[2]), lambda i, *_: (0, i, 0))
            return (array, (blk, array.shape[1]), lambda i, *_: (i, 0))

        def rows_out(shape, dtype):
            if len(shape) == 3:
                return (shape, dtype, (shape[0], blk, shape[2]), lambda i, *_: (0, i, 0))
            return (shape, dtype, (blk, shape[1]), lambda i, *_: (i, 0))

        ups = [(w, (width, hidden), lambda i, *_: (0, 0)) for w in ws2]
        outs_w = [(w, (width, 256), lambda i, *_: (0, hidden // 256)) for w in ws2]
        xh1, rstd1, u, small, bup_rows = call(
            out_kernel,
            (steps,),
            [rows_of(o) for o in o_parts] + [rows_of(x_flat), whole(sup)] + outs_w,
            [
                rows_out((count, width), F32),
                rows_out((count, 1), F32),
                rows_out((count, width), BF),
                whole_out((8, width), F32),
                whole_out((4, 8, hidden), F32),
            ],
            cost=8.0,
        )
        h, g = call(
            up_kernel,
            (steps,),
            [rows_of(u), whole(bup_rows)] + ups,
            [rows_out((4, count, hidden), BF), rows_out((4, count, hidden), BF)],
            cost=20.0,
        )
        code_spec = (sent_code, (1, blk), lambda i, *_: (0, i))
        span = blk // part_len
        part_out = lambda i, *_: (i * span // ntens, 0, 0)
        xh2, rstd2, y0, y1, y2, y3, pooled = call(
            down_kernel,
            (steps,),
            [rows_of(h), rows_of(xh1), whole(small), code_spec, whole(inv_count)] + [whole(w) for w in ws3],
            [rows_out((count, width), F32), rows_out((count, 1), F32)]
            + [((rows, part_len, width), BF, (1, part_len, width), part_out)] * ntens
            + [whole_out((nd * ntens, sents, width), BF)],
            scratch=[pltpu.VMEM((sents, width), F32)],
            cost=14.0,
        )

        def send_back(parts):
            return [parts[0]] + [across(parts[j], "tensor", j) for j in range(1, ntens)]

        def collected(parts, after=()):
            (out,) = call(
                collect_kernel,
                (part_len // deal_block,),
                [whole(t_arr)] + [(a, (rows, deal_block, width), lambda i, *_: (0, i, 0)) for a in parts],
                [((part_len * row_count, width), BF, (blk, width), lambda i, *_: (i, 0))],
                scalars=1,
                after=after,
                cost=2.0,
                limit=16,
            )
            return out.reshape(part_len, row_count, width)

        every = lax.all_to_all(pooled, ("dp", "tensor"), 0, 0, tiled=True).reshape(nd * ntens * sents, width)

        df, dz2, de, sums2, dbup = call(
            feed_back_kernel,
            (steps,),
            [whole(every), whole(own_ids), whole(mate), whole(goal), whole(inv_count), code_spec]
            + [rows_of(xh2), rows_of(rstd2), whole(small)]
            + [whole(w) for w in ws3]
            + [rows_of(g)],
            [
                rows_out((count, width), BF),
                rows_out((count, width), F32),
                rows_out((4, count, hidden), BF),
                whole_out((8, width), F32),
                whole_out((4, 8, hidden), F32),
            ],
            scratch=[pltpu.VMEM((3, sents, width), BF)],
            cost=14.0,
        )

        hidden_parts = send_back([y0, y1, y2, y3])

        def grad_part(a, b, odd, kernel, got, outs, after):
            return call(
                kernel,
                (2,),
                [whole(here), whole(a), (b, (1,) + b.shape[1:], lambda j, *_: (2 * j + odd, 0, 0))]
                + [(v, (1,) + v.shape[1:], lambda j, *_: (j, 0, 0, 0, 0)) for v in got],
                outs,
                scalars=1,
                after=after,
                cost=5.0,
            )

        shape = (2, 2, depth, rbk, hidden)
        half = (2,) + shape[2:]
        both_out = [(shape, BF, (1,) + shape[1:], lambda j, *_: (j, 0, 0, 0, 0))]
        (send3,) = grad_part(df, h, 1, grad_send_kernel, [], both_out, [])
        (sendu,) = grad_part(u, de, 1, grad_send_kernel, [], both_out, [send3])
        got = uncut(swap(cut(send3)))
        stay3, fly3 = grad_part(
            df, h, 0, functools.partial(grad_keep_kernel, True), [got],
            [(half, BF, (1,) + half[1:], lambda j, *_: (j, 0, 0, 0))] * 2, [sendu],
        )
        if not fused:
            both = cut(jnp.stack([stay3, fly3], axis=1))
            stay3, fly3 = both[:, 0], both[:, 1]
        got = uncut(swap(cut(sendu)))
        stayu, flyu = grad_part(
            u, de, 0, functools.partial(grad_keep_kernel, False), [got], [whole_out(half, BF)] * 2, [fly3]
        )
        stayu, flyu = cut(stayu), cut(flyu)
        got3x = across(fly3, "dp", 1)
        gotuy = across(flyu, "tensor", 2)

        dz1, da, do, sums1 = call(
            norm_back_kernel,
            (steps,),
            [rows_of(de), rows_of(dz2), rows_of(xh1), rows_of(rstd1), whole(small)] + ups + outs_w,
            [
                rows_out((count, width), F32),
                rows_out((count, width), BF),
                rows_out((4, count, local), BF),
                whole_out((8, width), F32),
            ],
            after=[flyu],
            cost=15.0,
        )

        do_rows = do.reshape(4, rows, seq, local)
        da_rows = da.reshape(rows, seq, width)
        per = lambda r, *_: (r, 0, 0)
        grad_cols = 4 * local

        def attend_back(j, dx, after):
            qkv, p, o = kept[j]
            if j > 0:
                dx_out = [((rows, seq, width), F32, (1, seq, width), per)]
            else:
                dx_out = [((rows, part_len, width), BF, (1, part_len, width), per)] * ntens
            piece, sums, *dx = call(
                attn_bwd_kernel,
                (rows,),
                [
                    whole(here),
                    (qkv, (1, seq, 3 * local), per),
                    (p, (1, heads, seq, seq), lambda r, *_: (r, 0, 0, 0)),
                    (o, (1, seq, local), per),
                    (do_rows[j], (1, seq, local), per),
                    (x, (1, seq, width), per),
                    (da_rows, (1, seq, width), per),
                    whole(w1[j]),
                    (dx, (1, seq, width), per),
                ],
                [whole_out((2, depth, rbk, grad_cols), BF), whole_out((8, 3 * local), F32)] + dx_out,
                scratch=[pltpu.VMEM((width, grad_cols), F32)],
                scalars=1,
                after=after,
                cost=14.0,
            )
            return cut(piece), sums, (dx[0] if j > 0 else dx)

        sums_of = {}
        back3, sums_of[3], dx = attend_back(3, dz1.reshape(rows, seq, width), [])
        got_far = swap(back3)
        got3x, gotuy = gate([got3x, gotuy], [back3])
        turn3 = total(stay3[1], got3x[1]).astype(BF)
        turnu = total(stayu[1], gotuy[1]).astype(BF)
        got3y = across(turn3, "tensor", 2)
        gotux = across(turnu, "dp", 1)
        back2, sums_of[2], dx = attend_back(2, dx, [turn3, turnu])
        got3y, gotux = gate([got3y, gotux], [back2])
        last3 = total(stay3[0], got3x[0], got3y).astype(BF)
        lastu = total(stayu[0], gotuy[0], gotux).astype(BF)
        end = along(jnp.concatenate([last3, lastu], axis=2))
        hidden_out = collected(hidden_parts, [back2])
        fly1 = total(back2[1], got_far[1]).astype(BF)
        got_fly1 = across(fly1, "dp", 1)
        back1, sums_of[1], dx = attend_back(1, dx, [last3, lastu, fly1, hidden_out])
        got_near = swap(back1)
        (got_fly1,) = gate([got_fly1], [back1])
        turn1 = total(back2[0], got_far[0], got_fly1).astype(BF)
        got_turn1 = across(turn1, "tensor", 2)
        back0, sums_of[0], dx_parts = attend_back(0, dx, [turn1])
        got1 = across(total(back0[1], got_near[1]).astype(BF), "dp", 1)
        grad_tokens = collected(send_back(dx_parts))
        (end,) = gate([end], [back0])
        got1, got_turn1 = gate([got1, got_turn1], [grad_tokens])
        last1 = total(back0[0], got_near[0], got1, got_turn1).astype(BF)

        def to_axes(rows_by_d):
            order = jnp.arange(ntens) ^ t
            return jnp.take(rows_by_d, order, axis=0).transpose(1, 0, 2)

        sums = jnp.stack([sums_of[j][0] for j in range(4)])
        qv_sum = jnp.stack([sums[:, :local], sums[:, 2 * local :]], axis=1)
        qv_sum = qv_sum.reshape(4, 2 * heads, nd, hb).transpose(0, 2, 1, 3).reshape(4, nd, 2 * heads * hb)
        up_sum = dbup[:, 0].reshape(4, hidden // hd, nd, hb).transpose(0, 2, 1, 3).reshape(4, nd, -1)
        norms = jnp.stack([sums1[0], sums2[0], sums1[2], sums1[1], sums2[2], sums2[1]])
        norms = norms.reshape(6, nd, ntens, -1).transpose(1, 2, 0, 3).reshape(nd, ntens, -1)
        message = jnp.concatenate([to_axes(qv_sum), to_axes(up_sum), norms], axis=2)
        (message,) = gate([message.reshape(nd * ntens, 1, -1)], [end])
        message = lax.all_to_all(message, ("dp", "tensor"), 0, 0, tiled=True)
        (last1,) = gate([last1], [message])
        grad_one = settle(along(last1))
        end = settle(end)
        grad_down, grad_up = end[:, :hidden], end[:, hidden:]
        got = jnp.sum(message, axis=(0, 1))
        n1 = qv_sum.shape[2]
        n2 = n1 + up_sum.shape[2]
        grad_b_qv = got[:n1].reshape(2, heads, hb)
        grad_b_up = got[n1:n2].reshape(hidden // hd, hb)
        rest = got[n2:].reshape(6, -1)
        return (
            hidden_out,
            grad_tokens,
            grad_one[:, : 3 * local].reshape(rb, 3, local),
            grad_b_qv,
            grad_one[:, 3 * local :].T,
            grad_up,
            grad_b_up,
            grad_down.T,
            rest[:2],
            rest[2:],
        )

    return shards


def solution(mesh):
    return jax.shard_map(
        make(mesh),
        mesh=mesh,
        in_specs=(
            P("tensor", "dp", None),
            P("dp", None, "tensor"),
            P(None, "tensor", "dp"),
            P("tensor", "dp"),
            P("dp", "tensor"),
            P("tensor", "dp"),
            P("tensor", "dp"),
            P(None, "dp"),
            P(None, "dp"),
            P("dp"),
            P("dp", None),
            P(),
            P(),
        ),
        out_specs=(
            P("tensor", "dp", None),
            P("tensor", "dp", None),
            P("dp", None, "tensor"),
            P(None, "tensor", "dp"),
            P("tensor", "dp"),
            P("dp", "tensor"),
            P("tensor", "dp"),
            P("tensor", "dp"),
            P(None, ("dp", "tensor")),
            P(None, ("dp", "tensor")),
        ),
        check_vma=False,
    )
```

profile of v0, /device:TPU:0, one launch (start us, length us, event | category | flops | bytes accessed | tf_op | source)
XLA Modules:
  0.0 421.7 jit_solution(1429546525399303194)
XLA Ops:
  2.8 5.1 %collective-permute-start.3 = (bf16[96,640]{1,0:T(8,128)(2,1)S(1)}, bf16[96,640]{1,0:T(8,128)(2,1)S(1)}, u32[]{:S(2)}, u32[]{:S(2)}) collective-permute-start(bf16[96,640]{1,0:T(8,128)(2,1)S(1)} %shard_map.223.refs_0_), channel_id=1, source_target_pairs={{8,0},{12,4},{16,8},{20,12},{24,16},{28,20},{0,24},{4,28},{9,1},{1... | collective-permute-start | bytes 368648 | tf_op jit(solution)/shard_map/ppermute | solution.py:495
  8.8 1.4 copy-done.21
  10.2 1.2 shard_map.222
  11.5 6.9 %collective-permute-done.4.refs_2_ = bf16[96,640]{1,0:T(8,128)(2,1)S(1)} collective-permute-done((bf16[96,640]{1,0:T(8,128)(2,1)S(1)}, bf16[96,640]{1,0:T(8,128)(2,1)S(1)}, u32[]{:S(2)}, u32[]{:S(2)}) %collective-permute-start.4) | collective-permute-done | bytes 122912 | tf_op jit(solution)/shard_map/ppermute | solution.py:495
  18.5 1.6 collective-permute-start.6
  20.0 1.5 collective-permute-start.1
  26.1 4.9 %collective-permute-done.6.other_ref.refs_1_ = bf16[4,96,640]{2,1,0:T(8,128)(2,1)S(1)} collective-permute-done((bf16[4,96,640]{2,1,0:T(8,128)(2,1)S(1)}, bf16[4,96,640]{2,1,0:T(8,128)(2,1)S(1)}, u32[]{:S(2)}, u32[]{:S(2)}) %collective-permute-start.6) | collective-permute-done | bytes 491552 | tf_op jit(solution)/shard_map/ppermute | solution.py:489
  31.8 4.3 %all-to-all-start = ((bf16[4,96,1024]{2,1,0:T(8,128)(2,1)}), bf16[4,96,1024]{2,1,0:T(8,128)(2,1)}, u32[]{:S(2)}, u32[]{:S(2)}) async-start(bf16[4,96,1024]{2,1,0:T(8,128)(2,1)} %shard_map.227.refs_8_), calls=%async_computation | async-start | bytes 1572864 | tf_op jit(solution)/shard_map/all_to_all | solution.py:492
  39.9 1.6 collective-permute-start.8
  44.0 9.8 %shard_map.228 = (bf16[2,512,576]{2,1,0:T(8,128)(2,1)}, bf16[2,3,512,512]{3,2,1,0:T(8,128)(2,1)}, bf16[2,512,192]{2,1,0:T(8,128)(2,1)}, bf16[2,512,768]{2,1,0:T(8,128)(2,1)}) custom-call(bf16[2,128,768]{2,1,0:T(8,128)(2,1)} %copy-done.22, bf16[2,128,768]{2,1,0:T(8,128)(2,1)} %copy-done.47, bf16[2,128,768]{2,1,0:T(8,128)(2,1)} %collective-permute-done.1.refs_2_, ...), custom_call_target="tpu_custom_call" | custom-call | flops 517500000 | bytes 1024 | tf_op jit(solution)/shard_map/pallas_call | solution.py:58
  53.7 1.5 all-to-all-done.refs_0_
  55.3 3.7 all-to-all-start.1
  59.0 1.6 collective-permute-start.10
  60.6 9.3 %shard_map.230 = (bf16[2,512,576]{2,1,0:T(8,128)(2,1)}, bf16[2,3,512,512]{3,2,1,0:T(8,128)(2,1)}, bf16[2,512,192]{2,1,0:T(8,128)(2,1)}) custom-call(bf16[2,512,768]{2,1,0:T(8,128)(2,1)} %get-tuple-element.82.refs_0_.x_ref.refs_5_, bf16[768,640]{1,0:T(8,128)(2,1)} %collective-permute-done.7.refs_1_.refs_7_, bf16[768,384]{1,0:T(8,128)(2,1)} %constant.96.clone.refs_5_.refs_2_, ...), custom_call_target="tpu_custom_call" | custom-call | flops 517500000 | bytes 1024 | tf_op jit(solution)/shard_map/pallas_call | solution.py:58
  70.0 1.5 collective-permute-start.12
  71.5 9.3 %shard_map.232 = (bf16[2,512,576]{2,1,0:T(8,128)(2,1)}, bf16[2,3,512,512]{3,2,1,0:T(8,128)(2,1)}, bf16[2,512,192]{2,1,0:T(8,128)(2,1)}) custom-call(bf16[2,512,768]{2,1,0:T(8,128)(2,1)} %get-tuple-element.82.refs_0_.x_ref.refs_5_, bf16[768,640]{1,0:T(8,128)(2,1)} %shard_map.231.refs_1_.refs_7_, bf16[768,384]{1,0:T(8,128)(2,1)} %constant.96.clone.refs_5_.refs_2_, ...), custom_call_target="tpu_custom_call" | custom-call | flops 517500000 | bytes 1024 | tf_op jit(solution)/shard_map/pallas_call | solution.py:58
  82.5 1.1 copy-done.16
  83.6 1.8 shard_map.236.refs_6_.w0.refs_5_.refs_9_
  85.4 1.1 copy-done.2
  87.5 9.3 %shard_map.237 = (bf16[2,512,576]{2,1,0:T(8,128)(2,1)}, bf16[2,3,512,512]{3,2,1,0:T(8,128)(2,1)}, bf16[2,512,192]{2,1,0:T(8,128)(2,1)}) custom-call(bf16[2,512,768]{2,1,0:T(8,128)(2,1)} %get-tuple-element.82.refs_0_.x_ref.refs_5_, bf16[768,640]{1,0:T(8,128)(2,1)} %copy-done.37, bf16[768,384]{1,0:T(8,128)(2,1)} %constant.96.clone.refs_5_.refs_2_, ...), custom_call_target="tpu_custom_call" | custom-call | flops 517500000 | bytes 1024 | tf_op jit(solution)/shard_map/pallas_call | solution.py:58
  97.7 1.5 collective-permute-start.13
  101.1 1.6 shard_map.240.refs_3_.w0
  103.3 14.1 %collective-permute-done.13.refs_2_ = bf16[4,96,1024]{2,1,0:T(8,128)(2,1)} collective-permute-done((bf16[4,96,1024]{2,1,0:T(8,128)(2,1)}, bf16[4,96,1024]{2,1,0:T(8,128)(2,1)}, u32[]{:S(2)}, u32[]{:S(2)}) %collective-permute-start.13) | collective-permute-done | bytes 786464 | tf_op jit(solution)/shard_map/ppermute | solution.py:489
  117.4 1.8 shard_map.241.w2.refs_7_.refs_11_
  119.8 10.7 %collective-permute-done.17.w2 = bf16[768,768]{1,0:T(8,128)(2,1)} collective-permute-done((bf16[768,768]{1,0:T(8,128)(2,1)}, bf16[768,768]{1,0:T(8,128)(2,1)}, u32[]{:S(2)}, u32[]{:S(2)}) %collective-permute-start.17) | collective-permute-done | bytes 1179680 | tf_op jit(solution)/shard_map/ppermute | solution.py:489
  132.1 8.6 %shard_map.242 = (f32[1024,768]{1,0:T(8,128)}, f32[1024,1]{1,0:T(8,128)}, bf16[1024,768]{1,0:T(8,128)(2,1)}, f32[8,768]{1,0:T(8,128)}, f32[4,8,768]{2,1,0:T(8,128)}) custom-call(bf16[1024,192]{1,0:T(8,128)(2,1)} %bitcast.100, bf16[1024,192]{1,0:T(8,128)(2,1)} %bitcast.98, bf16[1024,192]{1,0:T(8,128)(2,1)} %bitcast.99, bf16[1024,192]{1,0:T(8,128)(2,1)} %bitcast.93, ...), custom_call_target="tpu_custom_call" | custom-call | flops 460000000 | bytes 1024 | tf_op jit(solution)/shard_map/pallas_call | solution.py:58
  140.7 19.1 %shard_map.243 = (bf16[4,1024,768]{2,1,0:T(8,128)(2,1)}, bf16[4,1024,768]{2,1,0:T(8,128)(2,1)}) custom-call(bf16[1024,768]{1,0:T(8,128)(2,1)} %get-tuple-element.88.u_ref.refs_1_, f32[4,8,768]{2,1,0:T(8,128)} %get-tuple-element.89.bup_ref, bf16[768,1024]{1,0:T(8,128)(2,1)} %copy-done.2, bf16[768,1024]{1,0:T(8,128)(2,1)} %collective-permute-done.11.w1.refs_6_.refs_10_, ...), custom_call_target="tpu_custom_call" | custom-call | flops 1150000000 | bytes 1024 | tf_op jit(solution)/shard_map/pallas_call | solution.py:58
  159.8 13.9 %shard_map.244 = (f32[1024,768]{1,0:T(8,128)}, f32[1024,1]{1,0:T(8,128)}, bf16[2,128,768]{2,1,0:T(8,128)(2,1)}, bf16[2,128,768]{2,1,0:T(8,128)(2,1)}, bf16[2,128...) custom-call(bf16[4,1024,768]{2,1,0:T(8,128)(2,1)} %get-tuple-element.90.h_ref.refs_1_.refs_2_, ...), custom_call_target="tpu_custom_call" | custom-call | flops 805000000 | bytes 1024 | tf_op jit(solution)/shard_map/pallas_call | solution.py:58
  173.6 4.7 %all-to-all-start.2 = ((bf16[32,8,768]{2,1,0:T(8,128)(2,1)}), bf16[32,8,768]{2,1,0:T(8,128)(2,1)S(1)}, u32[]{:S(2)}, u32[]{:S(2)}) async-start(bf16[32,8,768]{2,1,0:T(8,128)(2,1)} %get-tuple-element.99), calls=%async_computation.2 | async-start | bytes 786432 | tf_op jit(solution)/shard_map/all_to_all | solution.py:770
  181.3 10.2 %all-to-all-done.2 = bf16[32,8,768]{2,1,0:T(8,128)(2,1)S(1)} async-done(((bf16[32,8,768]{2,1,0:T(8,128)(2,1)}), bf16[32,8,768]{2,1,0:T(8,128)(2,1)S(1)}, u32[]{:S(2)}, u32[]{:S(2)}) %all-to-all-start.2) | async-done | bytes 393248 | tf_op jit(solution)/shard_map/all_to_all | solution.py:770
  192.3 14.2 %shard_map.245 = (bf16[1024,768]{1,0:T(8,128)(2,1)}, f32[1024,768]{1,0:T(8,128)}, bf16[4,1024,768]{2,1,0:T(8,128)(2,1)}, f32[8,768]{1,0:T(8,128)}, f32[4,8,768]{2,1,0:T(8,128)}) custom-call(bf16[256,768]{1,0:T(8,128)(2,1)} %bitcast.106, s32[8,1]{1,0:T(8,128)} %iota_add_fusion.ids_ref, s32[8,1]{1,0:T(8,128)} %copy.119.mate_ref, f32[8,1]{1,0:T(8,128)} %copy.120.target_ref, ...), custom_call_target="tpu_custom_call" | custom-call | flops 805000000 | bytes 1024 | tf_op jit(solution)/shard_map/pallas_call | solution.py:58
  206.5 6.5 %shard_map.246.refs_3_ = bf16[2,2,4,96,768]{4,3,2,1,0:T(8,128)(2,1)} custom-call(s32[2]{0:T(128)} %copy-done.26, bf16[1024,768]{1,0:T(8,128)(2,1)} %get-tuple-element.106.refs_0_.refs_1_, bf16[4,1024,768]{2,1,0:T(8,128)(2,1)} %get-tuple-element.90.h_ref.refs_1_.refs_2_), custom_call_target="tpu_custom_call" | custom-call | flops 287500000 | bytes 1024 | tf_op jit(solution)/shard_map/pallas_call | solution.py:58
  213.0 6.5 %shard_map.247.refs_4_ = bf16[2,2,4,96,768]{4,3,2,1,0:T(8,128)(2,1)} custom-call(s32[2]{0:T(128)} %copy-done.26, bf16[1024,768]{1,0:T(8,128)(2,1)} %get-tuple-element.88.u_ref.refs_1_, bf16[4,1024,768]{2,1,0:T(8,128)(2,1)} %get-tuple-element.103.refs_2_.refs_0_, bf16[2,2,4,96,768]{4,3,2,1,0:T(8,128)(2,1)} %shard_map.246.refs_3_), custom_call_target="tpu_custom_call" | custom-call | flops 287500000 | bytes 1024 | tf_op jit(solution)/shard_map/pallas_call | solution.py:58
  220.1 1.4 copy-done.41
  221.4 6.9 %shard_map.248 = (bf16[2,4,96,768]{3,2,1,0:T(8,128)(2,1)}, bf16[2,4,96,768]{3,2,1,0:T(8,128)(2,1)}) custom-call(s32[2]{0:T(128)} %copy-done.26, bf16[1024,768]{1,0:T(8,128)(2,1)} %get-tuple-element.106.refs_0_.refs_1_, bf16[4,1024,768]{2,1,0:T(8,128)(2,1)} %get-tuple-element.90.h_ref.refs_1_.refs_2_, bf16[2,2,4,96,768]{4,3,2,1,0:T(8,128)(2,1)} %copy-done.41, ...), custom_call_target="tpu_custom_call" | custom-call | flops 287500000 | bytes 1024 | tf_op jit(solution)/shard_map/pallas_call | solution.py:58
  229.4 8.1 %shard_map.249 = (bf16[2,4,96,768]{3,2,1,0:T(8,128)(2,1)}, bf16[2,4,96,768]{3,2,1,0:T(8,128)(2,1)}) custom-call(s32[2]{0:T(128)} %copy-done.26, bf16[1024,768]{1,0:T(8,128)(2,1)} %get-tuple-element.88.u_ref.refs_1_, bf16[4,1024,768]{2,1,0:T(8,128)(2,1)} %get-tuple-element.103.refs_2_.refs_0_, bf16[2,2,4,96,768]{4,3,2,1,0:T(8,128)(2,1)} %collective-permute-done.22.refs_3_, ...), custom_call_target="tpu_custom_call" | custom-call | flops 287500000 | bytes 1024 | tf_op jit(solution)/shard_map/pallas_call | solution.py:58
  238.4 16.2 %shard_map.250 = (f32[1024,768]{1,0:T(8,128)}, bf16[1024,768]{1,0:T(8,128)(2,1)}, bf16[4,1024,192]{2,1,0:T(8,128)(2,1)}, f32[8,768]{1,0:T(8,128)}) custom-call(bf16[4,1024,768]{2,1,0:T(8,128)(2,1)} %get-tuple-element.103.refs_2_.refs_0_, f32[1024,768]{1,0:T(8,128)} %get-tuple-element.104.refs_1_, f32[1024,768]{1,0:T(8,128)} %get-tuple-element.91.xh1_ref.refs_2_, ...), custom_call_target="tpu_custom_call" | custom-call | flops 862499968 | bytes 1024 | tf_op jit(solution)/shard_map/pallas_call | solution.py:58
  254.6 2.9 fusion.14
  257.5 14.8 %shard_map.251 = (bf16[2,4,96,768]{3,2,1,0:T(8,128)(2,1)}, f32[8,576]{1,0:T(8,128)}, f32[2,512,768]{2,1,0:T(8,128)}) custom-call(s32[2]{0:T(128)} %copy-done.26, bf16[2,512,576]{2,1,0:T(8,128)(2,1)} %get-tuple-element.111.qkv_ref, bf16[2,3,512,512]{3,2,1,0:T(8,128)(2,1)} %get-tuple-element.112.p_ref, bf16[2,512,192]{2,1,0:T(8,128)(2,1)} %get-tuple-element.87.refs_1_.o_ref, ...), custom_call_target="tpu_custom_call" | custom-call | flops 805000000 | bytes 1024 | tf_op jit(solution)/shard_map/pallas_call | solution.py:58
  275.9 1.5 fusion.5.refs_9_
  278.5 1.2 fusion.6.refs_10_
  281.4 14.7 %shard_map.253 = (bf16[2,4,96,768]{3,2,1,0:T(8,128)(2,1)}, f32[8,576]{1,0:T(8,128)}, f32[2,512,768]{2,1,0:T(8,128)}) custom-call(s32[2]{0:T(128)} %copy-done.26, bf16[2,512,576]{2,1,0:T(8,128)(2,1)} %get-tuple-element.97.refs_1_, bf16[2,3,512,512]{3,2,1,0:T(8,128)(2,1)} %get-tuple-element.98.refs_2_, bf16[2,512,192]{2,1,0:T(8,128)(2,1)} %get-tuple-element.84.refs_2_.refs_3_, ...), custom_call_target="tpu_custom_call" | custom-call | flops 805000000 | bytes 1024 | tf_op jit(solution)/shard_map/pallas_call | solution.py:58
  296.2 1.3 copy-done.6
  297.5 2.4 shard_map.254
  299.9 2.0 fusion.7.refs_11_
  301.9 3.3 collective-permute-done.26.refs_0_
  305.2 2.4 fusion.4.refs_9_
  307.7 2.2 fusion.3.refs_10_
  309.8 15.0 %shard_map.256 = (bf16[2,4,96,768]{3,2,1,0:T(8,128)(2,1)}, f32[8,576]{1,0:T(8,128)}, f32[2,512,768]{2,1,0:T(8,128)}) custom-call(s32[2]{0:T(128)} %copy-done.26, bf16[2,512,576]{2,1,0:T(8,128)(2,1)} %get-tuple-element.123.refs_1_, bf16[2,3,512,512]{3,2,1,0:T(8,128)(2,1)} %get-tuple-element.124.refs_2_, ...), custom_call_target="tpu_custom_call" | custom-call | flops 805000000 | bytes 1024 | tf_op jit(solution)/shard_map/pallas_call | solution.py:58
  328.6 3.7 all-to-all-start.3
  333.2 9.5 %collective-permute-done.29.refs_0_ = bf16[4,96,768]{2,1,0:T(8,128)(2,1)} collective-permute-done((bf16[4,96,768]{2,1,0:T(8,128)(2,1)S(1)}, bf16[4,96,768]{2,1,0:T(8,128)(2,1)}, u32[]{:S(2)}, u32[]{:S(2)}) %collective-permute-start.29) | collective-permute-done | bytes 589856 | tf_op jit(solution)/shard_map/ppermute | solution.py:489
  342.7 2.3 fusion.2.refs_9_
  346.0 14.7 %shard_map.258 = (bf16[2,4,96,768]{3,2,1,0:T(8,128)(2,1)}, f32[8,576]{1,0:T(8,128)}, bf16[2,128,768]{2,1,0:T(8,128)(2,1)}, bf16[2,128,768]{2,1,0:T(8,128)(2,1)},...) custom-call(s32[2]{0:T(128)} %copy-done.26, bf16[2,512,576]{2,1,0:T(8,128)(2,1)} %get-tuple-element.121.refs_1_, ...), custom_call_target="tpu_custom_call" | custom-call | flops 805000000 | bytes 1024 | tf_op jit(solution)/shard_map/pallas_call | solution.py:58
  360.8 2.2 fusion.8
  367.2 1.4 collective-permute-start.32
  373.0 5.9 %collective-permute-done.31.refs_2_ = bf16[2,128,768]{2,1,0:T(8,128)(2,1)S(1)} collective-permute-done((bf16[2,128,768]{2,1,0:T(8,128)(2,1)}, bf16[2,128,768]{2,1,0:T(8,128)(2,1)S(1)}, u32[]{:S(2)}, u32[]{:S(2)}) %collective-permute-start.31) | collective-permute-done | bytes 393248 | tf_op jit(solution)/shard_map/ppermute | solution.py:489
  378.9 7.7 %collective-permute-done.32.refs_3_ = bf16[2,128,768]{2,1,0:T(8,128)(2,1)S(1)} collective-permute-done((bf16[2,128,768]{2,1,0:T(8,128)(2,1)}, bf16[2,128,768]{2,1,0:T(8,128)(2,1)S(1)}, u32[]{:S(2)}, u32[]{:S(2)}) %collective-permute-start.32) | collective-permute-done | bytes 393248 | tf_op jit(solution)/shard_map/ppermute | solution.py:489
  386.5 2.4 shard_map.259
  389.0 2.6 all-to-all-start.4
  392.5 1.3 copy-done.32
  393.7 2.5 fusion.1.refs_0_
  396.3 2.7 all-to-all-done.4.refs_1_
  399.6 3.5 all-to-all-start.5
  407.0 12.4 %all-to-all-done.5 = bf16[4,96,768]{2,1,0:T(8,128)(2,1)S(1)} async-done(((bf16[4,96,768]{2,1,0:T(8,128)(2,1)}), bf16[4,96,768]{2,1,0:T(8,128)(2,1)S(1)}, u32[]{:S(2)}, u32[]{:S(2)}) %all-to-all-start.5) | async-done | bytes 589856 | tf_op jit(solution)/shard_map/all_to_all | solution.py:492
  (283 shorter events, 57.1 us)
Async XLA Ops:
  0.6 21.2 %copy-start = (s32[8,512]{1,0:T(8,128)S(1)}, s32[8,512]{1,0:T(8,128)}, u32[]{:S(2)}) copy-start(s32[8,512]{1,0:T(8,128)} %param.25) | copy-start | bytes 49156
  2.8 8.8 %collective-permute-start.3 = (bf16[96,640]{1,0:T(8,128)(2,1)S(1)}, bf16[96,640]{1,0:T(8,128)(2,1)S(1)}, u32[]{:S(2)}, u32[]{:S(2)}) collective-permute-start(bf16[96,640]{1,0:T(8,128)(2,1)S(1)} %shard_map.223.refs_0_), channel_id=1, source_target_pairs={{8,0},{12,4},{16,8},{20,12},{24,16},{28,20},{0,24},{4,28},{9,1},{1... | collective-permute-start | bytes 368648 | tf_op jit(solution)/shard_map/ppermute | solution.py:495
  7.8 10.6 %collective-permute-start.4 = (bf16[96,640]{1,0:T(8,128)(2,1)S(1)}, bf16[96,640]{1,0:T(8,128)(2,1)S(1)}, u32[]{:S(2)}, u32[]{:S(2)}) collective-permute-start(bf16[96,640]{1,0:T(8,128)(2,1)S(1)} %shard_map.223.refs_0_), channel_id=1, source_target_pairs={{16,0},{20,4},{24,8},{28,12},{0,16},{4,20},{8,24},{12,28},{17,1},{... | collective-permute-start | bytes 368648 | tf_op jit(solution)/shard_map/ppermute | solution.py:495
  7.8 10.6 %collective-permute-start.5 = (bf16[96,640]{1,0:T(8,128)(2,1)S(1)}, bf16[96,640]{1,0:T(8,128)(2,1)S(1)}, u32[]{:S(2)}, u32[]{:S(2)}) collective-permute-start(bf16[96,640]{1,0:T(8,128)(2,1)S(1)} %shard_map.223.refs_0_), channel_id=1, source_target_pairs={{24,0},{28,4},{0,8},{4,12},{8,16},{12,20},{16,24},{20,28},{25,1},{... | collective-permute-start | bytes 368648 | tf_op jit(solution)/shard_map/ppermute | solution.py:495
  10.2 11.7 %copy-start.52 = (bf16[12,8]{0,1:T(8,128)(2,1)S(1)}, bf16[12,8]{0,1:T(8,128)(2,1)}, u32[]{:S(2)}) copy-start(bf16[12,8]{0,1:T(8,128)(2,1)} %param.20) | copy-start | bytes 580
  11.5 13.2 %copy-start.22 = (bf16[2,128,768]{2,1,0:T(8,128)(2,1)}, bf16[2,128,768]{2,1,0:T(8,128)(2,1)S(1)}, u32[]{:S(2)}) copy-start(bf16[2,128,768]{2,1,0:T(8,128)(2,1)S(1)} %get-tuple-element.77.refs_0_) | copy-start | bytes 1179652
  11.5 12.4 %copy-start.25 = (bf16[96,768]{1,0:T(8,128)(2,1)S(1)}, bf16[96,768]{1,0:T(8,128)(2,1)}, u32[]{:S(2)}) copy-start(bf16[96,768]{1,0:T(8,128)(2,1)} %refs_0_.2) | copy-start | bytes 442372
  11.5 12.4 %copy-start.27 = (bf16[192,96]{1,0:T(8,128)(2,1)S(1)}, bf16[192,96]{1,0:T(8,128)(2,1)}, u32[]{:S(2)}) copy-start(bf16[192,96]{1,0:T(8,128)(2,1)} %refs_1_.1) | copy-start | bytes 110596
  18.5 12.5 %collective-permute-start.6 = (bf16[4,96,640]{2,1,0:T(8,128)(2,1)S(1)}, bf16[4,96,640]{2,1,0:T(8,128)(2,1)S(1)}, u32[]{:S(2)}, u32[]{:S(2)}) collective-permute-start(bf16[4,96,640]{2,1,0:T(8,128)(2,1)S(1)} %shard_map.224.own_ref), channel_id=1, source_target_pairs={{0,4},{4,0},{8,12},{12,8},{16,20},{20,16},{24,28},{28,24},{1,5},{5... | collective-permute-start | bytes 1474568 | tf_op jit(solution)/shard_map/ppermute | solution.py:489
  20.0 23.2 %collective-permute-start = (bf16[2,128,768]{2,1,0:T(8,128)(2,1)S(1)}, bf16[2,128,768]{2,1,0:T(8,128)(2,1)S(1)}, u32[]{:S(2)}, u32[]{:S(2)}) collective-permute-start(bf16[2,128,768]{2,1,0:T(8,128)(2,1)S(1)} %get-tuple-element.78.refs_4_.refs_3_.refs_1_), channel_id=1, source_target_pairs={{0,1},{1,0},{2,3},{3,2},{4,5},{5,4},{6,7},{7,6},{8,9},{9,8},{10,11... | collective-permute-start | bytes 1179656 | tf_op jit(solution)/shard_map/ppermute | solution.py:489
  20.0 23.2 %collective-permute-start.1 = (bf16[2,128,768]{2,1,0:T(8,128)(2,1)S(1)}, bf16[2,128,768]{2,1,0:T(8,128)(2,1)}, u32[]{:S(2)}, u32[]{:S(2)}) collective-permute-start(bf16[2,128,768]{2,1,0:T(8,128)(2,1)S(1)} %get-tuple-element.79), channel_id=1, source_target_pairs={{0,2},{1,3},{2,0},{3,1},{4,6},{5,7},{6,4},{7,5},{8,10},{9,11},{10,... | collective-permute-start | bytes 1179656 | tf_op jit(solution)/shard_map/ppermute | solution.py:489
  21.5 21.7 %collective-permute-start.2 = (bf16[2,128,768]{2,1,0:T(8,128)(2,1)S(1)}, bf16[2,128,768]{2,1,0:T(8,128)(2,1)}, u32[]{:S(2)}, u32[]{:S(2)}) collective-permute-start(bf16[2,128,768]{2,1,0:T(8,128)(2,1)S(1)} %get-tuple-element.80), channel_id=1, source_target_pairs={{0,3},{1,2},{2,1},{3,0},{4,7},{5,6},{6,5},{7,4},{8,11},{9,10},{10,... | collective-permute-start | bytes 1179656 | tf_op jit(solution)/shard_map/ppermute | solution.py:489
  31.8 5.0 %copy-start.20 = (bf16[4,96,640]{2,1,0:T(8,128)(2,1)S(1)}, bf16[4,96,640]{2,1,0:T(8,128)(2,1)}, u32[]{:S(2)}) copy-start(bf16[4,96,640]{2,1,0:T(8,128)(2,1)} %copy-done.19) | copy-start | bytes 1474564
  31.8 23.5 %all-to-all-start = ((bf16[4,96,1024]{2,1,0:T(8,128)(2,1)}), bf16[4,96,1024]{2,1,0:T(8,128)(2,1)}, u32[]{:S(2)}, u32[]{:S(2)}) async-start(bf16[4,96,1024]{2,1,0:T(8,128)(2,1)} %shard_map.227.refs_8_), calls=%async_computation | async-start | bytes 1572864 | tf_op jit(solution)/shard_map/all_to_all | solution.py:492
  37.4 5.8 %copy-start.10 = (bf16[768,640]{1,0:T(8,128)(2,1)}, bf16[768,640]{1,0:T(8,128)(2,1)S(1)}, u32[]{:S(2)}) copy-start(bf16[768,640]{1,0:T(8,128)(2,1)S(1)} %shard_map.225.refs_4_.refs_7_) | copy-start | bytes 2949124
  37.4 4.1 copy-start.53
  37.4 4.1 copy-start.54
  37.4 23.1 %collective-permute-start.7 = (bf16[768,640]{1,0:T(8,128)(2,1)S(1)}, bf16[768,640]{1,0:T(8,128)(2,1)}, u32[]{:S(2)}, u32[]{:S(2)}) collective-permute-start(bf16[768,640]{1,0:T(8,128)(2,1)S(1)} %shard_map.225.refs_4_.refs_7_), channel_id=1, source_target_pairs={{0,1},{1,0},{2,3},{3,2},{4,5},{5,4},{6,7},{7,6},{8,9},{9,8},{10,11... | collective-permute-start | bytes 2949128 | tf_op jit(solution)/shard_map/ppermute | solution.py:489
  37.6 5.6 %copy-start.49 = (s32[2]{0:T(128)}, s32[2]{0:T(128)S(1)}, u32[]{:S(2)}) copy-start(s32[2]{0:T(128)S(1)} %dynamic_slice.19) | copy-start | bytes 28
  39.9 30.0 %collective-permute-start.8 = (bf16[768,640]{1,0:T(8,128)(2,1)S(1)}, bf16[768,640]{1,0:T(8,128)(2,1)}, u32[]{:S(2)}, u32[]{:S(2)}) collective-permute-start(bf16[768,640]{1,0:T(8,128)(2,1)S(1)} %shard_map.225.refs_4_.refs_7_), channel_id=1, source_target_pairs={{0,2},{1,3},{2,0},{3,1},{4,6},{5,7},{6,4},{7,5},{8,10},{9,11},{10,... | collective-permute-start | bytes 2949128 | tf_op jit(solution)/shard_map/ppermute | solution.py:489
  55.3 25.5 %all-to-all-start.1 = ((bf16[4,96,768]{2,1,0:T(8,128)(2,1)}), bf16[4,96,768]{2,1,0:T(8,128)(2,1)S(1)}, u32[]{:S(2)}, u32[]{:S(2)}) async-start(bf16[4,96,768]{2,1,0:T(8,128)(2,1)} %shard_map.234), calls=%async_computation.1 | async-start | bytes 1179648 | tf_op jit(solution)/shard_map/all_to_all | solution.py:492
  59.0 21.8 %collective-permute-start.10 = (bf16[4,96,1024]{2,1,0:T(8,128)(2,1)}, bf16[4,96,1024]{2,1,0:T(8,128)(2,1)S(1)}, u32[]{:S(2)}, u32[]{:S(2)}) collective-permute-start(bf16[4,96,1024]{2,1,0:T(8,128)(2,1)} %shard_map.229.refs_5_.refs_1_.own_ref), channel_id=1, source_target_pairs={{0,4},{4,0},{8,12},{12,8},{16,20},{20,16},{24,28},{28,24},{1,5},{5... | collective-permute-start | bytes 2359304 | tf_op jit(solution)/shard_map/ppermute | solution.py:489
  69.9 16.7 %collective-permute-start.9 = (bf16[768,640]{1,0:T(8,128)(2,1)}, bf16[768,640]{1,0:T(8,128)(2,1)S(1)}, u32[]{:S(2)}, u32[]{:S(2)}) collective-permute-start(bf16[768,640]{1,0:T(8,128)(2,1)} %shard_map.231.refs_1_.refs_7_), channel_id=1, source_target_pairs={{0,1},{1,0},{2,3},{3,2},{4,5},{5,4},{6,7},{7,6},{8,9},{9,8},{10,11... | collective-permute-start | bytes 2949128 | tf_op jit(solution)/shard_map/ppermute | solution.py:489
  70.0 26.8 %collective-permute-start.12 = (bf16[4,96,1024]{2,1,0:T(8,128)(2,1)}, bf16[4,96,1024]{2,1,0:T(8,128)(2,1)S(1)}, u32[]{:S(2)}, u32[]{:S(2)}) collective-permute-start(bf16[4,96,1024]{2,1,0:T(8,128)(2,1)} %shard_map.229.refs_5_.refs_1_.own_ref), channel_id=1, source_target_pairs={{0,2},{1,3},{2,0},{3,1},{4,6},{5,7},{6,4},{7,5},{8,10},{9,11},{10,... | collective-permute-start | bytes 2359304 | tf_op jit(solution)/shard_map/ppermute | solution.py:489
  81.9 17.3 %collective-permute-start.14 = (bf16[4,96,768]{2,1,0:T(8,128)(2,1)}, bf16[4,96,768]{2,1,0:T(8,128)(2,1)S(1)}, u32[]{:S(2)}, u32[]{:S(2)}) collective-permute-start(bf16[4,96,768]{2,1,0:T(8,128)(2,1)} %get-tuple-element.85.refs_5_.refs_1_), channel_id=1, source_target_pairs={{0,4},{4,0},{8,12},{12,8},{16,20},{20,16},{24,28},{28,24},{1,5},{5... | collective-permute-start | bytes 1769480 | tf_op jit(solution)/shard_map/ppermute | solution.py:489
  82.5 34.9 %copy-start.26 = (s32[2]{0:T(128)}, s32[2]{0:T(128)S(1)}, u32[]{:S(2)}) copy-start(s32[2]{0:T(128)S(1)} %pad_add_fusion.2.here_ref.refs_0_) | copy-start | bytes 28
  97.7 19.6 %collective-permute-start.13 = (bf16[4,96,1024]{2,1,0:T(8,128)(2,1)}, bf16[4,96,1024]{2,1,0:T(8,128)(2,1)}, u32[]{:S(2)}, u32[]{:S(2)}) collective-permute-start(bf16[4,96,1024]{2,1,0:T(8,128)(2,1)} %shard_map.238.refs_3_.refs_1_), channel_id=1, source_target_pairs={{0,4},{4,0},{8,12},{12,8},{16,20},{20,16},{24,28},{28,24},{1,5},{5... | collective-permute-start | bytes 2359304 | tf_op jit(solution)/shard_map/ppermute | solution.py:489
  101.1 16.3 %copy-start.13 = (bf16[4,96,1024]{2,1,0:T(8,128)(2,1)S(1)}, bf16[4,96,1024]{2,1,0:T(8,128)(2,1)}, u32[]{:S(2)}) copy-start(bf16[4,96,1024]{2,1,0:T(8,128)(2,1)} %shard_map.238.refs_3_.refs_1_) | copy-start | bytes 2359300
  102.7 16.5 %copy-start.50 = (s32[2]{0:T(128)S(1)}, s32[2]{0:T(128)}, u32[]{:S(2)}) copy-start(s32[2]{0:T(128)} %copy-done.49) | copy-start | bytes 28
  102.7 27.8 %collective-permute-start.17 = (bf16[768,768]{1,0:T(8,128)(2,1)}, bf16[768,768]{1,0:T(8,128)(2,1)}, u32[]{:S(2)}, u32[]{:S(2)}) collective-permute-start(bf16[768,768]{1,0:T(8,128)(2,1)} %shard_map.240.refs_3_.w0), channel_id=1, source_target_pairs={{0,2},{1,3},{2,0},{3,1},{4,6},{5,7},{6,4},{7,5},{8,10},{9,11},{10,... | collective-permute-start | bytes 3538952 | tf_op jit(solution)/shard_map/ppermute | solution.py:489
  103.3 28.8 %collective-permute-start.11 = (bf16[768,1024]{1,0:T(8,128)(2,1)S(1)}, bf16[768,1024]{1,0:T(8,128)(2,1)}, u32[]{:S(2)}, u32[]{:S(2)}) collective-permute-start(bf16[768,1024]{1,0:T(8,128)(2,1)S(1)} %copy-done.3), channel_id=1, source_target_pairs={{0,1},{1,0},{2,3},{3,2},{4,5},{5,4},{6,7},{7,6},{8,9},{9,8},{10,11... | collective-permute-start | bytes 4718600 | tf_op jit(solution)/shard_map/ppermute | solution.py:489
  119.1 12.9 %copy-start.4 = (bf16[768,1024]{1,0:T(8,128)(2,1)}, bf16[768,1024]{1,0:T(8,128)(2,1)S(1)}, u32[]{:S(2)}) copy-start(bf16[768,1024]{1,0:T(8,128)(2,1)S(1)} %shard_map.241.w2.refs_7_.refs_11_) | copy-start | bytes 4718596
  119.1 12.9 %collective-permute-start.15 = (bf16[768,1024]{1,0:T(8,128)(2,1)S(1)}, bf16[768,1024]{1,0:T(8,128)(2,1)}, u32[]{:S(2)}, u32[]{:S(2)}) collective-permute-start(bf16[768,1024]{1,0:T(8,128)(2,1)S(1)} %shard_map.241.w2.refs_7_.refs_11_), channel_id=1, source_target_pairs={{0,1},{1,0},{2,3},{3,2},{4,5},{5,4},{6,7},{7,6},{8,9},{9,8},{10,11... | collective-permute-start | bytes 4718600 | tf_op jit(solution)/shard_map/ppermute | solution.py:489
  119.3 40.4 %collective-permute-start.16 = (bf16[768,768]{1,0:T(8,128)(2,1)}, bf16[768,768]{1,0:T(8,128)(2,1)}, u32[]{:S(2)}, u32[]{:S(2)}) collective-permute-start(bf16[768,768]{1,0:T(8,128)(2,1)} %shard_map.240.refs_3_.w0), channel_id=1, source_target_pairs={{0,1},{1,0},{2,3},{3,2},{4,5},{5,4},{6,7},{7,6},{8,9},{9,8},{10,11... | collective-permute-start | bytes 3538952 | tf_op jit(solution)/shard_map/ppermute | solution.py:489
  130.5 29.2 %collective-permute-start.18 = (bf16[768,768]{1,0:T(8,128)(2,1)}, bf16[768,768]{1,0:T(8,128)(2,1)}, u32[]{:S(2)}, u32[]{:S(2)}) collective-permute-start(bf16[768,768]{1,0:T(8,128)(2,1)} %collective-permute-done.17.w2), channel_id=1, source_target_pairs={{0,1},{1,0},{2,3},{3,2},{4,5},{5,4},{6,7},{7,6},{8,9},{9,8},{10,11... | collective-permute-start | bytes 3538952 | tf_op jit(solution)/shard_map/ppermute | solution.py:489
  159.7 18.7 %copy-start.48 = (s32[256]{0:T(256)S(1)}, s32[256]{0:T(256)}, u32[]{:S(2)}) copy-start(s32[256]{0:T(256)} %param.26) | copy-start | bytes 3076
  159.7 19.9 %copy-start.55 = (f32[128]{0:T(128)S(1)}, f32[128]{0:T(128)}, u32[]{:S(2)}) copy-start(f32[128]{0:T(128)} %param.27) | copy-start | bytes 1540
  173.6 17.9 %all-to-all-start.2 = ((bf16[32,8,768]{2,1,0:T(8,128)(2,1)}), bf16[32,8,768]{2,1,0:T(8,128)(2,1)S(1)}, u32[]{:S(2)}, u32[]{:S(2)}) async-start(bf16[32,8,768]{2,1,0:T(8,128)(2,1)} %get-tuple-element.99), calls=%async_computation.2 | async-start | bytes 786432 | tf_op jit(solution)/shard_map/all_to_all | solution.py:770
  213.0 7.0 %collective-permute-start.23 = (bf16[2,2,4,96,768]{4,3,2,1,0:T(8,128)(2,1)}, bf16[2,2,4,96,768]{4,3,2,1,0:T(8,128)(2,1)S(1)}, u32[]{:S(2)}, u32[]{:S(2)}) collective-permute-start(bf16[2,2,4,96,768]{4,3,2,1,0:T(8,128)(2,1)} %shard_map.246.refs_3_), channel_id=1, source_target_pairs={{0,1},{1,0},{2,3},{3,2},{4,5},{5,4},{6,7},{7,6},{8,9},{9,8},{10,11... | collective-permute-start | bytes 7077896 | tf_op jit(solution)/shard_map/ppermute | solution.py:489
  219.5 9.8 %collective-permute-start.22 = (bf16[2,2,4,96,768]{4,3,2,1,0:T(8,128)(2,1)}, bf16[2,2,4,96,768]{4,3,2,1,0:T(8,128)(2,1)}, u32[]{:S(2)}, u32[]{:S(2)}) collective-permute-start(bf16[2,2,4,96,768]{4,3,2,1,0:T(8,128)(2,1)} %shard_map.247.refs_4_), channel_id=1, source_target_pairs={{0,1},{1,0},{2,3},{3,2},{4,5},{5,4},{6,7},{7,6},{8,9},{9,8},{10,11... | collective-permute-start | bytes 7077896 | tf_op jit(solution)/shard_map/ppermute | solution.py:489
  228.4 45.4 %collective-permute-start.24 = (bf16[2,4,96,768]{3,2,1,0:T(8,128)(2,1)}, bf16[2,4,96,768]{3,2,1,0:T(8,128)(2,1)S(1)}, u32[]{:S(2)}, u32[]{:S(2)}) collective-permute-start(bf16[2,4,96,768]{3,2,1,0:T(8,128)(2,1)} %get-tuple-element.107.refs_4_), channel_id=1, source_target_pairs={{0,4},{4,0},{8,12},{12,8},{16,20},{20,16},{24,28},{28,24},{1,5},{5... | collective-permute-start | bytes 3538952 | tf_op jit(solution)/shard_map/ppermute | solution.py:489
  237.4 36.7 %collective-permute-start.25 = (bf16[2,4,96,768]{3,2,1,0:T(8,128)(2,1)}, bf16[2,4,96,768]{3,2,1,0:T(8,128)(2,1)S(1)}, u32[]{:S(2)}, u32[]{:S(2)}) collective-permute-start(bf16[2,4,96,768]{3,2,1,0:T(8,128)(2,1)} %get-tuple-element.108.refs_13_), channel_id=1, source_target_pairs={{0,2},{1,3},{2,0},{3,1},{4,6},{5,7},{6,4},{7,5},{8,10},{9,11},{10,... | collective-permute-start | bytes 3538952 | tf_op jit(solution)/shard_map/ppermute | solution.py:489
  272.2 27.6 %collective-permute-start.28 = (bf16[2,4,96,768]{3,2,1,0:T(8,128)(2,1)}, bf16[2,4,96,768]{3,2,1,0:T(8,128)(2,1)}, u32[]{:S(2)}, u32[]{:S(2)}) collective-permute-start(bf16[2,4,96,768]{3,2,1,0:T(8,128)(2,1)} %get-tuple-element.116.refs_2_), channel_id=1, source_target_pairs={{0,1},{1,0},{2,3},{3,2},{4,5},{5,4},{6,7},{7,6},{8,9},{9,8},{10,11... | collective-permute-start | bytes 3538952 | tf_op jit(solution)/shard_map/ppermute | solution.py:489
  272.3 7.4 %collective-permute-start.19 = (bf16[2,128,768]{2,1,0:T(8,128)(2,1)}, bf16[2,128,768]{2,1,0:T(8,128)(2,1)S(1)}, u32[]{:S(2)}, u32[]{:S(2)}) collective-permute-start(bf16[2,128,768]{2,1,0:T(8,128)(2,1)} %get-tuple-element.94), channel_id=1, source_target_pairs={{0,1},{1,0},{2,3},{3,2},{4,5},{5,4},{6,7},{7,6},{8,9},{9,8},{10,11... | collective-permute-start | bytes 1179656 | tf_op jit(solution)/shard_map/ppermute | solution.py:489
  272.8 23.4 %collective-permute-start.20 = (bf16[2,128,768]{2,1,0:T(8,128)(2,1)}, bf16[2,128,768]{2,1,0:T(8,128)(2,1)S(1)}, u32[]{:S(2)}, u32[]{:S(2)}) collective-permute-start(bf16[2,128,768]{2,1,0:T(8,128)(2,1)} %get-tuple-element.95), channel_id=1, source_target_pairs={{0,2},{1,3},{2,0},{3,1},{4,6},{5,7},{6,4},{7,5},{8,10},{9,11},{10,... | collective-permute-start | bytes 1179656 | tf_op jit(solution)/shard_map/ppermute | solution.py:489
  273.8 22.4 %collective-permute-start.21 = (bf16[2,128,768]{2,1,0:T(8,128)(2,1)}, bf16[2,128,768]{2,1,0:T(8,128)(2,1)S(1)}, u32[]{:S(2)}, u32[]{:S(2)}) collective-permute-start(bf16[2,128,768]{2,1,0:T(8,128)(2,1)} %get-tuple-element.96), channel_id=1, source_target_pairs={{0,3},{1,2},{2,1},{3,0},{4,7},{5,6},{6,5},{7,4},{8,11},{9,10},{10,... | collective-permute-start | bytes 1179656 | tf_op jit(solution)/shard_map/ppermute | solution.py:489
  277.4 27.8 %collective-permute-start.26 = (bf16[4,96,768]{2,1,0:T(8,128)(2,1)S(1)}, bf16[4,96,768]{2,1,0:T(8,128)(2,1)}, u32[]{:S(2)}, u32[]{:S(2)}) collective-permute-start(bf16[4,96,768]{2,1,0:T(8,128)(2,1)S(1)} %fusion.5.refs_9_), channel_id=1, source_target_pairs={{0,2},{1,3},{2,0},{3,1},{4,6},{5,7},{6,4},{7,5},{8,10},{9,11},{10,... | collective-permute-start | bytes 1769480 | tf_op jit(solution)/shard_map/ppermute | solution.py:489
  279.7 25.6 %collective-permute-start.27 = (bf16[4,96,768]{2,1,0:T(8,128)(2,1)S(1)}, bf16[4,96,768]{2,1,0:T(8,128)(2,1)}, u32[]{:S(2)}, u32[]{:S(2)}) collective-permute-start(bf16[4,96,768]{2,1,0:T(8,128)(2,1)S(1)} %fusion.6.refs_10_), channel_id=1, source_target_pairs={{0,4},{4,0},{8,12},{12,8},{16,20},{20,16},{24,28},{28,24},{1,5},{5... | collective-permute-start | bytes 1769480 | tf_op jit(solution)/shard_map/ppermute | solution.py:489
  281.4 14.8 %copy-start.23 = (bf16[2,128,768]{2,1,0:T(8,128)(2,1)S(1)}, bf16[2,128,768]{2,1,0:T(8,128)(2,1)}, u32[]{:S(2)}) copy-start(bf16[2,128,768]{2,1,0:T(8,128)(2,1)} %get-tuple-element.93.refs_1_) | copy-start | bytes 1179652
  309.8 17.0 %copy-start.38 = (bf16[4,96,768]{2,1,0:T(8,128)(2,1)S(1)}, bf16[4,96,768]{2,1,0:T(8,128)(2,1)}, u32[]{:S(2)}) copy-start(bf16[4,96,768]{2,1,0:T(8,128)(2,1)} %fusion.7.refs_11_) | copy-start | bytes 1769476
  309.8 17.6 %copy-start.31 = (bf16[4,96,768]{2,1,0:T(8,128)(2,1)S(1)}, bf16[4,96,768]{2,1,0:T(8,128)(2,1)}, u32[]{:S(2)}) copy-start(bf16[4,96,768]{2,1,0:T(8,128)(2,1)} %fusion.3.refs_10_) | copy-start | bytes 1769476
  324.8 36.0 %collective-permute-start.33 = (bf16[2,4,96,768]{3,2,1,0:T(8,128)(2,1)}, bf16[2,4,96,768]{3,2,1,0:T(8,128)(2,1)}, u32[]{:S(2)}, u32[]{:S(2)}) collective-permute-start(bf16[2,4,96,768]{3,2,1,0:T(8,128)(2,1)} %get-tuple-element.129.refs_1_), channel_id=1, source_target_pairs={{0,1},{1,0},{2,3},{3,2},{4,5},{5,4},{6,7},{7,6},{8,9},{9,8},{10,11... | collective-permute-start | bytes 3538952 | tf_op jit(solution)/shard_map/ppermute | solution.py:489
  326.9 15.9 %collective-permute-start.29 = (bf16[4,96,768]{2,1,0:T(8,128)(2,1)S(1)}, bf16[4,96,768]{2,1,0:T(8,128)(2,1)}, u32[]{:S(2)}, u32[]{:S(2)}) collective-permute-start(bf16[4,96,768]{2,1,0:T(8,128)(2,1)S(1)} %copy-done.38), channel_id=1, source_target_pairs={{0,4},{4,0},{8,12},{12,8},{16,20},{20,16},{24,28},{28,24},{1,5},{5... | collective-permute-start | bytes 1769480 | tf_op jit(solution)/shard_map/ppermute | solution.py:489
  328.6 43.4 %all-to-all-start.3 = ((bf16[4,96,1536]{2,1,0:T(8,128)(2,1)}), bf16[4,96,1536]{2,1,0:T(8,128)(2,1)S(1)}, u32[]{:S(2)}, u32[]{:S(2)}) async-start(bf16[4,96,1536]{2,1,0:T(8,128)(2,1)} %pad_maximum_fusion), calls=%async_computation.3 | async-start | bytes 2359296 | tf_op jit(solution)/shard_map/all_to_all | solution.py:492
  333.2 9.5 %copy-start.7 = (bf16[2,4,96,768]{3,2,1,0:T(8,128)(2,1)S(1)}, bf16[2,4,96,768]{3,2,1,0:T(8,128)(2,1)}, u32[]{:S(2)}) copy-start(bf16[2,4,96,768]{3,2,1,0:T(8,128)(2,1)} %get-tuple-element.120.refs_5_.refs_2_) | copy-start | bytes 3538948
  345.0 46.6 %collective-permute-start.35 = (bf16[4,96,768]{2,1,0:T(8,128)(2,1)}, bf16[4,96,768]{2,1,0:T(8,128)(2,1)S(1)}, u32[]{:S(2)}, u32[]{:S(2)}) collective-permute-start(bf16[4,96,768]{2,1,0:T(8,128)(2,1)} %fusion.2.refs_9_), channel_id=1, source_target_pairs={{0,2},{1,3},{2,0},{3,1},{4,6},{5,7},{6,4},{7,5},{8,10},{9,11},{10,... | collective-permute-start | bytes 1769480 | tf_op jit(solution)/shard_map/ppermute | solution.py:489
  363.0 28.7 %collective-permute-start.34 = (bf16[4,96,768]{2,1,0:T(8,128)(2,1)}, bf16[4,96,768]{2,1,0:T(8,128)(2,1)}, u32[]{:S(2)}, u32[]{:S(2)}) collective-permute-start(bf16[4,96,768]{2,1,0:T(8,128)(2,1)} %fusion.8), channel_id=1, source_target_pairs={{0,4},{4,0},{8,12},{12,8},{16,20},{20,16},{24,28},{28,24},{1,5},{5... | collective-permute-start | bytes 1769480 | tf_op jit(solution)/shard_map/ppermute | solution.py:489
  366.8 6.2 %collective-permute-start.30 = (bf16[2,128,768]{2,1,0:T(8,128)(2,1)}, bf16[2,128,768]{2,1,0:T(8,128)(2,1)S(1)}, u32[]{:S(2)}, u32[]{:S(2)}) collective-permute-start(bf16[2,128,768]{2,1,0:T(8,128)(2,1)} %get-tuple-element.131), channel_id=1, source_target_pairs={{0,1},{1,0},{2,3},{3,2},{4,5},{5,4},{6,7},{7,6},{8,9},{9,8},{10,11... | collective-permute-start | bytes 1179656 | tf_op jit(solution)/shard_map/ppermute | solution.py:489
  366.8 12.1 %collective-permute-start.31 = (bf16[2,128,768]{2,1,0:T(8,128)(2,1)}, bf16[2,128,768]{2,1,0:T(8,128)(2,1)S(1)}, u32[]{:S(2)}, u32[]{:S(2)}) collective-permute-start(bf16[2,128,768]{2,1,0:T(8,128)(2,1)} %get-tuple-element.132), channel_id=1, source_target_pairs={{0,2},{1,3},{2,0},{3,1},{4,6},{5,7},{6,4},{7,5},{8,10},{9,11},{10,... | collective-permute-start | bytes 1179656 | tf_op jit(solution)/shard_map/ppermute | solution.py:489
  367.2 19.3 %collective-permute-start.32 = (bf16[2,128,768]{2,1,0:T(8,128)(2,1)}, bf16[2,128,768]{2,1,0:T(8,128)(2,1)S(1)}, u32[]{:S(2)}, u32[]{:S(2)}) collective-permute-start(bf16[2,128,768]{2,1,0:T(8,128)(2,1)} %get-tuple-element.133), channel_id=1, source_target_pairs={{0,3},{1,2},{2,1},{3,0},{4,7},{5,6},{6,5},{7,4},{8,11},{9,10},{10,... | collective-permute-start | bytes 1179656 | tf_op jit(solution)/shard_map/ppermute | solution.py:489
  371.9 14.6 %copy-start.24 = (bf16[2,128,768]{2,1,0:T(8,128)(2,1)S(1)}, bf16[2,128,768]{2,1,0:T(8,128)(2,1)}, u32[]{:S(2)}) copy-start(bf16[2,128,768]{2,1,0:T(8,128)(2,1)} %get-tuple-element.130.refs_0_) | copy-start | bytes 1179652
  389.0 10.0 %all-to-all-start.4 = ((f32[32,1,288]{2,1,0:T(1,128)}), f32[32,1,288]{2,1,0:T(1,128)S(1)}, u32[]{:S(2)}, u32[]{:S(2)}) async-start(f32[32,1,288]{2,1,0:T(1,128)} %shard_map.262), calls=%async_computation.4 | async-start | bytes 98304 | tf_op jit(solution)/shard_map/all_to_all | solution.py:912
  396.3 6.8 %copy-start.29 = (bf16[4,96,1536]{2,1,0:T(8,128)(2,1)S(1)}, bf16[4,96,1536]{2,1,0:T(8,128)(2,1)}, u32[]{:S(2)}) copy-start(bf16[4,96,1536]{2,1,0:T(8,128)(2,1)} %shard_map.261.refs_1_) | copy-start | bytes 3538948
  399.6 19.9 %all-to-all-start.5 = ((bf16[4,96,768]{2,1,0:T(8,128)(2,1)}), bf16[4,96,768]{2,1,0:T(8,128)(2,1)S(1)}, u32[]{:S(2)}, u32[]{:S(2)}) async-start(bf16[4,96,768]{2,1,0:T(8,128)(2,1)} %shard_map.263), calls=%async_computation.5 | async-start | bytes 1179648 | tf_op jit(solution)/shard_map/all_to_all | solution.py:492
  (36 other events, 60.0 us)
where the time goes:
time: 428 us; the launch traced here: 422 us
  Pallas kernels  210 us (49%)
  waiting for transfers between devices  89.9 us (21%)
  starting transfers between devices  50.7 us (12%)
  local copies, waits for them, and re-layouts  44.3 us (10%)
  other arithmetic  24.6 us (6%)
    pallas_call x28, Pallas kernels, call(): pl.pallas_call(body, grid_spec=pltpu.PrefetchScalarGridSpec(num_scalar_pr...  210 us
    ppermute x33, waiting for transfers between devices, across(): return lax.ppermute(array, axis, [(i, i ^ bit) for i in range(size)])  56.1 us
    unnamed x129, local copies, waits for them, and re-layouts  27.3 us
    ppermute x33, starting transfers between devices, across(): return lax.ppermute(array, axis, [(i, i ^ bit) for i in range(size)])  22.1 us
    all_to_all x4, starting transfers between devices, along(): lax.all_to_all(array, 'dp', 0, 0, tiled=True, axis_index_groups=groups)  15.2 us
    all_to_all x4, waiting for transfers between devices, along(): lax.all_to_all(array, 'dp', 0, 0, tiled=True, axis_index_groups=groups)  14 us
    all_to_all x1, waiting for transfers between devices, shards(): lax.all_to_all(pooled, ('dp', 'tensor'), 0, 0, tiled=True)  10.2 us
  transfers between devices with their start and end apart: 42, of which 12 were waited for; matrix products, arithmetic and copies ran while one was open for 10% of the time, Pallas kernels for 38%

commit v1 on v0

--- a/solution.py
+++ b/solution.py
@@ -19,7 +19,7 @@
 BF = jnp.bfloat16
 F32 = jnp.float32
 MIB = 1024 * 1024
-SHARE = 0.05
+SHARE = 0.3
 
 
 def dot(a, b, ca, cb):
@@ -38,8 +38,10 @@
     return dot(a, b, 0, 0)
 
 
-def call(kernel, grid, ins, outs, scratch=(), limit=60, cost=1.0, scalars=0, after=()):
+def call(kernel, grid, ins, outs, scratch=(), cost=1.0, scalars=0, limit=16, after=()):
     def spec(shape, block, index):
+        if block == "any":
+            return pl.BlockSpec(memory_space=pl.ANY)
         if block is None:
             zeros = (0,) * len(shape)
             return pl.BlockSpec(shape, lambda *_: zeros)
@@ -121,6 +123,20 @@
     *ins, out_ref = refs
     for i, ref in enumerate(ins):
         out_ref[i] = ref[...]
+
+
+def add_kernel(layout, *refs):
+    ins, outs = list(refs[: sum(map(sum, layout))]), refs[sum(map(sum, layout)) :]
+    for terms, out_ref in zip(layout, outs):
+        at = 0
+        for n in terms:
+            group = [ins.pop(0) for _ in range(n)]
+            value = group[0][...].astype(F32)
+            for ref in group[1:]:
+                value += ref[...].astype(F32)
+            rows, columns = value.shape[-2:]
+            out_ref[0, :, at : at + columns] = value.reshape(rows, columns).astype(BF)
+            at += columns
 
 
 def merge_kernel(here_ref, own_ref, other_ref, out_ref):
@@ -235,25 +251,37 @@
 
 
 def gelu_parts(e):
-    size = jnp.abs(e)
-    density = jnp.exp(-0.5 * e * e)
-    t = 1.0 / (1.0 + (0.3275911 / math.sqrt(2.0)) * size)
-    poly = t * (
-        0.5 * 0.254829592
-        + t * (0.5 * -0.284496736 + t * (0.5 * 1.421413741 + t * (0.5 * -1.453152027 + t * (0.5 * 1.061405429))))
-    )
-    tail = poly * density
-    cdf = jnp.where(e < 0, tail, 1.0 - tail)
-    return e * cdf, cdf + e * (density * (1.0 / math.sqrt(2.0 * math.pi)))
-
-
-def up_kernel(u_ref, bup_ref, w0, w1, w2, w3, h_ref, g_ref):
-    u = u_ref[...]
-    for j, w in enumerate((w0, w1, w2, w3)):
-        e = nn(u, w[...]) + bup_ref[j, 6:7]
-        h, g = gelu_parts(e)
-        h_ref[j] = h.astype(BF)
-        g_ref[j] = g.astype(BF)
+    cdf = 0.5 + 0.5 * lax.erf(e * (1.0 / math.sqrt(2.0)))
+    return e * cdf, cdf + e * (jnp.exp(-0.5 * e * e) * (1.0 / math.sqrt(2.0 * math.pi)))
+
+
+def fetch(moves, step, sems, body):
+    copies = [pltpu.make_async_copy(src, dst, sems.at[i]) for i, (src, dst) in enumerate(moves)]
+
+    @pl.when(step == 0)
+    def _():
+        for copy in copies:
+            copy.start()
+        body(lambda i: copies[i].wait())
+
+    @pl.when(step > 0)
+    def _():
+        body(lambda i: None)
+
+
+def up_kernel(u_ref, bup_ref, w0, w1, w2, w3, h_ref, g_ref, w_ref, sems):
+    width = w_ref.shape[2]
+
+    def body(ready):
+        u = u_ref[...]
+        for j in range(4):
+            ready(j)
+            e = nn(u, w_ref[j]) + bup_ref[j, 6:7]
+            h, g = gelu_parts(e)
+            h_ref[j] = h.astype(BF)
+            g_ref[j] = g.astype(BF)
+
+    fetch([(w.at[:, :width], w_ref.at[j]) for j, w in enumerate((w0, w1, w2, w3))], pl.program_id(0), sems, body)
 
 
 def split3(v):
@@ -266,7 +294,7 @@
 
 def down_kernel(
     h_ref, xh1_ref, small_ref, code_ref, inv_ref, w0, w1, w2, w3,
-    xh_ref, rstd_ref, y0, y1, y2, y3, pool_ref, acc_ref,
+    xh_ref, rstd_ref, y0, y1, y2, y3, pool_ref, acc_ref, w_ref, sems,
 ):
     y_refs = (y0, y1, y2, y3)
     step = pl.program_id(0)
@@ -275,26 +303,31 @@
     def _():
         acc_ref[...] = jnp.zeros_like(acc_ref)
 
-    f = nt(h_ref[0], w0[...])
-    for j, w in ((1, w1), (2, w2), (3, w3)):
-        f += nt(h_ref[j], w[...])
-    first = xh1_ref[...] * small_ref[0:1] + small_ref[3:4]
-    xh, rstd = norm(first + (f + small_ref[4:5]))
-    y2 = xh * small_ref[1:2] + small_ref[5:6]
-    xh_ref[...] = xh
-    rstd_ref[...] = rstd
-    low = y2.astype(BF)
-    size = y_refs[0].shape[1]
-    here = low.shape[0] // size
-    for j, ref in enumerate(y_refs):
-
-        @pl.when(lax.rem(step, 4 // here) == j // here)
-        def _():
-            ref[0] = low[(j % here) * size : (j % here + 1) * size]
-
-    member = (lax.broadcasted_iota(jnp.int32, (8, y2.shape[0]), 0) == code_ref[...]).astype(BF)
-    a, b, c = split3(y2)
-    acc_ref[...] += nn(member, a) + nn(member, b) + nn(member, c)
+    def body(ready):
+        ready(0)
+        f = nt(h_ref[0], w_ref[0])
+        for j in range(1, 4):
+            ready(j)
+            f += nt(h_ref[j], w_ref[j])
+        first = xh1_ref[...] * small_ref[0:1] + small_ref[3:4]
+        xh, rstd = norm(first + (f + small_ref[4:5]))
+        y2 = xh * small_ref[1:2] + small_ref[5:6]
+        xh_ref[...] = xh
+        rstd_ref[...] = rstd
+        low = y2.astype(BF)
+        size = y_refs[0].shape[1]
+        here = low.shape[0] // size
+        for j, ref in enumerate(y_refs):
+
+            @pl.when(lax.rem(step, 4 // here) == j // here)
+            def _():
+                ref[0] = low[(j % here) * size : (j % here + 1) * size]
+
+        member = (lax.broadcasted_iota(jnp.int32, (8, y2.shape[0]), 0) == code_ref[...]).astype(BF)
+        a, b, c = split3(y2)
+        acc_ref[...] += nn(member, a) + nn(member, b) + nn(member, c)
+
+    fetch([(w, w_ref.at[j]) for j, w in enumerate((w0, w1, w2, w3))], step, sems, body)
 
     @pl.when(step == pl.num_programs(0) - 1)
     def _():
@@ -325,8 +358,8 @@
 
 
 def feed_back_kernel(
-    pooled_ref, ids_ref, mate_ref, target_ref, inv_ref, code_ref, xh_ref, rstd_ref, small_ref, w0, w1, w2, w3, g_ref,
-    df_ref, dz_ref, de_ref, sum_ref, bup_ref, gp_ref,
+    blocks, here_ref, pooled_ref, ids_ref, mate_ref, target_ref, inv_ref, code_ref, xh_ref, rstd_ref, small_ref,
+    g_ref, h_ref, w0, w1, w2, w3, df_ref, dz_ref, de_ref, send_ref, sum_ref, bup_ref, gp_ref, all_ref, w_ref, sems,
 ):
     step = pl.program_id(0)
 
@@ -338,43 +371,66 @@
         sum_ref[...] = jnp.zeros_like(sum_ref)
         bup_ref[...] = jnp.zeros_like(bup_ref)
 
-    member = (lax.broadcasted_iota(jnp.int32, (8, xh_ref.shape[0]), 0) == code_ref[...]).astype(BF)
-    dy = tn(member, gp_ref[0]) + tn(member, gp_ref[1]) + tn(member, gp_ref[2])
-    xh = xh_ref[...]
-    dz = norm_back(dy, xh, rstd_ref[...], small_ref[1:2])
-    sum_ref[0:1] += rowsum(dy * xh)
-    sum_ref[1:2] += rowsum(dy)
-    sum_ref[2:3] += rowsum(dz)
-    df = dz.astype(BF)
-    df_ref[...] = df
-    dz_ref[...] = dz
-    for j, w in enumerate((w0, w1, w2, w3)):
-        de = (nn(df, w[...]) * g_ref[j].astype(F32)).astype(BF)
-        de_ref[j] = de
-        bup_ref[j, 0:1] += rowsum(de.astype(F32))
+    def body(ready):
+        size = xh_ref.shape[0]
+        member = (lax.broadcasted_iota(jnp.int32, (8, size), 0) == code_ref[...]).astype(BF)
+        dy = tn(member, gp_ref[0]) + tn(member, gp_ref[1]) + tn(member, gp_ref[2])
+        xh = xh_ref[...]
+        dz = norm_back(dy, xh, rstd_ref[...], small_ref[1:2])
+        sum_ref[0:1] += rowsum(dy * xh)
+        sum_ref[1:2] += rowsum(dy)
+        sum_ref[2:3] += rowsum(dz)
+        df = dz.astype(BF)
+        df_ref[...] = df
+        dz_ref[...] = dz
+        all_ref[pl.ds(pl.multiple_of(step * size, size), size), :] = df
+        for j in range(4):
+            ready(j)
+            de = (nn(df, w_ref[j]) * g_ref[j].astype(F32)).astype(BF)
+            de_ref[j] = de
+            bup_ref[j, 0:1] += rowsum(de.astype(F32))
+
+    @pl.when(step < blocks)
+    def _():
+        fetch([(w, w_ref.at[j]) for j, w in enumerate((w0, w1, w2, w3))], step, sems, body)
+
+    @pl.when(step >= blocks)
+    def _():
+        pieces(tn(all_ref[...], h_ref[0]), here_ref, send_ref.at[0], slice(0, h_ref.shape[2]))
 
 
 def norm_back_kernel(
-    de_ref, dz2_ref, xh_ref, rstd_ref, small_ref, w0, w1, w2, w3, o0, o1, o2, o3, dz_ref, da_ref, do_ref, sum_ref
+    de_ref, dz2_ref, xh_ref, rstd_ref, small_ref, w0, w1, w2, w3,
+    dz_ref, da_ref, do_ref, sum_ref, w_ref, wo_ref, sems,
 ):
-    @pl.when(pl.program_id(0) == 0)
+    step = pl.program_id(0)
+    hidden = w_ref.shape[2]
+    ups = (w0, w1, w2, w3)
+    moves = [(w.at[:, :hidden], w_ref.at[j]) for j, w in enumerate(ups)]
+    moves += [(w.at[:, hidden:], wo_ref.at[j]) for j, w in enumerate(ups)]
+
+    @pl.when(step == 0)
     def _():
         sum_ref[...] = jnp.zeros_like(sum_ref)
 
-    dy = nt(de_ref[0], w0[...])
-    for j, w in ((1, w1), (2, w2), (3, w3)):
-        dy += nt(de_ref[j], w[...])
-    dy = dz2_ref[...] + dy
-    xh = xh_ref[...]
-    dz = norm_back(dy, xh, rstd_ref[...], small_ref[0:1])
-    sum_ref[0:1] += rowsum(dy * xh)
-    sum_ref[1:2] += rowsum(dy)
-    sum_ref[2:3] += rowsum(dz)
-    da = dz.astype(BF)
-    dz_ref[...] = dz
-    da_ref[...] = da
-    for j, w in enumerate((o0, o1, o2, o3)):
-        do_ref[j] = nn(da, w[:, : do_ref.shape[2]]).astype(BF)
+    def body(ready):
+        dy = dz2_ref[...]
+        for j in range(4):
+            ready(j)
+            dy = dy + nt(de_ref[j], w_ref[j])
+        xh = xh_ref[...]
+        dz = norm_back(dy, xh, rstd_ref[...], small_ref[0:1])
+        sum_ref[0:1] += rowsum(dy * xh)
+        sum_ref[1:2] += rowsum(dy)
+        sum_ref[2:3] += rowsum(dz)
+        da = dz.astype(BF)
+        dz_ref[...] = dz
+        da_ref[...] = da
+        for j in range(4):
+            ready(4 + j)
+            do_ref[j] = nn(da, wo_ref[j, :, : do_ref.shape[2]]).astype(BF)
+
+    fetch(moves, step, sems, body)
 
 
 def pieces(grad, here_ref, ref, at):
@@ -426,14 +482,33 @@
         at += grad.shape[1]
 
 
-def attn_bwd_kernel(
-    here_ref, qkv_ref, p_ref, o_ref, do_ref, x_ref, da_ref, w_ref, dxin_ref, piece_ref, sum_ref, *refs
-):
-    *dx_refs, acc_ref = refs
+def attn_bwd_kernel(keeps, here_ref, qkv_ref, p_ref, o_ref, do_ref, x_any, da_any, *refs):
+    got_any, refs = refs[:keeps], refs[keeps:]
+    piece_refs, refs = refs[: 1 + keeps], refs[1 + keeps :]
+    sum_ref, dproj_ref, acc_ref, xs, das, sems = refs[: len(refs) - keeps]
+    got_refs = refs[len(refs) - keeps :]
     r = pl.program_id(0)
+    rows = xs.shape[0]
     local = o_ref.shape[2]
     heads = p_ref.shape[1]
     hd = local // heads
+
+    def row_copies(i):
+        pairs = ((x_any, xs), (da_any, das))
+        return [pltpu.make_async_copy(src.at[i], dst.at[i], sems.at[2 * i + n]) for n, (src, dst) in enumerate(pairs)]
+
+    others = [
+        pltpu.make_async_copy(src, dst, sems.at[2 * rows + n]) for n, (src, dst) in enumerate(zip(got_any, got_refs))
+    ]
+
+    @pl.when(r == 0)
+    def _():
+        for i in range(rows):
+            for copy in row_copies(i):
+                copy.start()
+        for copy in others:
+            copy.start()
+
     q_all, k_all, v_all = (qkv_ref[0, :, i * local : (i + 1) * local] for i in range(3))
     o_all, do_all = o_ref[0], do_ref[0]
     prod = o_all.astype(F32) * do_all.astype(F32)
@@ -449,34 +524,74 @@
         dq.append(nn(ds, k_all[:, at]))
         dk.append(tn(q_all[:, at], ds))
     dq = (jnp.concatenate(dq, axis=1).astype(BF).astype(F32) * 0.125).astype(BF)
-    dkv = jnp.concatenate(dk + dv, axis=0).astype(BF).astype(F32)
-    dkv = jnp.transpose(dkv).astype(BF)
+    dkv = jnp.transpose(jnp.concatenate(dk + dv, axis=0)).astype(BF)
     dproj = jnp.concatenate([dq, dkv], axis=1)
-    sums = rowsum(dproj.astype(F32))
-    grad = jnp.concatenate([tn(x_ref[0], dproj), tn(da_ref[0], o_all)], axis=1)
+    sums = jnp.broadcast_to(rowsum(dproj.astype(F32)), sum_ref.shape)
+
+    for copy in row_copies(r):
+        copy.wait()
 
     @pl.when(r == 0)
     def _():
-        acc_ref[...] = grad
-        sum_ref[...] = jnp.broadcast_to(sums, sum_ref.shape)
-
-    @pl.when(r > 0)
-    def _():
-        acc_ref[...] += grad
-        sum_ref[...] += jnp.broadcast_to(sums, sum_ref.shape)
-
-    @pl.when(r == pl.num_programs(0) - 1)
-    def _():
-        pieces(acc_ref[...], here_ref, piece_ref, slice(0, acc_ref.shape[1]))
-
-    dx = dxin_ref[0] + nt(dproj, w_ref[:, : 3 * local])
-    if len(dx_refs) == 1:
-        dx_refs[0][0] = dx
-    else:
+        acc_ref[...] = jnp.zeros_like(acc_ref)
+        sum_ref[...] = jnp.zeros_like(sum_ref)
+
+    sum_ref[...] += sums
+    acc_ref[:, : 3 * local] += tn(xs[r], dproj)
+    acc_ref[:, 3 * local :] += tn(das[r], o_all)
+    dproj_ref[0] = dproj
+
+    @pl.when(r == rows - 1)
+    def _():
+        if not keeps:
+            pieces(acc_ref[...], here_ref, piece_refs[0], slice(0, acc_ref.shape[1]))
+        else:
+            others[0].wait()
+            (got_ref,), (stay_ref, fly_ref) = got_refs, piece_refs
+            depth, size = stay_ref.shape[0], stay_ref.shape[1]
+            lo = here_ref[0]
+            for z in range(depth):
+                first, second = (acc_ref[(2 * z + b) * size : (2 * z + b + 1) * size] for b in range(2))
+                mine, theirs = jnp.where(lo == 0, first, second), jnp.where(lo == 0, second, first)
+                stay_ref[z] = (mine + got_ref[0, z].astype(F32)).astype(BF)
+                fly_ref[z] = (theirs + got_ref[1, z].astype(F32)).astype(BF)
+
+
+def small_kernel(norm1_ref, norm2_ref, up_ref, s1, s2, s3, keep_ref, send_ref):
+    local = s1.shape[1] // 3
+    parts = {1: s1, 2: s2, 3: s3}
+    for ref, pair in ((keep_ref, (0, 2)), (send_ref, (1, 3))):
+        ref[...] = jnp.zeros_like(ref)
+        for i, (src, row) in enumerate(
+            ((norm1_ref, 0), (norm2_ref, 0), (norm1_ref, 2), (norm1_ref, 1), (norm2_ref, 2), (norm2_ref, 1))
+        ):
+            ref[i : i + 1] = src[row : row + 1]
+        for n, j in enumerate(pair):
+            ref[8 + 8 * n : 9 + 8 * n] = up_ref[j, 0:1]
+            if j in parts:
+                ref[9 + 8 * n : 10 + 8 * n, :local] = parts[j][0:1, :local]
+                ref[9 + 8 * n : 10 + 8 * n, local : 2 * local] = parts[j][0:1, 2 * local :]
+
+
+def input_back_kernel(p0, p1, p2, p3, dz_ref, w0, w1, w2, w3, y0, y1, y2, y3, w_ref, sems):
+    step = pl.program_id(0)
+    y_refs = (y0, y1, y2, y3)
+
+    def body(ready):
+        dx = dz_ref[...]
+        for j, p in enumerate((p0, p1, p2, p3)):
+            ready(j)
+            dx = dx + nt(p[...], w_ref[j, :, : p.shape[1]])
         low = dx.astype(BF)
-        size = dx_refs[0].shape[1]
-        for j, ref in enumerate(dx_refs):
-            ref[0] = low[j * size : (j + 1) * size]
+        size = y_refs[0].shape[1]
+        here = low.shape[0] // size
+        for j, ref in enumerate(y_refs):
+
+            @pl.when(lax.rem(step, 4 // here) == j // here)
+            def _():
+                ref[0] = low[(j % here) * size : (j % here + 1) * size]
+
+    fetch([(w, w_ref.at[j]) for j, w in enumerate((w0, w1, w2, w3))], step, sems, body)
 
 
 def make(mesh):
@@ -490,6 +605,26 @@
 
     def along(array):
         return lax.all_to_all(array, "dp", 0, 0, tiled=True, axis_index_groups=groups)
+
+    def turn(array, k):
+        return lax.ppermute(array, "dp", [(2 * ((z + k) % nh) + b, 2 * z + b) for z in range(nh) for b in range(2)])
+
+    def swap(array):
+        return across(array, "tensor", 1)
+
+    def summed(*outs):
+        layout, ins, shapes = [], [], []
+        for ranges in outs:
+            layout.append([len(terms) for terms in ranges])
+            columns = 0
+            for terms in ranges:
+                for array, lead in terms:
+                    block = (1,) * (len(lead) + 1) + array.shape[-2:]
+                    ins.append((array, block, lambda z, lead=lead: (*lead, z, 0, 0)))
+                columns += array.shape[-1]
+            shape = (nh, array.shape[-2], columns)
+            shapes.append((shape, BF, (1,) + shape[1:], lambda z: (z, 0, 0)))
+        return call(functools.partial(add_kernel, layout), (nh,), ins, shapes, limit=63, cost=60.0)
 
     def turn(array, k):
         return lax.ppermute(array, "dp", [(2 * ((z + k) % nh) + b, 2 * z + b) for z in range(nh) for b in range(2)])
@@ -545,7 +680,7 @@
                 scalars=1,
                 after=after,
                 cost=1.0,
-                limit=16,
+                limit=63,
             )[0]
 
         def pack(kernel, arrays, columns, after):
@@ -555,7 +690,6 @@
                 [(a, None, None) for a in arrays],
                 [((nh, rb, columns), BF, (1, rb, columns), lambda i: (i, 0, 0))],
                 after=after,
-                limit=16,
             )[0]
 
         def cut(array):
@@ -583,7 +717,6 @@
             [((rows, part_len, width), BF, (rows, deal_block, width), lambda i, *_: (0, i, 0))] * ntens,
             scalars=1,
             cost=2.0,
-            limit=16,
         )
         x_parts = [dealt[0]] + [across(dealt[j], "tensor", j) for j in range(1, ntens)]
 
@@ -594,7 +727,6 @@
             (1,),
             [(w_qkv.reshape(rb, 3 * local), None, None), (qv_col, None, None)],
             [((rb, wide), BF, None, None)],
-            limit=16,
         )
         if nh <= 4:
             pieces1 = [first_piece] + [turn(first_piece, k) for k in range(1, nh)]
@@ -604,7 +736,6 @@
                 [(p, None, None) for p in pieces1],
                 [((nh, rb, wide), BF, None, None)],
                 after=[dealt[1]],
-                limit=16,
             )[0]
         else:
             own1 = along(jnp.broadcast_to(first_piece[None], (nh, rb, wide)))
@@ -614,7 +745,7 @@
         w1[2] = across(w1[0], "tensor", 2)
         extra = jnp.concatenate([ln_gains.T, shifts.T, b_up.reshape(-1, 1), jnp.zeros((rb, 57), BF)], axis=1)
         second_piece = pack(pack_two_kernel, [w_up, w_out, extra], hidden + 256, [dealt[1]])
-        (second_piece,) = gate([second_piece], [lo1])
+        (second_piece,) = gate([second_piece], [own1])
         own2 = along(second_piece)
         third_piece = pack(pack_three_kernel, [w_down], hidden, [dealt[1]])
 
@@ -653,55 +784,55 @@
         def whole_out(shape, dtype):
             return (shape, dtype, None, None)
 
+        by_row = lambda r, *_: (r, 0, 0)
+
         def attend(xs, w, before):
             outs = [
-                ((rows, seq, 3 * local), BF, (1, seq, 3 * local), lambda r, *_: (r, 0, 0)),
+                ((rows, seq, 3 * local), BF, (1, seq, 3 * local), by_row),
                 ((rows, heads, seq, seq), BF, (1, heads, seq, seq), lambda r, *_: (r, 0, 0, 0)),
-                ((rows, seq, local), BF, (1, seq, local), lambda r, *_: (r, 0, 0)),
+                ((rows, seq, local), BF, (1, seq, local), by_row),
             ]
             if len(xs) > 1:
-                outs.append(((rows, seq, width), BF, (1, seq, width), lambda r, *_: (r, 0, 0)))
+                outs.append(((rows, seq, width), BF, (1, seq, width), by_row))
             return call(
                 functools.partial(attn_fwd_kernel, len(xs)),
                 (rows,),
-                [(a, (1,) + a.shape[1:], lambda r, *_: (r, 0, 0)) for a in xs]
+                [(a, (1,) + a.shape[1:], by_row) for a in xs]
                 + [
                     whole(w),
                     whole(sqv),
-                    (key_code.reshape(rows, 1, seq), (1, 1, seq), lambda r, *_: (r, 0, 0)),
-                    (query_code.reshape(rows, seq, 1), (1, seq, 1), lambda r, *_: (r, 0, 0)),
+                    (key_code.reshape(rows, 1, seq), (1, 1, seq), by_row),
+                    (query_code.reshape(rows, seq, 1), (1, seq, 1), by_row),
                 ],
                 outs,
                 scratch=[pltpu.VMEM((8, 2 * local), F32), pltpu.VMEM((seq, seq), F32)],
                 after=before,
+                limit=63,
                 cost=9.0,
             )
 
         kept = {}
         *kept[0], x = attend(x_parts, w1[0], [second_piece])
         (own2,) = gate([own2], [kept[0][2]])
-        lo2 = across(own2, "dp", 1)
+        lo2, far2 = across(own2, "dp", 1), across(own2, "tensor", 2)
         (third_piece,) = gate([third_piece], [own2])
         own3 = along(third_piece)
         kept[1] = attend([x], w1[1], [own2])
         (w1[2],) = gate([w1[2]], [kept[1][2]])
-        far2 = across(own2, "tensor", 2)
         w1[3] = swap(w1[2])
         kept[2] = attend([x], w1[2], [])
-        own3, lo2 = gate([own3, lo2], [kept[2][2]])
-        lo3 = across(own3, "dp", 1)
+        lo2, far2 = gate([lo2, far2], [kept[2][2]])
+        far_lo2 = across(far2, "dp", 1)
         w2 = {0: merged(own2, lo2)}
         w2[1] = swap(w2[0])
-        kept[3] = attend([x], w1[3], [own3, w2[0]])
-        (far2,) = gate([far2], [kept[3][2]])
-        far_lo2 = across(far2, "dp", 1)
-        (lo3,) = gate([lo3], [kept[3][2]])
-        w3 = {0: merged(own3, lo3, [far2])}
-        w3[2] = across(w3[0], "tensor", 2)
-        w3[1], w3[3] = swap(w3[0]), swap(w3[2])
-        w2[2] = merged(far2, far_lo2, [w3[0]])
+        (own3,) = gate([own3], [w2[0]])
+        far3, lo3 = across(own3, "tensor", 2), across(own3, "dp", 1)
+        kept[3] = attend([x], w1[3], [own3])
+        far3, far_lo2 = gate([far3, far_lo2], [kept[3][2]])
+        far_lo3 = across(far3, "dp", 1)
+        w2[2] = merged(far2, far_lo2)
         w2[3] = swap(w2[2])
-        ws2, ws3 = [w2[j] for j in range(4)], [w3[j] for j in range(4)]
+        ws2 = [w2[j] for j in range(4)]
         o_parts = [kept[j][2].reshape(count, local) for j in range(4)]
         x_flat = x.reshape(count, width)
 
@@ -715,7 +846,9 @@
                 return (shape, dtype, (shape[0], blk, shape[2]), lambda i, *_: (0, i, 0))
             return (shape, dtype, (blk, shape[1]), lambda i, *_: (i, 0))
 
-        ups = [(w, (width, hidden), lambda i, *_: (0, 0)) for w in ws2]
+        ups = [(w, "any", None) for w in ws2]
+        all_w = pltpu.VMEM((4, width, hidden), BF)
+        sems = lambda n: pltpu.SemaphoreType.DMA((n,))
         outs_w = [(w, (width, 256), lambda i, *_: (0, hidden // 256)) for w in ws2]
         xh1, rstd1, u, small, bup_rows = call(
             out_kernel,
@@ -728,26 +861,38 @@
                 whole_out((8, width), F32),
                 whole_out((4, 8, hidden), F32),
             ],
+            limit=63,
             cost=8.0,
         )
+        (lo3,) = gate([lo3], [u])
+        w3 = {0: merged(own3, lo3)}
+        w3[1] = swap(w3[0])
         h, g = call(
             up_kernel,
             (steps,),
             [rows_of(u), whole(bup_rows)] + ups,
             [rows_out((4, count, hidden), BF), rows_out((4, count, hidden), BF)],
+            after=[w3[0]],
+            scratch=[all_w, sems(4)],
+            limit=63,
             cost=20.0,
         )
+        (far_lo3,) = gate([far_lo3], [h])
+        w3[2] = merged(far3, far_lo3)
+        w3[3] = swap(w3[2])
+        downs = [(w3[j], "any", None) for j in range(4)]
         code_spec = (sent_code, (1, blk), lambda i, *_: (0, i))
         span = blk // part_len
         part_out = lambda i, *_: (i * span // ntens, 0, 0)
         xh2, rstd2, y0, y1, y2, y3, pooled = call(
             down_kernel,
             (steps,),
-            [rows_of(h), rows_of(xh1), whole(small), code_spec, whole(inv_count)] + [whole(w) for w in ws3],
+            [rows_of(h), rows_of(xh1), whole(small), code_spec, whole(inv_count)] + downs,
             [rows_out((count, width), F32), rows_out((count, 1), F32)]
             + [((rows, part_len, width), BF, (1, part_len, width), part_out)] * ntens
             + [whole_out((nd * ntens, sents, width), BF)],
-            scratch=[pltpu.VMEM((sents, width), F32)],
+            scratch=[pltpu.VMEM((sents, width), F32), all_w, sems(4)],
+            limit=63,
             cost=14.0,
         )
 
@@ -762,29 +907,46 @@
                 [((part_len * row_count, width), BF, (blk, width), lambda i, *_: (i, 0))],
                 scalars=1,
                 after=after,
-                cost=2.0,
-                limit=16,
+                cost=30.0,
             )
             return out.reshape(part_len, row_count, width)
 
         every = lax.all_to_all(pooled, ("dp", "tensor"), 0, 0, tiled=True).reshape(nd * ntens * sents, width)
 
-        df, dz2, de, sums2, dbup = call(
-            feed_back_kernel,
-            (steps,),
-            [whole(every), whole(own_ids), whole(mate), whole(goal), whole(inv_count), code_spec]
-            + [rows_of(xh2), rows_of(rstd2), whole(small)]
-            + [whole(w) for w in ws3]
-            + [rows_of(g)],
+        shape = (2, 2, depth, rbk, hidden)
+        half = (2,) + shape[2:]
+
+        def blocked(array):
+            at = lambda i, *_: jnp.minimum(i, steps - 1)
+            if len(array.shape) == 3:
+                return (array.shape[0], blk, array.shape[2]), lambda i, *_: (0, at(i), 0)
+            return (blk, array.shape[1]), lambda i, *_: (at(i), 0)
+
+        def blocked_out(shape, dtype):
+            return (shape, dtype, *blocked(jax.ShapeDtypeStruct(shape, dtype)))
+
+        late = lambda i: jnp.maximum(i - steps, 0)
+        df, dz2, de, send3, sums2, dbup = call(
+            functools.partial(feed_back_kernel, steps),
+            (steps + 2,),
+            [whole(here), whole(every), whole(own_ids), whole(mate), whole(goal), whole(inv_count)]
+            + [(sent_code, (1, blk), lambda i, *_: (0, jnp.minimum(i, steps - 1)))]
+            + [(a, *blocked(a)) for a in (xh2, rstd2)]
+            + [whole(small), (g, *blocked(g))]
+            + [(h, (1, count, hidden), lambda i, *_: (2 * late(i) + 1, 0, 0))]
+            + downs,
             [
-                rows_out((count, width), BF),
-                rows_out((count, width), F32),
-                rows_out((4, count, hidden), BF),
+                blocked_out((count, width), BF),
+                blocked_out((count, width), F32),
+                blocked_out((4, count, hidden), BF),
+                (shape, BF, (1,) + shape[1:], lambda i, *_: (late(i), 0, 0, 0, 0)),
                 whole_out((8, width), F32),
                 whole_out((4, 8, hidden), F32),
             ],
-            scratch=[pltpu.VMEM((3, sents, width), BF)],
-            cost=14.0,
+            scratch=[pltpu.VMEM((3, sents, width), BF), pltpu.VMEM((count, width), BF), all_w, sems(4)],
+            scalars=1,
+            limit=63,
+            cost=32.0,
         )
 
         hidden_parts = send_back([y0, y1, y2, y3])
@@ -798,14 +960,13 @@
                 outs,
                 scalars=1,
                 after=after,
-                cost=5.0,
+                limit=63,
+                cost=40.0,
             )
 
-        shape = (2, 2, depth, rbk, hidden)
-        half = (2,) + shape[2:]
         both_out = [(shape, BF, (1,) + shape[1:], lambda j, *_: (j, 0, 0, 0, 0))]
-        (send3,) = grad_part(df, h, 1, grad_send_kernel, [], both_out, [])
-        (sendu,) = grad_part(u, de, 1, grad_send_kernel, [], both_out, [send3])
+        hidden_out = collected(hidden_parts, [send3])
+        (sendu,) = grad_part(u, de, 1, grad_send_kernel, [], both_out, [send3, hidden_out])
         got = uncut(swap(cut(send3)))
         stay3, fly3 = grad_part(
             df, h, 0, functools.partial(grad_keep_kernel, True), [got],
@@ -825,101 +986,116 @@
         dz1, da, do, sums1 = call(
             norm_back_kernel,
             (steps,),
-            [rows_of(de), rows_of(dz2), rows_of(xh1), rows_of(rstd1), whole(small)] + ups + outs_w,
+            [rows_of(de), rows_of(dz2), rows_of(xh1), rows_of(rstd1), whole(small)] + ups,
             [
                 rows_out((count, width), F32),
                 rows_out((count, width), BF),
                 rows_out((4, count, local), BF),
                 whole_out((8, width), F32),
             ],
+            scratch=[all_w, pltpu.VMEM((4, width, 256), BF), sems(8)],
             after=[flyu],
-            cost=15.0,
+            limit=63,
+            cost=14.0,
         )
-
-        do_rows = do.reshape(4, rows, seq, local)
         da_rows = da.reshape(rows, seq, width)
-        per = lambda r, *_: (r, 0, 0)
         grad_cols = 4 * local
 
-        def attend_back(j, dx, after):
+        def attend_back(j, got, after):
             qkv, p, o = kept[j]
-            if j > 0:
-                dx_out = [((rows, seq, width), F32, (1, seq, width), per)]
-            else:
-                dx_out = [((rows, part_len, width), BF, (1, part_len, width), per)] * ntens
-            piece, sums, *dx = call(
-                attn_bwd_kernel,
+            half = (depth, rbk, grad_cols)
+            kinds = [whole_out((2,) + half, BF)] if got is None else [whole_out(half, BF)] * 2
+            keeps = 0 if got is None else 1
+            whole_row = pltpu.VMEM((rows, seq, width), BF)
+            *outs, sums, dproj = call(
+                functools.partial(attn_bwd_kernel, keeps),
                 (rows,),
                 [
                     whole(here),
-                    (qkv, (1, seq, 3 * local), per),
+                    (qkv, (1, seq, 3 * local), by_row),
                     (p, (1, heads, seq, seq), lambda r, *_: (r, 0, 0, 0)),
-                    (o, (1, seq, local), per),
-                    (do_rows[j], (1, seq, local), per),
-                    (x, (1, seq, width), per),
-                    (da_rows, (1, seq, width), per),
-                    whole(w1[j]),
-                    (dx, (1, seq, width), per),
-                ],
-                [whole_out((2, depth, rbk, grad_cols), BF), whole_out((8, 3 * local), F32)] + dx_out,
-                scratch=[pltpu.VMEM((width, grad_cols), F32)],
+                    (o, (1, seq, local), by_row),
+                    (do, (1, seq, local), lambda r, *_: (j, r, 0)),
+                    (x, "any", None),
+                    (da_rows, "any", None),
+                ]
+                + ([] if got is None else [(uncut(got), "any", None)]),
+                kinds
+                + [whole_out((8, 3 * local), F32), ((rows, seq, 3 * local), BF, (1, seq, 3 * local), by_row)],
+                scratch=[pltpu.VMEM((width, grad_cols), F32), whole_row, whole_row, sems(2 * rows + keeps)]
+                + [pltpu.VMEM((2,) + half, BF)] * keeps,
                 scalars=1,
                 after=after,
-                cost=14.0,
+                limit=63,
+                cost=11.0,
             )
-            return cut(piece), sums, (dx[0] if j > 0 else dx)
-
-        sums_of = {}
-        back3, sums_of[3], dx = attend_back(3, dz1.reshape(rows, seq, width), [])
+            if got is None:
+                out = cut(outs[0])
+            elif fused:
+                out = tuple(outs)
+            else:
+                both = cut(jnp.stack(outs))
+                out = both[0], both[1]
+            sums_of[j], dprojs[j] = sums, dproj.reshape(count, 3 * local)
+            return out
+
+        sums_of, dprojs = {}, {}
+        back3 = attend_back(3, None, [flyu])
         got_far = swap(back3)
         got3x, gotuy = gate([got3x, gotuy], [back3])
-        turn3 = total(stay3[1], got3x[1]).astype(BF)
-        turnu = total(stayu[1], gotuy[1]).astype(BF)
-        got3y = across(turn3, "tensor", 2)
-        gotux = across(turnu, "dp", 1)
-        back2, sums_of[2], dx = attend_back(2, dx, [turn3, turnu])
-        got3y, gotux = gate([got3y, gotux], [back2])
-        last3 = total(stay3[0], got3x[0], got3y).astype(BF)
-        lastu = total(stayu[0], gotuy[0], gotux).astype(BF)
-        end = along(jnp.concatenate([last3, lastu], axis=2))
-        hidden_out = collected(hidden_parts, [back2])
-        fly1 = total(back2[1], got_far[1]).astype(BF)
-        got_fly1 = across(fly1, "dp", 1)
-        back1, sums_of[1], dx = attend_back(1, dx, [last3, lastu, fly1, hidden_out])
+        turn3, turnu = summed([[(stay3, (1,)), (got3x, (1,))]], [[(stayu, (1,)), (gotuy, (1,))]])
+        got3y, gotux = across(turn3, "tensor", 2), across(turnu, "dp", 1)
+        stay_far, fly_far = attend_back(2, got_far, [turn3, turnu])
+        got_fly = across(fly_far, "dp", 1)
+        got3y, gotux = gate([got3y, gotux], [stay_far])
+        (end,) = summed([[(stay3, (0,)), (got3x, (0,)), (got3y, ())], [(stayu, (0,)), (gotuy, (0,)), (gotux, ())]])
+        end_sent = end
+        end = along(end)
+        back1 = attend_back(1, None, [end_sent])
         got_near = swap(back1)
-        (got_fly1,) = gate([got_fly1], [back1])
-        turn1 = total(back2[0], got_far[0], got_fly1).astype(BF)
+        small_keep, small_send = call(
+            small_kernel,
+            (1,),
+            [whole(a) for a in (sums1, sums2, dbup, sums_of[1], sums_of[2], sums_of[3])],
+            [whole_out((24, width), F32)] * 2,
+            after=[back1],
+        )
+        small_keep = small_keep + swap(small_send)
+        small_got = across(jnp.concatenate([small_keep[:8], small_keep[16:]], axis=0), "tensor", 2)
+        (got_fly,) = gate([got_fly], [small_keep])
+        (turn1,) = summed([[(stay_far, ()), (got_fly, ())]])
         got_turn1 = across(turn1, "tensor", 2)
-        back0, sums_of[0], dx_parts = attend_back(0, dx, [turn1])
-        got1 = across(total(back0[1], got_near[1]).astype(BF), "dp", 1)
-        grad_tokens = collected(send_back(dx_parts))
-        (end,) = gate([end], [back0])
-        got1, got_turn1 = gate([got1, got_turn1], [grad_tokens])
-        last1 = total(back0[0], got_near[0], got1, got_turn1).astype(BF)
-
-        def to_axes(rows_by_d):
-            order = jnp.arange(ntens) ^ t
-            return jnp.take(rows_by_d, order, axis=0).transpose(1, 0, 2)
-
-        sums = jnp.stack([sums_of[j][0] for j in range(4)])
-        qv_sum = jnp.stack([sums[:, :local], sums[:, 2 * local :]], axis=1)
-        qv_sum = qv_sum.reshape(4, 2 * heads, nd, hb).transpose(0, 2, 1, 3).reshape(4, nd, 2 * heads * hb)
-        up_sum = dbup[:, 0].reshape(4, hidden // hd, nd, hb).transpose(0, 2, 1, 3).reshape(4, nd, -1)
-        norms = jnp.stack([sums1[0], sums2[0], sums1[2], sums1[1], sums2[2], sums2[1]])
-        norms = norms.reshape(6, nd, ntens, -1).transpose(1, 2, 0, 3).reshape(nd, ntens, -1)
-        message = jnp.concatenate([to_axes(qv_sum), to_axes(up_sum), norms], axis=2)
-        (message,) = gate([message.reshape(nd * ntens, 1, -1)], [end])
-        message = lax.all_to_all(message, ("dp", "tensor"), 0, 0, tiled=True)
-        (last1,) = gate([last1], [message])
+        stay_near, fly_near = attend_back(0, got_near, [turn1])
+        got1 = across(fly_near, "dp", 1)
+        span_out = lambda i, *_: (i * span // ntens, 0, 0)
+        dx_parts = call(
+            input_back_kernel,
+            (steps,),
+            [rows_of(dprojs[j]) for j in range(4)] + [rows_of(dz1)] + [(w1[j], "any", None) for j in range(4)],
+            [((rows, part_len, width), BF, (1, part_len, width), span_out)] * ntens,
+            scratch=[pltpu.VMEM((4, width, wide), BF), sems(4)],
+            limit=63,
+            after=[stay_near],
+            cost=8.0,
+        )
+        token_parts = send_back(dx_parts)
+
+        got1, got_turn1, end = gate([got1, got_turn1, end], [dx_parts[0]])
+        (last1,) = summed([[(stay_near, ()), (got1, ()), (got_turn1, ())]])
+        small_got, near_sums = gate([small_got, sums_of[0]], [last1])
+        near_sums = jnp.concatenate([near_sums[:1, :local], near_sums[:1, 2 * local :]], axis=1)
+        own = small_keep[:16] + small_got + jnp.pad(near_sums, ((9, 6), (0, width - 2 * local)))
+        bit = 1
+        while bit < nd:
+            own = own + across(own, "dp", bit)
+            bit *= 2
+        rest = lax.dynamic_slice_in_dim(own[:6], (d * ntens + t) * (width // (nd * ntens)), width // (nd * ntens), 1)
+        grad_b_up = lax.dynamic_slice_in_dim(own[8].reshape(hidden // hd, hd), d * hb, hb, 1)
+        grad_b_qv = lax.dynamic_slice_in_dim(own[9, : 2 * local].reshape(2, heads, hd), d * hb, hb, 2)
         grad_one = settle(along(last1))
+        grad_tokens = collected(token_parts, [last1])
         end = settle(end)
         grad_down, grad_up = end[:, :hidden], end[:, hidden:]
-        got = jnp.sum(message, axis=(0, 1))
-        n1 = qv_sum.shape[2]
-        n2 = n1 + up_sum.shape[2]
-        grad_b_qv = got[:n1].reshape(2, heads, hb)
-        grad_b_up = got[n1:n2].reshape(hidden // hd, hb)
-        rest = got[n2:].reshape(6, -1)
         return (
             hidden_out,
             grad_tokens,

time: 428 us -> 369 us (0.86)
  waiting for transfers between devices: 89.9 us -> 34.1 us
  local copies, waits for them, and re-layouts: 44.3 us -> 22.8 us
  Pallas kernels: 210 us -> 231 us
  other arithmetic: 24.6 us -> 8.86 us
  starting transfers between devices: 50.7 us -> 64.1 us
    ppermute x33 -> x39, waiting for transfers between devices: 56.1 us -> 25.8 us  [across(): return lax.ppermute(array, axis, [(i, i ^ bit) for i in range(size)])]
    pallas_call x28 -> x34, Pallas kernels: 210 us -> 231 us  [call(): pl.pallas_call(body, grid_spec=pltpu.PrefetchScalarGridSpec(num_scalar_pr...]
    convert_element_type x8 -> x0, other arithmetic: 16.3 us -> none  [the longest x1 2.53 us: shards(): last1 = total(back0[0], got_near[0], got1, got_turn1).astype(BF)]
    all_to_all x4, waiting for transfers between devices: 14 us -> 0.01 us  [along(): lax.all_to_all(array, 'dp', 0, 0, tiled=True, axis_index_groups=groups)]
    unnamed x129 -> x79, local copies, waits for them, and re-layouts: 27.3 us -> 15.1 us
    ppermute x33 -> x39, starting transfers between devices: 22.1 us -> 31.1 us  [across(): return lax.ppermute(array, axis, [(i, i ^ bit) for i in range(size)])]
    slice x8 -> x5, local copies, waits for them, and re-layouts: 8.49 us -> 0.76 us  [the longest x1 0.72 us: shards(): near_sums[:1, :local]]
    ppermute x3, waiting for transfers between devices: 6.9 us -> 0.14 us  [turn(): lax.ppermute(array, 'dp', [(2 * ((z + k) % nh) + b, 2 * z + b) for z in r...]
  transfers between devices with their start and end apart: 42 -> 47, of which waited for: 12 -> 14; matrix products, arithmetic and copies ran while one was open for 10% -> 5% of each run, Pallas kernels for 38% -> 57%
where the time goes in v1:
time: 369 us; the launch traced here: 363 us
  Pallas kernels  231 us (63%)
  starting transfers between devices  64.1 us (17%)
  waiting for transfers between devices  34.1 us (9%)
  local copies, waits for them, and re-layouts  22.8 us (6%)
  other arithmetic  8.86 us (2%)
    pallas_call x34, Pallas kernels, call(): pl.pallas_call(body, grid_spec=pltpu.PrefetchScalarGridSpec(num_scalar_pr...  231 us
    ppermute x39, starting transfers between devices, across(): return lax.ppermute(array, axis, [(i, i ^ bit) for i in range(size)])  31.1 us
    ppermute x39, waiting for transfers between devices, across(): return lax.ppermute(array, axis, [(i, i ^ bit) for i in range(size)])  25.8 us
    all_to_all x4, starting transfers between devices, along(): lax.all_to_all(array, 'dp', 0, 0, tiled=True, axis_index_groups=groups)  19.8 us
    unnamed x79, local copies, waits for them, and re-layouts  15.1 us
    all_to_all x1, waiting for transfers between devices, shards(): lax.all_to_all(pooled, ('dp', 'tensor'), 0, 0, tiled=True)  8.17 us
  transfers between devices with their start and end apart: 47, of which 14 were waited for; matrix products, arithmetic and copies ran while one was open for 5% of the time, Pallas kernels for 57%

profile of v1, /device:TPU:0, one launch (start us, length us, event | category | flops | bytes accessed | tf_op | source)
XLA Modules:
  0.0 362.9 jit_solution(4450303130097178817)
XLA Ops:
  2.8 3.1 collective-permute-start.5
  5.8 2.6 collective-permute-start.4
  8.4 1.3 collective-permute-start.3
  9.8 1.4 copy-done.16
  11.2 2.3 shard_map.222
  13.5 1.6 collective-permute-start.1
  16.6 1.6 collective-permute-start.6
  20.0 5.6 %all-to-all-start = ((bf16[4,96,1024]{2,1,0:T(8,128)(2,1)}), bf16[4,96,1024]{2,1,0:T(8,128)(2,1)}, u32[]{:S(2)}, u32[]{:S(2)}) async-start(bf16[4,96,1024]{2,1,0:T(8,128)(2,1)} %shard_map.227.refs_8_), calls=%async_computation | async-start | bytes 1572864 | tf_op jit(solution)/shard_map/all_to_all | solution.py:607
  26.4 1.1 reshape.359
  27.5 2.3 collective-permute-done.6.other_ref
  29.8 2.9 shard_map.225.refs_4_.refs_5_
  32.7 1.6 collective-permute-start.8
  35.0 2.0 compare_select_fusion.refs_7_.refs_4_
  36.9 9.8 %shard_map.228 = (bf16[2,512,576]{2,1,0:T(8,128)(2,1)}, bf16[2,3,512,512]{3,2,1,0:T(8,128)(2,1)}, bf16[2,512,192]{2,1,0:T(8,128)(2,1)}, bf16[2,512,768]{2,1,0:T(8,128)(2,1)}) custom-call(bf16[2,128,768]{2,1,0:T(8,128)(2,1)} %copy-done.17, bf16[2,128,768]{2,1,0:T(8,128)(2,1)} %collective-permute-done.refs_1_, ...), custom_call_target="tpu_custom_call" | custom-call | flops 3104999936 | bytes 1024 | tf_op jit(solution)/shard_map/pallas_call | solution.py:60
  47.3 1.5 collective-permute-start.10
  50.5 4.8 %all-to-all-start.1 = ((bf16[4,96,768]{2,1,0:T(8,128)(2,1)}), bf16[4,96,768]{2,1,0:T(8,128)(2,1)S(1)}, u32[]{:S(2)}, u32[]{:S(2)}) async-start(bf16[4,96,768]{2,1,0:T(8,128)(2,1)} %shard_map.234), calls=%async_computation.1 | async-start | bytes 1179648 | tf_op jit(solution)/shard_map/all_to_all | solution.py:607
  55.3 9.3 %shard_map.230 = (bf16[2,512,576]{2,1,0:T(8,128)(2,1)}, bf16[2,3,512,512]{3,2,1,0:T(8,128)(2,1)}, bf16[2,512,192]{2,1,0:T(8,128)(2,1)}) custom-call(bf16[2,512,768]{2,1,0:T(8,128)(2,1)} %get-tuple-element.95.refs_0_.refs_5_, bf16[768,640]{1,0:T(8,128)(2,1)} %collective-permute-done.7.refs_1_.refs_6_, bf16[768,384]{1,0:T(8,128)(2,1)} %constant.78.clone.refs_5_.refs_2_, ...), custom_call_target="tpu_custom_call" | custom-call | flops 3104999936 | bytes 1024 | tf_op jit(solution)/shard_map/pallas_call | solution.py:60
  64.7 9.3 %shard_map.232 = (bf16[2,512,576]{2,1,0:T(8,128)(2,1)}, bf16[2,3,512,512]{3,2,1,0:T(8,128)(2,1)}, bf16[2,512,192]{2,1,0:T(8,128)(2,1)}) custom-call(bf16[2,512,768]{2,1,0:T(8,128)(2,1)} %get-tuple-element.95.refs_0_.refs_5_, bf16[768,640]{1,0:T(8,128)(2,1)} %shard_map.231.refs_1_.refs_7_, bf16[768,384]{1,0:T(8,128)(2,1)} %constant.78.clone.refs_5_.refs_2_, ...), custom_call_target="tpu_custom_call" | custom-call | flops 3104999936 | bytes 1024 | tf_op jit(solution)/shard_map/pallas_call | solution.py:60
  74.1 1.5 collective-permute-start.14
  76.2 3.3 shard_map.236.refs_1_.w0.refs_2_.refs_5_
  80.3 1.5 collective-permute-start.13
  81.8 9.3 %shard_map.238 = (bf16[2,512,576]{2,1,0:T(8,128)(2,1)}, bf16[2,3,512,512]{3,2,1,0:T(8,128)(2,1)}, bf16[2,512,192]{2,1,0:T(8,128)(2,1)}) custom-call(bf16[2,512,768]{2,1,0:T(8,128)(2,1)} %get-tuple-element.95.refs_0_.refs_5_, bf16[768,640]{1,0:T(8,128)(2,1)} %collective-permute-done.9.refs_1_.refs_8_, bf16[768,384]{1,0:T(8,128)(2,1)} %constant.78.clone.refs_5_.refs_2_, ...), custom_call_target="tpu_custom_call" | custom-call | flops 3104999936 | bytes 1024 | tf_op jit(solution)/shard_map/pallas_call | solution.py:60
  91.2 4.0 %collective-permute-done.13.refs_0_ = bf16[4,96,768]{2,1,0:T(8,128)(2,1)S(1)} collective-permute-done((bf16[4,96,768]{2,1,0:T(8,128)(2,1)}, bf16[4,96,768]{2,1,0:T(8,128)(2,1)S(1)}, u32[]{:S(2)}, u32[]{:S(2)}) %collective-permute-start.13) | collective-permute-done | bytes 589856 | tf_op jit(solution)/shard_map/ppermute | solution.py:604
  96.0 3.4 shard_map.240.w2.refs_4_.refs_7_
  99.5 1.3 collective-permute-start.16
  101.5 1.7 collective-permute-done.15.w3.refs_5_.refs_8_
  103.2 8.6 %shard_map.241 = (f32[1024,768]{1,0:T(8,128)}, f32[1024,1]{1,0:T(8,128)}, bf16[1024,768]{1,0:T(8,128)(2,1)}, f32[8,768]{1,0:T(8,128)}, f32[4,8,768]{2,1,0:T(8,128)}) custom-call(bf16[1024,192]{1,0:T(8,128)(2,1)} %bitcast.45, bf16[1024,192]{1,0:T(8,128)(2,1)} %bitcast.44, bf16[1024,192]{1,0:T(8,128)(2,1)} %bitcast.46, bf16[1024,192]{1,0:T(8,128)(2,1)} %bitcast.47, ...), custom_call_target="tpu_custom_call" | custom-call | flops 2760000000 | bytes 1024 | tf_op jit(solution)/shard_map/pallas_call | solution.py:60
  111.8 3.9 %collective-permute-done.16.refs_0_ = bf16[4,96,768]{2,1,0:T(8,128)(2,1)} collective-permute-done((bf16[4,96,768]{2,1,0:T(8,128)(2,1)S(1)}, bf16[4,96,768]{2,1,0:T(8,128)(2,1)}, u32[]{:S(2)}, u32[]{:S(2)}) %collective-permute-start.16) | collective-permute-done | bytes 589856 | tf_op jit(solution)/shard_map/ppermute | solution.py:604
  115.7 3.0 shard_map.243.refs_6_.w0
  118.7 13.8 %shard_map.244 = (bf16[4,1024,768]{2,1,0:T(8,128)(2,1)}, bf16[4,1024,768]{2,1,0:T(8,128)(2,1)}) custom-call(bf16[1024,768]{1,0:T(8,128)(2,1)} %get-tuple-element.102.refs_1_.refs_0_, f32[4,8,768]{2,1,0:T(8,128)} %get-tuple-element.103.refs_1_, bf16[768,1024]{1,0:T(8,128)(2,1)} %shard_map.236.refs_1_.w0.refs_2_.refs_5_, ...), custom_call_target="tpu_custom_call" | custom-call | flops 6899999744 | bytes 1024 | tf_op jit(solution)/shard_map/pallas_call | solution.py:60
  132.5 3.0 shard_map.246.w2
  139.7 14.5 %shard_map.247 = (f32[1024,768]{1,0:T(8,128)}, f32[1024,1]{1,0:T(8,128)}, bf16[2,128,768]{2,1,0:T(8,128)(2,1)}, bf16[2,128,768]{2,1,0:T(8,128)(2,1)}, bf16[2,128...) custom-call(bf16[4,1024,768]{2,1,0:T(8,128)(2,1)} %get-tuple-element.104.refs_1_.h_ref.refs_2_, ...), custom_call_target="tpu_custom_call" | custom-call | flops 4830000128 | bytes 1024 | tf_op jit(solution)/shard_map/pallas_call | solution.py:60
  154.2 6.1 %all-to-all-start.2 = ((bf16[32,8,768]{2,1,0:T(8,128)(2,1)}), bf16[32,8,768]{2,1,0:T(8,128)(2,1)}, u32[]{:S(2)}, u32[]{:S(2)}) async-start(bf16[32,8,768]{2,1,0:T(8,128)(2,1)} %get-tuple-element.112), calls=%async_computation.2 | async-start | bytes 786432 | tf_op jit(solution)/shard_map/all_to_all | solution.py:914
  163.7 1.7 collective-permute-start.21
  165.3 8.2 %all-to-all-done.2 = bf16[32,8,768]{2,1,0:T(8,128)(2,1)} async-done(((bf16[32,8,768]{2,1,0:T(8,128)(2,1)}), bf16[32,8,768]{2,1,0:T(8,128)(2,1)}, u32[]{:S(2)}, u32[]{:S(2)}) %all-to-all-start.2) | async-done | bytes 393248 | tf_op jit(solution)/shard_map/all_to_all | solution.py:914
  173.5 19.7 %shard_map.248 = (bf16[1024,768]{1,0:T(8,128)(2,1)}, f32[1024,768]{1,0:T(8,128)}, bf16[4,1024,768]{2,1,0:T(8,128)(2,1)}, bf16[2,2,4,96,768]{4,3,2,1,0:T(8,128)(2...) custom-call(s32[2]{0:T(128)} %pad_add_fusion.2.here_ref.refs_0_, bf16[256,768]{1,0:T(8,128)(2,1)} %bitcast.15.pooled_ref, ...), custom_call_target="tpu_custom_call" | custom-call | flops 11040000000 | bytes 1024 | tf_op jit(solution)/shard_map/pallas_call | solution.py:60
  193.3 1.7 copy-done.15
  196.0 3.9 %shard_map.249 = bf16[1024,768]{1,0:T(8,128)(2,1)} custom-call(s32[1]{0:T(128)} %bitcast.t_ref.refs_0_, bf16[2,128,768]{2,1,0:T(8,128)(2,1)S(1)} %copy-done.18, bf16[2,128,768]{2,1,0:T(8,128)(2,1)S(1)} %collective-permute-done.20.refs_2_, bf16[2,128,768]{2,1,0:T(8,128)(2,1)S(1)} %collective-permute-done.21.refs_3_, ...), custom_call_target="tpu_custom_call" | custom-call | flops 10350000128 | bytes 1024 | tf_op jit(solution)/shard_map/pallas_call | solution.py:60
  199.8 6.5 %shard_map.250.refs_4_ = bf16[2,2,4,96,768]{4,3,2,1,0:T(8,128)(2,1)} custom-call(s32[2]{0:T(128)} %pad_add_fusion.2.here_ref.refs_0_, bf16[1024,768]{1,0:T(8,128)(2,1)} %get-tuple-element.102.refs_1_.refs_0_, bf16[4,1024,768]{2,1,0:T(8,128)(2,1)} %get-tuple-element.119.refs_2_.refs_0_, bf16[2,2,4,96,768]{4,3,2,1,0:T(8,128)(2,1)} %get-tuple-element.116.refs_5_.refs_3_, ...), custom_call_target="tpu_custom_call" | custom-call | flops 13799999488 | bytes 1024 | tf_op jit(solution)/shard_map/pallas_call | solution.py:60
  206.8 6.9 %shard_map.251 = (bf16[2,4,96,768]{3,2,1,0:T(8,128)(2,1)}, bf16[2,4,96,768]{3,2,1,0:T(8,128)(2,1)}) custom-call(s32[2]{0:T(128)} %pad_add_fusion.2.here_ref.refs_0_, bf16[1024,768]{1,0:T(8,128)(2,1)} %get-tuple-element.122.refs_1_, bf16[4,1024,768]{2,1,0:T(8,128)(2,1)} %get-tuple-element.104.refs_1_.h_ref.refs_2_, ...), custom_call_target="tpu_custom_call" | custom-call | flops 13799999488 | bytes 1024 | tf_op jit(solution)/shard_map/pallas_call | solution.py:60
  213.8 8.1 %shard_map.252 = (bf16[2,4,96,768]{3,2,1,0:T(8,128)(2,1)}, bf16[2,4,96,768]{3,2,1,0:T(8,128)(2,1)}) custom-call(s32[2]{0:T(128)} %pad_add_fusion.2.here_ref.refs_0_, bf16[1024,768]{1,0:T(8,128)(2,1)} %get-tuple-element.102.refs_1_.refs_0_, bf16[4,1024,768]{2,1,0:T(8,128)(2,1)} %get-tuple-element.119.refs_2_.refs_0_, ...), custom_call_target="tpu_custom_call" | custom-call | flops 13799999488 | bytes 1024 | tf_op jit(solution)/shard_map/pallas_call | solution.py:60
  222.4 1.5 collective-permute-start.25
  223.9 17.4 %shard_map.253 = (f32[1024,768]{1,0:T(8,128)}, bf16[1024,768]{1,0:T(8,128)(2,1)}, bf16[4,1024,192]{2,1,0:T(8,128)(2,1)}, f32[8,768]{1,0:T(8,128)}) custom-call(bf16[4,1024,768]{2,1,0:T(8,128)(2,1)} %get-tuple-element.119.refs_2_.refs_0_, f32[1024,768]{1,0:T(8,128)} %get-tuple-element.120.refs_1_, f32[1024,768]{1,0:T(8,128)} %get-tuple-element.105.xh1_ref.refs_2_, ...), custom_call_target="tpu_custom_call" | custom-call | flops 4830000128 | bytes 1024 | tf_op jit(solution)/shard_map/pallas_call | solution.py:60
  241.3 11.0 %shard_map.254 = (bf16[2,4,96,768]{3,2,1,0:T(8,128)(2,1)}, f32[8,576]{1,0:T(8,128)}, bf16[2,512,576]{2,1,0:T(8,128)(2,1)}) custom-call(s32[2]{0:T(128)} %pad_add_fusion.2.here_ref.refs_0_, bf16[2,512,576]{2,1,0:T(8,128)(2,1)} %get-tuple-element.130.refs_1_, bf16[2,3,512,512]{3,2,1,0:T(8,128)(2,1)} %get-tuple-element.131.refs_2_, ...), custom_call_target="tpu_custom_call" | custom-call | flops 3795000064 | bytes 1024 | tf_op jit(solution)/shard_map/pallas_call | solution.py:60
  252.4 3.7 %shard_map.256 = (bf16[4,96,768]{2,1,0:T(8,128)(2,1)}, bf16[4,96,768]{2,1,0:T(8,128)(2,1)}) custom-call(bf16[2,4,96,768]{3,2,1,0:T(8,128)(2,1)} %get-tuple-element.129.refs_0_, bf16[2,4,96,768]{3,2,1,0:T(8,128)(2,1)} %get-tuple-element.133.refs_1_, bf16[2,4,96,768]{3,2,1,0:T(8,128)(2,1)} %get-tuple-element.134.refs_2_.refs_3_, ...), custom_call_target="tpu_custom_call" | custom-call | flops 20700000256 | bytes 1024 | tf_op jit(solution)/shard_map/pallas_call | solution.py:60
  258.3 11.2 %shard_map.257 = (bf16[4,96,768]{2,1,0:T(8,128)(2,1)}, bf16[4,96,768]{2,1,0:T(8,128)(2,1)}, f32[8,576]{1,0:T(8,128)}, bf16[2,512,576]{2,1,0:T(8,128)(2,1)}) custom-call(s32[2]{0:T(128)} %pad_add_fusion.2.here_ref.refs_0_, bf16[2,512,576]{2,1,0:T(8,128)(2,1)} %get-tuple-element.138.refs_1_, bf16[2,3,512,512]{3,2,1,0:T(8,128)(2,1)} %get-tuple-element.139.refs_2_, ...), custom_call_target="tpu_custom_call" | custom-call | flops 3795000064 | bytes 1024 | tf_op jit(solution)/shard_map/pallas_call | solution.py:60
  270.5 1.5 collective-permute-done.27.refs_0_
  272.1 1.5 collective-permute-done.28.refs_1_
  273.6 4.1 %shard_map.259.refs_7_ = bf16[4,96,1536]{2,1,0:T(8,128)(2,1)} custom-call(bf16[2,4,96,768]{3,2,1,0:T(8,128)(2,1)} %get-tuple-element.129.refs_0_, bf16[2,4,96,768]{3,2,1,0:T(8,128)(2,1)} %get-tuple-element.133.refs_1_, bf16[4,96,768]{2,1,0:T(8,128)(2,1)} %get-tuple-element.141.refs_2_, bf16[2,4,96,768]{3,2,1,0:T(8,128)(2,1)} %get-tuple-element.134.refs_2_.refs_3_, ...), custom_call_target="tpu_custom_call" | custom-call | flops 20700000256 | bytes 1024 | tf_op jit(solution)/shard_map/pallas_call | solution.py:60
  277.7 11.4 %shard_map.260 = (bf16[2,4,96,768]{3,2,1,0:T(8,128)(2,1)}, f32[8,576]{1,0:T(8,128)}, bf16[2,512,576]{2,1,0:T(8,128)(2,1)}) custom-call(s32[2]{0:T(128)} %pad_add_fusion.2.here_ref.refs_0_, bf16[2,512,576]{2,1,0:T(8,128)(2,1)} %get-tuple-element.127.refs_1_, bf16[2,3,512,512]{3,2,1,0:T(8,128)(2,1)} %get-tuple-element.128.refs_2_, ...), custom_call_target="tpu_custom_call" | custom-call | flops 3795000064 | bytes 1024 | tf_op jit(solution)/shard_map/pallas_call | solution.py:60
  290.0 4.3 %all-to-all-start.3 = ((bf16[4,96,1536]{2,1,0:T(8,128)(2,1)}), bf16[4,96,1536]{2,1,0:T(8,128)(2,1)}, u32[]{:S(2)}, u32[]{:S(2)}) async-start(bf16[4,96,1536]{2,1,0:T(8,128)(2,1)} %shard_map.259.refs_7_), calls=%async_computation.3 | async-start | bytes 2359296 | tf_op jit(solution)/shard_map/all_to_all | solution.py:607
  295.5 3.4 shard_map.263.refs_8_
  300.1 11.3 %shard_map.264 = (bf16[4,96,768]{2,1,0:T(8,128)(2,1)}, bf16[4,96,768]{2,1,0:T(8,128)(2,1)}, f32[8,576]{1,0:T(8,128)}, bf16[2,512,576]{2,1,0:T(8,128)(2,1)}) custom-call(s32[2]{0:T(128)} %pad_add_fusion.2.here_ref.refs_0_, bf16[2,512,576]{2,1,0:T(8,128)(2,1)} %get-tuple-element.117.refs_1_, bf16[2,3,512,512]{3,2,1,0:T(8,128)(2,1)} %get-tuple-element.118.refs_2_, ...), custom_call_target="tpu_custom_call" | custom-call | flops 3795000064 | bytes 1024 | tf_op jit(solution)/shard_map/pallas_call | solution.py:60
  311.7 1.7 collective-permute-start.38
  313.4 10.8 %shard_map.265 = (bf16[2,128,768]{2,1,0:T(8,128)(2,1)}, bf16[2,128,768]{2,1,0:T(8,128)(2,1)}, bf16[2,128,768]{2,1,0:T(8,128)(2,1)}, bf16[2,128,768]{2,1,0:T(8,128)(2,1)}) custom-call(bf16[1024,576]{1,0:T(8,128)(2,1)} %bitcast.52, bf16[1024,576]{1,0:T(8,128)(2,1)} %bitcast.51, bf16[1024,576]{1,0:T(8,128)(2,1)} %bitcast.50, bf16[1024,576]{1,0:T(8,128)(2,1)} %bitcast.49, ...), custom_call_target="tpu_custom_call" | custom-call | flops 2760000000 | bytes 1024 | tf_op jit(solution)/shard_map/pallas_call | solution.py:60
  324.8 1.4 collective-permute-start.35
  326.7 3.5 shard_map.267.refs_5_.refs_2_
  330.3 5.1 %all-to-all-start.4 = ((bf16[4,96,768]{2,1,0:T(8,128)(2,1)}), bf16[4,96,768]{2,1,0:T(8,128)(2,1)S(1)}, u32[]{:S(2)}, u32[]{:S(2)}) async-start(bf16[4,96,768]{2,1,0:T(8,128)(2,1)} %shard_map.267.refs_5_.refs_2_), calls=%async_computation.4 | async-start | bytes 1179648 | tf_op jit(solution)/shard_map/all_to_all | solution.py:607
  337.9 6.2 %collective-permute-done.35.refs_4_ = bf16[2,128,768]{2,1,0:T(8,128)(2,1)} collective-permute-done((bf16[2,128,768]{2,1,0:T(8,128)(2,1)}, bf16[2,128,768]{2,1,0:T(8,128)(2,1)}, u32[]{:S(2)}, u32[]{:S(2)}) %collective-permute-start.35) | collective-permute-done | bytes 393248 | tf_op jit(solution)/shard_map/ppermute | solution.py:604
  344.2 3.9 %shard_map.268 = bf16[1024,768]{1,0:T(8,128)(2,1)} custom-call(s32[1]{0:T(128)} %bitcast.t_ref.refs_0_, bf16[2,128,768]{2,1,0:T(8,128)(2,1)S(1)} %copy-done.6, bf16[2,128,768]{2,1,0:T(8,128)(2,1)S(1)} %collective-permute-done.33.refs_2_, bf16[2,128,768]{2,1,0:T(8,128)(2,1)S(1)} %collective-permute-done.34.refs_3_, ...), custom_call_target="tpu_custom_call" | custom-call | flops 10350000128 | bytes 1024 | tf_op jit(solution)/shard_map/pallas_call | solution.py:60
  348.1 1.7 collective-permute-start.40
  349.8 1.5 convert_reduce_fusion
  352.2 2.6 collective-permute-start.41
  355.7 1.9 collective-permute-done.41
  (220 shorter events, 38.7 us)
Async XLA Ops:
  0.6 15.1 %copy-start = (s32[8,512]{1,0:T(8,128)S(1)}, s32[8,512]{1,0:T(8,128)}, u32[]{:S(2)}) copy-start(s32[8,512]{1,0:T(8,128)} %param.25) | copy-start | bytes 49156
  2.8 12.3 %copy-start.27 = (bf16[12,8]{0,1:T(8,128)(2,1)S(1)}, bf16[12,8]{0,1:T(8,128)(2,1)}, u32[]{:S(2)}) copy-start(bf16[12,8]{0,1:T(8,128)(2,1)} %param.20) | copy-start | bytes 580
  2.8 12.5 %copy-start.30 = (bf16[2,96]{1,0:T(2,128)(2,1)S(1)}, bf16[2,96]{1,0:T(2,128)(2,1)}, u32[]{:S(2)}) copy-start(bf16[2,96]{1,0:T(2,128)(2,1)} %param.22) | copy-start | bytes 1156
  2.8 13.0 %collective-permute-start.5 = (bf16[96,640]{1,0:T(8,128)(2,1)S(1)}, bf16[96,640]{1,0:T(8,128)(2,1)S(1)}, u32[]{:S(2)}, u32[]{:S(2)}) collective-permute-start(bf16[96,640]{1,0:T(8,128)(2,1)S(1)} %shard_map.223.refs_0_), channel_id=1, source_target_pairs={{24,0},{28,4},{0,8},{4,12},{8,16},{12,20},{16,24},{20,28},{25,1},{... | collective-permute-start | bytes 368648 | tf_op jit(solution)/shard_map/ppermute | solution.py:630
  5.8 10.7 %collective-permute-start.4 = (bf16[96,640]{1,0:T(8,128)(2,1)S(1)}, bf16[96,640]{1,0:T(8,128)(2,1)S(1)}, u32[]{:S(2)}, u32[]{:S(2)}) collective-permute-start(bf16[96,640]{1,0:T(8,128)(2,1)S(1)} %shard_map.223.refs_0_), channel_id=1, source_target_pairs={{16,0},{20,4},{24,8},{28,12},{0,16},{4,20},{8,24},{12,28},{17,1},{... | collective-permute-start | bytes 368648 | tf_op jit(solution)/shard_map/ppermute | solution.py:630
  8.4 8.1 %collective-permute-start.3 = (bf16[96,640]{1,0:T(8,128)(2,1)S(1)}, bf16[96,640]{1,0:T(8,128)(2,1)S(1)}, u32[]{:S(2)}, u32[]{:S(2)}) collective-permute-start(bf16[96,640]{1,0:T(8,128)(2,1)S(1)} %shard_map.223.refs_0_), channel_id=1, source_target_pairs={{8,0},{12,4},{16,8},{20,12},{24,16},{28,20},{0,24},{4,28},{9,1},{1... | collective-permute-start | bytes 368648 | tf_op jit(solution)/shard_map/ppermute | solution.py:630
  9.8 5.6 %copy-start.28 = (bf16[4,96]{1,0:T(4,128)(2,1)S(1)}, bf16[4,96]{1,0:T(4,128)(2,1)}, u32[]{:S(2)}) copy-start(bf16[4,96]{1,0:T(4,128)(2,1)} %param.23) | copy-start | bytes 2308
  13.5 4.8 %copy-start.9 = (bf16[192,96]{1,0:T(8,128)(2,1)S(1)}, bf16[192,96]{1,0:T(8,128)(2,1)}, u32[]{:S(2)}) copy-start(bf16[192,96]{1,0:T(8,128)(2,1)} %refs_1_.1) | copy-start | bytes 110596
  13.5 23.5 %collective-permute-start.1 = (bf16[2,128,768]{2,1,0:T(8,128)(2,1)}, bf16[2,128,768]{2,1,0:T(8,128)(2,1)}, u32[]{:S(2)}, u32[]{:S(2)}) collective-permute-start(bf16[2,128,768]{2,1,0:T(8,128)(2,1)} %get-tuple-element.92), channel_id=1, source_target_pairs={{0,2},{1,3},{2,0},{3,1},{4,6},{5,7},{6,4},{7,5},{8,10},{9,11},{10,... | collective-permute-start | bytes 1179656 | tf_op jit(solution)/shard_map/ppermute | solution.py:604
  15.0 21.9 %collective-permute-start.2 = (bf16[2,128,768]{2,1,0:T(8,128)(2,1)}, bf16[2,128,768]{2,1,0:T(8,128)(2,1)}, u32[]{:S(2)}, u32[]{:S(2)}) collective-permute-start(bf16[2,128,768]{2,1,0:T(8,128)(2,1)} %get-tuple-element.93), channel_id=1, source_target_pairs={{0,3},{1,2},{2,1},{3,0},{4,7},{5,6},{6,5},{7,4},{8,11},{9,10},{10,... | collective-permute-start | bytes 1179656 | tf_op jit(solution)/shard_map/ppermute | solution.py:604
  15.7 21.2 %collective-permute-start = (bf16[2,128,768]{2,1,0:T(8,128)(2,1)S(1)}, bf16[2,128,768]{2,1,0:T(8,128)(2,1)}, u32[]{:S(2)}, u32[]{:S(2)}) collective-permute-start(bf16[2,128,768]{2,1,0:T(8,128)(2,1)S(1)} %get-tuple-element.91.refs_4_.refs_3_.refs_1_), channel_id=1, source_target_pairs={{0,1},{1,0},{2,3},{3,2},{4,5},{5,4},{6,7},{7,6},{8,9},{9,8},{10,11... | collective-permute-start | bytes 1179656 | tf_op jit(solution)/shard_map/ppermute | solution.py:604
  16.6 13.2 %collective-permute-start.6 = (bf16[4,96,640]{2,1,0:T(8,128)(2,1)S(1)}, bf16[4,96,640]{2,1,0:T(8,128)(2,1)}, u32[]{:S(2)}, u32[]{:S(2)}) collective-permute-start(bf16[4,96,640]{2,1,0:T(8,128)(2,1)S(1)} %shard_map.224.own_ref.refs_1_), channel_id=1, source_target_pairs={{0,4},{4,0},{8,12},{12,8},{16,20},{20,16},{24,28},{28,24},{1,5},{5... | collective-permute-start | bytes 1474568 | tf_op jit(solution)/shard_map/ppermute | solution.py:604
  19.9 6.2 %copy-start.32 = (s32[8]{0:T(128)S(1)}, s32[8]{0:T(128)}, u32[]{:S(2)}) copy-start(s32[8]{0:T(128)} %param.24) | copy-start | bytes 100
  19.9 6.3 %copy-start.25 = (bf16[768,96]{0,1:T(8,128)(2,1)S(1)}, bf16[768,96]{0,1:T(8,128)(2,1)}, u32[]{:S(2)}) copy-start(bf16[768,96]{0,1:T(8,128)(2,1)} %param.21) | copy-start | bytes 442372
  20.0 26.8 %all-to-all-start = ((bf16[4,96,1024]{2,1,0:T(8,128)(2,1)}), bf16[4,96,1024]{2,1,0:T(8,128)(2,1)}, u32[]{:S(2)}, u32[]{:S(2)}) async-start(bf16[4,96,1024]{2,1,0:T(8,128)(2,1)} %shard_map.227.refs_8_), calls=%async_computation | async-start | bytes 1572864 | tf_op jit(solution)/shard_map/all_to_all | solution.py:607
  32.7 22.6 %collective-permute-start.7 = (bf16[768,640]{1,0:T(8,128)(2,1)}, bf16[768,640]{1,0:T(8,128)(2,1)}, u32[]{:S(2)}, u32[]{:S(2)}) collective-permute-start(bf16[768,640]{1,0:T(8,128)(2,1)} %shard_map.225.refs_4_.refs_5_), channel_id=1, source_target_pairs={{0,1},{1,0},{2,3},{3,2},{4,5},{5,4},{6,7},{7,6},{8,9},{9,8},{10,11... | collective-permute-start | bytes 2949128 | tf_op jit(solution)/shard_map/ppermute | solution.py:604
  32.7 31.9 %collective-permute-start.8 = (bf16[768,640]{1,0:T(8,128)(2,1)}, bf16[768,640]{1,0:T(8,128)(2,1)}, u32[]{:S(2)}, u32[]{:S(2)}) collective-permute-start(bf16[768,640]{1,0:T(8,128)(2,1)} %shard_map.225.refs_4_.refs_5_), channel_id=1, source_target_pairs={{0,2},{1,3},{2,0},{3,1},{4,6},{5,7},{6,4},{7,5},{8,10},{9,11},{10,... | collective-permute-start | bytes 2949128 | tf_op jit(solution)/shard_map/ppermute | solution.py:604
  46.8 27.3 %collective-permute-start.11 = (bf16[4,96,1024]{2,1,0:T(8,128)(2,1)}, bf16[4,96,1024]{2,1,0:T(8,128)(2,1)}, u32[]{:S(2)}, u32[]{:S(2)}) collective-permute-start(bf16[4,96,1024]{2,1,0:T(8,128)(2,1)} %shard_map.229.refs_5_.refs_1_.own_ref), channel_id=1, source_target_pairs={{0,2},{1,3},{2,0},{3,1},{4,6},{5,7},{6,4},{7,5},{8,10},{9,11},{10,... | collective-permute-start | bytes 2359304 | tf_op jit(solution)/shard_map/ppermute | solution.py:604
  47.3 26.8 %collective-permute-start.10 = (bf16[4,96,1024]{2,1,0:T(8,128)(2,1)}, bf16[4,96,1024]{2,1,0:T(8,128)(2,1)}, u32[]{:S(2)}, u32[]{:S(2)}) collective-permute-start(bf16[4,96,1024]{2,1,0:T(8,128)(2,1)} %shard_map.229.refs_5_.refs_1_.own_ref), channel_id=1, source_target_pairs={{0,4},{4,0},{8,12},{12,8},{16,20},{20,16},{24,28},{28,24},{1,5},{5... | collective-permute-start | bytes 2359304 | tf_op jit(solution)/shard_map/ppermute | solution.py:604
  50.5 29.0 %all-to-all-start.1 = ((bf16[4,96,768]{2,1,0:T(8,128)(2,1)}), bf16[4,96,768]{2,1,0:T(8,128)(2,1)S(1)}, u32[]{:S(2)}, u32[]{:S(2)}) async-start(bf16[4,96,768]{2,1,0:T(8,128)(2,1)} %shard_map.234), calls=%async_computation.1 | async-start | bytes 1179648 | tf_op jit(solution)/shard_map/all_to_all | solution.py:607
  64.7 17.2 %collective-permute-start.9 = (bf16[768,640]{1,0:T(8,128)(2,1)}, bf16[768,640]{1,0:T(8,128)(2,1)}, u32[]{:S(2)}, u32[]{:S(2)}) collective-permute-start(bf16[768,640]{1,0:T(8,128)(2,1)} %shard_map.231.refs_1_.refs_7_), channel_id=1, source_target_pairs={{0,1},{1,0},{2,3},{3,2},{4,5},{5,4},{6,7},{7,6},{8,9},{9,8},{10,11... | collective-permute-start | bytes 2949128 | tf_op jit(solution)/shard_map/ppermute | solution.py:604
  74.1 21.1 %collective-permute-start.14 = (bf16[4,96,1024]{2,1,0:T(8,128)(2,1)}, bf16[4,96,1024]{2,1,0:T(8,128)(2,1)}, u32[]{:S(2)}, u32[]{:S(2)}) collective-permute-start(bf16[4,96,1024]{2,1,0:T(8,128)(2,1)} %get-tuple-element.100.own_ref), channel_id=1, source_target_pairs={{0,4},{4,0},{8,12},{12,8},{16,20},{20,16},{24,28},{28,24},{1,5},{5... | collective-permute-start | bytes 2359304 | tf_op jit(solution)/shard_map/ppermute | solution.py:604
  80.3 14.9 %collective-permute-start.13 = (bf16[4,96,768]{2,1,0:T(8,128)(2,1)}, bf16[4,96,768]{2,1,0:T(8,128)(2,1)S(1)}, u32[]{:S(2)}, u32[]{:S(2)}) collective-permute-start(bf16[4,96,768]{2,1,0:T(8,128)(2,1)} %shard_map.237.refs_5_.own_ref), channel_id=1, source_target_pairs={{0,2},{1,3},{2,0},{3,1},{4,6},{5,7},{6,4},{7,5},{8,10},{9,11},{10,... | collective-permute-start | bytes 1769480 | tf_op jit(solution)/shard_map/ppermute | solution.py:604
  81.8 19.7 %collective-permute-start.12 = (bf16[768,1024]{1,0:T(8,128)(2,1)}, bf16[768,1024]{1,0:T(8,128)(2,1)}, u32[]{:S(2)}, u32[]{:S(2)}) collective-permute-start(bf16[768,1024]{1,0:T(8,128)(2,1)} %shard_map.236.refs_1_.w0.refs_2_.refs_5_), channel_id=1, source_target_pairs={{0,1},{1,0},{2,3},{3,2},{4,5},{5,4},{6,7},{7,6},{8,9},{9,8},{10,11... | collective-permute-start | bytes 4718600 | tf_op jit(solution)/shard_map/ppermute | solution.py:604
  99.5 3.8 %collective-permute-start.15 = (bf16[768,1024]{1,0:T(8,128)(2,1)}, bf16[768,1024]{1,0:T(8,128)(2,1)}, u32[]{:S(2)}, u32[]{:S(2)}) collective-permute-start(bf16[768,1024]{1,0:T(8,128)(2,1)} %shard_map.240.w2.refs_4_.refs_7_), channel_id=1, source_target_pairs={{0,1},{1,0},{2,3},{3,2},{4,5},{5,4},{6,7},{7,6},{8,9},{9,8},{10,11... | collective-permute-start | bytes 4718600 | tf_op jit(solution)/shard_map/ppermute | solution.py:604
  99.5 16.2 %collective-permute-start.16 = (bf16[4,96,768]{2,1,0:T(8,128)(2,1)S(1)}, bf16[4,96,768]{2,1,0:T(8,128)(2,1)}, u32[]{:S(2)}, u32[]{:S(2)}) collective-permute-start(bf16[4,96,768]{2,1,0:T(8,128)(2,1)S(1)} %copy-done.20), channel_id=1, source_target_pairs={{0,4},{4,0},{8,12},{12,8},{16,20},{20,16},{24,28},{28,24},{1,5},{5... | collective-permute-start | bytes 1769480 | tf_op jit(solution)/shard_map/ppermute | solution.py:604
  100.7 31.7 %collective-permute-start.18 = (bf16[4,96,768]{2,1,0:T(8,128)(2,1)}, bf16[4,96,768]{2,1,0:T(8,128)(2,1)}, u32[]{:S(2)}, u32[]{:S(2)}) collective-permute-start(bf16[4,96,768]{2,1,0:T(8,128)(2,1)} %get-tuple-element.107.own_ref), channel_id=1, source_target_pairs={{0,4},{4,0},{8,12},{12,8},{16,20},{20,16},{24,28},{28,24},{1,5},{5... | collective-permute-start | bytes 1769480 | tf_op jit(solution)/shard_map/ppermute | solution.py:604
  118.7 18.9 %collective-permute-start.17 = (bf16[768,768]{1,0:T(8,128)(2,1)}, bf16[768,768]{1,0:T(8,128)(2,1)}, u32[]{:S(2)}, u32[]{:S(2)}) collective-permute-start(bf16[768,768]{1,0:T(8,128)(2,1)} %shard_map.243.refs_6_.w0), channel_id=1, source_target_pairs={{0,1},{1,0},{2,3},{3,2},{4,5},{5,4},{6,7},{7,6},{8,9},{9,8},{10,11... | collective-permute-start | bytes 3538952 | tf_op jit(solution)/shard_map/ppermute | solution.py:604
  135.5 3.2 collective-permute-start.19
  139.7 20.7 %copy-start.29 = (f32[128]{0:T(128)S(1)}, f32[128]{0:T(128)}, u32[]{:S(2)}) copy-start(f32[128]{0:T(128)} %param.27) | copy-start | bytes 1540
  139.7 20.9 %copy-start.26 = (s32[256]{0:T(256)S(1)}, s32[256]{0:T(256)}, u32[]{:S(2)}) copy-start(s32[256]{0:T(256)} %param.26) | copy-start | bytes 3076
  154.2 19.3 %all-to-all-start.2 = ((bf16[32,8,768]{2,1,0:T(8,128)(2,1)}), bf16[32,8,768]{2,1,0:T(8,128)(2,1)}, u32[]{:S(2)}, u32[]{:S(2)}) async-start(bf16[32,8,768]{2,1,0:T(8,128)(2,1)} %get-tuple-element.112), calls=%async_computation.2 | async-start | bytes 786432 | tf_op jit(solution)/shard_map/all_to_all | solution.py:914
  163.3 30.0 %collective-permute-start.20 = (bf16[2,128,768]{2,1,0:T(8,128)(2,1)}, bf16[2,128,768]{2,1,0:T(8,128)(2,1)S(1)}, u32[]{:S(2)}, u32[]{:S(2)}) collective-permute-start(bf16[2,128,768]{2,1,0:T(8,128)(2,1)} %get-tuple-element.109), channel_id=1, source_target_pairs={{0,1},{1,0},{2,3},{3,2},{4,5},{5,4},{6,7},{7,6},{8,9},{9,8},{10,11... | collective-permute-start | bytes 1179656 | tf_op jit(solution)/shard_map/ppermute | solution.py:604
  163.7 29.6 %collective-permute-start.21 = (bf16[2,128,768]{2,1,0:T(8,128)(2,1)}, bf16[2,128,768]{2,1,0:T(8,128)(2,1)S(1)}, u32[]{:S(2)}, u32[]{:S(2)}) collective-permute-start(bf16[2,128,768]{2,1,0:T(8,128)(2,1)} %get-tuple-element.110), channel_id=1, source_target_pairs={{0,2},{1,3},{2,0},{3,1},{4,6},{5,7},{6,4},{7,5},{8,10},{9,11},{10,... | collective-permute-start | bytes 1179656 | tf_op jit(solution)/shard_map/ppermute | solution.py:604
  165.3 27.9 %collective-permute-start.22 = (bf16[2,128,768]{2,1,0:T(8,128)(2,1)}, bf16[2,128,768]{2,1,0:T(8,128)(2,1)}, u32[]{:S(2)}, u32[]{:S(2)}) collective-permute-start(bf16[2,128,768]{2,1,0:T(8,128)(2,1)} %get-tuple-element.111), channel_id=1, source_target_pairs={{0,3},{1,2},{2,1},{3,0},{4,7},{5,6},{6,5},{7,4},{8,11},{9,10},{10,... | collective-permute-start | bytes 1179656 | tf_op jit(solution)/shard_map/ppermute | solution.py:604
  193.2 13.7 %collective-permute-start.24 = (bf16[2,2,4,96,768]{4,3,2,1,0:T(8,128)(2,1)}, bf16[2,2,4,96,768]{4,3,2,1,0:T(8,128)(2,1)}, u32[]{:S(2)}, u32[]{:S(2)}) collective-permute-start(bf16[2,2,4,96,768]{4,3,2,1,0:T(8,128)(2,1)} %get-tuple-element.116.refs_5_.refs_3_), channel_id=1, source_target_pairs={{0,1},{1,0},{2,3},{3,2},{4,5},{5,4},{6,7},{7,6},{8,9},{9,8},{10,11... | collective-permute-start | bytes 7077896 | tf_op jit(solution)/shard_map/ppermute | solution.py:604
  206.4 7.4 %collective-permute-start.23 = (bf16[2,2,4,96,768]{4,3,2,1,0:T(8,128)(2,1)}, bf16[2,2,4,96,768]{4,3,2,1,0:T(8,128)(2,1)}, u32[]{:S(2)}, u32[]{:S(2)}) collective-permute-start(bf16[2,2,4,96,768]{4,3,2,1,0:T(8,128)(2,1)} %shard_map.250.refs_4_), channel_id=1, source_target_pairs={{0,1},{1,0},{2,3},{3,2},{4,5},{5,4},{6,7},{7,6},{8,9},{9,8},{10,11... | collective-permute-start | bytes 7077896 | tf_op jit(solution)/shard_map/ppermute | solution.py:604
  221.9 30.5 %collective-permute-start.26 = (bf16[2,4,96,768]{3,2,1,0:T(8,128)(2,1)}, bf16[2,4,96,768]{3,2,1,0:T(8,128)(2,1)}, u32[]{:S(2)}, u32[]{:S(2)}) collective-permute-start(bf16[2,4,96,768]{3,2,1,0:T(8,128)(2,1)} %get-tuple-element.124.refs_9_.refs_7_), channel_id=1, source_target_pairs={{0,2},{1,3},{2,0},{3,1},{4,6},{5,7},{6,4},{7,5},{8,10},{9,11},{10,... | collective-permute-start | bytes 3538952 | tf_op jit(solution)/shard_map/ppermute | solution.py:604
  222.4 30.0 %collective-permute-start.25 = (bf16[2,4,96,768]{3,2,1,0:T(8,128)(2,1)}, bf16[2,4,96,768]{3,2,1,0:T(8,128)(2,1)}, u32[]{:S(2)}, u32[]{:S(2)}) collective-permute-start(bf16[2,4,96,768]{3,2,1,0:T(8,128)(2,1)} %get-tuple-element.123.refs_4_), channel_id=1, source_target_pairs={{0,4},{4,0},{8,12},{12,8},{16,20},{20,16},{24,28},{28,24},{1,5},{5... | collective-permute-start | bytes 3538952 | tf_op jit(solution)/shard_map/ppermute | solution.py:604
  252.3 6.0 %collective-permute-start.29 = (bf16[2,4,96,768]{3,2,1,0:T(8,128)(2,1)}, bf16[2,4,96,768]{3,2,1,0:T(8,128)(2,1)}, u32[]{:S(2)}, u32[]{:S(2)}) collective-permute-start(bf16[2,4,96,768]{3,2,1,0:T(8,128)(2,1)} %get-tuple-element.132.refs_2_), channel_id=1, source_target_pairs={{0,1},{1,0},{2,3},{3,2},{4,5},{5,4},{6,7},{7,6},{8,9},{9,8},{10,11... | collective-permute-start | bytes 3538952 | tf_op jit(solution)/shard_map/ppermute | solution.py:604
  256.2 15.9 %collective-permute-start.27 = (bf16[4,96,768]{2,1,0:T(8,128)(2,1)}, bf16[4,96,768]{2,1,0:T(8,128)(2,1)S(1)}, u32[]{:S(2)}, u32[]{:S(2)}) collective-permute-start(bf16[4,96,768]{2,1,0:T(8,128)(2,1)} %get-tuple-element.136.refs_8_), channel_id=1, source_target_pairs={{0,2},{1,3},{2,0},{3,1},{4,6},{5,7},{6,4},{7,5},{8,10},{9,11},{10,... | collective-permute-start | bytes 1769480 | tf_op jit(solution)/shard_map/ppermute | solution.py:604
  257.3 16.3 %collective-permute-start.28 = (bf16[4,96,768]{2,1,0:T(8,128)(2,1)}, bf16[4,96,768]{2,1,0:T(8,128)(2,1)}, u32[]{:S(2)}, u32[]{:S(2)}) collective-permute-start(bf16[4,96,768]{2,1,0:T(8,128)(2,1)} %get-tuple-element.137.refs_9_), channel_id=1, source_target_pairs={{0,4},{4,0},{8,12},{12,8},{16,20},{20,16},{24,28},{28,24},{1,5},{5... | collective-permute-start | bytes 1769480 | tf_op jit(solution)/shard_map/ppermute | solution.py:604
  269.5 26.1 %collective-permute-start.31 = (bf16[4,96,768]{2,1,0:T(8,128)(2,1)}, bf16[4,96,768]{2,1,0:T(8,128)(2,1)}, u32[]{:S(2)}, u32[]{:S(2)}) collective-permute-start(bf16[4,96,768]{2,1,0:T(8,128)(2,1)} %get-tuple-element.144), channel_id=1, source_target_pairs={{0,4},{4,0},{8,12},{12,8},{16,20},{20,16},{24,28},{28,24},{1,5},{5... | collective-permute-start | bytes 1769480 | tf_op jit(solution)/shard_map/ppermute | solution.py:604
  277.7 11.5 %copy-start.8 = (f32[4,8,768]{2,1,0:T(8,128)S(1)}, f32[4,8,768]{2,1,0:T(8,128)}, u32[]{:S(2)}) copy-start(f32[4,8,768]{2,1,0:T(8,128)} %get-tuple-element.147.refs_2_) | copy-start | bytes 294916
  277.7 11.5 %copy-start.10 = (f32[8,768]{1,0:T(8,128)S(1)}, f32[8,768]{1,0:T(8,128)}, u32[]{:S(2)}) copy-start(f32[8,768]{1,0:T(8,128)} %get-tuple-element.146.refs_1_) | copy-start | bytes 73732
  277.7 11.5 %copy-start.11 = (f32[8,768]{1,0:T(8,128)S(1)}, f32[8,768]{1,0:T(8,128)}, u32[]{:S(2)}) copy-start(f32[8,768]{1,0:T(8,128)} %get-tuple-element.145.refs_0_) | copy-start | bytes 73732
  277.7 11.5 %copy-start.12 = (f32[8,576]{1,0:T(8,128)S(1)}, f32[8,576]{1,0:T(8,128)}, u32[]{:S(2)}) copy-start(f32[8,576]{1,0:T(8,128)} %get-tuple-element.150.refs_5_) | copy-start | bytes 55300
  277.7 11.5 %copy-start.13 = (f32[8,576]{1,0:T(8,128)S(1)}, f32[8,576]{1,0:T(8,128)}, u32[]{:S(2)}) copy-start(f32[8,576]{1,0:T(8,128)} %get-tuple-element.149.refs_4_) | copy-start | bytes 55300
  290.0 4.9 %collective-permute-start.32 = (f32[24,768]{1,0:T(8,128)S(1)}, f32[24,768]{1,0:T(8,128)S(1)}, u32[]{:S(2)}, u32[]{:S(2)}) collective-permute-start(f32[24,768]{1,0:T(8,128)S(1)} %get-tuple-element.152), channel_id=1, source_target_pairs={{0,1},{1,0},{2,3},{3,2},{4,5},{5,4},{6,7},{7,6},{8,9},{9,8},{10,11... | collective-permute-start | bytes 221192 | tf_op jit(solution)/shard_map/ppermute | solution.py:604
  290.0 36.2 %all-to-all-start.3 = ((bf16[4,96,1536]{2,1,0:T(8,128)(2,1)}), bf16[4,96,1536]{2,1,0:T(8,128)(2,1)}, u32[]{:S(2)}, u32[]{:S(2)}) async-start(bf16[4,96,1536]{2,1,0:T(8,128)(2,1)} %shard_map.259.refs_7_), calls=%async_computation.3 | async-start | bytes 2359296 | tf_op jit(solution)/shard_map/all_to_all | solution.py:607
  294.3 5.7 %collective-permute-start.30 = (bf16[2,4,96,768]{3,2,1,0:T(8,128)(2,1)}, bf16[2,4,96,768]{3,2,1,0:T(8,128)(2,1)}, u32[]{:S(2)}, u32[]{:S(2)}) collective-permute-start(bf16[2,4,96,768]{3,2,1,0:T(8,128)(2,1)} %get-tuple-element.143.refs_6_), channel_id=1, source_target_pairs={{0,1},{1,0},{2,3},{3,2},{4,5},{5,4},{6,7},{7,6},{8,9},{9,8},{10,11... | collective-permute-start | bytes 3538952 | tf_op jit(solution)/shard_map/ppermute | solution.py:604
  298.9 25.9 %collective-permute-start.37 = (bf16[4,96,768]{2,1,0:T(8,128)(2,1)}, bf16[4,96,768]{2,1,0:T(8,128)(2,1)}, u32[]{:S(2)}, u32[]{:S(2)}) collective-permute-start(bf16[4,96,768]{2,1,0:T(8,128)(2,1)} %shard_map.263.refs_8_), channel_id=1, source_target_pairs={{0,2},{1,3},{2,0},{3,1},{4,6},{5,7},{6,4},{7,5},{8,10},{9,11},{10,... | collective-permute-start | bytes 1769480 | tf_op jit(solution)/shard_map/ppermute | solution.py:604
  300.1 11.7 %copy-start.22 = (f32[24,768]{1,0:T(8,128)S(1)}, f32[24,768]{1,0:T(8,128)}, u32[]{:S(2)}) copy-start(f32[24,768]{1,0:T(8,128)} %add.166.refs_1_) | copy-start | bytes 221188
  311.4 15.4 %collective-permute-start.36 = (bf16[4,96,768]{2,1,0:T(8,128)(2,1)}, bf16[4,96,768]{2,1,0:T(8,128)(2,1)}, u32[]{:S(2)}, u32[]{:S(2)}) collective-permute-start(bf16[4,96,768]{2,1,0:T(8,128)(2,1)} %get-tuple-element.163), channel_id=1, source_target_pairs={{0,4},{4,0},{8,12},{12,8},{16,20},{20,16},{24,28},{28,24},{1,5},{5... | collective-permute-start | bytes 1769480 | tf_op jit(solution)/shard_map/ppermute | solution.py:604
  311.7 23.7 %collective-permute-start.38 = (f32[16,768]{1,0:T(8,128)S(1)}, f32[16,768]{1,0:T(8,128)S(1)}, u32[]{:S(2)}, u32[]{:S(2)}) collective-permute-start(f32[16,768]{1,0:T(8,128)S(1)} %pad_maximum_fusion), channel_id=1, source_target_pairs={{0,2},{1,3},{2,0},{3,1},{4,6},{5,7},{6,4},{7,5},{8,10},{9,11},{10,... | collective-permute-start | bytes 147464 | tf_op jit(solution)/shard_map/ppermute | solution.py:604
  324.3 13.7 %collective-permute-start.33 = (bf16[2,128,768]{2,1,0:T(8,128)(2,1)}, bf16[2,128,768]{2,1,0:T(8,128)(2,1)S(1)}, u32[]{:S(2)}, u32[]{:S(2)}) collective-permute-start(bf16[2,128,768]{2,1,0:T(8,128)(2,1)} %get-tuple-element.160), channel_id=1, source_target_pairs={{0,1},{1,0},{2,3},{3,2},{4,5},{5,4},{6,7},{7,6},{8,9},{9,8},{10,11... | collective-permute-start | bytes 1179656 | tf_op jit(solution)/shard_map/ppermute | solution.py:604
  324.4 13.6 %collective-permute-start.34 = (bf16[2,128,768]{2,1,0:T(8,128)(2,1)}, bf16[2,128,768]{2,1,0:T(8,128)(2,1)S(1)}, u32[]{:S(2)}, u32[]{:S(2)}) collective-permute-start(bf16[2,128,768]{2,1,0:T(8,128)(2,1)} %get-tuple-element.161), channel_id=1, source_target_pairs={{0,2},{1,3},{2,0},{3,1},{4,6},{5,7},{6,4},{7,5},{8,10},{9,11},{10,... | collective-permute-start | bytes 1179656 | tf_op jit(solution)/shard_map/ppermute | solution.py:604
  324.8 19.3 %collective-permute-start.35 = (bf16[2,128,768]{2,1,0:T(8,128)(2,1)}, bf16[2,128,768]{2,1,0:T(8,128)(2,1)}, u32[]{:S(2)}, u32[]{:S(2)}) collective-permute-start(bf16[2,128,768]{2,1,0:T(8,128)(2,1)} %get-tuple-element.162), channel_id=1, source_target_pairs={{0,3},{1,2},{2,1},{3,0},{4,7},{5,6},{6,5},{7,4},{8,11},{9,10},{10,... | collective-permute-start | bytes 1179656 | tf_op jit(solution)/shard_map/ppermute | solution.py:604
  330.3 13.9 %copy-start.4 = (bf16[4,96,768]{2,1,0:T(8,128)(2,1)S(1)}, bf16[4,96,768]{2,1,0:T(8,128)(2,1)}, u32[]{:S(2)}) copy-start(bf16[4,96,768]{2,1,0:T(8,128)(2,1)} %shard_map.267.refs_5_.refs_2_) | copy-start | bytes 1769476
  330.3 13.9 %copy-start.6 = (bf16[2,128,768]{2,1,0:T(8,128)(2,1)S(1)}, bf16[2,128,768]{2,1,0:T(8,128)(2,1)}, u32[]{:S(2)}) copy-start(bf16[2,128,768]{2,1,0:T(8,128)(2,1)} %get-tuple-element.159.refs_3_.refs_1_) | copy-start | bytes 1179652
  330.3 30.2 %all-to-all-start.4 = ((bf16[4,96,768]{2,1,0:T(8,128)(2,1)}), bf16[4,96,768]{2,1,0:T(8,128)(2,1)S(1)}, u32[]{:S(2)}, u32[]{:S(2)}) async-start(bf16[4,96,768]{2,1,0:T(8,128)(2,1)} %shard_map.267.refs_5_.refs_2_), calls=%async_computation.4 | async-start | bytes 1179648 | tf_op jit(solution)/shard_map/all_to_all | solution.py:607
  337.6 10.4 %collective-permute-start.39 = (f32[16,768]{1,0:T(8,128)S(1)}, f32[16,768]{1,0:T(8,128)S(1)}, u32[]{:S(2)}, u32[]{:S(2)}) collective-permute-start(f32[16,768]{1,0:T(8,128)S(1)} %fusion), channel_id=1, source_target_pairs={{0,4},{4,0},{8,12},{12,8},{16,20},{20,16},{24,28},{28,24},{1,5},{5... | collective-permute-start | bytes 147464 | tf_op jit(solution)/shard_map/ppermute | solution.py:604
  348.1 4.2 %collective-permute-start.40 = (f32[16,768]{1,0:T(8,128)S(1)}, f32[16,768]{1,0:T(8,128)S(1)}, u32[]{:S(2)}, u32[]{:S(2)}) collective-permute-start(f32[16,768]{1,0:T(8,128)S(1)} %add.169), channel_id=1, source_target_pairs={{0,8},{4,12},{8,0},{12,4},{16,24},{20,28},{24,16},{28,20},{1,9},{5... | collective-permute-start | bytes 147464 | tf_op jit(solution)/shard_map/ppermute | solution.py:604
  352.2 5.4 %collective-permute-start.41 = (f32[16,768]{1,0:T(8,128)S(1)}, f32[16,768]{1,0:T(8,128)S(1)}, u32[]{:S(2)}, u32[]{:S(2)}) collective-permute-start(f32[16,768]{1,0:T(8,128)S(1)} %add.170), channel_id=1, source_target_pairs={{0,16},{4,20},{8,24},{12,28},{16,0},{20,4},{24,8},{28,12},{1,17},{... | collective-permute-start | bytes 147464 | tf_op jit(solution)/shard_map/ppermute | solution.py:604
  (16 other events, 30.2 us)

commit v2 on v1

--- a/solution.py
+++ b/solution.py
@@ -40,7 +40,7 @@
 
 def call(kernel, grid, ins, outs, scratch=(), cost=1.0, scalars=0, limit=16, after=()):
     def spec(shape, block, index):
-        if block == "any":
+        if isinstance(block, str):
             return pl.BlockSpec(memory_space=pl.ANY)
         if block is None:
             zeros = (0,) * len(shape)
@@ -130,12 +130,11 @@
     for terms, out_ref in zip(layout, outs):
         at = 0
         for n in terms:
-            group = [ins.pop(0) for _ in range(n)]
-            value = group[0][...].astype(F32)
-            for ref in group[1:]:
-                value += ref[...].astype(F32)
-            rows, columns = value.shape[-2:]
-            out_ref[0, :, at : at + columns] = value.reshape(rows, columns).astype(BF)
+            value = 0.0
+            for ref in [ins.pop(0) for _ in range(n)]:
+                value = value + ref[...].astype(F32).reshape(out_ref.shape[:2] + ref.shape[-1:])
+            columns = value.shape[-1]
+            out_ref[:, :, at : at + columns] = value.astype(BF)
             at += columns
 
 
@@ -150,11 +149,32 @@
             out_ref[at : at + rows, :] = jnp.where(lo == b, mine, theirs)
 
 
+def weight_copies(pairs, here_ref, columns, dest, sems, first=0):
+    groups = []
+    n = first
+    for j, (own, other) in enumerate(pairs):
+        depth, rows = own.shape[0], own.shape[1]
+        size = columns.stop - columns.start
+        group = []
+        for z in range(depth):
+            src = lax.rem(z + depth - here_ref[1], depth)
+            for ref, b in ((own, here_ref[0]), (other, 1 - here_ref[0])):
+                to = dest.at[pl.ds(pl.multiple_of((2 * z + b) * rows, rows), rows), j * size : (j + 1) * size]
+                group.append(pltpu.make_async_copy(ref.at[src, :, columns], to, sems.at[n]))
+                n += 1
+        groups.append(group)
+    return groups
+
+
+def paired(refs):
+    return list(zip(refs[::2], refs[1::2]))
+
+
 def attn_fwd_kernel(parts, *refs):
     x_refs, refs = refs[:parts], refs[parts:]
     w_ref, sqv_ref, kc_ref, qc_ref, qkv_ref, p_ref, o_ref, *refs = refs
     *x_out, bias_ref, mask_ref = refs
-    local = o_ref.shape[2]
+    local = qkv_ref.shape[2] // 3
     heads = p_ref.shape[1]
     hd = local // heads
 
@@ -187,7 +207,8 @@
         p = (e * (1.0 / total)).astype(BF)
         p_ref[0, h] = p
         outs.append(nn(p, v_all[:, at]).astype(BF))
-    o_ref[0] = jnp.concatenate(outs, axis=1)
+    pad = jnp.zeros((outs[0].shape[0], o_ref.shape[2] - local), BF)
+    o_ref[0] = jnp.concatenate(outs + [pad], axis=1)
 
 
 def norm(z):
@@ -201,31 +222,6 @@
     mean = jnp.mean(dxh, axis=-1, keepdims=True)
     proj = jnp.mean(dxh * xh, axis=-1, keepdims=True)
     return rstd * (dxh - mean - xh * proj)
-
-
-def out_kernel(o0, o1, o2, o3, x_ref, sup_ref, w0, w1, w2, w3, xh_ref, rstd_ref, u_ref, small_ref, bup_ref):
-    local = o0.shape[1]
-    width = x_ref.shape[1]
-    ws = (w0, w1, w2, w3)
-
-    @pl.when(pl.program_id(0) == 0)
-    def _():
-        eye = (
-            lax.broadcasted_iota(jnp.int32, (width, width), 0)
-            == lax.broadcasted_iota(jnp.int32, (width, width), 1)
-        ).astype(BF)
-        small_ref[...] = tn(w0[:, local:][:, :8], eye)
-        for j in range(4):
-            bup_ref[j] = tn(ws[j][:, local:][:, :8], sup_ref[...])
-
-    a = nt(o0[...], w0[:, :local])
-    for w, o in ((w1, o1), (w2, o2), (w3, o3)):
-        a += nt(o[...], w[:, :local])
-    z = x_ref[...].astype(F32) + (a + small_ref[2:3])
-    xh, rstd = norm(z)
-    xh_ref[...] = xh
-    rstd_ref[...] = rstd
-    u_ref[...] = (xh * small_ref[0:1] + small_ref[3:4]).astype(BF)
 
 
 def turned(a):
@@ -255,33 +251,63 @@
     return e * cdf, cdf + e * (jnp.exp(-0.5 * e * e) * (1.0 / math.sqrt(2.0 * math.pi)))
 
 
-def fetch(moves, step, sems, body):
-    copies = [pltpu.make_async_copy(src, dst, sems.at[i]) for i, (src, dst) in enumerate(moves)]
-
+def fetch(groups, step, body):
     @pl.when(step == 0)
     def _():
-        for copy in copies:
-            copy.start()
-        body(lambda i: copies[i].wait())
+        for group in groups:
+            for copy in group:
+                copy.start()
+
+        def ready(i):
+            for copy in groups[i]:
+                copy.wait()
+
+        body(ready)
 
     @pl.when(step > 0)
     def _():
-        body(lambda i: None)
-
-
-def up_kernel(u_ref, bup_ref, w0, w1, w2, w3, h_ref, g_ref, w_ref, sems):
-    width = w_ref.shape[2]
+        body(None)
+
+
+def middle_kernel(here_ref, o0, o1, o2, o3, x_ref, sup_ref, *refs):
+    ws, refs = paired(refs[:8]), refs[8:]
+    xh_ref, rstd_ref, u_ref, h_ref, g_ref, small_ref, wo_ref, wu_ref, bup_ref, sems = refs
+    width = x_ref.shape[1]
+    hidden = wu_ref.shape[1] // 4
+    wide = wo_ref.shape[1] // 4
+    per = 2 * ws[0][0].shape[0]
+    groups = weight_copies(ws, here_ref, slice(hidden, hidden + wide), wo_ref, sems)
+    groups += weight_copies(ws, here_ref, slice(0, hidden), wu_ref, sems, 4 * per)
 
     def body(ready):
-        u = u_ref[...]
-        for j in range(4):
-            ready(j)
-            e = nn(u, w_ref[j]) + bup_ref[j, 6:7]
-            h, g = gelu_parts(e)
-            h_ref[j] = h.astype(BF)
-            g_ref[j] = g.astype(BF)
-
-    fetch([(w.at[:, :width], w_ref.at[j]) for j, w in enumerate((w0, w1, w2, w3))], pl.program_id(0), sems, body)
+        if ready:
+            for j in range(4):
+                ready(j)
+            eye = (
+                lax.broadcasted_iota(jnp.int32, (width, width), 0)
+                == lax.broadcasted_iota(jnp.int32, (width, width), 1)
+            ).astype(BF)
+            local = wide - 64
+            small_ref[...] = tn(wo_ref[:, local:wide][:, :8], eye)
+            for j in range(4):
+                cols = wo_ref[:, j * wide + local : (j + 1) * wide][:, :8]
+                bup_ref[:, j * hidden : (j + 1) * hidden] = tn(cols, sup_ref[...])
+        o = jnp.concatenate([o0[...], o1[...], o2[...], o3[...]], axis=1)
+        z = x_ref[...].astype(F32) + (nt(o, wo_ref[...]) + small_ref[2:3])
+        xh, rstd = norm(z)
+        xh_ref[...] = xh.astype(BF)
+        rstd_ref[...] = rstd
+        u = (xh * small_ref[0:1] + small_ref[3:4]).astype(BF)
+        u_ref[...] = u
+        for j in range(4 if ready else 1):
+            at = slice(j * hidden, (j + 1) * hidden) if ready else slice(0, 4 * hidden)
+            if ready:
+                ready(4 + j)
+            h, g = gelu_parts(nn(u, wu_ref[:, at]) + bup_ref[6:7, at])
+            h_ref[:, at] = h.astype(BF)
+            g_ref[:, at] = g.astype(BF)
+
+    fetch(groups, pl.program_id(0), body)
 
 
 def split3(v):
@@ -292,27 +318,29 @@
     return a, b, c
 
 
-def down_kernel(
-    h_ref, xh1_ref, small_ref, code_ref, inv_ref, w0, w1, w2, w3,
-    xh_ref, rstd_ref, y0, y1, y2, y3, pool_ref, acc_ref, w_ref, sems,
-):
+def down_kernel(here_ref, h_ref, u_ref, small_ref, code_ref, inv_ref, *refs):
+    ws, refs = paired(refs[:8]), refs[8:]
+    xh_ref, rstd_ref, y0, y1, y2, y3, pool_ref, acc_ref, w_ref, sems = refs
     y_refs = (y0, y1, y2, y3)
     step = pl.program_id(0)
+    hidden = w_ref.shape[1] // 4
 
     @pl.when(step == 0)
     def _():
         acc_ref[...] = jnp.zeros_like(acc_ref)
 
     def body(ready):
-        ready(0)
-        f = nt(h_ref[0], w_ref[0])
-        for j in range(1, 4):
-            ready(j)
-            f += nt(h_ref[j], w_ref[j])
-        first = xh1_ref[...] * small_ref[0:1] + small_ref[3:4]
-        xh, rstd = norm(first + (f + small_ref[4:5]))
+        if ready:
+            ready(0)
+            f = nt(h_ref[:, :hidden], w_ref[:, :hidden])
+            for j in range(1, 4):
+                ready(j)
+                f += nt(h_ref[:, j * hidden : (j + 1) * hidden], w_ref[:, j * hidden : (j + 1) * hidden])
+        else:
+            f = nt(h_ref[...], w_ref[...])
+        xh, rstd = norm(u_ref[...].astype(F32) + (f + small_ref[4:5]))
         y2 = xh * small_ref[1:2] + small_ref[5:6]
-        xh_ref[...] = xh
+        xh_ref[...] = xh.astype(BF)
         rstd_ref[...] = rstd
         low = y2.astype(BF)
         size = y_refs[0].shape[1]
@@ -327,7 +355,7 @@
         a, b, c = split3(y2)
         acc_ref[...] += nn(member, a) + nn(member, b) + nn(member, c)
 
-    fetch([(w, w_ref.at[j]) for j, w in enumerate((w0, w1, w2, w3))], step, sems, body)
+    fetch(weight_copies(ws, here_ref, slice(0, hidden), w_ref, sems), step, body)
 
     @pl.when(step == pl.num_programs(0) - 1)
     def _():
@@ -359,8 +387,11 @@
 
 def feed_back_kernel(
     blocks, here_ref, pooled_ref, ids_ref, mate_ref, target_ref, inv_ref, code_ref, xh_ref, rstd_ref, small_ref,
-    g_ref, h_ref, w0, w1, w2, w3, df_ref, dz_ref, de_ref, send_ref, sum_ref, bup_ref, gp_ref, all_ref, w_ref, sems,
+    g_ref, h_ref, *refs,
 ):
+    ws, refs = paired(refs[:8]), refs[8:]
+    df_ref, de_ref, send_ref, sum_ref, bup_ref, gp_ref, all_ref, w_ref, sems = refs
+    hidden = w_ref.shape[1] // 4
     step = pl.program_id(0)
 
     @pl.when(step == 0)
@@ -375,78 +406,79 @@
         size = xh_ref.shape[0]
         member = (lax.broadcasted_iota(jnp.int32, (8, size), 0) == code_ref[...]).astype(BF)
         dy = tn(member, gp_ref[0]) + tn(member, gp_ref[1]) + tn(member, gp_ref[2])
-        xh = xh_ref[...]
+        xh = xh_ref[...].astype(F32)
         dz = norm_back(dy, xh, rstd_ref[...], small_ref[1:2])
         sum_ref[0:1] += rowsum(dy * xh)
         sum_ref[1:2] += rowsum(dy)
         sum_ref[2:3] += rowsum(dz)
         df = dz.astype(BF)
         df_ref[...] = df
-        dz_ref[...] = dz
         all_ref[pl.ds(pl.multiple_of(step * size, size), size), :] = df
-        for j in range(4):
-            ready(j)
-            de = (nn(df, w_ref[j]) * g_ref[j].astype(F32)).astype(BF)
-            de_ref[j] = de
-            bup_ref[j, 0:1] += rowsum(de.astype(F32))
+        for j in range(4 if ready else 1):
+            at = slice(j * hidden, (j + 1) * hidden) if ready else slice(0, 4 * hidden)
+            if ready:
+                ready(j)
+            de = (nn(df, w_ref[:, at]) * g_ref[:, at].astype(F32)).astype(BF)
+            de_ref[:, at] = de
+            bup_ref[0:1, at] += rowsum(de.astype(F32))
 
     @pl.when(step < blocks)
     def _():
-        fetch([(w, w_ref.at[j]) for j, w in enumerate((w0, w1, w2, w3))], step, sems, body)
+        fetch(weight_copies(ws, here_ref, slice(0, hidden), w_ref, sems), step, body)
 
     @pl.when(step >= blocks)
     def _():
-        pieces(tn(all_ref[...], h_ref[0]), here_ref, send_ref.at[0], slice(0, h_ref.shape[2]))
-
-
-def norm_back_kernel(
-    de_ref, dz2_ref, xh_ref, rstd_ref, small_ref, w0, w1, w2, w3,
-    dz_ref, da_ref, do_ref, sum_ref, w_ref, wo_ref, sems,
-):
+        pieces(tn(all_ref[...], h_ref[...]), here_ref, send_ref.at[0], slice(0, hidden))
+
+
+def norm_back_kernel(here_ref, de_ref, df_ref, xh_ref, rstd_ref, small_ref, *refs):
+    ws, refs = paired(refs[:8]), refs[8:]
+    da_ref, do_ref, sum_ref, w_ref, wo_ref, sems = refs
     step = pl.program_id(0)
-    hidden = w_ref.shape[2]
-    ups = (w0, w1, w2, w3)
-    moves = [(w.at[:, :hidden], w_ref.at[j]) for j, w in enumerate(ups)]
-    moves += [(w.at[:, hidden:], wo_ref.at[j]) for j, w in enumerate(ups)]
+    hidden, wide = w_ref.shape[1] // 4, wo_ref.shape[1] // 4
+    per = 2 * ws[0][0].shape[0]
+    groups = weight_copies(ws, here_ref, slice(0, hidden), w_ref, sems)
+    groups += weight_copies(ws, here_ref, slice(hidden, hidden + wide), wo_ref, sems, 4 * per)
 
     @pl.when(step == 0)
     def _():
         sum_ref[...] = jnp.zeros_like(sum_ref)
 
     def body(ready):
-        dy = dz2_ref[...]
-        for j in range(4):
-            ready(j)
-            dy = dy + nt(de_ref[j], w_ref[j])
-        xh = xh_ref[...]
+        dy = df_ref[...].astype(F32)
+        for j in range(4 if ready else 1):
+            at = slice(j * hidden, (j + 1) * hidden) if ready else slice(0, 4 * hidden)
+            if ready:
+                ready(j)
+            dy = dy + nt(de_ref[:, at], w_ref[:, at])
+        xh = xh_ref[...].astype(F32)
         dz = norm_back(dy, xh, rstd_ref[...], small_ref[0:1])
         sum_ref[0:1] += rowsum(dy * xh)
         sum_ref[1:2] += rowsum(dy)
         sum_ref[2:3] += rowsum(dz)
         da = dz.astype(BF)
-        dz_ref[...] = dz
         da_ref[...] = da
-        for j in range(4):
-            ready(4 + j)
-            do_ref[j] = nn(da, wo_ref[j, :, : do_ref.shape[2]]).astype(BF)
-
-    fetch(moves, step, sems, body)
+        if ready:
+            for j in range(4):
+                ready(4 + j)
+        do_ref[...] = nn(da, wo_ref[...]).astype(BF)
+
+    fetch(groups, step, body)
 
 
 def pieces(grad, here_ref, ref, at):
     depth, rows = ref.shape[1], ref.shape[2]
-    lo = here_ref[0]
     low = grad.astype(BF)
     for z in range(depth):
-        first, second = (low[(2 * z + b) * rows : (2 * z + b + 1) * rows] for b in range(2))
-        ref[0, z, :, at] = jnp.where(lo == 0, first, second)
-        ref[1, z, :, at] = jnp.where(lo == 0, second, first)
+        for b in range(2):
+            part = low[(2 * z + b) * rows : (2 * z + b + 1) * rows]
+            ref[here_ref[0] if b == 0 else 1 - here_ref[0], z, :, at] = part
 
 
 def grad_send_kernel(here_ref, *refs):
     *ins, send_ref = refs
     at = 0
-    for grad in (tn(a[...], b[0]) for a, b in zip(ins[::2], ins[1::2])):
+    for grad in (tn(a[...], b[...]) for a, b in zip(ins[::2], ins[1::2])):
         pieces(grad, here_ref, send_ref.at[0], slice(at, at + grad.shape[1]))
         at += grad.shape[1]
 
@@ -457,7 +489,7 @@
     lo = here_ref[0]
     j = pl.program_id(0)
     at = 0
-    for grad in (tn(a[...], b[0]) for a, b in zip(ins[::2], ins[1::2])):
+    for grad in (tn(a[...], b[...]) for a, b in zip(ins[::2], ins[1::2])):
         cols = slice(at, at + grad.shape[1])
         for z in range(depth):
             first, second = (grad[(2 * z + b) * rows : (2 * z + b + 1) * rows] for b in range(2))
@@ -489,7 +521,7 @@
     got_refs = refs[len(refs) - keeps :]
     r = pl.program_id(0)
     rows = xs.shape[0]
-    local = o_ref.shape[2]
+    local = qkv_ref.shape[2] // 3
     heads = p_ref.shape[1]
     hd = local // heads
 
@@ -510,7 +542,7 @@
             copy.start()
 
     q_all, k_all, v_all = (qkv_ref[0, :, i * local : (i + 1) * local] for i in range(3))
-    o_all, do_all = o_ref[0], do_ref[0]
+    o_all, do_all = o_ref[0, :, :local], do_ref[0, :, :local]
     prod = o_all.astype(F32) * do_all.astype(F32)
     dq, dk, dv = [], [], []
     for h in range(heads):
@@ -539,7 +571,7 @@
     sum_ref[...] += sums
     acc_ref[:, : 3 * local] += tn(xs[r], dproj)
     acc_ref[:, 3 * local :] += tn(das[r], o_all)
-    dproj_ref[0] = dproj
+    dproj_ref[0] = jnp.concatenate([dproj, jnp.zeros((dproj.shape[0], 64), BF)], axis=1)
 
     @pl.when(r == rows - 1)
     def _():
@@ -567,21 +599,25 @@
         ):
             ref[i : i + 1] = src[row : row + 1]
         for n, j in enumerate(pair):
-            ref[8 + 8 * n : 9 + 8 * n] = up_ref[j, 0:1]
+            ref[8 + 8 * n : 9 + 8 * n] = up_ref[0:1, j * ref.shape[1] : (j + 1) * ref.shape[1]]
             if j in parts:
                 ref[9 + 8 * n : 10 + 8 * n, :local] = parts[j][0:1, :local]
                 ref[9 + 8 * n : 10 + 8 * n, local : 2 * local] = parts[j][0:1, 2 * local :]
 
 
-def input_back_kernel(p0, p1, p2, p3, dz_ref, w0, w1, w2, w3, y0, y1, y2, y3, w_ref, sems):
+def input_back_kernel(p0, p1, p2, p3, da_ref, w0, w1, w2, w3, y0, y1, y2, y3, w_ref, sems):
     step = pl.program_id(0)
-    y_refs = (y0, y1, y2, y3)
+    y_refs, p_refs = (y0, y1, y2, y3), (p0, p1, p2, p3)
+    wide = p0.shape[1]
 
     def body(ready):
-        dx = dz_ref[...]
-        for j, p in enumerate((p0, p1, p2, p3)):
-            ready(j)
-            dx = dx + nt(p[...], w_ref[j, :, : p.shape[1]])
+        dx = da_ref[...].astype(F32)
+        if ready:
+            for j, p in enumerate(p_refs):
+                ready(j)
+                dx = dx + nt(p[...], w_ref[:, j * wide : (j + 1) * wide])
+        else:
+            dx = dx + nt(jnp.concatenate([p[...] for p in p_refs], axis=1), w_ref[...])
         low = dx.astype(BF)
         size = y_refs[0].shape[1]
         here = low.shape[0] // size
@@ -591,7 +627,10 @@
             def _():
                 ref[0] = low[(j % here) * size : (j % here + 1) * size]
 
-    fetch([(w, w_ref.at[j]) for j, w in enumerate((w0, w1, w2, w3))], step, sems, body)
+    groups = []
+    for j, w in enumerate((w0, w1, w2, w3)):
+        groups.append([pltpu.make_async_copy(w, w_ref.at[:, j * wide : (j + 1) * wide], sems.at[j])])
+    fetch(groups, step, body)
 
 
 def make(mesh):
@@ -619,24 +658,18 @@
             columns = 0
             for terms in ranges:
                 for array, lead in terms:
-                    block = (1,) * (len(lead) + 1) + array.shape[-2:]
+                    block = (1,) * len(lead) + (nh // 2,) + array.shape[-2:]
                     ins.append((array, block, lambda z, lead=lead: (*lead, z, 0, 0)))
                 columns += array.shape[-1]
             shape = (nh, array.shape[-2], columns)
-            shapes.append((shape, BF, (1,) + shape[1:], lambda z: (z, 0, 0)))
-        return call(functools.partial(add_kernel, layout), (nh,), ins, shapes, limit=63, cost=60.0)
+            shapes.append((shape, BF, (nh // 2,) + shape[1:], lambda z: (z, 0, 0)))
+        return call(functools.partial(add_kernel, layout), (2,), ins, shapes, limit=63, cost=60.0)
 
     def turn(array, k):
         return lax.ppermute(array, "dp", [(2 * ((z + k) % nh) + b, 2 * z + b) for z in range(nh) for b in range(2)])
 
     def swap(array):
         return across(array, "tensor", 1)
-
-    def total(*arrays):
-        out = arrays[0].astype(F32)
-        for a in arrays[1:]:
-            out = out + a.astype(F32)
-        return out
 
     def settle(array):
         return jnp.sum(array.astype(F32), axis=0)
@@ -666,22 +699,33 @@
         here, here_first = jnp.stack([lo_bit, lo_bit * 0]), jnp.stack([lo_bit, turned_by])
         t_arr = t.astype(jnp.int32).reshape(1)
 
-        def merged(own, other, after=(), place=here):
+        def ready(own, other):
+            if fused:
+                return [own, other]
+            first = jnp.where(d % 2 == 0, own, other)
+            second = jnp.where(d % 2 == 0, other, own)
+            full = jnp.stack([first, second], axis=1).reshape(2, 1, width // 2, own.shape[2])
+            return [full[0], full[1]]
+
+        def merged(own, other, place, after):
             if not fused:
                 first = jnp.where(d % 2 == 0, own, other)
                 second = jnp.where(d % 2 == 0, other, own)
                 return jnp.stack([first, second], axis=1).reshape(width, own.shape[2])
-            columns = own.shape[2]
             return call(
                 merge_kernel,
                 (1,),
                 [(place, None, None), (own, None, None), (other, None, None)],
-                [((width, columns), BF, None, None)],
+                [((width, own.shape[2]), BF, None, None)],
                 scalars=1,
                 after=after,
-                cost=1.0,
-                limit=63,
             )[0]
+
+        def weights(pairs):
+            return [(a, "any", None) for pair in pairs for a in ready(*pair)]
+
+        def sems(n):
+            return pltpu.SemaphoreType.DMA((n,))
 
         def pack(kernel, arrays, columns, after):
             return call(
@@ -709,16 +753,36 @@
             first, second = jnp.where(d % 2 == 0, mine, theirs), jnp.where(d % 2 == 0, theirs, mine)
             return jnp.stack([first, second], axis=-3).reshape(*array.shape[:-4], 2, 1, width // 2, array.shape[-1])
 
-        deal_block = blk // row_count
+        deal_size = min(512, part_len * row_count)
+        deal_block = deal_size // row_count
         dealt = call(
             deal_kernel,
             (part_len // deal_block,),
-            [(t_arr, None, None), (tokens.reshape(part_len * row_count, width), (blk, width), lambda i, *_: (i, 0))],
+            [(t_arr, None, None), (tokens.reshape(part_len * row_count, width), (deal_size, width), lambda i, *_: (i, 0))],
             [((rows, part_len, width), BF, (rows, deal_block, width), lambda i, *_: (0, i, 0))] * ntens,
             scalars=1,
             cost=2.0,
         )
         x_parts = [dealt[0]] + [across(dealt[j], "tensor", j) for j in range(1, ntens)]
+
+        mine = lax.dynamic_slice_in_dim(segments, t * rows, rows, 0).reshape(rows, ntens, part_len)
+        own_len = lax.dynamic_slice_in_dim(lengths, t * rows, rows, 0)
+        seg = jnp.stack([lax.dynamic_index_in_dim(mine, t ^ j, 1, False) for j in range(ntens)], axis=1)
+        place = jnp.stack([(t ^ j) * part_len + jnp.arange(part_len) for j in range(ntens)])
+        live = (place[None] < own_len[:, None, None]).reshape(rows, seq)
+        seg = seg.reshape(rows, seq)
+        key_code = jnp.where(live, seg, -1)
+        query_code = jnp.where(live, seg, DEAD)
+        sent_code = jnp.where(live, seg + SEGS * jnp.arange(rows)[:, None], -1).reshape(1, count)
+        member = (key_code[:, None, :] == jnp.arange(SEGS)[None, :, None]).astype(F32)
+        key_codes, query_codes = key_code.reshape(rows, 1, seq), query_code.reshape(rows, seq, 1)
+        inv_count = (1.0 / jnp.sum(member, axis=2)).reshape(sents, 1)
+        own_ids = (d * row_count + t * rows) * SEGS + jnp.arange(sents, dtype=jnp.int32)
+        is_mine = pair_ids[None, :] == own_ids[:, None]
+        mates = pair_ids.reshape(-1, 2)[:, ::-1].reshape(-1)
+        mate = jnp.sum(jnp.where(is_mine, mates[None, :], 0), axis=1, keepdims=True)
+        goal = jnp.sum(jnp.where(is_mine, jnp.repeat(targets, 2)[None, :], 0.0), axis=1, keepdims=True)
+        own_ids = own_ids[:, None]
 
         qv_col = jnp.pad(b_qv.reshape(-1, 1), ((0, rb - b_qv.size), (0, 63)))
         wide = 3 * local + 64
@@ -740,7 +804,7 @@
         else:
             own1 = along(jnp.broadcast_to(first_piece[None], (nh, rb, wide)))
         lo1 = across(own1, "dp", 1)
-        w1 = {0: merged(own1, lo1, place=here_first)}
+        w1 = {0: merged(own1, lo1, here_first, [key_codes, query_codes])}
         w1[1] = swap(w1[0])
         w1[2] = across(w1[0], "tensor", 2)
         extra = jnp.concatenate([ln_gains.T, shifts.T, b_up.reshape(-1, 1), jnp.zeros((rb, 57), BF)], axis=1)
@@ -748,24 +812,6 @@
         (second_piece,) = gate([second_piece], [own1])
         own2 = along(second_piece)
         third_piece = pack(pack_three_kernel, [w_down], hidden, [dealt[1]])
-
-        mine = lax.dynamic_slice_in_dim(segments, t * rows, rows, 0).reshape(rows, ntens, part_len)
-        own_len = lax.dynamic_slice_in_dim(lengths, t * rows, rows, 0)
-        seg = jnp.stack([lax.dynamic_index_in_dim(mine, t ^ j, 1, False) for j in range(ntens)], axis=1)
-        place = jnp.stack([(t ^ j) * part_len + jnp.arange(part_len) for j in range(ntens)])
-        live = (place[None] < own_len[:, None, None]).reshape(rows, seq)
-        seg = seg.reshape(rows, seq)
-        key_code = jnp.where(live, seg, -1)
-        query_code = jnp.where(live, seg, DEAD)
-        sent_code = jnp.where(live, seg + SEGS * jnp.arange(rows)[:, None], -1).reshape(1, count)
-        member = (key_code[:, None, :] == jnp.arange(SEGS)[None, :, None]).astype(F32)
-        inv_count = (1.0 / jnp.sum(member, axis=2)).reshape(sents, 1)
-        own_ids = (d * row_count + t * rows) * SEGS + jnp.arange(sents, dtype=jnp.int32)
-        is_mine = pair_ids[None, :] == own_ids[:, None]
-        mates = pair_ids.reshape(-1, 2)[:, ::-1].reshape(-1)
-        mate = jnp.sum(jnp.where(is_mine, mates[None, :], 0), axis=1, keepdims=True)
-        goal = jnp.sum(jnp.where(is_mine, jnp.repeat(targets, 2)[None, :], 0.0), axis=1, keepdims=True)
-        own_ids = own_ids[:, None]
 
         k = np.arange(width)
         dd, within = k // rb, k % rb
@@ -786,11 +832,11 @@
 
         by_row = lambda r, *_: (r, 0, 0)
 
-        def attend(xs, w, before):
+        def attend(xs, w, before, cost=9.0):
             outs = [
                 ((rows, seq, 3 * local), BF, (1, seq, 3 * local), by_row),
                 ((rows, heads, seq, seq), BF, (1, heads, seq, seq), lambda r, *_: (r, 0, 0, 0)),
-                ((rows, seq, local), BF, (1, seq, local), by_row),
+                ((rows, seq, 256), BF, (1, seq, 256), by_row),
             ]
             if len(xs) > 1:
                 outs.append(((rows, seq, width), BF, (1, seq, width), by_row))
@@ -801,97 +847,75 @@
                 + [
                     whole(w),
                     whole(sqv),
-                    (key_code.reshape(rows, 1, seq), (1, 1, seq), by_row),
-                    (query_code.reshape(rows, seq, 1), (1, seq, 1), by_row),
+                    (key_codes, (1, 1, seq), by_row),
+                    (query_codes, (1, seq, 1), by_row),
                 ],
                 outs,
                 scratch=[pltpu.VMEM((8, 2 * local), F32), pltpu.VMEM((seq, seq), F32)],
                 after=before,
                 limit=63,
-                cost=9.0,
+                cost=cost,
             )
 
         kept = {}
-        *kept[0], x = attend(x_parts, w1[0], [second_piece])
+        *kept[0], x = attend(x_parts, w1[0], [second_piece], 25.0)
         (own2,) = gate([own2], [kept[0][2]])
         lo2, far2 = across(own2, "dp", 1), across(own2, "tensor", 2)
         (third_piece,) = gate([third_piece], [own2])
         own3 = along(third_piece)
         kept[1] = attend([x], w1[1], [own2])
-        (w1[2],) = gate([w1[2]], [kept[1][2]])
+        w1[2], lo2 = gate([w1[2], lo2], [kept[1][2]])
         w1[3] = swap(w1[2])
-        kept[2] = attend([x], w1[2], [])
-        lo2, far2 = gate([lo2, far2], [kept[2][2]])
-        far_lo2 = across(far2, "dp", 1)
-        w2 = {0: merged(own2, lo2)}
-        w2[1] = swap(w2[0])
-        (own3,) = gate([own3], [w2[0]])
-        far3, lo3 = across(own3, "tensor", 2), across(own3, "dp", 1)
-        kept[3] = attend([x], w1[3], [own3])
-        far3, far_lo2 = gate([far3, far_lo2], [kept[3][2]])
-        far_lo3 = across(far3, "dp", 1)
-        w2[2] = merged(far2, far_lo2)
-        w2[3] = swap(w2[2])
-        ws2 = [w2[j] for j in range(4)]
-        o_parts = [kept[j][2].reshape(count, local) for j in range(4)]
+        far_lo2 = across(lo2, "tensor", 2)
+        kept[2] = attend([x], w1[2], [lo2])
+        own3, far2 = gate([own3, far2], [kept[2][2]])
+        lo3, far3 = across(own3, "dp", 1), across(own3, "tensor", 2)
+        kept[3] = attend([x], w1[3], [own3, far2])
+        far_lo2, lo3 = gate([far_lo2, lo3], [kept[3][2]])
+        far_lo3 = across(lo3, "tensor", 2)
+        w2 = [(own2, lo2), (swap(own2), swap(lo2)), (far2, far_lo2), (swap(far2), swap(far_lo2))]
+        o_parts = [kept[j][2].reshape(count, 256) for j in range(4)]
         x_flat = x.reshape(count, width)
 
-        def rows_of(array, *lead):
-            if array.ndim == 3:
-                return (array, (array.shape[0], blk, array.shape[2]), lambda i, *_: (0, i, 0))
+        def rows_of(array):
             return (array, (blk, array.shape[1]), lambda i, *_: (i, 0))
 
         def rows_out(shape, dtype):
-            if len(shape) == 3:
-                return (shape, dtype, (shape[0], blk, shape[2]), lambda i, *_: (0, i, 0))
             return (shape, dtype, (blk, shape[1]), lambda i, *_: (i, 0))
 
-        ups = [(w, "any", None) for w in ws2]
-        all_w = pltpu.VMEM((4, width, hidden), BF)
-        sems = lambda n: pltpu.SemaphoreType.DMA((n,))
-        outs_w = [(w, (width, 256), lambda i, *_: (0, hidden // 256)) for w in ws2]
-        xh1, rstd1, u, small, bup_rows = call(
-            out_kernel,
+        all_w, all_o = pltpu.VMEM((width, 4 * hidden), BF), pltpu.VMEM((width, 4 * 256), BF)
+        xh1, rstd1, u, h, g, small = call(
+            middle_kernel,
             (steps,),
-            [rows_of(o) for o in o_parts] + [rows_of(x_flat), whole(sup)] + outs_w,
+            [whole(here)] + [rows_of(o) for o in o_parts] + [rows_of(x_flat), whole(sup)] + weights(w2),
             [
-                rows_out((count, width), F32),
+                rows_out((count, width), BF),
                 rows_out((count, 1), F32),
                 rows_out((count, width), BF),
+                rows_out((count, 4 * hidden), BF),
+                rows_out((count, 4 * hidden), BF),
                 whole_out((8, width), F32),
-                whole_out((4, 8, hidden), F32),
             ],
-            limit=63,
-            cost=8.0,
-        )
-        (lo3,) = gate([lo3], [u])
-        w3 = {0: merged(own3, lo3)}
-        w3[1] = swap(w3[0])
-        h, g = call(
-            up_kernel,
-            (steps,),
-            [rows_of(u), whole(bup_rows)] + ups,
-            [rows_out((4, count, hidden), BF), rows_out((4, count, hidden), BF)],
-            after=[w3[0]],
-            scratch=[all_w, sems(4)],
+            scratch=[all_o, all_w, pltpu.VMEM((8, 4 * hidden), F32), sems(16 * depth)],
+            scalars=1,
+            after=[lo3],
             limit=63,
             cost=20.0,
         )
-        (far_lo3,) = gate([far_lo3], [h])
-        w3[2] = merged(far3, far_lo3)
-        w3[3] = swap(w3[2])
-        downs = [(w3[j], "any", None) for j in range(4)]
+        far3, far_lo3 = gate([far3, far_lo3], [u])
+        w3 = [(own3, lo3), (swap(own3), swap(lo3)), (far3, far_lo3), (swap(far3), swap(far_lo3))]
         code_spec = (sent_code, (1, blk), lambda i, *_: (0, i))
         span = blk // part_len
         part_out = lambda i, *_: (i * span // ntens, 0, 0)
         xh2, rstd2, y0, y1, y2, y3, pooled = call(
             down_kernel,
             (steps,),
-            [rows_of(h), rows_of(xh1), whole(small), code_spec, whole(inv_count)] + downs,
-            [rows_out((count, width), F32), rows_out((count, 1), F32)]
+            [whole(here), rows_of(h), rows_of(u), whole(small), code_spec, whole(inv_count)] + weights(w3),
+            [rows_out((count, width), BF), rows_out((count, 1), F32)]
             + [((rows, part_len, width), BF, (1, part_len, width), part_out)] * ntens
             + [whole_out((nd * ntens, sents, width), BF)],
-            scratch=[pltpu.VMEM((sents, width), F32), all_w, sems(4)],
+            scratch=[pltpu.VMEM((sents, width), F32), all_w, sems(8 * depth)],
+            scalars=1,
             limit=63,
             cost=14.0,
         )
@@ -904,9 +928,10 @@
                 collect_kernel,
                 (part_len // deal_block,),
                 [whole(t_arr)] + [(a, (rows, deal_block, width), lambda i, *_: (0, i, 0)) for a in parts],
-                [((part_len * row_count, width), BF, (blk, width), lambda i, *_: (i, 0))],
+                [((part_len * row_count, width), BF, (deal_size, width), lambda i, *_: (i, 0))],
                 scalars=1,
                 after=after,
+                limit=63,
                 cost=30.0,
             )
             return out.reshape(part_len, row_count, width)
@@ -917,33 +942,29 @@
         half = (2,) + shape[2:]
 
         def blocked(array):
-            at = lambda i, *_: jnp.minimum(i, steps - 1)
-            if len(array.shape) == 3:
-                return (array.shape[0], blk, array.shape[2]), lambda i, *_: (0, at(i), 0)
-            return (blk, array.shape[1]), lambda i, *_: (at(i), 0)
+            return (blk, array.shape[1]), lambda i, *_: (jnp.minimum(i, steps - 1), 0)
 
         def blocked_out(shape, dtype):
             return (shape, dtype, *blocked(jax.ShapeDtypeStruct(shape, dtype)))
 
         late = lambda i: jnp.maximum(i - steps, 0)
-        df, dz2, de, send3, sums2, dbup = call(
+        df, de, send3, sums2, dbup = call(
             functools.partial(feed_back_kernel, steps),
             (steps + 2,),
             [whole(here), whole(every), whole(own_ids), whole(mate), whole(goal), whole(inv_count)]
             + [(sent_code, (1, blk), lambda i, *_: (0, jnp.minimum(i, steps - 1)))]
             + [(a, *blocked(a)) for a in (xh2, rstd2)]
             + [whole(small), (g, *blocked(g))]
-            + [(h, (1, count, hidden), lambda i, *_: (2 * late(i) + 1, 0, 0))]
-            + downs,
+            + [(h, (count, hidden), lambda i, *_: (0, 2 * late(i) + 1))]
+            + weights(w3),
             [
                 blocked_out((count, width), BF),
-                blocked_out((count, width), F32),
-                blocked_out((4, count, hidden), BF),
+                blocked_out((count, 4 * hidden), BF),
                 (shape, BF, (1,) + shape[1:], lambda i, *_: (late(i), 0, 0, 0, 0)),
                 whole_out((8, width), F32),
-                whole_out((4, 8, hidden), F32),
+                whole_out((8, 4 * hidden), F32),
             ],
-            scratch=[pltpu.VMEM((3, sents, width), BF), pltpu.VMEM((count, width), BF), all_w, sems(4)],
+            scratch=[pltpu.VMEM((3, sents, width), BF), pltpu.VMEM((count, width), BF), all_w, sems(8 * depth)],
             scalars=1,
             limit=63,
             cost=32.0,
@@ -955,7 +976,7 @@
             return call(
                 kernel,
                 (2,),
-                [whole(here), whole(a), (b, (1,) + b.shape[1:], lambda j, *_: (2 * j + odd, 0, 0))]
+                [whole(here), whole(a), (b, (count, hidden), lambda j, *_: (0, 2 * j + odd))]
                 + [(v, (1,) + v.shape[1:], lambda j, *_: (j, 0, 0, 0, 0)) for v in got],
                 outs,
                 scalars=1,
@@ -983,22 +1004,22 @@
         got3x = across(fly3, "dp", 1)
         gotuy = across(flyu, "tensor", 2)
 
-        dz1, da, do, sums1 = call(
+        da, do, sums1 = call(
             norm_back_kernel,
             (steps,),
-            [rows_of(de), rows_of(dz2), rows_of(xh1), rows_of(rstd1), whole(small)] + ups,
+            [whole(here), rows_of(de), rows_of(df), rows_of(xh1), rows_of(rstd1), whole(small)] + weights(w2),
             [
-                rows_out((count, width), F32),
                 rows_out((count, width), BF),
-                rows_out((4, count, local), BF),
+                rows_out((count, 4 * 256), BF),
                 whole_out((8, width), F32),
             ],
-            scratch=[all_w, pltpu.VMEM((4, width, 256), BF), sems(8)],
+            scratch=[all_w, all_o, sems(16 * depth)],
+            scalars=1,
             after=[flyu],
             limit=63,
             cost=14.0,
         )
-        da_rows = da.reshape(rows, seq, width)
+        da_rows, do_rows = da.reshape(rows, seq, width), do.reshape(rows, seq, 4 * 256)
         grad_cols = 4 * local
 
         def attend_back(j, got, after):
@@ -1014,14 +1035,14 @@
                     whole(here),
                     (qkv, (1, seq, 3 * local), by_row),
                     (p, (1, heads, seq, seq), lambda r, *_: (r, 0, 0, 0)),
-                    (o, (1, seq, local), by_row),
-                    (do, (1, seq, local), lambda r, *_: (j, r, 0)),
+                    (o, (1, seq, 256), by_row),
+                    (do_rows, (1, seq, 256), lambda r, *_: (r, 0, j)),
                     (x, "any", None),
                     (da_rows, "any", None),
                 ]
                 + ([] if got is None else [(uncut(got), "any", None)]),
                 kinds
-                + [whole_out((8, 3 * local), F32), ((rows, seq, 3 * local), BF, (1, seq, 3 * local), by_row)],
+                + [whole_out((8, 3 * local), F32), ((rows, seq, wide), BF, (1, seq, wide), by_row)],
                 scratch=[pltpu.VMEM((width, grad_cols), F32), whole_row, whole_row, sems(2 * rows + keeps)]
                 + [pltpu.VMEM((2,) + half, BF)] * keeps,
                 scalars=1,
@@ -1036,7 +1057,7 @@
             else:
                 both = cut(jnp.stack(outs))
                 out = both[0], both[1]
-            sums_of[j], dprojs[j] = sums, dproj.reshape(count, 3 * local)
+            sums_of[j], dprojs[j] = sums, dproj.reshape(count, wide)
             return out
 
         sums_of, dprojs = {}, {}
@@ -1071,9 +1092,9 @@
         dx_parts = call(
             input_back_kernel,
             (steps,),
-            [rows_of(dprojs[j]) for j in range(4)] + [rows_of(dz1)] + [(w1[j], "any", None) for j in range(4)],
+            [rows_of(dprojs[j]) for j in range(4)] + [rows_of(da)] + [(w1[j], "any", None) for j in range(4)],
             [((rows, part_len, width), BF, (1, part_len, width), span_out)] * ntens,
-            scratch=[pltpu.VMEM((4, width, wide), BF), sems(4)],
+            scratch=[pltpu.VMEM((width, 4 * wide), BF), sems(4)],
             limit=63,
             after=[stay_near],
             cost=8.0,

time: 369 us -> 350 us (0.949)
  Pallas kernels: 231 us -> 215 us
  waiting for transfers between devices: 34.1 us -> 40.4 us
    pallas_call x34 -> x29, Pallas kernels: 231 us -> 215 us  [call(): pl.pallas_call(body, grid_spec=pltpu.PrefetchScalarGridSpec(num_scalar_pr...]
    ppermute x39 -> x43, waiting for transfers between devices: 25.8 us -> 32 us  [across(): return lax.ppermute(array, axis, [(i, i ^ bit) for i in range(size)])]
    unnamed x79 -> x83, local copies, waits for them, and re-layouts: 15.1 us -> 13.1 us
    ppermute x39 -> x43, starting transfers between devices: 31.1 us -> 30.7 us  [across(): return lax.ppermute(array, axis, [(i, i ^ bit) for i in range(size)])]
  transfers between devices with their start and end apart: 47 -> 51, of which waited for: 14 -> 13; matrix products, arithmetic and copies ran while one was open for 5% -> 4% of each run, Pallas kernels for 57% -> 55%
where the time goes in v2:
time: 350 us; the launch traced here: 344 us
  Pallas kernels  215 us (61%)
  starting transfers between devices  61.8 us (18%)
  waiting for transfers between devices  40.4 us (12%)
  local copies, waits for them, and re-layouts  19.9 us (6%)
  other arithmetic  5.92 us (2%)
    pallas_call x29, Pallas kernels, call(): pl.pallas_call(body, grid_spec=pltpu.PrefetchScalarGridSpec(num_scalar_pr...  215 us
    ppermute x43, waiting for transfers between devices, across(): return lax.ppermute(array, axis, [(i, i ^ bit) for i in range(size)])  32 us
    ppermute x43, starting transfers between devices, across(): return lax.ppermute(array, axis, [(i, i ^ bit) for i in range(size)])  30.7 us
    all_to_all x4, starting transfers between devices, along(): lax.all_to_all(array, 'dp', 0, 0, tiled=True, axis_index_groups=groups)  19.2 us
    unnamed x83, local copies, waits for them, and re-layouts  13.1 us
    all_to_all x1, waiting for transfers between devices, shards(): lax.all_to_all(pooled, ('dp', 'tensor'), 0, 0, tiled=True)  8.29 us
  transfers between devices with their start and end apart: 51, of which 13 were waited for; matrix products, arithmetic and copies ran while one was open for 4% of the time, Pallas kernels for 55%

profile of v2, /device:TPU:0, one launch (start us, length us, event | category | flops | bytes accessed | tf_op | source)
XLA Modules:
  0.0 344.2 jit_solution(17906692598035108065)
XLA Ops:
  1.6 1.1 copy.96
  2.9 3.0 collective-permute-start.5
  5.9 2.6 collective-permute-start.4
  8.5 1.3 collective-permute-start.3
  9.9 2.0 shard_map.222
  11.9 1.5 collective-permute-start.1
  15.0 0.9 copy-done.2
  17.8 1.5 collective-permute-start.6
  19.4 5.0 %all-to-all-start = ((bf16[4,96,1024]{2,1,0:T(8,128)(2,1)}), bf16[4,96,1024]{2,1,0:T(8,128)(2,1)}, u32[]{:S(2)}, u32[]{:S(2)}) async-start(bf16[4,96,1024]{2,1,0:T(8,128)(2,1)} %shard_map.227.refs_8_), calls=%async_computation | async-start | bytes 1572864 | tf_op jit(solution)/shard_map/all_to_all | solution.py:646
  24.7 6.5 %collective-permute-done.6.refs_2_ = bf16[4,96,640]{2,1,0:T(8,128)(2,1)S(1)} collective-permute-done((bf16[4,96,640]{2,1,0:T(8,128)(2,1)}, bf16[4,96,640]{2,1,0:T(8,128)(2,1)S(1)}, u32[]{:S(2)}, u32[]{:S(2)}) %collective-permute-start.6) | collective-permute-done | bytes 491552 | tf_op jit(solution)/shard_map/ppermute | solution.py:643
  31.2 2.6 shard_map.225.refs_4_.refs_5_
  33.8 1.5 collective-permute-start.8
  36.8 9.8 %shard_map.228 = (bf16[2,512,576]{2,1,0:T(8,128)(2,1)}, bf16[2,3,512,512]{3,2,1,0:T(8,128)(2,1)}, bf16[2,512,256]{2,1,0:T(8,128)(2,1)}, bf16[2,512,768]{2,1,0:T(8,128)(2,1)}) custom-call(bf16[2,128,768]{2,1,0:T(8,128)(2,1)} %copy-done.15, bf16[2,128,768]{2,1,0:T(8,128)(2,1)} %copy-done.32, bf16[2,128,768]{2,1,0:T(8,128)(2,1)} %copy-done.31, ...), custom_call_target="tpu_custom_call" | custom-call | flops 8625000448 | bytes 1024 | tf_op jit(solution)/shard_map/pallas_call | solution.py:60
  46.7 1.6 collective-permute-start.9
  50.6 4.5 %all-to-all-start.1 = ((bf16[4,96,768]{2,1,0:T(8,128)(2,1)}), bf16[4,96,768]{2,1,0:T(8,128)(2,1)S(1)}, u32[]{:S(2)}, u32[]{:S(2)}) async-start(bf16[4,96,768]{2,1,0:T(8,128)(2,1)} %shard_map.234), calls=%async_computation.1 | async-start | bytes 1179648 | tf_op jit(solution)/shard_map/all_to_all | solution.py:646
  55.1 9.3 %shard_map.230 = (bf16[2,512,576]{2,1,0:T(8,128)(2,1)}, bf16[2,3,512,512]{3,2,1,0:T(8,128)(2,1)}, bf16[2,512,256]{2,1,0:T(8,128)(2,1)}) custom-call(bf16[2,512,768]{2,1,0:T(8,128)(2,1)} %get-tuple-element.96.refs_0_.refs_5_, bf16[768,640]{1,0:T(8,128)(2,1)} %collective-permute-done.7.refs_1_.refs_6_, bf16[768,384]{1,0:T(8,128)(2,1)} %constant.78.clone.refs_5_.refs_2_, ...), custom_call_target="tpu_custom_call" | custom-call | flops 3104999936 | bytes 1024 | tf_op jit(solution)/shard_map/pallas_call | solution.py:60
  64.5 2.6 collective-permute-done.9.refs_1_
  67.5 9.3 %shard_map.232 = (bf16[2,512,576]{2,1,0:T(8,128)(2,1)}, bf16[2,3,512,512]{3,2,1,0:T(8,128)(2,1)}, bf16[2,512,256]{2,1,0:T(8,128)(2,1)}) custom-call(bf16[2,512,768]{2,1,0:T(8,128)(2,1)} %get-tuple-element.96.refs_0_.refs_5_, bf16[768,640]{1,0:T(8,128)(2,1)} %get-tuple-element.98.refs_1_.refs_7_, bf16[768,384]{1,0:T(8,128)(2,1)} %constant.78.clone.refs_5_.refs_2_, ...), custom_call_target="tpu_custom_call" | custom-call | flops 3104999936 | bytes 1024 | tf_op jit(solution)/shard_map/pallas_call | solution.py:60
  77.7 1.5 collective-permute-start.15
  79.7 9.4 %shard_map.236 = (bf16[2,512,576]{2,1,0:T(8,128)(2,1)}, bf16[2,3,512,512]{3,2,1,0:T(8,128)(2,1)}, bf16[2,512,256]{2,1,0:T(8,128)(2,1)}) custom-call(bf16[2,512,768]{2,1,0:T(8,128)(2,1)} %get-tuple-element.96.refs_0_.refs_5_, bf16[768,640]{1,0:T(8,128)(2,1)} %collective-permute-done.10.refs_1_.refs_8_, bf16[768,384]{1,0:T(8,128)(2,1)} %constant.78.clone.refs_5_.refs_2_, ...), custom_call_target="tpu_custom_call" | custom-call | flops 3104999936 | bytes 1024 | tf_op jit(solution)/shard_map/pallas_call | solution.py:60
  89.0 4.4 %collective-permute-done.15.refs_1_ = bf16[4,96,768]{2,1,0:T(8,128)(2,1)} collective-permute-done((bf16[4,96,768]{2,1,0:T(8,128)(2,1)}, bf16[4,96,768]{2,1,0:T(8,128)(2,1)}, u32[]{:S(2)}, u32[]{:S(2)}) %collective-permute-start.15) | collective-permute-done | bytes 589856 | tf_op jit(solution)/shard_map/ppermute | solution.py:643
  94.2 1.5 collective-permute-start.20
  96.5 22.4 %shard_map.238 = (bf16[1024,768]{1,0:T(8,128)(2,1)}, f32[1024,1]{1,0:T(8,128)}, bf16[1024,768]{1,0:T(8,128)(2,1)}, bf16[1024,3072]{1,0:T(8,128)(2,1)}, bf16[1024,3072]{1,0:T(8,128)(2,1)}, /*index=5*/f32[8,768]{1,0:T(8,128)}) custom-call(s32[2]{0:T(128)} %pad_add_fusion.1.refs_0_.here_ref, bf16[1024,256]{1,0:T(8,128)(2,1)} %bitcast.55, ...), custom_call_target="tpu_custom_call" | custom-call | flops 6899999744 | bytes 1024 | tf_op jit(solution)/shard_map/pallas_call | solution.py:60
  118.9 3.8 %collective-permute-done.21.refs_1_ = bf16[4,96,768]{2,1,0:T(8,128)(2,1)} collective-permute-done((bf16[4,96,768]{2,1,0:T(8,128)(2,1)}, bf16[4,96,768]{2,1,0:T(8,128)(2,1)}, u32[]{:S(2)}, u32[]{:S(2)}) %collective-permute-start.21) | collective-permute-done | bytes 589856 | tf_op jit(solution)/shard_map/ppermute | solution.py:643
  126.6 15.6 %shard_map.240 = (bf16[1024,768]{1,0:T(8,128)(2,1)}, f32[1024,1]{1,0:T(8,128)}, bf16[2,128,768]{2,1,0:T(8,128)(2,1)}, bf16[2,128,768]{2,1,0:T(8,128)(2,1)}, bf16...) custom-call(s32[2]{0:T(128)} %pad_add_fusion.1.refs_0_.here_ref, ...), custom_call_target="tpu_custom_call" | custom-call | flops 4830000128 | bytes 1024 | tf_op jit(solution)/shard_map/pallas_call | solution.py:60
  142.2 5.0 %all-to-all-start.2 = ((bf16[32,8,768]{2,1,0:T(8,128)(2,1)}), bf16[32,8,768]{2,1,0:T(8,128)(2,1)S(1)}, u32[]{:S(2)}, u32[]{:S(2)}) async-start(bf16[32,8,768]{2,1,0:T(8,128)(2,1)} %get-tuple-element.115), calls=%async_computation.2 | async-start | bytes 786432 | tf_op jit(solution)/shard_map/all_to_all | solution.py:939
  150.4 1.7 collective-permute-start.25
  152.1 8.3 %all-to-all-done.2 = bf16[32,8,768]{2,1,0:T(8,128)(2,1)S(1)} async-done(((bf16[32,8,768]{2,1,0:T(8,128)(2,1)}), bf16[32,8,768]{2,1,0:T(8,128)(2,1)S(1)}, u32[]{:S(2)}, u32[]{:S(2)}) %all-to-all-start.2) | async-done | bytes 393248 | tf_op jit(solution)/shard_map/all_to_all | solution.py:939
  161.1 20.5 %shard_map.241 = (bf16[1024,768]{1,0:T(8,128)(2,1)}, bf16[1024,3072]{1,0:T(8,128)(2,1)}, bf16[2,2,4,96,768]{4,3,2,1,0:T(8,128)(2,1)}, f32[8,768]{1,0:T(8,128)}, f32[8,3072]{1,0:T(8,128)}) custom-call(s32[2]{0:T(128)} %pad_add_fusion.1.refs_0_.here_ref, bf16[256,768]{1,0:T(8,128)(2,1)} %bitcast.59, s32[8,1]{1,0:T(8,128)} %iota_add_fusion.ids_ref, ...), custom_call_target="tpu_custom_call" | custom-call | flops 11040000000 | bytes 1024 | tf_op jit(solution)/shard_map/pallas_call | solution.py:60
  182.4 3.3 shard_map.242
  185.7 6.5 %shard_map.243.refs_4_ = bf16[2,2,4,96,768]{4,3,2,1,0:T(8,128)(2,1)} custom-call(s32[2]{0:T(128)} %pad_add_fusion.1.refs_0_.here_ref, bf16[1024,768]{1,0:T(8,128)(2,1)} %get-tuple-element.107.refs_2_.u_ref.refs_1_, bf16[1024,3072]{1,0:T(8,128)(2,1)} %get-tuple-element.122.refs_2_.refs_1_, bf16[2,2,4,96,768]{4,3,2,1,0:T(8,128)(2,1)} %get-tuple-element.119.refs_5_.refs_3_, ...), custom_call_target="tpu_custom_call" | custom-call | flops 13799999488 | bytes 1024 | tf_op jit(solution)/shard_map/pallas_call | solution.py:60
  192.7 6.9 %shard_map.244 = (bf16[2,4,96,768]{3,2,1,0:T(8,128)(2,1)}, bf16[2,4,96,768]{3,2,1,0:T(8,128)(2,1)}) custom-call(s32[2]{0:T(128)} %pad_add_fusion.1.refs_0_.here_ref, bf16[1024,768]{1,0:T(8,128)(2,1)} %get-tuple-element.123.refs_1_.refs_2_, bf16[1024,3072]{1,0:T(8,128)(2,1)} %get-tuple-element.106.h_ref.refs_2_, ...), custom_call_target="tpu_custom_call" | custom-call | flops 13799999488 | bytes 1024 | tf_op jit(solution)/shard_map/pallas_call | solution.py:60
  199.6 8.1 %shard_map.245 = (bf16[2,4,96,768]{3,2,1,0:T(8,128)(2,1)}, bf16[2,4,96,768]{3,2,1,0:T(8,128)(2,1)}) custom-call(s32[2]{0:T(128)} %pad_add_fusion.1.refs_0_.here_ref, bf16[1024,768]{1,0:T(8,128)(2,1)} %get-tuple-element.107.refs_2_.u_ref.refs_1_, bf16[1024,3072]{1,0:T(8,128)(2,1)} %get-tuple-element.122.refs_2_.refs_1_, ...), custom_call_target="tpu_custom_call" | custom-call | flops 13799999488 | bytes 1024 | tf_op jit(solution)/shard_map/pallas_call | solution.py:60
  208.2 1.5 collective-permute-start.29
  209.7 18.2 %shard_map.246 = (bf16[1024,768]{1,0:T(8,128)(2,1)}, bf16[1024,1024]{1,0:T(8,128)(2,1)}, f32[8,768]{1,0:T(8,128)}) custom-call(s32[2]{0:T(128)} %pad_add_fusion.1.refs_0_.here_ref, bf16[1024,3072]{1,0:T(8,128)(2,1)} %get-tuple-element.122.refs_2_.refs_1_, bf16[1024,768]{1,0:T(8,128)(2,1)} %get-tuple-element.123.refs_1_.refs_2_, ...), custom_call_target="tpu_custom_call" | custom-call | flops 4830000128 | bytes 1024 | tf_op jit(solution)/shard_map/pallas_call | solution.py:60
  227.9 11.0 %shard_map.247 = (bf16[2,4,96,768]{3,2,1,0:T(8,128)(2,1)}, f32[8,576]{1,0:T(8,128)}, bf16[2,512,640]{2,1,0:T(8,128)(2,1)}) custom-call(s32[2]{0:T(128)} %pad_add_fusion.1.refs_0_.here_ref, bf16[2,512,576]{2,1,0:T(8,128)(2,1)} %get-tuple-element.133.refs_1_, bf16[2,3,512,512]{3,2,1,0:T(8,128)(2,1)} %get-tuple-element.134.refs_2_, ...), custom_call_target="tpu_custom_call" | custom-call | flops 3795000064 | bytes 1024 | tf_op jit(solution)/shard_map/pallas_call | solution.py:60
  239.0 2.5 shard_map.249
  241.5 1.1 collective-permute-start.31
  242.6 1.0 collective-permute-start.32
  243.6 11.3 %shard_map.250 = (bf16[4,96,768]{2,1,0:T(8,128)(2,1)}, bf16[4,96,768]{2,1,0:T(8,128)(2,1)}, f32[8,576]{1,0:T(8,128)}, bf16[2,512,640]{2,1,0:T(8,128)(2,1)}) custom-call(s32[2]{0:T(128)} %pad_add_fusion.1.refs_0_.here_ref, bf16[2,512,576]{2,1,0:T(8,128)(2,1)} %get-tuple-element.141.refs_1_, bf16[2,3,512,512]{3,2,1,0:T(8,128)(2,1)} %get-tuple-element.142.refs_2_, ...), custom_call_target="tpu_custom_call" | custom-call | flops 3795000064 | bytes 1024 | tf_op jit(solution)/shard_map/pallas_call | solution.py:60
  255.0 1.1 collective-permute-start.35
  256.0 1.4 collective-permute-done.31.refs_0_
  257.4 1.3 collective-permute-done.32.refs_1_
  258.8 3.0 shard_map.252.refs_7_
  261.8 11.1 %shard_map.253 = (bf16[2,4,96,768]{3,2,1,0:T(8,128)(2,1)}, f32[8,576]{1,0:T(8,128)}, bf16[2,512,640]{2,1,0:T(8,128)(2,1)}) custom-call(s32[2]{0:T(128)} %pad_add_fusion.1.refs_0_.here_ref, bf16[2,512,576]{2,1,0:T(8,128)(2,1)} %get-tuple-element.130.refs_1_, bf16[2,3,512,512]{3,2,1,0:T(8,128)(2,1)} %get-tuple-element.131.refs_2_, ...), custom_call_target="tpu_custom_call" | custom-call | flops 3795000064 | bytes 1024 | tf_op jit(solution)/shard_map/pallas_call | solution.py:60
  273.8 4.5 %all-to-all-start.3 = ((bf16[4,96,1536]{2,1,0:T(8,128)(2,1)}), bf16[4,96,1536]{2,1,0:T(8,128)(2,1)}, u32[]{:S(2)}, u32[]{:S(2)}) async-start(bf16[4,96,1536]{2,1,0:T(8,128)(2,1)} %shard_map.252.refs_7_), calls=%async_computation.3 | async-start | bytes 2359296 | tf_op jit(solution)/shard_map/all_to_all | solution.py:646
  279.6 2.0 shard_map.256.refs_8_
  281.6 1.3 collective-permute-start.41
  282.9 11.3 %shard_map.257 = (bf16[4,96,768]{2,1,0:T(8,128)(2,1)}, bf16[4,96,768]{2,1,0:T(8,128)(2,1)}, f32[8,576]{1,0:T(8,128)}, bf16[2,512,640]{2,1,0:T(8,128)(2,1)}) custom-call(s32[2]{0:T(128)} %pad_add_fusion.1.refs_0_.here_ref, bf16[2,512,576]{2,1,0:T(8,128)(2,1)} %get-tuple-element.120.refs_1_, bf16[2,3,512,512]{3,2,1,0:T(8,128)(2,1)} %get-tuple-element.121.refs_2_, ...), custom_call_target="tpu_custom_call" | custom-call | flops 3795000064 | bytes 1024 | tf_op jit(solution)/shard_map/pallas_call | solution.py:60
  294.6 1.5 collective-permute-start.42
  296.1 10.3 %shard_map.258 = (bf16[2,128,768]{2,1,0:T(8,128)(2,1)}, bf16[2,128,768]{2,1,0:T(8,128)(2,1)}, bf16[2,128,768]{2,1,0:T(8,128)(2,1)}, bf16[2,128,768]{2,1,0:T(8,128)(2,1)}) custom-call(bf16[1024,640]{1,0:T(8,128)(2,1)} %bitcast.52, bf16[1024,640]{1,0:T(8,128)(2,1)} %bitcast.51, bf16[1024,640]{1,0:T(8,128)(2,1)} %bitcast.50, bf16[1024,640]{1,0:T(8,128)(2,1)} %bitcast.49, ...), custom_call_target="tpu_custom_call" | custom-call | flops 2760000000 | bytes 1024 | tf_op jit(solution)/shard_map/pallas_call | solution.py:60
  307.1 1.2 collective-permute-start.39
  308.3 1.2 collective-permute-done.40.refs_0_
  309.6 2.2 shard_map.260.refs_5_.refs_2_
  311.8 5.1 %all-to-all-start.4 = ((bf16[4,96,768]{2,1,0:T(8,128)(2,1)}), bf16[4,96,768]{2,1,0:T(8,128)(2,1)S(1)}, u32[]{:S(2)}, u32[]{:S(2)}) async-start(bf16[4,96,768]{2,1,0:T(8,128)(2,1)} %shard_map.260.refs_5_.refs_2_), calls=%async_computation.4 | async-start | bytes 1179648 | tf_op jit(solution)/shard_map/all_to_all | solution.py:646
  318.2 0.9 fusion
  319.4 6.9 %collective-permute-done.39.refs_4_ = bf16[2,128,768]{2,1,0:T(8,128)(2,1)} collective-permute-done((bf16[2,128,768]{2,1,0:T(8,128)(2,1)}, bf16[2,128,768]{2,1,0:T(8,128)(2,1)}, u32[]{:S(2)}, u32[]{:S(2)}) %collective-permute-start.39) | collective-permute-done | bytes 393248 | tf_op jit(solution)/shard_map/ppermute | solution.py:643
  326.3 3.3 shard_map.261
  329.5 1.8 collective-permute-start.44
  331.3 1.5 convert_reduce_fusion
  332.8 0.9 collective-permute-done.44
  333.7 2.7 collective-permute-start.45
  337.3 1.9 collective-permute-done.45
  343.1 0.9 copy.112
  (225 shorter events, 31.2 us)
Async XLA Ops:
  0.6 12.8 %copy-start = (s32[8,512]{1,0:T(8,128)S(1)}, s32[8,512]{1,0:T(8,128)}, u32[]{:S(2)}) copy-start(s32[8,512]{1,0:T(8,128)} %param.25) | copy-start | bytes 49156
  0.7 9.2 %copy-start.14 = (bf16[128,8,768]{2,1,0:T(8,128)(2,1)S(1)}, bf16[128,8,768]{2,1,0:T(8,128)(2,1)}, u32[]{:S(2)}) copy-start(bf16[128,8,768]{2,1,0:T(8,128)(2,1)} %param.15) | copy-start | bytes 4718596
  2.9 13.4 %collective-permute-start.5 = (bf16[96,640]{1,0:T(8,128)(2,1)S(1)}, bf16[96,640]{1,0:T(8,128)(2,1)S(1)}, u32[]{:S(2)}, u32[]{:S(2)}) collective-permute-start(bf16[96,640]{1,0:T(8,128)(2,1)S(1)} %shard_map.223.refs_0_), channel_id=1, source_target_pairs={{24,0},{28,4},{0,8},{4,12},{8,16},{12,20},{16,24},{20,28},{25,1},{... | collective-permute-start | bytes 368648 | tf_op jit(solution)/shard_map/ppermute | solution.py:669
  5.9 11.1 %collective-permute-start.4 = (bf16[96,640]{1,0:T(8,128)(2,1)S(1)}, bf16[96,640]{1,0:T(8,128)(2,1)S(1)}, u32[]{:S(2)}, u32[]{:S(2)}) collective-permute-start(bf16[96,640]{1,0:T(8,128)(2,1)S(1)} %shard_map.223.refs_0_), channel_id=1, source_target_pairs={{16,0},{20,4},{24,8},{28,12},{0,16},{4,20},{8,24},{12,28},{17,1},{... | collective-permute-start | bytes 368648 | tf_op jit(solution)/shard_map/ppermute | solution.py:669
  8.5 8.5 %collective-permute-start.3 = (bf16[96,640]{1,0:T(8,128)(2,1)S(1)}, bf16[96,640]{1,0:T(8,128)(2,1)S(1)}, u32[]{:S(2)}, u32[]{:S(2)}) collective-permute-start(bf16[96,640]{1,0:T(8,128)(2,1)S(1)} %shard_map.223.refs_0_), channel_id=1, source_target_pairs={{8,0},{12,4},{16,8},{20,12},{24,16},{28,20},{0,24},{4,28},{9,1},{1... | collective-permute-start | bytes 368648 | tf_op jit(solution)/shard_map/ppermute | solution.py:669
  11.9 5.9 %copy-start.15 = (bf16[2,128,768]{2,1,0:T(8,128)(2,1)}, bf16[2,128,768]{2,1,0:T(8,128)(2,1)S(1)}, u32[]{:S(2)}) copy-start(bf16[2,128,768]{2,1,0:T(8,128)(2,1)S(1)} %get-tuple-element.91.refs_0_) | copy-start | bytes 1179652
  11.9 23.4 %collective-permute-start.1 = (bf16[2,128,768]{2,1,0:T(8,128)(2,1)}, bf16[2,128,768]{2,1,0:T(8,128)(2,1)S(1)}, u32[]{:S(2)}, u32[]{:S(2)}) collective-permute-start(bf16[2,128,768]{2,1,0:T(8,128)(2,1)} %get-tuple-element.93), channel_id=1, source_target_pairs={{0,2},{1,3},{2,0},{3,1},{4,6},{5,7},{6,4},{7,5},{8,10},{9,11},{10,... | collective-permute-start | bytes 1179656 | tf_op jit(solution)/shard_map/ppermute | solution.py:643
  13.5 21.9 %collective-permute-start = (bf16[2,128,768]{2,1,0:T(8,128)(2,1)S(1)}, bf16[2,128,768]{2,1,0:T(8,128)(2,1)S(1)}, u32[]{:S(2)}, u32[]{:S(2)}) collective-permute-start(bf16[2,128,768]{2,1,0:T(8,128)(2,1)S(1)} %get-tuple-element.92.refs_4_.refs_3_.refs_1_), channel_id=1, source_target_pairs={{0,1},{1,0},{2,3},{3,2},{4,5},{5,4},{6,7},{7,6},{8,9},{9,8},{10,11... | collective-permute-start | bytes 1179656 | tf_op jit(solution)/shard_map/ppermute | solution.py:643
  16.3 19.0 %collective-permute-start.2 = (bf16[2,128,768]{2,1,0:T(8,128)(2,1)}, bf16[2,128,768]{2,1,0:T(8,128)(2,1)}, u32[]{:S(2)}, u32[]{:S(2)}) collective-permute-start(bf16[2,128,768]{2,1,0:T(8,128)(2,1)} %get-tuple-element.94), channel_id=1, source_target_pairs={{0,3},{1,2},{2,1},{3,0},{4,7},{5,6},{6,5},{7,4},{8,11},{9,10},{10,... | collective-permute-start | bytes 1179656 | tf_op jit(solution)/shard_map/ppermute | solution.py:643
  17.8 13.3 %collective-permute-start.6 = (bf16[4,96,640]{2,1,0:T(8,128)(2,1)}, bf16[4,96,640]{2,1,0:T(8,128)(2,1)S(1)}, u32[]{:S(2)}, u32[]{:S(2)}) collective-permute-start(bf16[4,96,640]{2,1,0:T(8,128)(2,1)} %shard_map.224.refs_1_), channel_id=1, source_target_pairs={{0,4},{4,0},{8,12},{12,8},{16,20},{20,16},{24,28},{28,24},{1,5},{5... | collective-permute-start | bytes 1474568 | tf_op jit(solution)/shard_map/ppermute | solution.py:643
  19.4 11.8 %copy-start.13 = (s32[2,1,512]{2,1,0:T(1,128)}, s32[2,1,512]{2,1,0:T(1,128)S(1)}, u32[]{:S(2)}) copy-start(s32[2,1,512]{2,1,0:T(1,128)S(1)} %compare_select_fusion.1.refs_3_.refs_6_) | copy-start | bytes 12292
  19.4 27.3 %all-to-all-start = ((bf16[4,96,1024]{2,1,0:T(8,128)(2,1)}), bf16[4,96,1024]{2,1,0:T(8,128)(2,1)}, u32[]{:S(2)}, u32[]{:S(2)}) async-start(bf16[4,96,1024]{2,1,0:T(8,128)(2,1)} %shard_map.227.refs_8_), calls=%async_computation | async-start | bytes 1572864 | tf_op jit(solution)/shard_map/all_to_all | solution.py:646
  24.7 12.2 %copy-start.4 = (s32[2,512,1]{2,1,0:T(8,128)}, s32[2,512,1]{2,1,0:T(8,128)S(1)}, u32[]{:S(2)}) copy-start(s32[2,512,1]{2,1,0:T(8,128)S(1)} %compare_select_fusion.refs_4_.refs_7_) | copy-start | bytes 12292
  33.8 30.7 %collective-permute-start.8 = (bf16[768,640]{1,0:T(8,128)(2,1)}, bf16[768,640]{1,0:T(8,128)(2,1)}, u32[]{:S(2)}, u32[]{:S(2)}) collective-permute-start(bf16[768,640]{1,0:T(8,128)(2,1)} %shard_map.225.refs_4_.refs_5_), channel_id=1, source_target_pairs={{0,2},{1,3},{2,0},{3,1},{4,6},{5,7},{6,4},{7,5},{8,10},{9,11},{10,... | collective-permute-start | bytes 2949128 | tf_op jit(solution)/shard_map/ppermute | solution.py:643
  35.3 19.8 %collective-permute-start.7 = (bf16[768,640]{1,0:T(8,128)(2,1)}, bf16[768,640]{1,0:T(8,128)(2,1)}, u32[]{:S(2)}, u32[]{:S(2)}) collective-permute-start(bf16[768,640]{1,0:T(8,128)(2,1)} %shard_map.225.refs_4_.refs_5_), channel_id=1, source_target_pairs={{0,1},{1,0},{2,3},{3,2},{4,5},{5,4},{6,7},{7,6},{8,9},{9,8},{10,11... | collective-permute-start | bytes 2949128 | tf_op jit(solution)/shard_map/ppermute | solution.py:643
  46.7 20.3 %collective-permute-start.9 = (bf16[4,96,1024]{2,1,0:T(8,128)(2,1)}, bf16[4,96,1024]{2,1,0:T(8,128)(2,1)}, u32[]{:S(2)}, u32[]{:S(2)}) collective-permute-start(bf16[4,96,1024]{2,1,0:T(8,128)(2,1)} %shard_map.229.refs_5_.refs_1_.refs_7_.refs_6_), channel_id=1, source_target_pairs={{0,4},{4,0},{8,12},{12,8},{16,20},{20,16},{24,28},{28,24},{1,5},{5... | collective-permute-start | bytes 2359304 | tf_op jit(solution)/shard_map/ppermute | solution.py:643
  50.1 26.7 %collective-permute-start.11 = (bf16[4,96,1024]{2,1,0:T(8,128)(2,1)}, bf16[4,96,1024]{2,1,0:T(8,128)(2,1)}, u32[]{:S(2)}, u32[]{:S(2)}) collective-permute-start(bf16[4,96,1024]{2,1,0:T(8,128)(2,1)} %shard_map.229.refs_5_.refs_1_.refs_7_.refs_6_), channel_id=1, source_target_pairs={{0,2},{1,3},{2,0},{3,1},{4,6},{5,7},{6,4},{7,5},{8,10},{9,11},{10,... | collective-permute-start | bytes 2359304 | tf_op jit(solution)/shard_map/ppermute | solution.py:643
  50.6 26.2 %all-to-all-start.1 = ((bf16[4,96,768]{2,1,0:T(8,128)(2,1)}), bf16[4,96,768]{2,1,0:T(8,128)(2,1)S(1)}, u32[]{:S(2)}, u32[]{:S(2)}) async-start(bf16[4,96,768]{2,1,0:T(8,128)(2,1)} %shard_map.234), calls=%async_computation.1 | async-start | bytes 1179648 | tf_op jit(solution)/shard_map/all_to_all | solution.py:646
  67.0 12.6 %collective-permute-start.10 = (bf16[768,640]{1,0:T(8,128)(2,1)}, bf16[768,640]{1,0:T(8,128)(2,1)}, u32[]{:S(2)}, u32[]{:S(2)}) collective-permute-start(bf16[768,640]{1,0:T(8,128)(2,1)} %get-tuple-element.98.refs_1_.refs_7_), channel_id=1, source_target_pairs={{0,1},{1,0},{2,3},{3,2},{4,5},{5,4},{6,7},{7,6},{8,9},{9,8},{10,11... | collective-permute-start | bytes 2949128 | tf_op jit(solution)/shard_map/ppermute | solution.py:643
  67.0 26.4 %collective-permute-start.14 = (bf16[4,96,1024]{2,1,0:T(8,128)(2,1)}, bf16[4,96,1024]{2,1,0:T(8,128)(2,1)}, u32[]{:S(2)}, u32[]{:S(2)}) collective-permute-start(bf16[4,96,1024]{2,1,0:T(8,128)(2,1)} %get-tuple-element.99.refs_5_.refs_8_.refs_7_), channel_id=1, source_target_pairs={{0,2},{1,3},{2,0},{3,1},{4,6},{5,7},{6,4},{7,5},{8,10},{9,11},{10,... | collective-permute-start | bytes 2359304 | tf_op jit(solution)/shard_map/ppermute | solution.py:643
  77.7 15.8 %collective-permute-start.15 = (bf16[4,96,768]{2,1,0:T(8,128)(2,1)}, bf16[4,96,768]{2,1,0:T(8,128)(2,1)}, u32[]{:S(2)}, u32[]{:S(2)}) collective-permute-start(bf16[4,96,768]{2,1,0:T(8,128)(2,1)} %get-tuple-element.101.refs_5_.refs_0_), channel_id=1, source_target_pairs={{0,4},{4,0},{8,12},{12,8},{16,20},{20,16},{24,28},{28,24},{1,5},{5... | collective-permute-start | bytes 1769480 | tf_op jit(solution)/shard_map/ppermute | solution.py:643
  79.1 16.6 %collective-permute-start.12 = (bf16[4,96,1024]{2,1,0:T(8,128)(2,1)}, bf16[4,96,1024]{2,1,0:T(8,128)(2,1)}, u32[]{:S(2)}, u32[]{:S(2)}) collective-permute-start(bf16[4,96,1024]{2,1,0:T(8,128)(2,1)} %shard_map.229.refs_5_.refs_1_.refs_7_.refs_6_), channel_id=1, source_target_pairs={{0,1},{1,0},{2,3},{3,2},{4,5},{5,4},{6,7},{7,6},{8,9},{9,8},{10,11... | collective-permute-start | bytes 2359304 | tf_op jit(solution)/shard_map/ppermute | solution.py:643
  79.2 16.8 %collective-permute-start.13 = (bf16[4,96,1024]{2,1,0:T(8,128)(2,1)}, bf16[4,96,1024]{2,1,0:T(8,128)(2,1)}, u32[]{:S(2)}, u32[]{:S(2)}) collective-permute-start(bf16[4,96,1024]{2,1,0:T(8,128)(2,1)} %get-tuple-element.99.refs_5_.refs_8_.refs_7_), channel_id=1, source_target_pairs={{0,1},{1,0},{2,3},{3,2},{4,5},{5,4},{6,7},{7,6},{8,9},{9,8},{10,11... | collective-permute-start | bytes 2359304 | tf_op jit(solution)/shard_map/ppermute | solution.py:643
  79.7 16.8 %collective-permute-start.16 = (bf16[4,96,1024]{2,1,0:T(8,128)(2,1)}, bf16[4,96,1024]{2,1,0:T(8,128)(2,1)}, u32[]{:S(2)}, u32[]{:S(2)}) collective-permute-start(bf16[4,96,1024]{2,1,0:T(8,128)(2,1)} %get-tuple-element.102.refs_6_.refs_11_.refs_10_), channel_id=1, source_target_pairs={{0,1},{1,0},{2,3},{3,2},{4,5},{5,4},{6,7},{7,6},{8,9},{9,8},{10,11... | collective-permute-start | bytes 2359304 | tf_op jit(solution)/shard_map/ppermute | solution.py:643
  93.4 3.0 collective-permute-start.17
  94.2 24.7 %collective-permute-start.20 = (bf16[4,96,768]{2,1,0:T(8,128)(2,1)S(1)}, bf16[4,96,768]{2,1,0:T(8,128)(2,1)}, u32[]{:S(2)}, u32[]{:S(2)}) collective-permute-start(bf16[4,96,768]{2,1,0:T(8,128)(2,1)S(1)} %copy-done.17), channel_id=1, source_target_pairs={{0,2},{1,3},{2,0},{3,1},{4,6},{5,7},{6,4},{7,5},{8,10},{9,11},{10,... | collective-permute-start | bytes 1769480 | tf_op jit(solution)/shard_map/ppermute | solution.py:643
  95.7 28.9 %collective-permute-start.18 = (bf16[4,96,768]{2,1,0:T(8,128)(2,1)S(1)}, bf16[4,96,768]{2,1,0:T(8,128)(2,1)}, u32[]{:S(2)}, u32[]{:S(2)}) collective-permute-start(bf16[4,96,768]{2,1,0:T(8,128)(2,1)S(1)} %copy-done.17), channel_id=1, source_target_pairs={{0,1},{1,0},{2,3},{3,2},{4,5},{5,4},{6,7},{7,6},{8,9},{9,8},{10,11... | collective-permute-start | bytes 1769480 | tf_op jit(solution)/shard_map/ppermute | solution.py:643
  95.9 26.7 %collective-permute-start.21 = (bf16[4,96,768]{2,1,0:T(8,128)(2,1)}, bf16[4,96,768]{2,1,0:T(8,128)(2,1)}, u32[]{:S(2)}, u32[]{:S(2)}) collective-permute-start(bf16[4,96,768]{2,1,0:T(8,128)(2,1)} %get-tuple-element.105.refs_15_.refs_1_), channel_id=1, source_target_pairs={{0,2},{1,3},{2,0},{3,1},{4,6},{5,7},{6,4},{7,5},{8,10},{9,11},{10,... | collective-permute-start | bytes 1769480 | tf_op jit(solution)/shard_map/ppermute | solution.py:643
  96.5 28.2 %collective-permute-start.19 = (bf16[4,96,768]{2,1,0:T(8,128)(2,1)}, bf16[4,96,768]{2,1,0:T(8,128)(2,1)}, u32[]{:S(2)}, u32[]{:S(2)}) collective-permute-start(bf16[4,96,768]{2,1,0:T(8,128)(2,1)} %get-tuple-element.105.refs_15_.refs_1_), channel_id=1, source_target_pairs={{0,1},{1,0},{2,3},{3,2},{4,5},{5,4},{6,7},{7,6},{8,9},{9,8},{10,11... | collective-permute-start | bytes 1769480 | tf_op jit(solution)/shard_map/ppermute | solution.py:643
  122.7 2.2 collective-permute-start.22
  122.7 3.1 collective-permute-start.23
  126.6 20.6 %copy-start.27 = (f32[128]{0:T(128)S(1)}, f32[128]{0:T(128)}, u32[]{:S(2)}) copy-start(f32[128]{0:T(128)} %param.27) | copy-start | bytes 1540
  126.6 20.9 %copy-start.24 = (s32[256]{0:T(256)S(1)}, s32[256]{0:T(256)}, u32[]{:S(2)}) copy-start(s32[256]{0:T(256)} %param.26) | copy-start | bytes 3076
  142.2 18.2 %all-to-all-start.2 = ((bf16[32,8,768]{2,1,0:T(8,128)(2,1)}), bf16[32,8,768]{2,1,0:T(8,128)(2,1)S(1)}, u32[]{:S(2)}, u32[]{:S(2)}) async-start(bf16[32,8,768]{2,1,0:T(8,128)(2,1)} %get-tuple-element.115), calls=%async_computation.2 | async-start | bytes 786432 | tf_op jit(solution)/shard_map/all_to_all | solution.py:939
  150.1 31.5 %collective-permute-start.24 = (bf16[2,128,768]{2,1,0:T(8,128)(2,1)}, bf16[2,128,768]{2,1,0:T(8,128)(2,1)S(1)}, u32[]{:S(2)}, u32[]{:S(2)}) collective-permute-start(bf16[2,128,768]{2,1,0:T(8,128)(2,1)} %get-tuple-element.112), channel_id=1, source_target_pairs={{0,1},{1,0},{2,3},{3,2},{4,5},{5,4},{6,7},{7,6},{8,9},{9,8},{10,11... | collective-permute-start | bytes 1179656 | tf_op jit(solution)/shard_map/ppermute | solution.py:643
  150.4 31.3 %collective-permute-start.25 = (bf16[2,128,768]{2,1,0:T(8,128)(2,1)}, bf16[2,128,768]{2,1,0:T(8,128)(2,1)}, u32[]{:S(2)}, u32[]{:S(2)}) collective-permute-start(bf16[2,128,768]{2,1,0:T(8,128)(2,1)} %get-tuple-element.113), channel_id=1, source_target_pairs={{0,2},{1,3},{2,0},{3,1},{4,6},{5,7},{6,4},{7,5},{8,10},{9,11},{10,... | collective-permute-start | bytes 1179656 | tf_op jit(solution)/shard_map/ppermute | solution.py:643
  152.1 29.6 %collective-permute-start.26 = (bf16[2,128,768]{2,1,0:T(8,128)(2,1)}, bf16[2,128,768]{2,1,0:T(8,128)(2,1)}, u32[]{:S(2)}, u32[]{:S(2)}) collective-permute-start(bf16[2,128,768]{2,1,0:T(8,128)(2,1)} %get-tuple-element.114), channel_id=1, source_target_pairs={{0,3},{1,2},{2,1},{3,0},{4,7},{5,6},{6,5},{7,4},{8,11},{9,10},{10,... | collective-permute-start | bytes 1179656 | tf_op jit(solution)/shard_map/ppermute | solution.py:643
  181.6 11.1 %collective-permute-start.28 = (bf16[2,2,4,96,768]{4,3,2,1,0:T(8,128)(2,1)}, bf16[2,2,4,96,768]{4,3,2,1,0:T(8,128)(2,1)}, u32[]{:S(2)}, u32[]{:S(2)}) collective-permute-start(bf16[2,2,4,96,768]{4,3,2,1,0:T(8,128)(2,1)} %get-tuple-element.119.refs_5_.refs_3_), channel_id=1, source_target_pairs={{0,1},{1,0},{2,3},{3,2},{4,5},{5,4},{6,7},{7,6},{8,9},{9,8},{10,11... | collective-permute-start | bytes 7077896 | tf_op jit(solution)/shard_map/ppermute | solution.py:643
  192.2 7.4 %collective-permute-start.27 = (bf16[2,2,4,96,768]{4,3,2,1,0:T(8,128)(2,1)}, bf16[2,2,4,96,768]{4,3,2,1,0:T(8,128)(2,1)}, u32[]{:S(2)}, u32[]{:S(2)}) collective-permute-start(bf16[2,2,4,96,768]{4,3,2,1,0:T(8,128)(2,1)} %shard_map.243.refs_4_), channel_id=1, source_target_pairs={{0,1},{1,0},{2,3},{3,2},{4,5},{5,4},{6,7},{7,6},{8,9},{9,8},{10,11... | collective-permute-start | bytes 7077896 | tf_op jit(solution)/shard_map/ppermute | solution.py:643
  207.7 31.3 %collective-permute-start.30 = (bf16[2,4,96,768]{3,2,1,0:T(8,128)(2,1)}, bf16[2,4,96,768]{3,2,1,0:T(8,128)(2,1)}, u32[]{:S(2)}, u32[]{:S(2)}) collective-permute-start(bf16[2,4,96,768]{3,2,1,0:T(8,128)(2,1)} %get-tuple-element.127.refs_14_.refs_7_), channel_id=1, source_target_pairs={{0,2},{1,3},{2,0},{3,1},{4,6},{5,7},{6,4},{7,5},{8,10},{9,11},{10,... | collective-permute-start | bytes 3538952 | tf_op jit(solution)/shard_map/ppermute | solution.py:643
  208.2 30.8 %collective-permute-start.29 = (bf16[2,4,96,768]{3,2,1,0:T(8,128)(2,1)}, bf16[2,4,96,768]{3,2,1,0:T(8,128)(2,1)}, u32[]{:S(2)}, u32[]{:S(2)}) collective-permute-start(bf16[2,4,96,768]{3,2,1,0:T(8,128)(2,1)} %get-tuple-element.126.refs_4_), channel_id=1, source_target_pairs={{0,4},{4,0},{8,12},{12,8},{16,20},{20,16},{24,28},{28,24},{1,5},{5... | collective-permute-start | bytes 3538952 | tf_op jit(solution)/shard_map/ppermute | solution.py:643
  238.9 4.7 %collective-permute-start.33 = (bf16[2,4,96,768]{3,2,1,0:T(8,128)(2,1)}, bf16[2,4,96,768]{3,2,1,0:T(8,128)(2,1)}, u32[]{:S(2)}, u32[]{:S(2)}) collective-permute-start(bf16[2,4,96,768]{3,2,1,0:T(8,128)(2,1)} %get-tuple-element.135.refs_2_), channel_id=1, source_target_pairs={{0,1},{1,0},{2,3},{3,2},{4,5},{5,4},{6,7},{7,6},{8,9},{9,8},{10,11... | collective-permute-start | bytes 3538952 | tf_op jit(solution)/shard_map/ppermute | solution.py:643
  241.5 15.9 %collective-permute-start.31 = (bf16[4,96,768]{2,1,0:T(8,128)(2,1)}, bf16[4,96,768]{2,1,0:T(8,128)(2,1)S(1)}, u32[]{:S(2)}, u32[]{:S(2)}) collective-permute-start(bf16[4,96,768]{2,1,0:T(8,128)(2,1)} %get-tuple-element.139.refs_8_), channel_id=1, source_target_pairs={{0,2},{1,3},{2,0},{3,1},{4,6},{5,7},{6,4},{7,5},{8,10},{9,11},{10,... | collective-permute-start | bytes 1769480 | tf_op jit(solution)/shard_map/ppermute | solution.py:643
  242.6 16.2 %collective-permute-start.32 = (bf16[4,96,768]{2,1,0:T(8,128)(2,1)}, bf16[4,96,768]{2,1,0:T(8,128)(2,1)}, u32[]{:S(2)}, u32[]{:S(2)}) collective-permute-start(bf16[4,96,768]{2,1,0:T(8,128)(2,1)} %get-tuple-element.140.refs_9_), channel_id=1, source_target_pairs={{0,4},{4,0},{8,12},{12,8},{16,20},{20,16},{24,28},{28,24},{1,5},{5... | collective-permute-start | bytes 1769480 | tf_op jit(solution)/shard_map/ppermute | solution.py:643
  255.0 24.6 %collective-permute-start.35 = (bf16[4,96,768]{2,1,0:T(8,128)(2,1)}, bf16[4,96,768]{2,1,0:T(8,128)(2,1)}, u32[]{:S(2)}, u32[]{:S(2)}) collective-permute-start(bf16[4,96,768]{2,1,0:T(8,128)(2,1)} %get-tuple-element.147), channel_id=1, source_target_pairs={{0,4},{4,0},{8,12},{12,8},{16,20},{20,16},{24,28},{28,24},{1,5},{5... | collective-permute-start | bytes 1769480 | tf_op jit(solution)/shard_map/ppermute | solution.py:643
  261.8 11.2 %copy-start.6 = (f32[8,3072]{1,0:T(8,128)S(1)}, f32[8,3072]{1,0:T(8,128)}, u32[]{:S(2)}) copy-start(f32[8,3072]{1,0:T(8,128)} %get-tuple-element.150.refs_2_) | copy-start | bytes 294916
  261.8 11.2 %copy-start.8 = (f32[8,768]{1,0:T(8,128)S(1)}, f32[8,768]{1,0:T(8,128)}, u32[]{:S(2)}) copy-start(f32[8,768]{1,0:T(8,128)} %get-tuple-element.149.refs_1_) | copy-start | bytes 73732
  261.8 11.2 %copy-start.9 = (f32[8,768]{1,0:T(8,128)S(1)}, f32[8,768]{1,0:T(8,128)}, u32[]{:S(2)}) copy-start(f32[8,768]{1,0:T(8,128)} %get-tuple-element.148.refs_0_) | copy-start | bytes 73732
  261.8 11.2 %copy-start.10 = (f32[8,576]{1,0:T(8,128)S(1)}, f32[8,576]{1,0:T(8,128)}, u32[]{:S(2)}) copy-start(f32[8,576]{1,0:T(8,128)} %get-tuple-element.153.refs_5_) | copy-start | bytes 55300
  261.8 11.2 %copy-start.11 = (f32[8,576]{1,0:T(8,128)S(1)}, f32[8,576]{1,0:T(8,128)}, u32[]{:S(2)}) copy-start(f32[8,576]{1,0:T(8,128)} %get-tuple-element.152.refs_4_) | copy-start | bytes 55300
  273.8 5.1 %collective-permute-start.36 = (f32[24,768]{1,0:T(8,128)S(1)}, f32[24,768]{1,0:T(8,128)S(1)}, u32[]{:S(2)}, u32[]{:S(2)}) collective-permute-start(f32[24,768]{1,0:T(8,128)S(1)} %get-tuple-element.155), channel_id=1, source_target_pairs={{0,1},{1,0},{2,3},{3,2},{4,5},{5,4},{6,7},{7,6},{8,9},{9,8},{10,11... | collective-permute-start | bytes 221192 | tf_op jit(solution)/shard_map/ppermute | solution.py:643
  273.8 34.5 %all-to-all-start.3 = ((bf16[4,96,1536]{2,1,0:T(8,128)(2,1)}), bf16[4,96,1536]{2,1,0:T(8,128)(2,1)}, u32[]{:S(2)}, u32[]{:S(2)}) async-start(bf16[4,96,1536]{2,1,0:T(8,128)(2,1)} %shard_map.252.refs_7_), calls=%async_computation.3 | async-start | bytes 2359296 | tf_op jit(solution)/shard_map/all_to_all | solution.py:646
  278.4 4.5 %collective-permute-start.34 = (bf16[2,4,96,768]{3,2,1,0:T(8,128)(2,1)}, bf16[2,4,96,768]{3,2,1,0:T(8,128)(2,1)}, u32[]{:S(2)}, u32[]{:S(2)}) collective-permute-start(bf16[2,4,96,768]{3,2,1,0:T(8,128)(2,1)} %get-tuple-element.146.refs_6_), channel_id=1, source_target_pairs={{0,1},{1,0},{2,3},{3,2},{4,5},{5,4},{6,7},{7,6},{8,9},{9,8},{10,11... | collective-permute-start | bytes 3538952 | tf_op jit(solution)/shard_map/ppermute | solution.py:643
  281.6 25.5 %collective-permute-start.41 = (bf16[4,96,768]{2,1,0:T(8,128)(2,1)}, bf16[4,96,768]{2,1,0:T(8,128)(2,1)S(1)}, u32[]{:S(2)}, u32[]{:S(2)}) collective-permute-start(bf16[4,96,768]{2,1,0:T(8,128)(2,1)} %shard_map.256.refs_8_), channel_id=1, source_target_pairs={{0,2},{1,3},{2,0},{3,1},{4,6},{5,7},{6,4},{7,5},{8,10},{9,11},{10,... | collective-permute-start | bytes 1769480 | tf_op jit(solution)/shard_map/ppermute | solution.py:643
  282.9 11.7 %copy-start.18 = (f32[24,768]{1,0:T(8,128)S(1)}, f32[24,768]{1,0:T(8,128)}, u32[]{:S(2)}) copy-start(f32[24,768]{1,0:T(8,128)} %add.166.refs_1_) | copy-start | bytes 221188
  294.2 15.4 %collective-permute-start.40 = (bf16[4,96,768]{2,1,0:T(8,128)(2,1)}, bf16[4,96,768]{2,1,0:T(8,128)(2,1)}, u32[]{:S(2)}, u32[]{:S(2)}) collective-permute-start(bf16[4,96,768]{2,1,0:T(8,128)(2,1)} %get-tuple-element.165), channel_id=1, source_target_pairs={{0,4},{4,0},{8,12},{12,8},{16,20},{20,16},{24,28},{28,24},{1,5},{5... | collective-permute-start | bytes 1769480 | tf_op jit(solution)/shard_map/ppermute | solution.py:643
  294.6 22.3 %collective-permute-start.42 = (f32[16,768]{1,0:T(8,128)S(1)}, f32[16,768]{1,0:T(8,128)S(1)}, u32[]{:S(2)}, u32[]{:S(2)}) collective-permute-start(f32[16,768]{1,0:T(8,128)S(1)} %pad_maximum_fusion), channel_id=1, source_target_pairs={{0,2},{1,3},{2,0},{3,1},{4,6},{5,7},{6,4},{7,5},{8,10},{9,11},{10,... | collective-permute-start | bytes 147464 | tf_op jit(solution)/shard_map/ppermute | solution.py:643
  306.4 13.0 %collective-permute-start.37 = (bf16[2,128,768]{2,1,0:T(8,128)(2,1)}, bf16[2,128,768]{2,1,0:T(8,128)(2,1)}, u32[]{:S(2)}, u32[]{:S(2)}) collective-permute-start(bf16[2,128,768]{2,1,0:T(8,128)(2,1)} %get-tuple-element.162), channel_id=1, source_target_pairs={{0,1},{1,0},{2,3},{3,2},{4,5},{5,4},{6,7},{7,6},{8,9},{9,8},{10,11... | collective-permute-start | bytes 1179656 | tf_op jit(solution)/shard_map/ppermute | solution.py:643
  306.4 13.0 %collective-permute-start.38 = (bf16[2,128,768]{2,1,0:T(8,128)(2,1)}, bf16[2,128,768]{2,1,0:T(8,128)(2,1)}, u32[]{:S(2)}, u32[]{:S(2)}) collective-permute-start(bf16[2,128,768]{2,1,0:T(8,128)(2,1)} %get-tuple-element.163), channel_id=1, source_target_pairs={{0,2},{1,3},{2,0},{3,1},{4,6},{5,7},{6,4},{7,5},{8,10},{9,11},{10,... | collective-permute-start | bytes 1179656 | tf_op jit(solution)/shard_map/ppermute | solution.py:643
  307.1 19.2 %collective-permute-start.39 = (bf16[2,128,768]{2,1,0:T(8,128)(2,1)}, bf16[2,128,768]{2,1,0:T(8,128)(2,1)}, u32[]{:S(2)}, u32[]{:S(2)}) collective-permute-start(bf16[2,128,768]{2,1,0:T(8,128)(2,1)} %get-tuple-element.164), channel_id=1, source_target_pairs={{0,3},{1,2},{2,1},{3,0},{4,7},{5,6},{6,5},{7,4},{8,11},{9,10},{10,... | collective-permute-start | bytes 1179656 | tf_op jit(solution)/shard_map/ppermute | solution.py:643
  311.8 30.2 %all-to-all-start.4 = ((bf16[4,96,768]{2,1,0:T(8,128)(2,1)}), bf16[4,96,768]{2,1,0:T(8,128)(2,1)S(1)}, u32[]{:S(2)}, u32[]{:S(2)}) async-start(bf16[4,96,768]{2,1,0:T(8,128)(2,1)} %shard_map.260.refs_5_.refs_2_), calls=%async_computation.4 | async-start | bytes 1179648 | tf_op jit(solution)/shard_map/all_to_all | solution.py:646
  319.1 10.5 %collective-permute-start.43 = (f32[16,768]{1,0:T(8,128)S(1)}, f32[16,768]{1,0:T(8,128)S(1)}, u32[]{:S(2)}, u32[]{:S(2)}) collective-permute-start(f32[16,768]{1,0:T(8,128)S(1)} %fusion), channel_id=1, source_target_pairs={{0,4},{4,0},{8,12},{12,8},{16,20},{20,16},{24,28},{28,24},{1,5},{5... | collective-permute-start | bytes 147464 | tf_op jit(solution)/shard_map/ppermute | solution.py:643
  329.5 4.2 %collective-permute-start.44 = (f32[16,768]{1,0:T(8,128)S(1)}, f32[16,768]{1,0:T(8,128)S(1)}, u32[]{:S(2)}, u32[]{:S(2)}) collective-permute-start(f32[16,768]{1,0:T(8,128)S(1)} %add.169), channel_id=1, source_target_pairs={{0,8},{4,12},{8,0},{12,4},{16,24},{20,28},{24,16},{28,20},{1,9},{5... | collective-permute-start | bytes 147464 | tf_op jit(solution)/shard_map/ppermute | solution.py:643
  333.7 5.5 %collective-permute-start.45 = (f32[16,768]{1,0:T(8,128)S(1)}, f32[16,768]{1,0:T(8,128)S(1)}, u32[]{:S(2)}, u32[]{:S(2)}) collective-permute-start(f32[16,768]{1,0:T(8,128)S(1)} %add.170), channel_id=1, source_target_pairs={{0,16},{4,20},{8,24},{12,28},{16,0},{20,4},{24,8},{28,12},{1,17},{... | collective-permute-start | bytes 147464 | tf_op jit(solution)/shard_map/ppermute | solution.py:643
  (22 other events, 45.9 us)

commit v3 on v2

--- a/solution.py
+++ b/solution.py
@@ -14,7 +14,6 @@
 EPS_COS = 1e-06
 LOSS_SCALE = 4096.0
 NEG = -1e30
-DEAD = 99
 
 BF = jnp.bfloat16
 F32 = jnp.float32
@@ -172,8 +171,8 @@
 
 def attn_fwd_kernel(parts, *refs):
     x_refs, refs = refs[:parts], refs[parts:]
-    w_ref, sqv_ref, kc_ref, qc_ref, qkv_ref, p_ref, o_ref, *refs = refs
-    *x_out, bias_ref, mask_ref = refs
+    w_ref, sqv_ref, kf_ref, qf_ref, qkv_ref, p_ref, o_ref, *refs = refs
+    *x_out, bias_ref = refs
     local = qkv_ref.shape[2] // 3
     heads = p_ref.shape[1]
     hd = local // heads
@@ -186,10 +185,6 @@
     if parts > 1:
         x = jnp.concatenate([ref[0] for ref in x_refs], axis=0)
         x_out[0][0] = x
-    kc, qc = kc_ref[0], qc_ref[0]
-    allowed = (kc == qc) | ((qc == DEAD) & (kc >= 0))
-    mask_ref[...] = jnp.where(allowed, 0.0, NEG)
-
     projected = nn(x, w_ref[:, : 3 * local])
     q_all = ((projected[:, :local] + bias_ref[0:1, :local]) * 0.125).astype(BF)
     k_all = projected[:, local : 2 * local].astype(BF)
@@ -200,7 +195,9 @@
     outs = []
     for h in range(heads):
         at = slice(h * hd, (h + 1) * hd)
-        s = nt(q_all[:, at], k_all[:, at]) + mask_ref[...]
+        q = jnp.concatenate([q_all[:, at], qf_ref[0]], axis=1)
+        k = jnp.concatenate([k_all[:, at], kf_ref[0]], axis=1)
+        s = nt(q, k)
         top = jnp.max(s, axis=-1, keepdims=True)
         e = jnp.exp(s - top)
         total = jnp.sum(e, axis=-1, keepdims=True)
@@ -289,9 +286,10 @@
             ).astype(BF)
             local = wide - 64
             small_ref[...] = tn(wo_ref[:, local:wide][:, :8], eye)
+            cols = [wo_ref[:, j * wide + local : (j + 1) * wide][:, :8] for j in range(4)]
+            rows = tn(jnp.concatenate(cols, axis=1), sup_ref[...])
             for j in range(4):
-                cols = wo_ref[:, j * wide + local : (j + 1) * wide][:, :8]
-                bup_ref[:, j * hidden : (j + 1) * hidden] = tn(cols, sup_ref[...])
+                bup_ref[:, j * hidden : (j + 1) * hidden] = rows[8 * j : 8 * j + 8]
         o = jnp.concatenate([o0[...], o1[...], o2[...], o3[...]], axis=1)
         z = x_ref[...].astype(F32) + (nt(o, wo_ref[...]) + small_ref[2:3])
         xh, rstd = norm(z)
@@ -589,9 +587,9 @@
                 fly_ref[z] = (theirs + got_ref[1, z].astype(F32)).astype(BF)
 
 
-def small_kernel(norm1_ref, norm2_ref, up_ref, s1, s2, s3, keep_ref, send_ref):
-    local = s1.shape[1] // 3
-    parts = {1: s1, 2: s2, 3: s3}
+def small_kernel(norm1_ref, norm2_ref, up_ref, s2, s3, keep_ref, send_ref):
+    local = s2.shape[1] // 3
+    parts = {2: s2, 3: s3}
     for ref, pair in ((keep_ref, (0, 2)), (send_ref, (1, 3))):
         ref[...] = jnp.zeros_like(ref)
         for i, (src, row) in enumerate(
@@ -603,6 +601,59 @@
             if j in parts:
                 ref[9 + 8 * n : 10 + 8 * n, :local] = parts[j][0:1, :local]
                 ref[9 + 8 * n : 10 + 8 * n, local : 2 * local] = parts[j][0:1, 2 * local :]
+
+
+def split_small(own):
+    rows = jnp.concatenate([own[0:6], own[8:10]], axis=0)
+    high = rows.astype(BF)
+    return jnp.concatenate([high, (rows - high.astype(F32)).astype(BF)], axis=0)
+
+
+def last_kernel(here_ref, a_ref, b_ref, c_ref, own_ref, got_ref, *out_refs):
+    depth, rows = a_ref.shape[0], a_ref.shape[1]
+    small = split_small(own_ref[...] + got_ref[...])
+    for k, out_ref in enumerate(out_refs):
+        z = lax.rem(here_ref[1] + k, depth)
+        total = a_ref[z].astype(F32) + b_ref[z].astype(F32) + c_ref[z].astype(F32)
+        out_ref[:rows, :] = total.astype(BF)
+        out_ref[rows:, :] = small
+
+
+def final_kernel(place_ref, *refs):
+    *parts, qkv_ref, out_ref, gains_ref, shifts_ref, up_ref, qv_ref = refs
+    rows = qkv_ref.shape[0]
+    total = parts[0][...].astype(F32)
+    for ref in parts[1:]:
+        total += ref[...].astype(F32)
+    local = qkv_ref.shape[2]
+    for i in range(3):
+        qkv_ref[:, i, :] = total[:rows, i * local : (i + 1) * local]
+    out_ref[...] = jnp.transpose(total[:rows, 3 * local :])
+    small = total[rows : rows + 8] + total[rows + 8 :]
+    width = small.shape[1]
+    hd = width // up_ref.shape[0]
+    lane = lax.broadcasted_iota(jnp.int32, (width, 128), 0)
+    column = lax.broadcasted_iota(jnp.int32, (width, 128), 1)
+
+    def pick(values, ones):
+        ones = ones.astype(BF)
+        a, b, c = split3(values)
+        return nn(a, ones) + nn(b, ones) + nn(c, ones)
+
+    size = gains_ref.shape[1]
+    norms = pick(small, (lane == place_ref[0] + column) & (column < size))
+    gains_ref[...] = norms[0:2, :size]
+    shifts_ref[...] = norms[2:6, :size]
+    group = up_ref.shape[1]
+    ones = (lane % hd == place_ref[1] + column) & (column < group)
+    head = lax.broadcasted_iota(jnp.int32, (16, width), 1) // hd
+    row = lax.broadcasted_iota(jnp.int32, (16, width), 0)
+    ups = pick(jnp.where(head == row, small[6:7], 0.0), ones)
+    up_ref[...] = ups[: up_ref.shape[0], :group]
+    qvs = pick(jnp.where(head == row, small[7:8], 0.0), ones)
+    heads = qv_ref.shape[1]
+    for i in range(2):
+        qv_ref[i] = qvs[i * heads : (i + 1) * heads, :group]
 
 
 def input_back_kernel(p0, p1, p2, p3, da_ref, w0, w1, w2, w3, y0, y1, y2, y3, w_ref, sems):
@@ -644,12 +695,6 @@
 
     def along(array):
         return lax.all_to_all(array, "dp", 0, 0, tiled=True, axis_index_groups=groups)
-
-    def turn(array, k):
-        return lax.ppermute(array, "dp", [(2 * ((z + k) % nh) + b, 2 * z + b) for z in range(nh) for b in range(2)])
-
-    def swap(array):
-        return across(array, "tensor", 1)
 
     def summed(*outs):
         layout, ins, shapes = [], [], []
@@ -772,10 +817,12 @@
         live = (place[None] < own_len[:, None, None]).reshape(rows, seq)
         seg = seg.reshape(rows, seq)
         key_code = jnp.where(live, seg, -1)
-        query_code = jnp.where(live, seg, DEAD)
+        classes = jnp.arange(hd)
+        query_features = (jnp.where(live, seg, SEGS)[:, :, None] == classes).astype(BF)
+        open_key = live[:, :, None] & ((seg[:, :, None] == classes) | (classes == SEGS))
+        key_features = jnp.where(open_key | (classes > SEGS), 0.0, NEG).astype(BF)
         sent_code = jnp.where(live, seg + SEGS * jnp.arange(rows)[:, None], -1).reshape(1, count)
         member = (key_code[:, None, :] == jnp.arange(SEGS)[None, :, None]).astype(F32)
-        key_codes, query_codes = key_code.reshape(rows, 1, seq), query_code.reshape(rows, seq, 1)
         inv_count = (1.0 / jnp.sum(member, axis=2)).reshape(sents, 1)
         own_ids = (d * row_count + t * rows) * SEGS + jnp.arange(sents, dtype=jnp.int32)
         is_mine = pair_ids[None, :] == own_ids[:, None]
@@ -804,7 +851,7 @@
         else:
             own1 = along(jnp.broadcast_to(first_piece[None], (nh, rb, wide)))
         lo1 = across(own1, "dp", 1)
-        w1 = {0: merged(own1, lo1, here_first, [key_codes, query_codes])}
+        w1 = {0: merged(own1, lo1, here_first, [key_features, query_features])}
         w1[1] = swap(w1[0])
         w1[2] = across(w1[0], "tensor", 2)
         extra = jnp.concatenate([ln_gains.T, shifts.T, b_up.reshape(-1, 1), jnp.zeros((rb, 57), BF)], axis=1)
@@ -847,11 +894,11 @@
                 + [
                     whole(w),
                     whole(sqv),
-                    (key_codes, (1, 1, seq), by_row),
-                    (query_codes, (1, seq, 1), by_row),
+                    (key_features, (1, seq, hd), by_row),
+                    (query_features, (1, seq, hd), by_row),
                 ],
                 outs,
-                scratch=[pltpu.VMEM((8, 2 * local), F32), pltpu.VMEM((seq, seq), F32)],
+                scratch=[pltpu.VMEM((8, 2 * local), F32)],
                 after=before,
                 limit=63,
                 cost=cost,
@@ -1068,22 +1115,24 @@
         got3y, gotux = across(turn3, "tensor", 2), across(turnu, "dp", 1)
         stay_far, fly_far = attend_back(2, got_far, [turn3, turnu])
         got_fly = across(fly_far, "dp", 1)
-        got3y, gotux = gate([got3y, gotux], [stay_far])
+        small_keep, small_send = call(
+            small_kernel,
+            (1,),
+            [whole(a) for a in (sums1, sums2, dbup, sums_of[2], sums_of[3])],
+            [whole_out((24, width), F32)] * 2,
+            limit=63,
+            after=[stay_far],
+        )
+        small_keep = small_keep + swap(small_send)
+        small_got = across(jnp.concatenate([small_keep[:8], small_keep[16:]], axis=0), "tensor", 2)
+        got3y, gotux = gate([got3y, gotux], [small_keep])
         (end,) = summed([[(stay3, (0,)), (got3x, (0,)), (got3y, ())], [(stayu, (0,)), (gotuy, (0,)), (gotux, ())]])
         end_sent = end
         end = along(end)
         back1 = attend_back(1, None, [end_sent])
         got_near = swap(back1)
-        small_keep, small_send = call(
-            small_kernel,
-            (1,),
-            [whole(a) for a in (sums1, sums2, dbup, sums_of[1], sums_of[2], sums_of[3])],
-            [whole_out((24, width), F32)] * 2,
-            after=[back1],
-        )
-        small_keep = small_keep + swap(small_send)
-        small_got = across(jnp.concatenate([small_keep[:8], small_keep[16:]], axis=0), "tensor", 2)
-        (got_fly,) = gate([got_fly], [small_keep])
+        got_sums = swap(sums_of[1])
+        (got_fly,) = gate([got_fly], [back1])
         (turn1,) = summed([[(stay_far, ()), (got_fly, ())]])
         got_turn1 = across(turn1, "tensor", 2)
         stay_near, fly_near = attend_back(0, got_near, [turn1])
@@ -1102,32 +1151,63 @@
         token_parts = send_back(dx_parts)
 
         got1, got_turn1, end = gate([got1, got_turn1, end], [dx_parts[0]])
-        (last1,) = summed([[(stay_near, ()), (got1, ()), (got_turn1, ())]])
-        small_got, near_sums = gate([small_got, sums_of[0]], [last1])
+        near_sums = sums_of[0] + got_sums
         near_sums = jnp.concatenate([near_sums[:1, :local], near_sums[:1, 2 * local :]], axis=1)
         own = small_keep[:16] + small_got + jnp.pad(near_sums, ((9, 6), (0, width - 2 * local)))
-        bit = 1
-        while bit < nd:
-            own = own + across(own, "dp", bit)
-            bit *= 2
-        rest = lax.dynamic_slice_in_dim(own[:6], (d * ntens + t) * (width // (nd * ntens)), width // (nd * ntens), 1)
-        grad_b_up = lax.dynamic_slice_in_dim(own[8].reshape(hidden // hd, hd), d * hb, hb, 1)
-        grad_b_qv = lax.dynamic_slice_in_dim(own[9, : 2 * local].reshape(2, heads, hd), d * hb, hb, 2)
-        grad_one = settle(along(last1))
-        grad_tokens = collected(token_parts, [last1])
+        got = across(own, "dp", 1)
+        if fused and nh <= 4:
+            last = call(
+                last_kernel,
+                (1,),
+                [whole(here_first)] + [whole(v) for v in (stay_near, got1, got_turn1, own, got)],
+                [whole_out((rb + 16, width), BF)] * nh,
+                scalars=1,
+                after=[token_parts[1]],
+                limit=63,
+                cost=60.0,
+            )
+            last_sent = last[0]
+            mine = width // (nd * ntens)
+            at = jnp.stack([(d * ntens + t) * mine, d * hb]).astype(jnp.int32)
+            grad_qkv, grad_out, grad_gains, grad_shifts, grad_b_up, grad_b_qv = call(
+                final_kernel,
+                (1,),
+                [whole(at)] + [whole(v) for v in [last[0]] + [turn(last[k], nh - k) for k in range(1, nh)]],
+                [
+                    whole_out((rb, 3, local), F32),
+                    whole_out((local, rb), F32),
+                    whole_out((2, mine), F32),
+                    whole_out((4, mine), F32),
+                    whole_out((hidden // hd, hb), F32),
+                    whole_out((2, heads, hb), F32),
+                ],
+                scalars=1,
+                limit=32,
+            )
+        else:
+            (last_sent,) = summed([[(stay_near, ()), (got1, ()), (got_turn1, ())]])
+            small = jnp.broadcast_to(split_small(own + got)[None], (nh, 16, width))
+            total = settle(along(jnp.concatenate([last_sent, small], axis=1)))
+            grad_qkv, grad_out = total[:rb, : 3 * local].reshape(rb, 3, local), total[:rb, 3 * local :].T
+            small = total[rb : rb + 8] + total[rb + 8 :]
+            rest = lax.dynamic_slice_in_dim(small[:6], (d * ntens + t) * (width // (nd * ntens)), width // (nd * ntens), 1)
+            grad_b_up = lax.dynamic_slice_in_dim(small[6].reshape(hidden // hd, hd), d * hb, hb, 1)
+            grad_b_qv = lax.dynamic_slice_in_dim(small[7, : 2 * local].reshape(2, heads, hd), d * hb, hb, 2)
+            grad_gains, grad_shifts = rest[:2], rest[2:]
+        grad_tokens = collected(token_parts, [last_sent])
         end = settle(end)
         grad_down, grad_up = end[:, :hidden], end[:, hidden:]
         return (
             hidden_out,
             grad_tokens,
-            grad_one[:, : 3 * local].reshape(rb, 3, local),
+            grad_qkv,
             grad_b_qv,
-            grad_one[:, 3 * local :].T,
+            grad_out,
             grad_up,
             grad_b_up,
             grad_down.T,
-            rest[:2],
-            rest[2:],
+            grad_gains,
+            grad_shifts,
         )
 
     return shards

time: 350 us -> 340 us (0.971)
  waiting for transfers between devices: 40.4 us -> 32.8 us
    ppermute x43 -> x42, waiting for transfers between devices: 32 us -> 23.9 us  [across(): return lax.ppermute(array, axis, [(i, i ^ bit) for i in range(size)])]
    ppermute x3 -> x6, starting transfers between devices: 6.96 us -> 12.8 us  [turn(): lax.ppermute(array, 'dp', [(2 * ((z + k) % nh) + b, 2 * z + b) for z in r...]
    all_to_all x4 -> x3, starting transfers between devices: 19.2 us -> 14.6 us  [along(): lax.all_to_all(array, 'dp', 0, 0, tiled=True, axis_index_groups=groups)]
    ppermute x43 -> x42, starting transfers between devices: 30.7 us -> 26.7 us  [across(): return lax.ppermute(array, axis, [(i, i ^ bit) for i in range(size)])]
    pallas_call x29 -> x30, Pallas kernels: 215 us -> 215 us  [call(): pl.pallas_call(body, grid_spec=pltpu.PrefetchScalarGridSpec(num_scalar_pr...]
    unnamed x83 -> x85, local copies, waits for them, and re-layouts: 13.1 us -> 13.2 us
  transfers between devices with their start and end apart: 51 -> 52, of which waited for: 13 -> 12; matrix products, arithmetic and copies ran while one was open for 4% -> 4% of each run, Pallas kernels for 55% -> 57%
where the time goes in v3:
time: 340 us; the launch traced here: 334 us
  Pallas kernels  215 us (63%)
  starting transfers between devices  59.9 us (18%)
  waiting for transfers between devices  32.8 us (10%)
  local copies, waits for them, and re-layouts  18.3 us (5%)
  other arithmetic  6.47 us (2%)
    pallas_call x30, Pallas kernels, call(): pl.pallas_call(body, grid_spec=pltpu.PrefetchScalarGridSpec(num_scalar_pr...  215 us
    ppermute x42, starting transfers between devices, across(): return lax.ppermute(array, axis, [(i, i ^ bit) for i in range(size)])  26.7 us
    ppermute x42, waiting for transfers between devices, across(): return lax.ppermute(array, axis, [(i, i ^ bit) for i in range(size)])  23.9 us
    all_to_all x3, starting transfers between devices, along(): lax.all_to_all(array, 'dp', 0, 0, tiled=True, axis_index_groups=groups)  14.6 us
    unnamed x85, local copies, waits for them, and re-layouts  13.2 us
    ppermute x6, starting transfers between devices, turn(): lax.ppermute(array, 'dp', [(2 * ((z + k) % nh) + b, 2 * z + b) for z in r...  12.8 us
    all_to_all x1, waiting for transfers between devices, shards(): lax.all_to_all(pooled, ('dp', 'tensor'), 0, 0, tiled=True)  8.18 us
  transfers between devices with their start and end apart: 52, of which 12 were waited for; matrix products, arithmetic and copies ran while one was open for 4% of the time, Pallas kernels for 57%

profile of v3, /device:TPU:0, one launch (start us, length us, event | category | flops | bytes accessed | tf_op | source)
XLA Modules:
  0.0 334.1 jit_solution(9119323193535049593)
XLA Ops:
  1.6 1.1 copy.75
  2.9 3.0 collective-permute-start.5
  5.9 2.6 collective-permute-start.4
  8.5 1.3 collective-permute-start.3
  9.9 2.0 shard_map.222
  12.6 1.5 collective-permute-start.1
  17.5 1.5 collective-permute-start.6
  19.9 0.9 copy-done.2
  20.8 5.4 %all-to-all-start = ((bf16[4,96,1024]{2,1,0:T(8,128)(2,1)}), bf16[4,96,1024]{2,1,0:T(8,128)(2,1)}, u32[]{:S(2)}, u32[]{:S(2)}) async-start(bf16[4,96,1024]{2,1,0:T(8,128)(2,1)} %shard_map.227.refs_8_), calls=%async_computation | async-start | bytes 1572864 | tf_op jit(solution)/shard_map/all_to_all | solution.py:697
  26.6 4.1 %collective-permute-done.6.refs_2_ = bf16[4,96,640]{2,1,0:T(8,128)(2,1)S(1)} collective-permute-done((bf16[4,96,640]{2,1,0:T(8,128)(2,1)}, bf16[4,96,640]{2,1,0:T(8,128)(2,1)S(1)}, u32[]{:S(2)}, u32[]{:S(2)}) %collective-permute-start.6) | collective-permute-done | bytes 491552 | tf_op jit(solution)/shard_map/ppermute | solution.py:694
  30.7 2.6 shard_map.225.refs_4_.refs_5_
  33.4 1.5 collective-permute-start.8
  36.5 9.2 %shard_map.228 = (bf16[2,512,576]{2,1,0:T(8,128)(2,1)}, bf16[2,3,512,512]{3,2,1,0:T(8,128)(2,1)}, bf16[2,512,256]{2,1,0:T(8,128)(2,1)}, bf16[2,512,768]{2,1,0:T(8,128)(2,1)}) custom-call(bf16[2,128,768]{2,1,0:T(8,128)(2,1)} %copy-done.11, bf16[2,128,768]{2,1,0:T(8,128)(2,1)} %copy-done.30, bf16[2,128,768]{2,1,0:T(8,128)(2,1)} %copy-done.28, ...), custom_call_target="tpu_custom_call" | custom-call | flops 8625000448 | bytes 1024 | tf_op jit(solution)/shard_map/pallas_call | solution.py:59
  45.8 1.5 collective-permute-start.9
  47.5 0.9 shard_map.233.refs_0_
  49.7 4.6 %all-to-all-start.1 = ((bf16[4,96,768]{2,1,0:T(8,128)(2,1)}), bf16[4,96,768]{2,1,0:T(8,128)(2,1)S(1)}, u32[]{:S(2)}, u32[]{:S(2)}) async-start(bf16[4,96,768]{2,1,0:T(8,128)(2,1)} %shard_map.234), calls=%async_computation.1 | async-start | bytes 1179648 | tf_op jit(solution)/shard_map/all_to_all | solution.py:697
  54.4 8.6 %shard_map.230 = (bf16[2,512,576]{2,1,0:T(8,128)(2,1)}, bf16[2,3,512,512]{3,2,1,0:T(8,128)(2,1)}, bf16[2,512,256]{2,1,0:T(8,128)(2,1)}) custom-call(bf16[2,512,768]{2,1,0:T(8,128)(2,1)} %get-tuple-element.104.refs_0_.refs_5_, bf16[768,640]{1,0:T(8,128)(2,1)} %collective-permute-done.7.refs_1_.refs_6_, bf16[768,384]{1,0:T(8,128)(2,1)} %constant.75.clone.refs_5_.refs_2_, ...), custom_call_target="tpu_custom_call" | custom-call | flops 3104999936 | bytes 1024 | tf_op jit(solution)/shard_map/pallas_call | solution.py:59
  63.0 3.1 collective-permute-done.9.refs_1_
  66.6 8.6 %shard_map.232 = (bf16[2,512,576]{2,1,0:T(8,128)(2,1)}, bf16[2,3,512,512]{3,2,1,0:T(8,128)(2,1)}, bf16[2,512,256]{2,1,0:T(8,128)(2,1)}) custom-call(bf16[2,512,768]{2,1,0:T(8,128)(2,1)} %get-tuple-element.104.refs_0_.refs_5_, bf16[768,640]{1,0:T(8,128)(2,1)} %get-tuple-element.106.refs_1_.refs_7_, bf16[768,384]{1,0:T(8,128)(2,1)} %constant.75.clone.refs_5_.refs_2_, ...), custom_call_target="tpu_custom_call" | custom-call | flops 3104999936 | bytes 1024 | tf_op jit(solution)/shard_map/pallas_call | solution.py:59
  76.1 1.5 collective-permute-start.15
  78.1 8.6 %shard_map.236 = (bf16[2,512,576]{2,1,0:T(8,128)(2,1)}, bf16[2,3,512,512]{3,2,1,0:T(8,128)(2,1)}, bf16[2,512,256]{2,1,0:T(8,128)(2,1)}) custom-call(bf16[2,512,768]{2,1,0:T(8,128)(2,1)} %get-tuple-element.104.refs_0_.refs_5_, bf16[768,640]{1,0:T(8,128)(2,1)} %collective-permute-done.10.refs_1_.refs_8_, bf16[768,384]{1,0:T(8,128)(2,1)} %constant.75.clone.refs_5_.refs_2_, ...), custom_call_target="tpu_custom_call" | custom-call | flops 3104999936 | bytes 1024 | tf_op jit(solution)/shard_map/pallas_call | solution.py:59
  86.7 5.2 %collective-permute-done.15.refs_1_ = bf16[4,96,768]{2,1,0:T(8,128)(2,1)} collective-permute-done((bf16[4,96,768]{2,1,0:T(8,128)(2,1)}, bf16[4,96,768]{2,1,0:T(8,128)(2,1)}, u32[]{:S(2)}, u32[]{:S(2)}) %collective-permute-start.15) | collective-permute-done | bytes 589856 | tf_op jit(solution)/shard_map/ppermute | solution.py:694
  92.5 1.5 collective-permute-start.20
  94.8 22.2 %shard_map.238 = (bf16[1024,768]{1,0:T(8,128)(2,1)}, f32[1024,1]{1,0:T(8,128)}, bf16[1024,768]{1,0:T(8,128)(2,1)}, bf16[1024,3072]{1,0:T(8,128)(2,1)}, bf16[1024,3072]{1,0:T(8,128)(2,1)}, /*index=5*/f32[8,768]{1,0:T(8,128)}) custom-call(s32[2]{0:T(128)} %pad_add_fusion.1.refs_0_.here_ref, bf16[1024,256]{1,0:T(8,128)(2,1)} %bitcast.56, ...), custom_call_target="tpu_custom_call" | custom-call | flops 6899999744 | bytes 1024 | tf_op jit(solution)/shard_map/pallas_call | solution.py:59
  117.0 4.0 %collective-permute-done.21.refs_1_ = bf16[4,96,768]{2,1,0:T(8,128)(2,1)} collective-permute-done((bf16[4,96,768]{2,1,0:T(8,128)(2,1)}, bf16[4,96,768]{2,1,0:T(8,128)(2,1)}, u32[]{:S(2)}, u32[]{:S(2)}) %collective-permute-start.21) | collective-permute-done | bytes 589856 | tf_op jit(solution)/shard_map/ppermute | solution.py:694
  124.9 15.4 %shard_map.240 = (bf16[1024,768]{1,0:T(8,128)(2,1)}, f32[1024,1]{1,0:T(8,128)}, bf16[2,128,768]{2,1,0:T(8,128)(2,1)}, bf16[2,128,768]{2,1,0:T(8,128)(2,1)}, bf16...) custom-call(s32[2]{0:T(128)} %pad_add_fusion.1.refs_0_.here_ref, ...), custom_call_target="tpu_custom_call" | custom-call | flops 4830000128 | bytes 1024 | tf_op jit(solution)/shard_map/pallas_call | solution.py:59
  140.3 5.9 %all-to-all-start.2 = ((bf16[32,8,768]{2,1,0:T(8,128)(2,1)}), bf16[32,8,768]{2,1,0:T(8,128)(2,1)S(1)}, u32[]{:S(2)}, u32[]{:S(2)}) async-start(bf16[32,8,768]{2,1,0:T(8,128)(2,1)} %get-tuple-element.123), calls=%async_computation.2 | async-start | bytes 786432 | tf_op jit(solution)/shard_map/all_to_all | solution.py:986
  149.5 1.7 collective-permute-start.25
  151.2 8.2 %all-to-all-done.2 = bf16[32,8,768]{2,1,0:T(8,128)(2,1)S(1)} async-done(((bf16[32,8,768]{2,1,0:T(8,128)(2,1)}), bf16[32,8,768]{2,1,0:T(8,128)(2,1)S(1)}, u32[]{:S(2)}, u32[]{:S(2)}) %all-to-all-start.2) | async-done | bytes 393248 | tf_op jit(solution)/shard_map/all_to_all | solution.py:986
  160.2 20.5 %shard_map.241 = (bf16[1024,768]{1,0:T(8,128)(2,1)}, bf16[1024,3072]{1,0:T(8,128)(2,1)}, bf16[2,2,4,96,768]{4,3,2,1,0:T(8,128)(2,1)}, f32[8,768]{1,0:T(8,128)}, f32[8,3072]{1,0:T(8,128)}) custom-call(s32[2]{0:T(128)} %pad_add_fusion.1.refs_0_.here_ref, bf16[256,768]{1,0:T(8,128)(2,1)} %bitcast.60, s32[8,1]{1,0:T(8,128)} %iota_add_fusion.ids_ref, ...), custom_call_target="tpu_custom_call" | custom-call | flops 11040000000 | bytes 1024 | tf_op jit(solution)/shard_map/pallas_call | solution.py:59
  181.5 3.3 shard_map.242
  184.8 6.5 %shard_map.243.refs_4_ = bf16[2,2,4,96,768]{4,3,2,1,0:T(8,128)(2,1)} custom-call(s32[2]{0:T(128)} %pad_add_fusion.1.refs_0_.here_ref, bf16[1024,768]{1,0:T(8,128)(2,1)} %get-tuple-element.115.refs_2_.u_ref.refs_1_, bf16[1024,3072]{1,0:T(8,128)(2,1)} %get-tuple-element.130.refs_2_.refs_1_, bf16[2,2,4,96,768]{4,3,2,1,0:T(8,128)(2,1)} %get-tuple-element.127.refs_5_.refs_3_, ...), custom_call_target="tpu_custom_call" | custom-call | flops 13799999488 | bytes 1024 | tf_op jit(solution)/shard_map/pallas_call | solution.py:59
  191.8 6.9 %shard_map.244 = (bf16[2,4,96,768]{3,2,1,0:T(8,128)(2,1)}, bf16[2,4,96,768]{3,2,1,0:T(8,128)(2,1)}) custom-call(s32[2]{0:T(128)} %pad_add_fusion.1.refs_0_.here_ref, bf16[1024,768]{1,0:T(8,128)(2,1)} %get-tuple-element.131.refs_1_.refs_2_, bf16[1024,3072]{1,0:T(8,128)(2,1)} %get-tuple-element.114.h_ref.refs_2_, ...), custom_call_target="tpu_custom_call" | custom-call | flops 13799999488 | bytes 1024 | tf_op jit(solution)/shard_map/pallas_call | solution.py:59
  198.7 8.1 %shard_map.245 = (bf16[2,4,96,768]{3,2,1,0:T(8,128)(2,1)}, bf16[2,4,96,768]{3,2,1,0:T(8,128)(2,1)}) custom-call(s32[2]{0:T(128)} %pad_add_fusion.1.refs_0_.here_ref, bf16[1024,768]{1,0:T(8,128)(2,1)} %get-tuple-element.115.refs_2_.u_ref.refs_1_, bf16[1024,3072]{1,0:T(8,128)(2,1)} %get-tuple-element.130.refs_2_.refs_1_, ...), custom_call_target="tpu_custom_call" | custom-call | flops 13799999488 | bytes 1024 | tf_op jit(solution)/shard_map/pallas_call | solution.py:59
  207.3 1.5 collective-permute-start.29
  208.8 18.0 %shard_map.246 = (bf16[1024,768]{1,0:T(8,128)(2,1)}, bf16[1024,1024]{1,0:T(8,128)(2,1)}, f32[8,768]{1,0:T(8,128)}) custom-call(s32[2]{0:T(128)} %pad_add_fusion.1.refs_0_.here_ref, bf16[1024,3072]{1,0:T(8,128)(2,1)} %get-tuple-element.130.refs_2_.refs_1_, bf16[1024,768]{1,0:T(8,128)(2,1)} %get-tuple-element.131.refs_1_.refs_2_, ...), custom_call_target="tpu_custom_call" | custom-call | flops 4830000128 | bytes 1024 | tf_op jit(solution)/shard_map/pallas_call | solution.py:59
  226.8 11.0 %shard_map.247 = (bf16[2,4,96,768]{3,2,1,0:T(8,128)(2,1)}, f32[8,576]{1,0:T(8,128)}, bf16[2,512,640]{2,1,0:T(8,128)(2,1)}) custom-call(s32[2]{0:T(128)} %pad_add_fusion.1.refs_0_.here_ref, bf16[2,512,576]{2,1,0:T(8,128)(2,1)} %get-tuple-element.141.refs_1_, bf16[2,3,512,512]{3,2,1,0:T(8,128)(2,1)} %get-tuple-element.142.refs_2_, ...), custom_call_target="tpu_custom_call" | custom-call | flops 3795000064 | bytes 1024 | tf_op jit(solution)/shard_map/pallas_call | solution.py:59
  237.9 2.5 shard_map.249
  240.4 1.1 collective-permute-start.31
  241.5 1.0 collective-permute-start.32
  242.5 11.2 %shard_map.250 = (bf16[4,96,768]{2,1,0:T(8,128)(2,1)}, bf16[4,96,768]{2,1,0:T(8,128)(2,1)}, f32[8,576]{1,0:T(8,128)}, bf16[2,512,640]{2,1,0:T(8,128)(2,1)}) custom-call(s32[2]{0:T(128)} %pad_add_fusion.1.refs_0_.here_ref, bf16[2,512,576]{2,1,0:T(8,128)(2,1)} %get-tuple-element.152.refs_1_, bf16[2,3,512,512]{3,2,1,0:T(8,128)(2,1)} %get-tuple-element.153.refs_2_, ...), custom_call_target="tpu_custom_call" | custom-call | flops 3795000064 | bytes 1024 | tf_op jit(solution)/shard_map/pallas_call | solution.py:59
  253.7 1.7 shard_map.251
  255.4 1.0 collective-permute-start.36
  256.9 0.9 add.153.refs_2_
  259.2 3.0 shard_map.253.refs_7_
  262.2 4.5 %all-to-all-start.3 = ((bf16[4,96,1536]{2,1,0:T(8,128)(2,1)}), bf16[4,96,1536]{2,1,0:T(8,128)(2,1)}, u32[]{:S(2)}, u32[]{:S(2)}) async-start(bf16[4,96,1536]{2,1,0:T(8,128)(2,1)} %shard_map.253.refs_7_), calls=%async_computation.3 | async-start | bytes 2359296 | tf_op jit(solution)/shard_map/all_to_all | solution.py:697
  266.7 11.0 %shard_map.254 = (bf16[2,4,96,768]{3,2,1,0:T(8,128)(2,1)}, f32[8,576]{1,0:T(8,128)}, bf16[2,512,640]{2,1,0:T(8,128)(2,1)}) custom-call(s32[2]{0:T(128)} %pad_add_fusion.1.refs_0_.here_ref, bf16[2,512,576]{2,1,0:T(8,128)(2,1)} %get-tuple-element.138.refs_1_, bf16[2,3,512,512]{3,2,1,0:T(8,128)(2,1)} %get-tuple-element.139.refs_2_, ...), custom_call_target="tpu_custom_call" | custom-call | flops 3795000064 | bytes 1024 | tf_op jit(solution)/shard_map/pallas_call | solution.py:59
  277.8 2.1 shard_map.256.refs_8_
  280.3 1.5 collective-permute-start.41
  281.9 11.2 %shard_map.257 = (bf16[4,96,768]{2,1,0:T(8,128)(2,1)}, bf16[4,96,768]{2,1,0:T(8,128)(2,1)}, f32[8,576]{1,0:T(8,128)}, bf16[2,512,640]{2,1,0:T(8,128)(2,1)}) custom-call(s32[2]{0:T(128)} %pad_add_fusion.1.refs_0_.here_ref, bf16[2,512,576]{2,1,0:T(8,128)(2,1)} %get-tuple-element.128.refs_1_, bf16[2,3,512,512]{3,2,1,0:T(8,128)(2,1)} %get-tuple-element.129.refs_2_, ...), custom_call_target="tpu_custom_call" | custom-call | flops 3795000064 | bytes 1024 | tf_op jit(solution)/shard_map/pallas_call | solution.py:59
  293.1 1.1 collective-permute-start.40
  294.2 10.2 %shard_map.258 = (bf16[2,128,768]{2,1,0:T(8,128)(2,1)}, bf16[2,128,768]{2,1,0:T(8,128)(2,1)}, bf16[2,128,768]{2,1,0:T(8,128)(2,1)}, bf16[2,128,768]{2,1,0:T(8,128)(2,1)}) custom-call(bf16[1024,640]{1,0:T(8,128)(2,1)} %bitcast.54, bf16[1024,640]{1,0:T(8,128)(2,1)} %bitcast.53, bf16[1024,640]{1,0:T(8,128)(2,1)} %bitcast.52, bf16[1024,640]{1,0:T(8,128)(2,1)} %bitcast.51, ...), custom_call_target="tpu_custom_call" | custom-call | flops 2760000000 | bytes 1024 | tf_op jit(solution)/shard_map/pallas_call | solution.py:59
  304.6 1.0 collective-permute-start.44
  306.4 0.9 collective-permute-start.39
  307.3 1.7 collective-permute-done.40.refs_0_
  310.1 3.1 shard_map.260
  313.1 2.0 collective-permute-start.45
  315.1 2.4 collective-permute-start.46
  317.5 1.5 collective-permute-start.47
  319.0 2.3 convert_reduce_fusion
  321.3 3.7 %collective-permute-done.39.refs_4_ = bf16[2,128,768]{2,1,0:T(8,128)(2,1)} collective-permute-done((bf16[2,128,768]{2,1,0:T(8,128)(2,1)}, bf16[2,128,768]{2,1,0:T(8,128)(2,1)}, u32[]{:S(2)}, u32[]{:S(2)}) %collective-permute-start.39) | collective-permute-done | bytes 393248 | tf_op jit(solution)/shard_map/ppermute | solution.py:694
  325.0 3.3 shard_map.261
  328.3 1.9 slice_bitcast_fusion
  330.2 1.6 shard_map.262
  (214 shorter events, 28.9 us)
Async XLA Ops:
  0.6 13.6 %copy-start = (s32[8,512]{1,0:T(8,128)S(1)}, s32[8,512]{1,0:T(8,128)}, u32[]{:S(2)}) copy-start(s32[8,512]{1,0:T(8,128)} %param.25) | copy-start | bytes 49156
  0.7 9.2 %copy-start.9 = (bf16[128,8,768]{2,1,0:T(8,128)(2,1)S(1)}, bf16[128,8,768]{2,1,0:T(8,128)(2,1)}, u32[]{:S(2)}) copy-start(bf16[128,8,768]{2,1,0:T(8,128)(2,1)} %param.15) | copy-start | bytes 4718596
  2.9 11.3 %copy-start.35 = (s32[8]{0:T(128)S(1)}, s32[8]{0:T(128)}, u32[]{:S(2)}) copy-start(s32[8]{0:T(128)} %param.24) | copy-start | bytes 100
  2.9 12.3 %collective-permute-start.5 = (bf16[96,640]{1,0:T(8,128)(2,1)S(1)}, bf16[96,640]{1,0:T(8,128)(2,1)S(1)}, u32[]{:S(2)}, u32[]{:S(2)}) collective-permute-start(bf16[96,640]{1,0:T(8,128)(2,1)S(1)} %shard_map.223.refs_0_), channel_id=1, source_target_pairs={{24,0},{28,4},{0,8},{4,12},{8,16},{12,20},{16,24},{20,28},{25,1},{... | collective-permute-start | bytes 368648 | tf_op jit(solution)/shard_map/ppermute | solution.py:714
  5.9 10.7 %collective-permute-start.4 = (bf16[96,640]{1,0:T(8,128)(2,1)S(1)}, bf16[96,640]{1,0:T(8,128)(2,1)S(1)}, u32[]{:S(2)}, u32[]{:S(2)}) collective-permute-start(bf16[96,640]{1,0:T(8,128)(2,1)S(1)} %shard_map.223.refs_0_), channel_id=1, source_target_pairs={{16,0},{20,4},{24,8},{28,12},{0,16},{4,20},{8,24},{12,28},{17,1},{... | collective-permute-start | bytes 368648 | tf_op jit(solution)/shard_map/ppermute | solution.py:714
  8.5 8.1 %collective-permute-start.3 = (bf16[96,640]{1,0:T(8,128)(2,1)S(1)}, bf16[96,640]{1,0:T(8,128)(2,1)S(1)}, u32[]{:S(2)}, u32[]{:S(2)}) collective-permute-start(bf16[96,640]{1,0:T(8,128)(2,1)S(1)} %shard_map.223.refs_0_), channel_id=1, source_target_pairs={{8,0},{12,4},{16,8},{20,12},{24,16},{28,20},{0,24},{4,28},{9,1},{1... | collective-permute-start | bytes 368648 | tf_op jit(solution)/shard_map/ppermute | solution.py:714
  12.6 6.5 %copy-start.7 = (bf16[192,96]{1,0:T(8,128)(2,1)S(1)}, bf16[192,96]{1,0:T(8,128)(2,1)}, u32[]{:S(2)}) copy-start(bf16[192,96]{1,0:T(8,128)(2,1)} %refs_1_.1) | copy-start | bytes 110596
  12.6 22.2 %collective-permute-start.1 = (bf16[2,128,768]{2,1,0:T(8,128)(2,1)}, bf16[2,128,768]{2,1,0:T(8,128)(2,1)S(1)}, u32[]{:S(2)}, u32[]{:S(2)}) collective-permute-start(bf16[2,128,768]{2,1,0:T(8,128)(2,1)} %get-tuple-element.101), channel_id=1, source_target_pairs={{0,2},{1,3},{2,0},{3,1},{4,6},{5,7},{6,4},{7,5},{8,10},{9,11},{10,... | collective-permute-start | bytes 1179656 | tf_op jit(solution)/shard_map/ppermute | solution.py:694
  14.2 20.7 %collective-permute-start.2 = (bf16[2,128,768]{2,1,0:T(8,128)(2,1)S(1)}, bf16[2,128,768]{2,1,0:T(8,128)(2,1)S(1)}, u32[]{:S(2)}, u32[]{:S(2)}) collective-permute-start(bf16[2,128,768]{2,1,0:T(8,128)(2,1)S(1)} %get-tuple-element.102), channel_id=1, source_target_pairs={{0,3},{1,2},{2,1},{3,0},{4,7},{5,6},{6,5},{7,4},{8,11},{9,10},{10,... | collective-permute-start | bytes 1179656 | tf_op jit(solution)/shard_map/ppermute | solution.py:694
  15.2 15.5 %copy-start.4 = (bf16[2,512,64]{2,1,0:T(8,128)(2,1)}, bf16[2,512,64]{2,1,0:T(8,128)(2,1)S(1)}, u32[]{:S(2)}) copy-start(bf16[2,512,64]{2,1,0:T(8,128)(2,1)S(1)} %fusion.3.refs_4_.refs_7_) | copy-start | bytes 393220
  15.2 19.7 %collective-permute-start = (bf16[2,128,768]{2,1,0:T(8,128)(2,1)S(1)}, bf16[2,128,768]{2,1,0:T(8,128)(2,1)S(1)}, u32[]{:S(2)}, u32[]{:S(2)}) collective-permute-start(bf16[2,128,768]{2,1,0:T(8,128)(2,1)S(1)} %get-tuple-element.100.refs_4_.refs_3_.refs_1_), channel_id=1, source_target_pairs={{0,1},{1,0},{2,3},{3,2},{4,5},{5,4},{6,7},{7,6},{8,9},{9,8},{10,11... | collective-permute-start | bytes 1179656 | tf_op jit(solution)/shard_map/ppermute | solution.py:694
  17.5 13.3 %collective-permute-start.6 = (bf16[4,96,640]{2,1,0:T(8,128)(2,1)}, bf16[4,96,640]{2,1,0:T(8,128)(2,1)S(1)}, u32[]{:S(2)}, u32[]{:S(2)}) collective-permute-start(bf16[4,96,640]{2,1,0:T(8,128)(2,1)} %shard_map.224.refs_1_), channel_id=1, source_target_pairs={{0,4},{4,0},{8,12},{12,8},{16,20},{20,16},{24,28},{28,24},{1,5},{5... | collective-permute-start | bytes 1474568 | tf_op jit(solution)/shard_map/ppermute | solution.py:694
  20.8 25.0 %all-to-all-start = ((bf16[4,96,1024]{2,1,0:T(8,128)(2,1)}), bf16[4,96,1024]{2,1,0:T(8,128)(2,1)}, u32[]{:S(2)}, u32[]{:S(2)}) async-start(bf16[4,96,1024]{2,1,0:T(8,128)(2,1)} %shard_map.227.refs_8_), calls=%async_computation | async-start | bytes 1572864 | tf_op jit(solution)/shard_map/all_to_all | solution.py:697
  26.3 7.1 %copy-start.8 = (s32[2]{0:T(128)}, s32[2]{0:T(128)S(1)}, u32[]{:S(2)}) copy-start(s32[2]{0:T(128)S(1)} %pad_add_fusion.2.refs_0_) | copy-start | bytes 28
  26.6 9.9 %copy-start.5 = (bf16[2,512,64]{2,1,0:T(8,128)(2,1)}, bf16[2,512,64]{2,1,0:T(8,128)(2,1)S(1)}, u32[]{:S(2)}) copy-start(bf16[2,512,64]{2,1,0:T(8,128)(2,1)S(1)} %select_convert_fusion.refs_3_.refs_6_) | copy-start | bytes 393220
  33.4 29.6 %collective-permute-start.8 = (bf16[768,640]{1,0:T(8,128)(2,1)}, bf16[768,640]{1,0:T(8,128)(2,1)}, u32[]{:S(2)}, u32[]{:S(2)}) collective-permute-start(bf16[768,640]{1,0:T(8,128)(2,1)} %shard_map.225.refs_4_.refs_5_), channel_id=1, source_target_pairs={{0,2},{1,3},{2,0},{3,1},{4,6},{5,7},{6,4},{7,5},{8,10},{9,11},{10,... | collective-permute-start | bytes 2949128 | tf_op jit(solution)/shard_map/ppermute | solution.py:694
  34.9 19.5 %collective-permute-start.7 = (bf16[768,640]{1,0:T(8,128)(2,1)}, bf16[768,640]{1,0:T(8,128)(2,1)}, u32[]{:S(2)}, u32[]{:S(2)}) collective-permute-start(bf16[768,640]{1,0:T(8,128)(2,1)} %shard_map.225.refs_4_.refs_5_), channel_id=1, source_target_pairs={{0,1},{1,0},{2,3},{3,2},{4,5},{5,4},{6,7},{7,6},{8,9},{9,8},{10,11... | collective-permute-start | bytes 2949128 | tf_op jit(solution)/shard_map/ppermute | solution.py:694
  45.8 20.3 %collective-permute-start.9 = (bf16[4,96,1024]{2,1,0:T(8,128)(2,1)}, bf16[4,96,1024]{2,1,0:T(8,128)(2,1)}, u32[]{:S(2)}, u32[]{:S(2)}) collective-permute-start(bf16[4,96,1024]{2,1,0:T(8,128)(2,1)} %shard_map.229.refs_5_.refs_1_.refs_7_.refs_6_), channel_id=1, source_target_pairs={{0,4},{4,0},{8,12},{12,8},{16,20},{20,16},{24,28},{28,24},{1,5},{5... | collective-permute-start | bytes 2359304 | tf_op jit(solution)/shard_map/ppermute | solution.py:694
  49.2 26.1 %collective-permute-start.11 = (bf16[4,96,1024]{2,1,0:T(8,128)(2,1)}, bf16[4,96,1024]{2,1,0:T(8,128)(2,1)}, u32[]{:S(2)}, u32[]{:S(2)}) collective-permute-start(bf16[4,96,1024]{2,1,0:T(8,128)(2,1)} %shard_map.229.refs_5_.refs_1_.refs_7_.refs_6_), channel_id=1, source_target_pairs={{0,2},{1,3},{2,0},{3,1},{4,6},{5,7},{6,4},{7,5},{8,10},{9,11},{10,... | collective-permute-start | bytes 2359304 | tf_op jit(solution)/shard_map/ppermute | solution.py:694
  49.7 25.6 %all-to-all-start.1 = ((bf16[4,96,768]{2,1,0:T(8,128)(2,1)}), bf16[4,96,768]{2,1,0:T(8,128)(2,1)S(1)}, u32[]{:S(2)}, u32[]{:S(2)}) async-start(bf16[4,96,768]{2,1,0:T(8,128)(2,1)} %shard_map.234), calls=%async_computation.1 | async-start | bytes 1179648 | tf_op jit(solution)/shard_map/all_to_all | solution.py:697
  66.1 12.0 %collective-permute-start.10 = (bf16[768,640]{1,0:T(8,128)(2,1)}, bf16[768,640]{1,0:T(8,128)(2,1)}, u32[]{:S(2)}, u32[]{:S(2)}) collective-permute-start(bf16[768,640]{1,0:T(8,128)(2,1)} %get-tuple-element.106.refs_1_.refs_7_), channel_id=1, source_target_pairs={{0,1},{1,0},{2,3},{3,2},{4,5},{5,4},{6,7},{7,6},{8,9},{9,8},{10,11... | collective-permute-start | bytes 2949128 | tf_op jit(solution)/shard_map/ppermute | solution.py:694
  66.1 25.8 %collective-permute-start.14 = (bf16[4,96,1024]{2,1,0:T(8,128)(2,1)}, bf16[4,96,1024]{2,1,0:T(8,128)(2,1)}, u32[]{:S(2)}, u32[]{:S(2)}) collective-permute-start(bf16[4,96,1024]{2,1,0:T(8,128)(2,1)} %get-tuple-element.107.refs_5_.refs_8_.refs_7_), channel_id=1, source_target_pairs={{0,2},{1,3},{2,0},{3,1},{4,6},{5,7},{6,4},{7,5},{8,10},{9,11},{10,... | collective-permute-start | bytes 2359304 | tf_op jit(solution)/shard_map/ppermute | solution.py:694
  76.1 15.8 %collective-permute-start.15 = (bf16[4,96,768]{2,1,0:T(8,128)(2,1)}, bf16[4,96,768]{2,1,0:T(8,128)(2,1)}, u32[]{:S(2)}, u32[]{:S(2)}) collective-permute-start(bf16[4,96,768]{2,1,0:T(8,128)(2,1)} %get-tuple-element.109.refs_5_.refs_0_), channel_id=1, source_target_pairs={{0,4},{4,0},{8,12},{12,8},{16,20},{20,16},{24,28},{28,24},{1,5},{5... | collective-permute-start | bytes 1769480 | tf_op jit(solution)/shard_map/ppermute | solution.py:694
  77.6 16.4 %collective-permute-start.12 = (bf16[4,96,1024]{2,1,0:T(8,128)(2,1)}, bf16[4,96,1024]{2,1,0:T(8,128)(2,1)}, u32[]{:S(2)}, u32[]{:S(2)}) collective-permute-start(bf16[4,96,1024]{2,1,0:T(8,128)(2,1)} %shard_map.229.refs_5_.refs_1_.refs_7_.refs_6_), channel_id=1, source_target_pairs={{0,1},{1,0},{2,3},{3,2},{4,5},{5,4},{6,7},{7,6},{8,9},{9,8},{10,11... | collective-permute-start | bytes 2359304 | tf_op jit(solution)/shard_map/ppermute | solution.py:694
  77.6 16.6 %collective-permute-start.13 = (bf16[4,96,1024]{2,1,0:T(8,128)(2,1)}, bf16[4,96,1024]{2,1,0:T(8,128)(2,1)}, u32[]{:S(2)}, u32[]{:S(2)}) collective-permute-start(bf16[4,96,1024]{2,1,0:T(8,128)(2,1)} %get-tuple-element.107.refs_5_.refs_8_.refs_7_), channel_id=1, source_target_pairs={{0,1},{1,0},{2,3},{3,2},{4,5},{5,4},{6,7},{7,6},{8,9},{9,8},{10,11... | collective-permute-start | bytes 2359304 | tf_op jit(solution)/shard_map/ppermute | solution.py:694
  78.1 16.6 %collective-permute-start.16 = (bf16[4,96,1024]{2,1,0:T(8,128)(2,1)}, bf16[4,96,1024]{2,1,0:T(8,128)(2,1)}, u32[]{:S(2)}, u32[]{:S(2)}) collective-permute-start(bf16[4,96,1024]{2,1,0:T(8,128)(2,1)} %get-tuple-element.110.refs_6_.refs_11_.refs_10_), channel_id=1, source_target_pairs={{0,1},{1,0},{2,3},{3,2},{4,5},{5,4},{6,7},{7,6},{8,9},{9,8},{10,11... | collective-permute-start | bytes 2359304 | tf_op jit(solution)/shard_map/ppermute | solution.py:694
  91.9 2.9 collective-permute-start.17
  92.5 24.4 %collective-permute-start.20 = (bf16[4,96,768]{2,1,0:T(8,128)(2,1)S(1)}, bf16[4,96,768]{2,1,0:T(8,128)(2,1)}, u32[]{:S(2)}, u32[]{:S(2)}) collective-permute-start(bf16[4,96,768]{2,1,0:T(8,128)(2,1)S(1)} %copy-done.13), channel_id=1, source_target_pairs={{0,2},{1,3},{2,0},{3,1},{4,6},{5,7},{6,4},{7,5},{8,10},{9,11},{10,... | collective-permute-start | bytes 1769480 | tf_op jit(solution)/shard_map/ppermute | solution.py:694
  94.0 28.9 %collective-permute-start.18 = (bf16[4,96,768]{2,1,0:T(8,128)(2,1)S(1)}, bf16[4,96,768]{2,1,0:T(8,128)(2,1)}, u32[]{:S(2)}, u32[]{:S(2)}) collective-permute-start(bf16[4,96,768]{2,1,0:T(8,128)(2,1)S(1)} %copy-done.13), channel_id=1, source_target_pairs={{0,1},{1,0},{2,3},{3,2},{4,5},{5,4},{6,7},{7,6},{8,9},{9,8},{10,11... | collective-permute-start | bytes 1769480 | tf_op jit(solution)/shard_map/ppermute | solution.py:694
  94.3 26.7 %collective-permute-start.21 = (bf16[4,96,768]{2,1,0:T(8,128)(2,1)}, bf16[4,96,768]{2,1,0:T(8,128)(2,1)}, u32[]{:S(2)}, u32[]{:S(2)}) collective-permute-start(bf16[4,96,768]{2,1,0:T(8,128)(2,1)} %get-tuple-element.113.refs_15_.refs_1_), channel_id=1, source_target_pairs={{0,2},{1,3},{2,0},{3,1},{4,6},{5,7},{6,4},{7,5},{8,10},{9,11},{10,... | collective-permute-start | bytes 1769480 | tf_op jit(solution)/shard_map/ppermute | solution.py:694
  94.8 28.2 %collective-permute-start.19 = (bf16[4,96,768]{2,1,0:T(8,128)(2,1)}, bf16[4,96,768]{2,1,0:T(8,128)(2,1)}, u32[]{:S(2)}, u32[]{:S(2)}) collective-permute-start(bf16[4,96,768]{2,1,0:T(8,128)(2,1)} %get-tuple-element.113.refs_15_.refs_1_), channel_id=1, source_target_pairs={{0,1},{1,0},{2,3},{3,2},{4,5},{5,4},{6,7},{7,6},{8,9},{9,8},{10,11... | collective-permute-start | bytes 1769480 | tf_op jit(solution)/shard_map/ppermute | solution.py:694
  121.0 2.2 collective-permute-start.22
  121.0 3.1 collective-permute-start.23
  124.9 21.4 %copy-start.24 = (f32[128]{0:T(128)S(1)}, f32[128]{0:T(128)}, u32[]{:S(2)}) copy-start(f32[128]{0:T(128)} %param.27) | copy-start | bytes 1540
  124.9 21.6 %copy-start.21 = (s32[256]{0:T(256)S(1)}, s32[256]{0:T(256)}, u32[]{:S(2)}) copy-start(s32[256]{0:T(256)} %param.26) | copy-start | bytes 3076
  140.3 19.1 %all-to-all-start.2 = ((bf16[32,8,768]{2,1,0:T(8,128)(2,1)}), bf16[32,8,768]{2,1,0:T(8,128)(2,1)S(1)}, u32[]{:S(2)}, u32[]{:S(2)}) async-start(bf16[32,8,768]{2,1,0:T(8,128)(2,1)} %get-tuple-element.123), calls=%async_computation.2 | async-start | bytes 786432 | tf_op jit(solution)/shard_map/all_to_all | solution.py:986
  149.2 31.5 %collective-permute-start.24 = (bf16[2,128,768]{2,1,0:T(8,128)(2,1)}, bf16[2,128,768]{2,1,0:T(8,128)(2,1)S(1)}, u32[]{:S(2)}, u32[]{:S(2)}) collective-permute-start(bf16[2,128,768]{2,1,0:T(8,128)(2,1)} %get-tuple-element.120), channel_id=1, source_target_pairs={{0,1},{1,0},{2,3},{3,2},{4,5},{5,4},{6,7},{7,6},{8,9},{9,8},{10,11... | collective-permute-start | bytes 1179656 | tf_op jit(solution)/shard_map/ppermute | solution.py:694
  149.5 31.2 %collective-permute-start.25 = (bf16[2,128,768]{2,1,0:T(8,128)(2,1)}, bf16[2,128,768]{2,1,0:T(8,128)(2,1)}, u32[]{:S(2)}, u32[]{:S(2)}) collective-permute-start(bf16[2,128,768]{2,1,0:T(8,128)(2,1)} %get-tuple-element.121), channel_id=1, source_target_pairs={{0,2},{1,3},{2,0},{3,1},{4,6},{5,7},{6,4},{7,5},{8,10},{9,11},{10,... | collective-permute-start | bytes 1179656 | tf_op jit(solution)/shard_map/ppermute | solution.py:694
  151.2 29.5 %collective-permute-start.26 = (bf16[2,128,768]{2,1,0:T(8,128)(2,1)}, bf16[2,128,768]{2,1,0:T(8,128)(2,1)}, u32[]{:S(2)}, u32[]{:S(2)}) collective-permute-start(bf16[2,128,768]{2,1,0:T(8,128)(2,1)} %get-tuple-element.122), channel_id=1, source_target_pairs={{0,3},{1,2},{2,1},{3,0},{4,7},{5,6},{6,5},{7,4},{8,11},{9,10},{10,... | collective-permute-start | bytes 1179656 | tf_op jit(solution)/shard_map/ppermute | solution.py:694
  180.6 11.2 %collective-permute-start.28 = (bf16[2,2,4,96,768]{4,3,2,1,0:T(8,128)(2,1)}, bf16[2,2,4,96,768]{4,3,2,1,0:T(8,128)(2,1)}, u32[]{:S(2)}, u32[]{:S(2)}) collective-permute-start(bf16[2,2,4,96,768]{4,3,2,1,0:T(8,128)(2,1)} %get-tuple-element.127.refs_5_.refs_3_), channel_id=1, source_target_pairs={{0,1},{1,0},{2,3},{3,2},{4,5},{5,4},{6,7},{7,6},{8,9},{9,8},{10,11... | collective-permute-start | bytes 7077896 | tf_op jit(solution)/shard_map/ppermute | solution.py:694
  191.3 7.4 %collective-permute-start.27 = (bf16[2,2,4,96,768]{4,3,2,1,0:T(8,128)(2,1)}, bf16[2,2,4,96,768]{4,3,2,1,0:T(8,128)(2,1)}, u32[]{:S(2)}, u32[]{:S(2)}) collective-permute-start(bf16[2,2,4,96,768]{4,3,2,1,0:T(8,128)(2,1)} %shard_map.243.refs_4_), channel_id=1, source_target_pairs={{0,1},{1,0},{2,3},{3,2},{4,5},{5,4},{6,7},{7,6},{8,9},{9,8},{10,11... | collective-permute-start | bytes 7077896 | tf_op jit(solution)/shard_map/ppermute | solution.py:694
  206.8 31.1 %collective-permute-start.30 = (bf16[2,4,96,768]{3,2,1,0:T(8,128)(2,1)}, bf16[2,4,96,768]{3,2,1,0:T(8,128)(2,1)}, u32[]{:S(2)}, u32[]{:S(2)}) collective-permute-start(bf16[2,4,96,768]{3,2,1,0:T(8,128)(2,1)} %get-tuple-element.135.refs_14_.refs_7_), channel_id=1, source_target_pairs={{0,2},{1,3},{2,0},{3,1},{4,6},{5,7},{6,4},{7,5},{8,10},{9,11},{10,... | collective-permute-start | bytes 3538952 | tf_op jit(solution)/shard_map/ppermute | solution.py:694
  207.3 30.6 %collective-permute-start.29 = (bf16[2,4,96,768]{3,2,1,0:T(8,128)(2,1)}, bf16[2,4,96,768]{3,2,1,0:T(8,128)(2,1)}, u32[]{:S(2)}, u32[]{:S(2)}) collective-permute-start(bf16[2,4,96,768]{3,2,1,0:T(8,128)(2,1)} %get-tuple-element.134.refs_4_), channel_id=1, source_target_pairs={{0,4},{4,0},{8,12},{12,8},{16,20},{20,16},{24,28},{28,24},{1,5},{5... | collective-permute-start | bytes 3538952 | tf_op jit(solution)/shard_map/ppermute | solution.py:694
  237.8 4.7 %collective-permute-start.33 = (bf16[2,4,96,768]{3,2,1,0:T(8,128)(2,1)}, bf16[2,4,96,768]{3,2,1,0:T(8,128)(2,1)}, u32[]{:S(2)}, u32[]{:S(2)}) collective-permute-start(bf16[2,4,96,768]{3,2,1,0:T(8,128)(2,1)} %get-tuple-element.143.refs_2_), channel_id=1, source_target_pairs={{0,1},{1,0},{2,3},{3,2},{4,5},{5,4},{6,7},{7,6},{8,9},{9,8},{10,11... | collective-permute-start | bytes 3538952 | tf_op jit(solution)/shard_map/ppermute | solution.py:694
  240.4 17.9 %collective-permute-start.31 = (bf16[4,96,768]{2,1,0:T(8,128)(2,1)}, bf16[4,96,768]{2,1,0:T(8,128)(2,1)S(1)}, u32[]{:S(2)}, u32[]{:S(2)}) collective-permute-start(bf16[4,96,768]{2,1,0:T(8,128)(2,1)} %get-tuple-element.147.refs_8_), channel_id=1, source_target_pairs={{0,2},{1,3},{2,0},{3,1},{4,6},{5,7},{6,4},{7,5},{8,10},{9,11},{10,... | collective-permute-start | bytes 1769480 | tf_op jit(solution)/shard_map/ppermute | solution.py:694
  241.5 16.9 %collective-permute-start.32 = (bf16[4,96,768]{2,1,0:T(8,128)(2,1)}, bf16[4,96,768]{2,1,0:T(8,128)(2,1)}, u32[]{:S(2)}, u32[]{:S(2)}) collective-permute-start(bf16[4,96,768]{2,1,0:T(8,128)(2,1)} %get-tuple-element.148.refs_9_), channel_id=1, source_target_pairs={{0,4},{4,0},{8,12},{12,8},{16,20},{20,16},{24,28},{28,24},{1,5},{5... | collective-permute-start | bytes 1769480 | tf_op jit(solution)/shard_map/ppermute | solution.py:694
  255.4 1.5 collective-permute-start.34
  255.4 22.4 %collective-permute-start.36 = (bf16[4,96,768]{2,1,0:T(8,128)(2,1)}, bf16[4,96,768]{2,1,0:T(8,128)(2,1)}, u32[]{:S(2)}, u32[]{:S(2)}) collective-permute-start(bf16[4,96,768]{2,1,0:T(8,128)(2,1)} %get-tuple-element.162), channel_id=1, source_target_pairs={{0,4},{4,0},{8,12},{12,8},{16,20},{20,16},{24,28},{28,24},{1,5},{5... | collective-permute-start | bytes 1769480 | tf_op jit(solution)/shard_map/ppermute | solution.py:694
  257.8 46.7 %collective-permute-start.42 = (f32[16,768]{1,0:T(8,128)S(1)}, f32[16,768]{1,0:T(8,128)S(1)}, u32[]{:S(2)}, u32[]{:S(2)}) collective-permute-start(f32[16,768]{1,0:T(8,128)S(1)} %pad_maximum_fusion), channel_id=1, source_target_pairs={{0,2},{1,3},{2,0},{3,1},{4,6},{5,7},{6,4},{7,5},{8,10},{9,11},{10,... | collective-permute-start | bytes 147464 | tf_op jit(solution)/shard_map/ppermute | solution.py:694
  262.2 45.1 %all-to-all-start.3 = ((bf16[4,96,1536]{2,1,0:T(8,128)(2,1)}), bf16[4,96,1536]{2,1,0:T(8,128)(2,1)}, u32[]{:S(2)}, u32[]{:S(2)}) async-start(bf16[4,96,1536]{2,1,0:T(8,128)(2,1)} %shard_map.253.refs_7_), calls=%async_computation.3 | async-start | bytes 2359296 | tf_op jit(solution)/shard_map/all_to_all | solution.py:697
  277.7 4.2 %collective-permute-start.35 = (bf16[2,4,96,768]{3,2,1,0:T(8,128)(2,1)}, bf16[2,4,96,768]{3,2,1,0:T(8,128)(2,1)}, u32[]{:S(2)}, u32[]{:S(2)}) collective-permute-start(bf16[2,4,96,768]{3,2,1,0:T(8,128)(2,1)} %get-tuple-element.161.refs_1_), channel_id=1, source_target_pairs={{0,1},{1,0},{2,3},{3,2},{4,5},{5,4},{6,7},{7,6},{8,9},{9,8},{10,11... | collective-permute-start | bytes 3538952 | tf_op jit(solution)/shard_map/ppermute | solution.py:694
  279.9 24.6 %collective-permute-start.43 = (f32[8,576]{1,0:T(8,128)S(1)}, f32[8,576]{1,0:T(8,128)S(1)}, u32[]{:S(2)}, u32[]{:S(2)}) collective-permute-start(f32[8,576]{1,0:T(8,128)S(1)} %copy-done.34), channel_id=1, source_target_pairs={{0,1},{1,0},{2,3},{3,2},{4,5},{5,4},{6,7},{7,6},{8,9},{9,8},{10,11... | collective-permute-start | bytes 55304 | tf_op jit(solution)/shard_map/ppermute | solution.py:694
  280.3 26.0 %collective-permute-start.41 = (bf16[4,96,768]{2,1,0:T(8,128)(2,1)}, bf16[4,96,768]{2,1,0:T(8,128)(2,1)}, u32[]{:S(2)}, u32[]{:S(2)}) collective-permute-start(bf16[4,96,768]{2,1,0:T(8,128)(2,1)} %shard_map.256.refs_8_), channel_id=1, source_target_pairs={{0,2},{1,3},{2,0},{3,1},{4,6},{5,7},{6,4},{7,5},{8,10},{9,11},{10,... | collective-permute-start | bytes 1769480 | tf_op jit(solution)/shard_map/ppermute | solution.py:694
  293.1 15.9 %collective-permute-start.40 = (bf16[4,96,768]{2,1,0:T(8,128)(2,1)}, bf16[4,96,768]{2,1,0:T(8,128)(2,1)}, u32[]{:S(2)}, u32[]{:S(2)}) collective-permute-start(bf16[4,96,768]{2,1,0:T(8,128)(2,1)} %get-tuple-element.172), channel_id=1, source_target_pairs={{0,4},{4,0},{8,12},{12,8},{16,20},{20,16},{24,28},{28,24},{1,5},{5... | collective-permute-start | bytes 1769480 | tf_op jit(solution)/shard_map/ppermute | solution.py:694
  294.2 10.3 %copy-start.20 = (f32[8,576]{1,0:T(8,128)S(1)}, f32[8,576]{1,0:T(8,128)}, u32[]{:S(2)}) copy-start(f32[8,576]{1,0:T(8,128)} %get-tuple-element.175) | copy-start | bytes 55300
  294.2 10.4 %copy-start.15 = (f32[24,768]{1,0:T(8,128)S(1)}, f32[24,768]{1,0:T(8,128)}, u32[]{:S(2)}) copy-start(f32[24,768]{1,0:T(8,128)} %copy-done.14) | copy-start | bytes 221188
  304.4 5.0 %collective-permute-start.37 = (bf16[2,128,768]{2,1,0:T(8,128)(2,1)}, bf16[2,128,768]{2,1,0:T(8,128)(2,1)}, u32[]{:S(2)}, u32[]{:S(2)}) collective-permute-start(bf16[2,128,768]{2,1,0:T(8,128)(2,1)} %get-tuple-element.169), channel_id=1, source_target_pairs={{0,1},{1,0},{2,3},{3,2},{4,5},{5,4},{6,7},{7,6},{8,9},{9,8},{10,11... | collective-permute-start | bytes 1179656 | tf_op jit(solution)/shard_map/ppermute | solution.py:694
  304.6 4.8 %collective-permute-start.44 = (f32[16,768]{1,0:T(8,128)S(1)}, f32[16,768]{1,0:T(8,128)S(1)}, u32[]{:S(2)}, u32[]{:S(2)}) collective-permute-start(f32[16,768]{1,0:T(8,128)S(1)} %fusion.4.refs_4_), channel_id=1, source_target_pairs={{0,4},{4,0},{8,12},{12,8},{16,20},{20,16},{24,28},{28,24},{1,5},{5... | collective-permute-start | bytes 147464 | tf_op jit(solution)/shard_map/ppermute | solution.py:694
  305.7 15.5 %collective-permute-start.38 = (bf16[2,128,768]{2,1,0:T(8,128)(2,1)}, bf16[2,128,768]{2,1,0:T(8,128)(2,1)S(1)}, u32[]{:S(2)}, u32[]{:S(2)}) collective-permute-start(bf16[2,128,768]{2,1,0:T(8,128)(2,1)} %get-tuple-element.170), channel_id=1, source_target_pairs={{0,2},{1,3},{2,0},{3,1},{4,6},{5,7},{6,4},{7,5},{8,10},{9,11},{10,... | collective-permute-start | bytes 1179656 | tf_op jit(solution)/shard_map/ppermute | solution.py:694
  306.4 18.6 %collective-permute-start.39 = (bf16[2,128,768]{2,1,0:T(8,128)(2,1)}, bf16[2,128,768]{2,1,0:T(8,128)(2,1)}, u32[]{:S(2)}, u32[]{:S(2)}) collective-permute-start(bf16[2,128,768]{2,1,0:T(8,128)(2,1)} %get-tuple-element.171), channel_id=1, source_target_pairs={{0,3},{1,2},{2,1},{3,0},{4,7},{5,6},{6,5},{7,4},{8,11},{9,10},{10,... | collective-permute-start | bytes 1179656 | tf_op jit(solution)/shard_map/ppermute | solution.py:694
  313.1 17.0 %collective-permute-start.45 = (bf16[112,768]{1,0:T(8,128)(2,1)}, bf16[112,768]{1,0:T(8,128)(2,1)S(1)}, u32[]{:S(2)}, u32[]{:S(2)}) collective-permute-start(bf16[112,768]{1,0:T(8,128)(2,1)} %get-tuple-element.178), channel_id=1, source_target_pairs={{24,0},{28,4},{0,8},{4,12},{8,16},{12,20},{16,24},{20,28},{25,1},{... | collective-permute-start | bytes 516104 | tf_op jit(solution)/shard_map/ppermute | solution.py:714
  315.1 15.0 %collective-permute-start.46 = (bf16[112,768]{1,0:T(8,128)(2,1)}, bf16[112,768]{1,0:T(8,128)(2,1)S(1)}, u32[]{:S(2)}, u32[]{:S(2)}) collective-permute-start(bf16[112,768]{1,0:T(8,128)(2,1)} %get-tuple-element.179), channel_id=1, source_target_pairs={{16,0},{20,4},{24,8},{28,12},{0,16},{4,20},{8,24},{12,28},{17,1},{... | collective-permute-start | bytes 516104 | tf_op jit(solution)/shard_map/ppermute | solution.py:714
  317.5 12.7 %collective-permute-start.47 = (bf16[112,768]{1,0:T(8,128)(2,1)}, bf16[112,768]{1,0:T(8,128)(2,1)S(1)}, u32[]{:S(2)}, u32[]{:S(2)}) collective-permute-start(bf16[112,768]{1,0:T(8,128)(2,1)} %get-tuple-element.180), channel_id=1, source_target_pairs={{8,0},{12,4},{16,8},{20,12},{24,16},{28,20},{0,24},{4,28},{9,1},{1... | collective-permute-start | bytes 516104 | tf_op jit(solution)/shard_map/ppermute | solution.py:714
  325.0 8.9 %copy-start.1 = (s32[8,512]{1,0:T(8,128)S(1)}, s32[8,512]{1,0:T(8,128)}, u32[]{:S(2)}) copy-start(s32[8,512]{1,0:T(8,128)} %param.25) | copy-start | bytes 49156
  (24 other events, 54.2 us)

commit v4 on v3

--- a/solution.py
+++ b/solution.py
@@ -18,7 +18,7 @@
 BF = jnp.bfloat16
 F32 = jnp.float32
 MIB = 1024 * 1024
-SHARE = 0.3
+SHARE = 0.2
 
 
 def dot(a, b, ca, cb):
@@ -839,6 +839,9 @@
             [(w_qkv.reshape(rb, 3 * local), None, None), (qv_col, None, None)],
             [((rb, wide), BF, None, None)],
         )
+        extra = jnp.concatenate([ln_gains.T, shifts.T, b_up.reshape(-1, 1), jnp.zeros((rb, 57), BF)], axis=1)
+        second_piece = pack(pack_two_kernel, [w_up, w_out, extra], hidden + 256, [])
+        third_piece = pack(pack_three_kernel, [w_down], hidden, [])
         if nh <= 4:
             pieces1 = [first_piece] + [turn(first_piece, k) for k in range(1, nh)]
             own1 = call(
@@ -846,19 +849,16 @@
                 (1,),
                 [(p, None, None) for p in pieces1],
                 [((nh, rb, wide), BF, None, None)],
-                after=[dealt[1]],
+                after=[dealt[1], second_piece, third_piece],
             )[0]
         else:
             own1 = along(jnp.broadcast_to(first_piece[None], (nh, rb, wide)))
         lo1 = across(own1, "dp", 1)
-        w1 = {0: merged(own1, lo1, here_first, [key_features, query_features])}
+        w1 = {0: merged(own1, lo1, here_first, [key_features, query_features, third_piece, inv_count, sent_code])}
         w1[1] = swap(w1[0])
         w1[2] = across(w1[0], "tensor", 2)
-        extra = jnp.concatenate([ln_gains.T, shifts.T, b_up.reshape(-1, 1), jnp.zeros((rb, 57), BF)], axis=1)
-        second_piece = pack(pack_two_kernel, [w_up, w_out, extra], hidden + 256, [dealt[1]])
         (second_piece,) = gate([second_piece], [own1])
         own2 = along(second_piece)
-        third_piece = pack(pack_three_kernel, [w_down], hidden, [dealt[1]])
 
         k = np.arange(width)
         dd, within = k // rb, k % rb

time: 340 us -> 338 us (level)
  waiting for transfers between devices: 32.8 us -> 39 us
  starting transfers between devices: 59.9 us -> 56 us
    ppermute x42, waiting for transfers between devices: 23.9 us -> 30.4 us  [across(): return lax.ppermute(array, axis, [(i, i ^ bit) for i in range(size)])]
    unnamed x85 -> x81, local copies, waits for them, and re-layouts: 13.2 us -> 12.3 us
  transfers between devices with their start and end apart: 52 -> 52, of which waited for: 12 -> 14; matrix products, arithmetic and copies ran while one was open for 4% -> 3% of each run, Pallas kernels for 57% -> 56%
where the time goes in v4:
time: 338 us; the launch traced here: 332 us
  Pallas kernels  213 us (63%)
  starting transfers between devices  56 us (17%)
  waiting for transfers between devices  39 us (12%)
  local copies, waits for them, and re-layouts  16.7 us (5%)
  other arithmetic  5.9 us (2%)
    pallas_call x30, Pallas kernels, call(): pl.pallas_call(body, grid_spec=pltpu.PrefetchScalarGridSpec(num_scalar_pr...  213 us
    ppermute x42, waiting for transfers between devices, across(): return lax.ppermute(array, axis, [(i, i ^ bit) for i in range(size)])  30.4 us
    ppermute x42, starting transfers between devices, across(): return lax.ppermute(array, axis, [(i, i ^ bit) for i in range(size)])  27.6 us
    ppermute x6, starting transfers between devices, turn(): lax.ppermute(array, 'dp', [(2 * ((z + k) % nh) + b, 2 * z + b) for z in r...  12.8 us
    all_to_all x3, starting transfers between devices, along(): lax.all_to_all(array, 'dp', 0, 0, tiled=True, axis_index_groups=groups)  12.6 us
    unnamed x81, local copies, waits for them, and re-layouts  12.3 us
    all_to_all x1, waiting for transfers between devices, shards(): lax.all_to_all(pooled, ('dp', 'tensor'), 0, 0, tiled=True)  8.17 us
  transfers between devices with their start and end apart: 52, of which 14 were waited for; matrix products, arithmetic and copies ran while one was open for 3% of the time, Pallas kernels for 56%

profile of v4, /device:TPU:0, one launch (start us, length us, event | category | flops | bytes accessed | tf_op | source)
XLA Modules:
  0.0 331.9 jit_solution(1390028262673047639)
XLA Ops:
  1.4 1.1 copy.77
  2.8 3.0 collective-permute-start.5
  5.8 2.6 collective-permute-start.4
  8.4 1.3 collective-permute-start.3
  9.8 1.4 copy-done.13
  11.2 1.3 shard_map.222
  13.3 1.5 collective-permute-start.1
  20.6 1.5 collective-permute-start.6
  22.1 4.2 %all-to-all-start = ((bf16[4,96,1024]{2,1,0:T(8,128)(2,1)}), bf16[4,96,1024]{2,1,0:T(8,128)(2,1)}, u32[]{:S(2)}, u32[]{:S(2)}) async-start(bf16[4,96,1024]{2,1,0:T(8,128)(2,1)} %shard_map.228.refs_8_), calls=%async_computation | async-start | bytes 1572864 | tf_op jit(solution)/shard_map/all_to_all | solution.py:697
  26.8 7.5 %collective-permute-done.6.refs_2_ = bf16[4,96,640]{2,1,0:T(8,128)(2,1)S(1)} collective-permute-done((bf16[4,96,640]{2,1,0:T(8,128)(2,1)S(1)}, bf16[4,96,640]{2,1,0:T(8,128)(2,1)S(1)}, u32[]{:S(2)}, u32[]{:S(2)}) %collective-permute-start.6) | collective-permute-done | bytes 491552 | tf_op jit(solution)/shard_map/ppermute | solution.py:694
  34.3 1.6 shard_map.227.refs_4_.refs_5_
  36.0 1.6 collective-permute-start.8
  37.6 9.3 %shard_map.229 = (bf16[2,512,576]{2,1,0:T(8,128)(2,1)}, bf16[2,3,512,512]{3,2,1,0:T(8,128)(2,1)}, bf16[2,512,256]{2,1,0:T(8,128)(2,1)}, bf16[2,512,768]{2,1,0:T(8,128)(2,1)}) custom-call(bf16[2,128,768]{2,1,0:T(8,128)(2,1)} %copy-done.14, bf16[2,128,768]{2,1,0:T(8,128)(2,1)} %collective-permute-done.refs_1_, ...), custom_call_target="tpu_custom_call" | custom-call | flops 5750000128 | bytes 1024 | tf_op jit(solution)/shard_map/pallas_call | solution.py:59
  47.2 1.2 collective-permute-start.9
  48.4 3.9 %all-to-all-start.1 = ((bf16[4,96,768]{2,1,0:T(8,128)(2,1)}), bf16[4,96,768]{2,1,0:T(8,128)(2,1)S(1)}, u32[]{:S(2)}, u32[]{:S(2)}) async-start(bf16[4,96,768]{2,1,0:T(8,128)(2,1)} %shard_map.234), calls=%async_computation.1 | async-start | bytes 1179648 | tf_op jit(solution)/shard_map/all_to_all | solution.py:697
  53.3 8.6 %shard_map.231 = (bf16[2,512,576]{2,1,0:T(8,128)(2,1)}, bf16[2,3,512,512]{3,2,1,0:T(8,128)(2,1)}, bf16[2,512,256]{2,1,0:T(8,128)(2,1)}) custom-call(bf16[2,512,768]{2,1,0:T(8,128)(2,1)} %get-tuple-element.104.refs_0_.refs_5_, bf16[768,640]{1,0:T(8,128)(2,1)} %collective-permute-done.7.refs_1_.refs_6_, bf16[768,384]{1,0:T(8,128)(2,1)} %constant.75.clone.refs_5_.refs_2_, ...), custom_call_target="tpu_custom_call" | custom-call | flops 2070000000 | bytes 1024 | tf_op jit(solution)/shard_map/pallas_call | solution.py:59
  61.9 5.3 %collective-permute-done.9.refs_1_ = bf16[4,96,1024]{2,1,0:T(8,128)(2,1)} collective-permute-done((bf16[4,96,1024]{2,1,0:T(8,128)(2,1)}, bf16[4,96,1024]{2,1,0:T(8,128)(2,1)}, u32[]{:S(2)}, u32[]{:S(2)}) %collective-permute-start.9) | collective-permute-done | bytes 786464 | tf_op jit(solution)/shard_map/ppermute | solution.py:694
  67.2 1.0 collective-permute-start.14
  68.2 8.6 %shard_map.233 = (bf16[2,512,576]{2,1,0:T(8,128)(2,1)}, bf16[2,3,512,512]{3,2,1,0:T(8,128)(2,1)}, bf16[2,512,256]{2,1,0:T(8,128)(2,1)}) custom-call(bf16[2,512,768]{2,1,0:T(8,128)(2,1)} %get-tuple-element.104.refs_0_.refs_5_, bf16[768,640]{1,0:T(8,128)(2,1)} %get-tuple-element.106.refs_1_.refs_7_, bf16[768,384]{1,0:T(8,128)(2,1)} %constant.75.clone.refs_5_.refs_2_, ...), custom_call_target="tpu_custom_call" | custom-call | flops 2070000000 | bytes 1024 | tf_op jit(solution)/shard_map/pallas_call | solution.py:59
  76.8 1.0 collective-permute-done.11.refs_1_
  78.7 1.5 collective-permute-start.15
  80.7 8.6 %shard_map.236 = (bf16[2,512,576]{2,1,0:T(8,128)(2,1)}, bf16[2,3,512,512]{3,2,1,0:T(8,128)(2,1)}, bf16[2,512,256]{2,1,0:T(8,128)(2,1)}) custom-call(bf16[2,512,768]{2,1,0:T(8,128)(2,1)} %get-tuple-element.104.refs_0_.refs_5_, bf16[768,640]{1,0:T(8,128)(2,1)} %collective-permute-done.10.refs_1_.refs_8_, bf16[768,384]{1,0:T(8,128)(2,1)} %constant.75.clone.refs_5_.refs_2_, ...), custom_call_target="tpu_custom_call" | custom-call | flops 2070000000 | bytes 1024 | tf_op jit(solution)/shard_map/pallas_call | solution.py:59
  89.3 4.1 %collective-permute-done.15.refs_1_ = bf16[4,96,768]{2,1,0:T(8,128)(2,1)} collective-permute-done((bf16[4,96,768]{2,1,0:T(8,128)(2,1)}, bf16[4,96,768]{2,1,0:T(8,128)(2,1)}, u32[]{:S(2)}, u32[]{:S(2)}) %collective-permute-start.15) | collective-permute-done | bytes 589856 | tf_op jit(solution)/shard_map/ppermute | solution.py:694
  93.7 1.6 collective-permute-start.20
  96.8 22.1 %shard_map.238 = (bf16[1024,768]{1,0:T(8,128)(2,1)}, f32[1024,1]{1,0:T(8,128)}, bf16[1024,768]{1,0:T(8,128)(2,1)}, bf16[1024,3072]{1,0:T(8,128)(2,1)}, bf16[1024,3072]{1,0:T(8,128)(2,1)}, /*index=5*/f32[8,768]{1,0:T(8,128)}) custom-call(s32[2]{0:T(128)} %pad_add_fusion.1.refs_0_.here_ref, bf16[1024,256]{1,0:T(8,128)(2,1)} %bitcast.56, ...), custom_call_target="tpu_custom_call" | custom-call | flops 4600000000 | bytes 1024 | tf_op jit(solution)/shard_map/pallas_call | solution.py:59
  118.9 3.2 collective-permute-done.21.refs_1_
  122.7 1.8 collective-permute-done.22.refs_6_
  125.3 15.4 %shard_map.240 = (bf16[1024,768]{1,0:T(8,128)(2,1)}, f32[1024,1]{1,0:T(8,128)}, bf16[2,128,768]{2,1,0:T(8,128)(2,1)}, bf16[2,128,768]{2,1,0:T(8,128)(2,1)}, bf16...) custom-call(s32[2]{0:T(128)} %pad_add_fusion.1.refs_0_.here_ref, ...), custom_call_target="tpu_custom_call" | custom-call | flops 3220000000 | bytes 1024 | tf_op jit(solution)/shard_map/pallas_call | solution.py:59
  140.8 3.1 all-to-all-start.2
  147.2 1.7 collective-permute-start.25
  148.9 8.2 %all-to-all-done.2 = bf16[32,8,768]{2,1,0:T(8,128)(2,1)S(1)} async-done(((bf16[32,8,768]{2,1,0:T(8,128)(2,1)}), bf16[32,8,768]{2,1,0:T(8,128)(2,1)S(1)}, u32[]{:S(2)}, u32[]{:S(2)}) %all-to-all-start.2) | async-done | bytes 393248 | tf_op jit(solution)/shard_map/all_to_all | solution.py:986
  157.8 20.5 %shard_map.241 = (bf16[1024,768]{1,0:T(8,128)(2,1)}, bf16[1024,3072]{1,0:T(8,128)(2,1)}, bf16[2,2,4,96,768]{4,3,2,1,0:T(8,128)(2,1)}, f32[8,768]{1,0:T(8,128)}, f32[8,3072]{1,0:T(8,128)}) custom-call(s32[2]{0:T(128)} %pad_add_fusion.1.refs_0_.here_ref, bf16[256,768]{1,0:T(8,128)(2,1)} %bitcast.65, s32[8,1]{1,0:T(8,128)} %iota_add_fusion.ids_ref, ...), custom_call_target="tpu_custom_call" | custom-call | flops 7360000000 | bytes 1024 | tf_op jit(solution)/shard_map/pallas_call | solution.py:59
  179.1 3.3 shard_map.242
  182.4 6.5 %shard_map.243.refs_4_ = bf16[2,2,4,96,768]{4,3,2,1,0:T(8,128)(2,1)} custom-call(s32[2]{0:T(128)} %pad_add_fusion.1.refs_0_.here_ref, bf16[1024,768]{1,0:T(8,128)(2,1)} %get-tuple-element.115.refs_2_.u_ref.refs_1_, bf16[1024,3072]{1,0:T(8,128)(2,1)} %get-tuple-element.130.refs_2_.refs_1_, bf16[2,2,4,96,768]{4,3,2,1,0:T(8,128)(2,1)} %get-tuple-element.127.refs_5_.refs_3_, ...), custom_call_target="tpu_custom_call" | custom-call | flops 9200000000 | bytes 1024 | tf_op jit(solution)/shard_map/pallas_call | solution.py:59
  189.4 6.9 %shard_map.244 = (bf16[2,4,96,768]{3,2,1,0:T(8,128)(2,1)}, bf16[2,4,96,768]{3,2,1,0:T(8,128)(2,1)}) custom-call(s32[2]{0:T(128)} %pad_add_fusion.1.refs_0_.here_ref, bf16[1024,768]{1,0:T(8,128)(2,1)} %get-tuple-element.131.refs_1_.refs_2_, bf16[1024,3072]{1,0:T(8,128)(2,1)} %get-tuple-element.114.h_ref.refs_2_, ...), custom_call_target="tpu_custom_call" | custom-call | flops 9200000000 | bytes 1024 | tf_op jit(solution)/shard_map/pallas_call | solution.py:59
  196.4 8.1 %shard_map.245 = (bf16[2,4,96,768]{3,2,1,0:T(8,128)(2,1)}, bf16[2,4,96,768]{3,2,1,0:T(8,128)(2,1)}) custom-call(s32[2]{0:T(128)} %pad_add_fusion.1.refs_0_.here_ref, bf16[1024,768]{1,0:T(8,128)(2,1)} %get-tuple-element.115.refs_2_.u_ref.refs_1_, bf16[1024,3072]{1,0:T(8,128)(2,1)} %get-tuple-element.130.refs_2_.refs_1_, ...), custom_call_target="tpu_custom_call" | custom-call | flops 9200000000 | bytes 1024 | tf_op jit(solution)/shard_map/pallas_call | solution.py:59
  204.9 1.5 collective-permute-start.29
  206.4 18.3 %shard_map.246 = (bf16[1024,768]{1,0:T(8,128)(2,1)}, bf16[1024,1024]{1,0:T(8,128)(2,1)}, f32[8,768]{1,0:T(8,128)}) custom-call(s32[2]{0:T(128)} %pad_add_fusion.1.refs_0_.here_ref, bf16[1024,3072]{1,0:T(8,128)(2,1)} %get-tuple-element.130.refs_2_.refs_1_, bf16[1024,768]{1,0:T(8,128)(2,1)} %get-tuple-element.131.refs_1_.refs_2_, ...), custom_call_target="tpu_custom_call" | custom-call | flops 3220000000 | bytes 1024 | tf_op jit(solution)/shard_map/pallas_call | solution.py:59
  224.7 11.0 %shard_map.247 = (bf16[2,4,96,768]{3,2,1,0:T(8,128)(2,1)}, f32[8,576]{1,0:T(8,128)}, bf16[2,512,640]{2,1,0:T(8,128)(2,1)}) custom-call(s32[2]{0:T(128)} %pad_add_fusion.1.refs_0_.here_ref, bf16[2,512,576]{2,1,0:T(8,128)(2,1)} %get-tuple-element.141.refs_1_, bf16[2,3,512,512]{3,2,1,0:T(8,128)(2,1)} %get-tuple-element.142.refs_2_, ...), custom_call_target="tpu_custom_call" | custom-call | flops 2529999872 | bytes 1024 | tf_op jit(solution)/shard_map/pallas_call | solution.py:59
  235.8 2.5 shard_map.249
  238.4 1.1 collective-permute-start.31
  239.4 1.0 collective-permute-start.32
  240.4 11.2 %shard_map.250 = (bf16[4,96,768]{2,1,0:T(8,128)(2,1)}, bf16[4,96,768]{2,1,0:T(8,128)(2,1)}, f32[8,576]{1,0:T(8,128)}, bf16[2,512,640]{2,1,0:T(8,128)(2,1)}) custom-call(s32[2]{0:T(128)} %pad_add_fusion.1.refs_0_.here_ref, bf16[2,512,576]{2,1,0:T(8,128)(2,1)} %get-tuple-element.152.refs_1_, bf16[2,3,512,512]{3,2,1,0:T(8,128)(2,1)} %get-tuple-element.153.refs_2_, ...), custom_call_target="tpu_custom_call" | custom-call | flops 2529999872 | bytes 1024 | tf_op jit(solution)/shard_map/pallas_call | solution.py:59
  251.6 1.7 shard_map.251
  253.3 1.0 collective-permute-start.36
  257.1 3.0 shard_map.253.refs_7_
  260.1 4.4 %all-to-all-start.3 = ((bf16[4,96,1536]{2,1,0:T(8,128)(2,1)}), bf16[4,96,1536]{2,1,0:T(8,128)(2,1)}, u32[]{:S(2)}, u32[]{:S(2)}) async-start(bf16[4,96,1536]{2,1,0:T(8,128)(2,1)} %shard_map.253.refs_7_), calls=%async_computation.3 | async-start | bytes 2359296 | tf_op jit(solution)/shard_map/all_to_all | solution.py:697
  264.6 11.0 %shard_map.254 = (bf16[2,4,96,768]{3,2,1,0:T(8,128)(2,1)}, f32[8,576]{1,0:T(8,128)}, bf16[2,512,640]{2,1,0:T(8,128)(2,1)}) custom-call(s32[2]{0:T(128)} %pad_add_fusion.1.refs_0_.here_ref, bf16[2,512,576]{2,1,0:T(8,128)(2,1)} %get-tuple-element.138.refs_1_, bf16[2,3,512,512]{3,2,1,0:T(8,128)(2,1)} %get-tuple-element.139.refs_2_, ...), custom_call_target="tpu_custom_call" | custom-call | flops 2529999872 | bytes 1024 | tf_op jit(solution)/shard_map/pallas_call | solution.py:59
  276.2 2.0 shard_map.256.refs_8_
  278.2 1.5 collective-permute-start.41
  279.7 11.2 %shard_map.257 = (bf16[4,96,768]{2,1,0:T(8,128)(2,1)}, bf16[4,96,768]{2,1,0:T(8,128)(2,1)}, f32[8,576]{1,0:T(8,128)}, bf16[2,512,640]{2,1,0:T(8,128)(2,1)}) custom-call(s32[2]{0:T(128)} %pad_add_fusion.1.refs_0_.here_ref, bf16[2,512,576]{2,1,0:T(8,128)(2,1)} %get-tuple-element.128.refs_1_, bf16[2,3,512,512]{3,2,1,0:T(8,128)(2,1)} %get-tuple-element.129.refs_2_, ...), custom_call_target="tpu_custom_call" | custom-call | flops 2529999872 | bytes 1024 | tf_op jit(solution)/shard_map/pallas_call | solution.py:59
  290.9 1.1 collective-permute-start.40
  292.0 10.2 %shard_map.258 = (bf16[2,128,768]{2,1,0:T(8,128)(2,1)}, bf16[2,128,768]{2,1,0:T(8,128)(2,1)}, bf16[2,128,768]{2,1,0:T(8,128)(2,1)}, bf16[2,128,768]{2,1,0:T(8,128)(2,1)}) custom-call(bf16[1024,640]{1,0:T(8,128)(2,1)} %bitcast.63, bf16[1024,640]{1,0:T(8,128)(2,1)} %bitcast.62, bf16[1024,640]{1,0:T(8,128)(2,1)} %bitcast.61, bf16[1024,640]{1,0:T(8,128)(2,1)} %bitcast.60, ...), custom_call_target="tpu_custom_call" | custom-call | flops 1840000000 | bytes 1024 | tf_op jit(solution)/shard_map/pallas_call | solution.py:59
  302.5 1.0 collective-permute-start.44
  305.1 1.7 collective-permute-done.40.refs_0_
  307.9 3.1 shard_map.260
  311.0 2.0 collective-permute-start.45
  313.0 2.4 collective-permute-start.46
  315.3 1.5 collective-permute-start.47
  316.8 2.3 convert_reduce_fusion
  319.1 3.7 %collective-permute-done.39.refs_4_ = bf16[2,128,768]{2,1,0:T(8,128)(2,1)} collective-permute-done((bf16[2,128,768]{2,1,0:T(8,128)(2,1)}, bf16[2,128,768]{2,1,0:T(8,128)(2,1)}, u32[]{:S(2)}, u32[]{:S(2)}) %collective-permute-start.39) | collective-permute-done | bytes 393248 | tf_op jit(solution)/shard_map/ppermute | solution.py:694
  322.8 3.3 shard_map.261
  326.1 1.9 slice_bitcast_fusion
  328.0 1.6 shard_map.262
  (210 shorter events, 28.0 us)
Async XLA Ops:
  0.6 14.4 %copy-start = (s32[8,512]{1,0:T(8,128)S(1)}, s32[8,512]{1,0:T(8,128)}, u32[]{:S(2)}) copy-start(s32[8,512]{1,0:T(8,128)} %param.25) | copy-start | bytes 49156
  2.7 12.2 %copy-start.33 = (s32[8]{0:T(128)S(1)}, s32[8]{0:T(128)}, u32[]{:S(2)}) copy-start(s32[8]{0:T(128)} %param.24) | copy-start | bytes 100
  2.7 12.3 %copy-start.27 = (bf16[12,8]{0,1:T(8,128)(2,1)S(1)}, bf16[12,8]{0,1:T(8,128)(2,1)}, u32[]{:S(2)}) copy-start(bf16[12,8]{0,1:T(8,128)(2,1)} %param.20) | copy-start | bytes 580
  2.7 12.7 %copy-start.30 = (bf16[2,96]{1,0:T(2,128)(2,1)S(1)}, bf16[2,96]{1,0:T(2,128)(2,1)}, u32[]{:S(2)}) copy-start(bf16[2,96]{1,0:T(2,128)(2,1)} %param.22) | copy-start | bytes 1156
  2.7 12.8 %copy-start.28 = (bf16[4,96]{1,0:T(4,128)(2,1)S(1)}, bf16[4,96]{1,0:T(4,128)(2,1)}, u32[]{:S(2)}) copy-start(bf16[4,96]{1,0:T(4,128)(2,1)} %param.23) | copy-start | bytes 2308
  2.7 13.3 %copy-start.23 = (bf16[768,96]{0,1:T(8,128)(2,1)S(1)}, bf16[768,96]{0,1:T(8,128)(2,1)}, u32[]{:S(2)}) copy-start(bf16[768,96]{0,1:T(8,128)(2,1)} %param.21) | copy-start | bytes 442372
  2.8 15.1 %collective-permute-start.5 = (bf16[96,640]{1,0:T(8,128)(2,1)S(1)}, bf16[96,640]{1,0:T(8,128)(2,1)S(1)}, u32[]{:S(2)}, u32[]{:S(2)}) collective-permute-start(bf16[96,640]{1,0:T(8,128)(2,1)S(1)} %shard_map.223.refs_0_), channel_id=1, source_target_pairs={{24,0},{28,4},{0,8},{4,12},{8,16},{12,20},{16,24},{20,28},{25,1},{... | collective-permute-start | bytes 368648 | tf_op jit(solution)/shard_map/ppermute | solution.py:714
  5.8 12.8 %collective-permute-start.4 = (bf16[96,640]{1,0:T(8,128)(2,1)S(1)}, bf16[96,640]{1,0:T(8,128)(2,1)S(1)}, u32[]{:S(2)}, u32[]{:S(2)}) collective-permute-start(bf16[96,640]{1,0:T(8,128)(2,1)S(1)} %shard_map.223.refs_0_), channel_id=1, source_target_pairs={{16,0},{20,4},{24,8},{28,12},{0,16},{4,20},{8,24},{12,28},{17,1},{... | collective-permute-start | bytes 368648 | tf_op jit(solution)/shard_map/ppermute | solution.py:714
  8.4 10.2 %collective-permute-start.3 = (bf16[96,640]{1,0:T(8,128)(2,1)S(1)}, bf16[96,640]{1,0:T(8,128)(2,1)S(1)}, u32[]{:S(2)}, u32[]{:S(2)}) collective-permute-start(bf16[96,640]{1,0:T(8,128)(2,1)S(1)} %shard_map.223.refs_0_), channel_id=1, source_target_pairs={{8,0},{12,4},{16,8},{20,12},{24,16},{28,20},{0,24},{4,28},{9,1},{1... | collective-permute-start | bytes 368648 | tf_op jit(solution)/shard_map/ppermute | solution.py:714
  13.3 24.3 %collective-permute-start.1 = (bf16[2,128,768]{2,1,0:T(8,128)(2,1)S(1)}, bf16[2,128,768]{2,1,0:T(8,128)(2,1)}, u32[]{:S(2)}, u32[]{:S(2)}) collective-permute-start(bf16[2,128,768]{2,1,0:T(8,128)(2,1)S(1)} %get-tuple-element.101), channel_id=1, source_target_pairs={{0,2},{1,3},{2,0},{3,1},{4,6},{5,7},{6,4},{7,5},{8,10},{9,11},{10,... | collective-permute-start | bytes 1179656 | tf_op jit(solution)/shard_map/ppermute | solution.py:694
  14.8 22.7 %collective-permute-start.2 = (bf16[2,128,768]{2,1,0:T(8,128)(2,1)S(1)}, bf16[2,128,768]{2,1,0:T(8,128)(2,1)}, u32[]{:S(2)}, u32[]{:S(2)}) collective-permute-start(bf16[2,128,768]{2,1,0:T(8,128)(2,1)S(1)} %get-tuple-element.102), channel_id=1, source_target_pairs={{0,3},{1,2},{2,1},{3,0},{4,7},{5,6},{6,5},{7,4},{8,11},{9,10},{10,... | collective-permute-start | bytes 1179656 | tf_op jit(solution)/shard_map/ppermute | solution.py:694
  15.9 18.5 %copy-start.6 = (bf16[2,512,64]{2,1,0:T(8,128)(2,1)}, bf16[2,512,64]{2,1,0:T(8,128)(2,1)S(1)}, u32[]{:S(2)}) copy-start(bf16[2,512,64]{2,1,0:T(8,128)(2,1)S(1)} %fusion.3.refs_4_.refs_7_) | copy-start | bytes 393220
  16.1 18.3 %copy-start.11 = (s32[1,1024]{1,0:T(1,128)}, s32[1,1024]{1,0:T(1,128)S(1)}, u32[]{:S(2)}) copy-start(s32[1,1024]{1,0:T(1,128)S(1)} %add_select_fusion.refs_7_.code_ref) | copy-start | bytes 12292
  17.1 17.2 %copy-start.3 = (bf16[4,96,768]{2,1,0:T(8,128)(2,1)}, bf16[4,96,768]{2,1,0:T(8,128)(2,1)S(1)}, u32[]{:S(2)}) copy-start(bf16[4,96,768]{2,1,0:T(8,128)(2,1)S(1)} %shard_map.225.refs_6_.refs_5_.refs_0_) | copy-start | bytes 1769476
  17.9 19.6 %collective-permute-start = (bf16[2,128,768]{2,1,0:T(8,128)(2,1)S(1)}, bf16[2,128,768]{2,1,0:T(8,128)(2,1)}, u32[]{:S(2)}, u32[]{:S(2)}) collective-permute-start(bf16[2,128,768]{2,1,0:T(8,128)(2,1)S(1)} %get-tuple-element.100.refs_4_), channel_id=1, source_target_pairs={{0,1},{1,0},{2,3},{3,2},{4,5},{5,4},{6,7},{7,6},{8,9},{9,8},{10,11... | collective-permute-start | bytes 1179656 | tf_op jit(solution)/shard_map/ppermute | solution.py:694
  20.6 13.7 %collective-permute-start.6 = (bf16[4,96,640]{2,1,0:T(8,128)(2,1)S(1)}, bf16[4,96,640]{2,1,0:T(8,128)(2,1)S(1)}, u32[]{:S(2)}, u32[]{:S(2)}) collective-permute-start(bf16[4,96,640]{2,1,0:T(8,128)(2,1)S(1)} %copy-done.5), channel_id=1, source_target_pairs={{0,4},{4,0},{8,12},{12,8},{16,20},{20,16},{24,28},{28,24},{1,5},{5... | collective-permute-start | bytes 1474568 | tf_op jit(solution)/shard_map/ppermute | solution.py:694
  22.1 25.1 %all-to-all-start = ((bf16[4,96,1024]{2,1,0:T(8,128)(2,1)}), bf16[4,96,1024]{2,1,0:T(8,128)(2,1)}, u32[]{:S(2)}, u32[]{:S(2)}) async-start(bf16[4,96,1024]{2,1,0:T(8,128)(2,1)} %shard_map.228.refs_8_), calls=%async_computation | async-start | bytes 1572864 | tf_op jit(solution)/shard_map/all_to_all | solution.py:697
  36.0 25.9 %collective-permute-start.8 = (bf16[768,640]{1,0:T(8,128)(2,1)}, bf16[768,640]{1,0:T(8,128)(2,1)}, u32[]{:S(2)}, u32[]{:S(2)}) collective-permute-start(bf16[768,640]{1,0:T(8,128)(2,1)} %shard_map.227.refs_4_.refs_5_), channel_id=1, source_target_pairs={{0,2},{1,3},{2,0},{3,1},{4,6},{5,7},{6,4},{7,5},{8,10},{9,11},{10,... | collective-permute-start | bytes 2949128 | tf_op jit(solution)/shard_map/ppermute | solution.py:694
  37.6 15.7 %collective-permute-start.7 = (bf16[768,640]{1,0:T(8,128)(2,1)}, bf16[768,640]{1,0:T(8,128)(2,1)}, u32[]{:S(2)}, u32[]{:S(2)}) collective-permute-start(bf16[768,640]{1,0:T(8,128)(2,1)} %shard_map.227.refs_4_.refs_5_), channel_id=1, source_target_pairs={{0,1},{1,0},{2,3},{3,2},{4,5},{5,4},{6,7},{7,6},{8,9},{9,8},{10,11... | collective-permute-start | bytes 2949128 | tf_op jit(solution)/shard_map/ppermute | solution.py:694
  47.2 20.0 %collective-permute-start.9 = (bf16[4,96,1024]{2,1,0:T(8,128)(2,1)}, bf16[4,96,1024]{2,1,0:T(8,128)(2,1)}, u32[]{:S(2)}, u32[]{:S(2)}) collective-permute-start(bf16[4,96,1024]{2,1,0:T(8,128)(2,1)} %shard_map.230.refs_5_.refs_1_.refs_7_.refs_6_), channel_id=1, source_target_pairs={{0,4},{4,0},{8,12},{12,8},{16,20},{20,16},{24,28},{28,24},{1,5},{5... | collective-permute-start | bytes 2359304 | tf_op jit(solution)/shard_map/ppermute | solution.py:694
  48.4 29.4 %all-to-all-start.1 = ((bf16[4,96,768]{2,1,0:T(8,128)(2,1)}), bf16[4,96,768]{2,1,0:T(8,128)(2,1)S(1)}, u32[]{:S(2)}, u32[]{:S(2)}) async-start(bf16[4,96,768]{2,1,0:T(8,128)(2,1)} %shard_map.234), calls=%async_computation.1 | async-start | bytes 1179648 | tf_op jit(solution)/shard_map/all_to_all | solution.py:697
  52.4 25.5 %collective-permute-start.11 = (bf16[4,96,1024]{2,1,0:T(8,128)(2,1)}, bf16[4,96,1024]{2,1,0:T(8,128)(2,1)}, u32[]{:S(2)}, u32[]{:S(2)}) collective-permute-start(bf16[4,96,1024]{2,1,0:T(8,128)(2,1)} %shard_map.230.refs_5_.refs_1_.refs_7_.refs_6_), channel_id=1, source_target_pairs={{0,2},{1,3},{2,0},{3,1},{4,6},{5,7},{6,4},{7,5},{8,10},{9,11},{10,... | collective-permute-start | bytes 2359304 | tf_op jit(solution)/shard_map/ppermute | solution.py:694
  67.2 13.5 %collective-permute-start.10 = (bf16[768,640]{1,0:T(8,128)(2,1)}, bf16[768,640]{1,0:T(8,128)(2,1)}, u32[]{:S(2)}, u32[]{:S(2)}) collective-permute-start(bf16[768,640]{1,0:T(8,128)(2,1)} %get-tuple-element.106.refs_1_.refs_7_), channel_id=1, source_target_pairs={{0,1},{1,0},{2,3},{3,2},{4,5},{5,4},{6,7},{7,6},{8,9},{9,8},{10,11... | collective-permute-start | bytes 2949128 | tf_op jit(solution)/shard_map/ppermute | solution.py:694
  67.2 26.5 %collective-permute-start.14 = (bf16[4,96,1024]{2,1,0:T(8,128)(2,1)}, bf16[4,96,1024]{2,1,0:T(8,128)(2,1)}, u32[]{:S(2)}, u32[]{:S(2)}) collective-permute-start(bf16[4,96,1024]{2,1,0:T(8,128)(2,1)} %get-tuple-element.107.refs_5_.refs_8_.refs_7_), channel_id=1, source_target_pairs={{0,2},{1,3},{2,0},{3,1},{4,6},{5,7},{6,4},{7,5},{8,10},{9,11},{10,... | collective-permute-start | bytes 2359304 | tf_op jit(solution)/shard_map/ppermute | solution.py:694
  78.7 14.8 %collective-permute-start.15 = (bf16[4,96,768]{2,1,0:T(8,128)(2,1)}, bf16[4,96,768]{2,1,0:T(8,128)(2,1)}, u32[]{:S(2)}, u32[]{:S(2)}) collective-permute-start(bf16[4,96,768]{2,1,0:T(8,128)(2,1)} %get-tuple-element.109.refs_5_.refs_0_), channel_id=1, source_target_pairs={{0,4},{4,0},{8,12},{12,8},{16,20},{20,16},{24,28},{28,24},{1,5},{5... | collective-permute-start | bytes 1769480 | tf_op jit(solution)/shard_map/ppermute | solution.py:694
  80.2 15.0 %collective-permute-start.12 = (bf16[4,96,1024]{2,1,0:T(8,128)(2,1)}, bf16[4,96,1024]{2,1,0:T(8,128)(2,1)}, u32[]{:S(2)}, u32[]{:S(2)}) collective-permute-start(bf16[4,96,1024]{2,1,0:T(8,128)(2,1)} %shard_map.230.refs_5_.refs_1_.refs_7_.refs_6_), channel_id=1, source_target_pairs={{0,1},{1,0},{2,3},{3,2},{4,5},{5,4},{6,7},{7,6},{8,9},{9,8},{10,11... | collective-permute-start | bytes 2359304 | tf_op jit(solution)/shard_map/ppermute | solution.py:694
  80.2 16.1 %collective-permute-start.13 = (bf16[4,96,1024]{2,1,0:T(8,128)(2,1)}, bf16[4,96,1024]{2,1,0:T(8,128)(2,1)}, u32[]{:S(2)}, u32[]{:S(2)}) collective-permute-start(bf16[4,96,1024]{2,1,0:T(8,128)(2,1)} %get-tuple-element.107.refs_5_.refs_8_.refs_7_), channel_id=1, source_target_pairs={{0,1},{1,0},{2,3},{3,2},{4,5},{5,4},{6,7},{7,6},{8,9},{9,8},{10,11... | collective-permute-start | bytes 2359304 | tf_op jit(solution)/shard_map/ppermute | solution.py:694
  80.7 15.6 %collective-permute-start.16 = (bf16[4,96,1024]{2,1,0:T(8,128)(2,1)}, bf16[4,96,1024]{2,1,0:T(8,128)(2,1)}, u32[]{:S(2)}, u32[]{:S(2)}) collective-permute-start(bf16[4,96,1024]{2,1,0:T(8,128)(2,1)} %get-tuple-element.110.refs_6_.refs_11_.refs_10_), channel_id=1, source_target_pairs={{0,1},{1,0},{2,3},{3,2},{4,5},{5,4},{6,7},{7,6},{8,9},{9,8},{10,11... | collective-permute-start | bytes 2359304 | tf_op jit(solution)/shard_map/ppermute | solution.py:694
  93.7 3.1 collective-permute-start.17
  93.7 25.3 %collective-permute-start.20 = (bf16[4,96,768]{2,1,0:T(8,128)(2,1)S(1)}, bf16[4,96,768]{2,1,0:T(8,128)(2,1)}, u32[]{:S(2)}, u32[]{:S(2)}) collective-permute-start(bf16[4,96,768]{2,1,0:T(8,128)(2,1)S(1)} %copy-done.17), channel_id=1, source_target_pairs={{0,2},{1,3},{2,0},{3,1},{4,6},{5,7},{6,4},{7,5},{8,10},{9,11},{10,... | collective-permute-start | bytes 1769480 | tf_op jit(solution)/shard_map/ppermute | solution.py:694
  95.2 26.9 %collective-permute-start.21 = (bf16[4,96,768]{2,1,0:T(8,128)(2,1)}, bf16[4,96,768]{2,1,0:T(8,128)(2,1)}, u32[]{:S(2)}, u32[]{:S(2)}) collective-permute-start(bf16[4,96,768]{2,1,0:T(8,128)(2,1)} %get-tuple-element.113.refs_15_.refs_1_), channel_id=1, source_target_pairs={{0,2},{1,3},{2,0},{3,1},{4,6},{5,7},{6,4},{7,5},{8,10},{9,11},{10,... | collective-permute-start | bytes 1769480 | tf_op jit(solution)/shard_map/ppermute | solution.py:694
  96.3 26.4 %collective-permute-start.18 = (bf16[4,96,768]{2,1,0:T(8,128)(2,1)S(1)}, bf16[4,96,768]{2,1,0:T(8,128)(2,1)}, u32[]{:S(2)}, u32[]{:S(2)}) collective-permute-start(bf16[4,96,768]{2,1,0:T(8,128)(2,1)S(1)} %copy-done.17), channel_id=1, source_target_pairs={{0,1},{1,0},{2,3},{3,2},{4,5},{5,4},{6,7},{7,6},{8,9},{9,8},{10,11... | collective-permute-start | bytes 1769480 | tf_op jit(solution)/shard_map/ppermute | solution.py:694
  96.3 26.4 %collective-permute-start.19 = (bf16[4,96,768]{2,1,0:T(8,128)(2,1)}, bf16[4,96,768]{2,1,0:T(8,128)(2,1)}, u32[]{:S(2)}, u32[]{:S(2)}) collective-permute-start(bf16[4,96,768]{2,1,0:T(8,128)(2,1)} %get-tuple-element.113.refs_15_.refs_1_), channel_id=1, source_target_pairs={{0,1},{1,0},{2,3},{3,2},{4,5},{5,4},{6,7},{7,6},{8,9},{9,8},{10,11... | collective-permute-start | bytes 1769480 | tf_op jit(solution)/shard_map/ppermute | solution.py:694
  122.2 2.3 collective-permute-start.22
  122.2 3.2 collective-permute-start.23
  125.3 18.5 %copy-start.29 = (f32[128]{0:T(128)S(1)}, f32[128]{0:T(128)}, u32[]{:S(2)}) copy-start(f32[128]{0:T(128)} %param.27) | copy-start | bytes 1540
  125.3 18.8 %copy-start.26 = (s32[256]{0:T(256)S(1)}, s32[256]{0:T(256)}, u32[]{:S(2)}) copy-start(s32[256]{0:T(256)} %param.26) | copy-start | bytes 3076
  140.8 16.2 %all-to-all-start.2 = ((bf16[32,8,768]{2,1,0:T(8,128)(2,1)}), bf16[32,8,768]{2,1,0:T(8,128)(2,1)S(1)}, u32[]{:S(2)}, u32[]{:S(2)}) async-start(bf16[32,8,768]{2,1,0:T(8,128)(2,1)} %get-tuple-element.123), calls=%async_computation.2 | async-start | bytes 786432 | tf_op jit(solution)/shard_map/all_to_all | solution.py:986
  146.8 31.6 %collective-permute-start.24 = (bf16[2,128,768]{2,1,0:T(8,128)(2,1)}, bf16[2,128,768]{2,1,0:T(8,128)(2,1)S(1)}, u32[]{:S(2)}, u32[]{:S(2)}) collective-permute-start(bf16[2,128,768]{2,1,0:T(8,128)(2,1)} %get-tuple-element.120), channel_id=1, source_target_pairs={{0,1},{1,0},{2,3},{3,2},{4,5},{5,4},{6,7},{7,6},{8,9},{9,8},{10,11... | collective-permute-start | bytes 1179656 | tf_op jit(solution)/shard_map/ppermute | solution.py:694
  147.2 31.2 %collective-permute-start.25 = (bf16[2,128,768]{2,1,0:T(8,128)(2,1)}, bf16[2,128,768]{2,1,0:T(8,128)(2,1)}, u32[]{:S(2)}, u32[]{:S(2)}) collective-permute-start(bf16[2,128,768]{2,1,0:T(8,128)(2,1)} %get-tuple-element.121), channel_id=1, source_target_pairs={{0,2},{1,3},{2,0},{3,1},{4,6},{5,7},{6,4},{7,5},{8,10},{9,11},{10,... | collective-permute-start | bytes 1179656 | tf_op jit(solution)/shard_map/ppermute | solution.py:694
  148.9 29.5 %collective-permute-start.26 = (bf16[2,128,768]{2,1,0:T(8,128)(2,1)}, bf16[2,128,768]{2,1,0:T(8,128)(2,1)}, u32[]{:S(2)}, u32[]{:S(2)}) collective-permute-start(bf16[2,128,768]{2,1,0:T(8,128)(2,1)} %get-tuple-element.122), channel_id=1, source_target_pairs={{0,3},{1,2},{2,1},{3,0},{4,7},{5,6},{6,5},{7,4},{8,11},{9,10},{10,... | collective-permute-start | bytes 1179656 | tf_op jit(solution)/shard_map/ppermute | solution.py:694
  178.3 11.1 %collective-permute-start.28 = (bf16[2,2,4,96,768]{4,3,2,1,0:T(8,128)(2,1)}, bf16[2,2,4,96,768]{4,3,2,1,0:T(8,128)(2,1)}, u32[]{:S(2)}, u32[]{:S(2)}) collective-permute-start(bf16[2,2,4,96,768]{4,3,2,1,0:T(8,128)(2,1)} %get-tuple-element.127.refs_5_.refs_3_), channel_id=1, source_target_pairs={{0,1},{1,0},{2,3},{3,2},{4,5},{5,4},{6,7},{7,6},{8,9},{9,8},{10,11... | collective-permute-start | bytes 7077896 | tf_op jit(solution)/shard_map/ppermute | solution.py:694
  189.0 7.4 %collective-permute-start.27 = (bf16[2,2,4,96,768]{4,3,2,1,0:T(8,128)(2,1)}, bf16[2,2,4,96,768]{4,3,2,1,0:T(8,128)(2,1)}, u32[]{:S(2)}, u32[]{:S(2)}) collective-permute-start(bf16[2,2,4,96,768]{4,3,2,1,0:T(8,128)(2,1)} %shard_map.243.refs_4_), channel_id=1, source_target_pairs={{0,1},{1,0},{2,3},{3,2},{4,5},{5,4},{6,7},{7,6},{8,9},{9,8},{10,11... | collective-permute-start | bytes 7077896 | tf_op jit(solution)/shard_map/ppermute | solution.py:694
  204.4 31.4 %collective-permute-start.30 = (bf16[2,4,96,768]{3,2,1,0:T(8,128)(2,1)}, bf16[2,4,96,768]{3,2,1,0:T(8,128)(2,1)}, u32[]{:S(2)}, u32[]{:S(2)}) collective-permute-start(bf16[2,4,96,768]{3,2,1,0:T(8,128)(2,1)} %get-tuple-element.135.refs_14_.refs_7_), channel_id=1, source_target_pairs={{0,2},{1,3},{2,0},{3,1},{4,6},{5,7},{6,4},{7,5},{8,10},{9,11},{10,... | collective-permute-start | bytes 3538952 | tf_op jit(solution)/shard_map/ppermute | solution.py:694
  204.9 30.9 %collective-permute-start.29 = (bf16[2,4,96,768]{3,2,1,0:T(8,128)(2,1)}, bf16[2,4,96,768]{3,2,1,0:T(8,128)(2,1)}, u32[]{:S(2)}, u32[]{:S(2)}) collective-permute-start(bf16[2,4,96,768]{3,2,1,0:T(8,128)(2,1)} %get-tuple-element.134.refs_4_), channel_id=1, source_target_pairs={{0,4},{4,0},{8,12},{12,8},{16,20},{20,16},{24,28},{28,24},{1,5},{5... | collective-permute-start | bytes 3538952 | tf_op jit(solution)/shard_map/ppermute | solution.py:694
  235.7 4.7 %collective-permute-start.33 = (bf16[2,4,96,768]{3,2,1,0:T(8,128)(2,1)}, bf16[2,4,96,768]{3,2,1,0:T(8,128)(2,1)}, u32[]{:S(2)}, u32[]{:S(2)}) collective-permute-start(bf16[2,4,96,768]{3,2,1,0:T(8,128)(2,1)} %get-tuple-element.143.refs_2_), channel_id=1, source_target_pairs={{0,1},{1,0},{2,3},{3,2},{4,5},{5,4},{6,7},{7,6},{8,9},{9,8},{10,11... | collective-permute-start | bytes 3538952 | tf_op jit(solution)/shard_map/ppermute | solution.py:694
  238.4 18.0 %collective-permute-start.31 = (bf16[4,96,768]{2,1,0:T(8,128)(2,1)}, bf16[4,96,768]{2,1,0:T(8,128)(2,1)S(1)}, u32[]{:S(2)}, u32[]{:S(2)}) collective-permute-start(bf16[4,96,768]{2,1,0:T(8,128)(2,1)} %get-tuple-element.147.refs_8_), channel_id=1, source_target_pairs={{0,2},{1,3},{2,0},{3,1},{4,6},{5,7},{6,4},{7,5},{8,10},{9,11},{10,... | collective-permute-start | bytes 1769480 | tf_op jit(solution)/shard_map/ppermute | solution.py:694
  239.4 16.9 %collective-permute-start.32 = (bf16[4,96,768]{2,1,0:T(8,128)(2,1)}, bf16[4,96,768]{2,1,0:T(8,128)(2,1)}, u32[]{:S(2)}, u32[]{:S(2)}) collective-permute-start(bf16[4,96,768]{2,1,0:T(8,128)(2,1)} %get-tuple-element.148.refs_9_), channel_id=1, source_target_pairs={{0,4},{4,0},{8,12},{12,8},{16,20},{20,16},{24,28},{28,24},{1,5},{5... | collective-permute-start | bytes 1769480 | tf_op jit(solution)/shard_map/ppermute | solution.py:694
  253.3 1.5 collective-permute-start.34
  253.3 22.8 %collective-permute-start.36 = (bf16[4,96,768]{2,1,0:T(8,128)(2,1)}, bf16[4,96,768]{2,1,0:T(8,128)(2,1)}, u32[]{:S(2)}, u32[]{:S(2)}) collective-permute-start(bf16[4,96,768]{2,1,0:T(8,128)(2,1)} %get-tuple-element.162), channel_id=1, source_target_pairs={{0,4},{4,0},{8,12},{12,8},{16,20},{20,16},{24,28},{28,24},{1,5},{5... | collective-permute-start | bytes 1769480 | tf_op jit(solution)/shard_map/ppermute | solution.py:694
  255.7 46.6 %collective-permute-start.42 = (f32[16,768]{1,0:T(8,128)S(1)}, f32[16,768]{1,0:T(8,128)S(1)}, u32[]{:S(2)}, u32[]{:S(2)}) collective-permute-start(f32[16,768]{1,0:T(8,128)S(1)} %pad_maximum_fusion), channel_id=1, source_target_pairs={{0,2},{1,3},{2,0},{3,1},{4,6},{5,7},{6,4},{7,5},{8,10},{9,11},{10,... | collective-permute-start | bytes 147464 | tf_op jit(solution)/shard_map/ppermute | solution.py:694
  260.1 45.0 %all-to-all-start.3 = ((bf16[4,96,1536]{2,1,0:T(8,128)(2,1)}), bf16[4,96,1536]{2,1,0:T(8,128)(2,1)}, u32[]{:S(2)}, u32[]{:S(2)}) async-start(bf16[4,96,1536]{2,1,0:T(8,128)(2,1)} %shard_map.253.refs_7_), calls=%async_computation.3 | async-start | bytes 2359296 | tf_op jit(solution)/shard_map/all_to_all | solution.py:697
  275.6 26.7 %collective-permute-start.43 = (f32[8,576]{1,0:T(8,128)}, f32[8,576]{1,0:T(8,128)S(1)}, u32[]{:S(2)}, u32[]{:S(2)}) collective-permute-start(f32[8,576]{1,0:T(8,128)} %get-tuple-element.176), channel_id=1, source_target_pairs={{0,1},{1,0},{2,3},{3,2},{4,5},{5,4},{6,7},{7,6},{8,9},{9,8},{10,11... | collective-permute-start | bytes 55304 | tf_op jit(solution)/shard_map/ppermute | solution.py:694
  275.7 4.1 %collective-permute-start.35 = (bf16[2,4,96,768]{3,2,1,0:T(8,128)(2,1)}, bf16[2,4,96,768]{3,2,1,0:T(8,128)(2,1)}, u32[]{:S(2)}, u32[]{:S(2)}) collective-permute-start(bf16[2,4,96,768]{3,2,1,0:T(8,128)(2,1)} %get-tuple-element.161.refs_1_), channel_id=1, source_target_pairs={{0,1},{1,0},{2,3},{3,2},{4,5},{5,4},{6,7},{7,6},{8,9},{9,8},{10,11... | collective-permute-start | bytes 3538952 | tf_op jit(solution)/shard_map/ppermute | solution.py:694
  278.2 26.2 %collective-permute-start.41 = (bf16[4,96,768]{2,1,0:T(8,128)(2,1)}, bf16[4,96,768]{2,1,0:T(8,128)(2,1)S(1)}, u32[]{:S(2)}, u32[]{:S(2)}) collective-permute-start(bf16[4,96,768]{2,1,0:T(8,128)(2,1)} %shard_map.256.refs_8_), channel_id=1, source_target_pairs={{0,2},{1,3},{2,0},{3,1},{4,6},{5,7},{6,4},{7,5},{8,10},{9,11},{10,... | collective-permute-start | bytes 1769480 | tf_op jit(solution)/shard_map/ppermute | solution.py:694
  290.9 15.9 %collective-permute-start.40 = (bf16[4,96,768]{2,1,0:T(8,128)(2,1)}, bf16[4,96,768]{2,1,0:T(8,128)(2,1)}, u32[]{:S(2)}, u32[]{:S(2)}) collective-permute-start(bf16[4,96,768]{2,1,0:T(8,128)(2,1)} %get-tuple-element.172), channel_id=1, source_target_pairs={{0,4},{4,0},{8,12},{12,8},{16,20},{20,16},{24,28},{28,24},{1,5},{5... | collective-permute-start | bytes 1769480 | tf_op jit(solution)/shard_map/ppermute | solution.py:694
  292.0 10.4 %copy-start.19 = (f32[24,768]{1,0:T(8,128)S(1)}, f32[24,768]{1,0:T(8,128)}, u32[]{:S(2)}) copy-start(f32[24,768]{1,0:T(8,128)} %copy-done.18) | copy-start | bytes 221188
  302.2 5.0 %collective-permute-start.37 = (bf16[2,128,768]{2,1,0:T(8,128)(2,1)}, bf16[2,128,768]{2,1,0:T(8,128)(2,1)}, u32[]{:S(2)}, u32[]{:S(2)}) collective-permute-start(bf16[2,128,768]{2,1,0:T(8,128)(2,1)} %get-tuple-element.169), channel_id=1, source_target_pairs={{0,1},{1,0},{2,3},{3,2},{4,5},{5,4},{6,7},{7,6},{8,9},{9,8},{10,11... | collective-permute-start | bytes 1179656 | tf_op jit(solution)/shard_map/ppermute | solution.py:694
  302.5 4.8 %collective-permute-start.44 = (f32[16,768]{1,0:T(8,128)S(1)}, f32[16,768]{1,0:T(8,128)S(1)}, u32[]{:S(2)}, u32[]{:S(2)}) collective-permute-start(f32[16,768]{1,0:T(8,128)S(1)} %fusion.4.refs_4_), channel_id=1, source_target_pairs={{0,4},{4,0},{8,12},{12,8},{16,20},{20,16},{24,28},{28,24},{1,5},{5... | collective-permute-start | bytes 147464 | tf_op jit(solution)/shard_map/ppermute | solution.py:694
  303.6 15.5 %collective-permute-start.38 = (bf16[2,128,768]{2,1,0:T(8,128)(2,1)}, bf16[2,128,768]{2,1,0:T(8,128)(2,1)}, u32[]{:S(2)}, u32[]{:S(2)}) collective-permute-start(bf16[2,128,768]{2,1,0:T(8,128)(2,1)} %get-tuple-element.170), channel_id=1, source_target_pairs={{0,2},{1,3},{2,0},{3,1},{4,6},{5,7},{6,4},{7,5},{8,10},{9,11},{10,... | collective-permute-start | bytes 1179656 | tf_op jit(solution)/shard_map/ppermute | solution.py:694
  304.4 18.4 %collective-permute-start.39 = (bf16[2,128,768]{2,1,0:T(8,128)(2,1)}, bf16[2,128,768]{2,1,0:T(8,128)(2,1)}, u32[]{:S(2)}, u32[]{:S(2)}) collective-permute-start(bf16[2,128,768]{2,1,0:T(8,128)(2,1)} %get-tuple-element.171), channel_id=1, source_target_pairs={{0,3},{1,2},{2,1},{3,0},{4,7},{5,6},{6,5},{7,4},{8,11},{9,10},{10,... | collective-permute-start | bytes 1179656 | tf_op jit(solution)/shard_map/ppermute | solution.py:694
  311.0 17.0 %collective-permute-start.45 = (bf16[112,768]{1,0:T(8,128)(2,1)}, bf16[112,768]{1,0:T(8,128)(2,1)S(1)}, u32[]{:S(2)}, u32[]{:S(2)}) collective-permute-start(bf16[112,768]{1,0:T(8,128)(2,1)} %get-tuple-element.178), channel_id=1, source_target_pairs={{24,0},{28,4},{0,8},{4,12},{8,16},{12,20},{16,24},{20,28},{25,1},{... | collective-permute-start | bytes 516104 | tf_op jit(solution)/shard_map/ppermute | solution.py:714
  313.0 15.0 %collective-permute-start.46 = (bf16[112,768]{1,0:T(8,128)(2,1)}, bf16[112,768]{1,0:T(8,128)(2,1)S(1)}, u32[]{:S(2)}, u32[]{:S(2)}) collective-permute-start(bf16[112,768]{1,0:T(8,128)(2,1)} %get-tuple-element.179), channel_id=1, source_target_pairs={{16,0},{20,4},{24,8},{28,12},{0,16},{4,20},{8,24},{12,28},{17,1},{... | collective-permute-start | bytes 516104 | tf_op jit(solution)/shard_map/ppermute | solution.py:714
  315.3 12.7 %collective-permute-start.47 = (bf16[112,768]{1,0:T(8,128)(2,1)}, bf16[112,768]{1,0:T(8,128)(2,1)S(1)}, u32[]{:S(2)}, u32[]{:S(2)}) collective-permute-start(bf16[112,768]{1,0:T(8,128)(2,1)} %get-tuple-element.180), channel_id=1, source_target_pairs={{8,0},{12,4},{16,8},{20,12},{24,16},{28,20},{0,24},{4,28},{9,1},{1... | collective-permute-start | bytes 516104 | tf_op jit(solution)/shard_map/ppermute | solution.py:714
  (22 other events, 81.3 us)
